TPU v7x, 32 devices: a whole 2x2x4 slice. The times are simulated.
32 devices in a mesh: dp: 4 (over z), ctx: 2 (over x), tensor: 4 (over y, core).
Axes of the slice: x: 2, y: 2, z: 4, core: 2. Of those that a mesh axis runs over, the one named last changes fastest.
Arguments:
- tokens: bfloat16 [2, 4, 512, 2048], P(None, 'dp', 'ctx'), may hold values from -6 to 6
- doc_lengths: int32 [2, 4, 6], P(None, 'dp'), may hold values from 1 to 384, as said below
- w_query: bfloat16 [2, 2048, 1280], P(None, ('dp', 'ctx'), 'tensor'), may hold values from -0.125 to 0.125
- w_key: bfloat16 [2, 2048, 320], P(None, ('dp', 'ctx')), may hold values from -0.125 to 0.125
- w_value: bfloat16 [2, 2048, 320], P(None, ('dp', 'ctx')), may hold values from -0.125 to 0.125
- w_out: bfloat16 [2, 1280, 2048], P(None, 'tensor', ('dp', 'ctx')), may hold values from -0.625 to 0.625
- w_gate: bfloat16 [2, 2048, 5120], P(None, ('dp', 'ctx'), 'tensor'), may hold values from -0.125 to 0.125
- w_up: bfloat16 [2, 2048, 5120], P(None, ('dp', 'ctx'), 'tensor'), may hold values from -0.125 to 0.125
- w_down: bfloat16 [2, 5120, 2048], P(None, 'tensor', ('dp', 'ctx')), may hold values from -0.078125 to 0.078125
- norm_gains: bfloat16 [2, 4224], P(None, ('dp', 'ctx')), may hold values from 0.25 to 1.75
- cotangent: bfloat16 [2, 4, 512, 2048], P(None, 'dp', 'ctx'), may hold values from -6 to 6
Outputs:
- output: bfloat16 [2, 4, 512, 2048], P(None, 'dp', 'ctx')
- grad_input: float32 [2, 4, 512, 2048], P(None, 'dp', 'ctx')
- grad_query: float32 [2, 2048, 1280], P(None, ('dp', 'ctx'), 'tensor')
- grad_key: float32 [2, 2048, 320], P(None, ('dp', 'ctx'))
- grad_value: float32 [2, 2048, 320], P(None, ('dp', 'ctx'))
- grad_out: float32 [2, 1280, 2048], P(None, 'tensor', ('dp', 'ctx'))
- grad_gate: float32 [2, 2048, 5120], P(None, ('dp', 'ctx'), 'tensor')
- grad_up: float32 [2, 2048, 5120], P(None, ('dp', 'ctx'), 'tensor')
- grad_down: float32 [2, 5120, 2048], P(None, 'tensor', ('dp', 'ctx'))
- grad_gains: float32 [2, 4224], P(None, ('dp', 'ctx'))
Inputs may be any that keep to these rules, and one draw needn't show every extreme that they name: `doc_lengths`: each sequence holds 6 documents from its start, followed by padding of one token or more. One document of each sequence, at a place drawn from the seed, is exactly 384 tokens long.
All inputs are finite; a program needn't handle non-finite values.
Results may differ from a plain program's by a relative error of at most 0.034.
Values may be sent and summed in bfloat16 or wider, within the bound.
A program may use at most 320 MiB of HBM per device.

v0:
```python
import jax
import jax.numpy as jnp
from jax import lax
from jax.sharding import PartitionSpec as P

HQ = 20
HK = 5
HD = 64
LAYERS = 2


epsilon = 1e-05
rope_base = 10000.0


def product(left_side, right_side, contract):
    return lax.dot_general(
        left_side, right_side, (contract, ((), ())), preferred_element_type=jnp.float32
    )


def layout(doc_lengths, length):
    ends = jnp.cumsum(doc_lengths, axis=-1, dtype=jnp.int32)
    starts = ends - doc_lengths
    places = jnp.arange(length, dtype=jnp.int32)
    document = jnp.sum(
        (places[:, None] >= ends[..., None, :]).astype(jnp.int32), axis=-1, dtype=jnp.int32
    )
    chosen = document[..., None] == jnp.arange(doc_lengths.shape[-1], dtype=jnp.int32)
    begins = jnp.sum(jnp.where(chosen, starts[..., None, :], 0), axis=-1, dtype=jnp.int32)
    segment = jnp.where(document < doc_lengths.shape[-1], document, -1)
    return (segment, places - begins)


def rotation(position):
    half_size = HD // 2
    frequency = rope_base ** (-jnp.arange(half_size, dtype=jnp.float32) * (2.0 / HD))
    angle = position.astype(jnp.float32)[..., None, None] * frequency
    return (jnp.cos(angle), jnp.sin(angle))


def rotate(values, cosine, sine_value):
    half_size = values.shape[-1] // 2
    first_half = values[..., :half_size]
    second_half = values[..., half_size:]
    return jnp.concatenate(
        [
            first_half * cosine - second_half * sine_value,
            second_half * cosine + first_half * sine_value,
        ],
        axis=-1,
    )


def scale_of(values):
    return lax.rsqrt(jnp.mean(values * values, axis=-1, keepdims=True) + epsilon)


def norm_back(gradient, values, scaling, gain_vector):
    scaled = gradient * gain_vector
    cubed = scaling * scaling * scaling
    return scaling * scaled - values * cubed * jnp.mean(scaled * values, axis=-1, keepdims=True)


def head_pairs(pair_rows, first_pair):
    return jnp.where(first_pair[:, None, None], pair_rows[None, :, 0], pair_rows[None, :, 1])


def allowed_of(seg_query, seg_keys, place_query):
    place_keys = jnp.arange(seg_keys.shape[0], dtype=jnp.int32)
    same_doc = (seg_query[:, None] == seg_keys[None, :]) & (seg_query[:, None] >= 0)
    return same_doc & (place_keys[None, :] <= place_query[:, None])


def attend(queries, key_rows, value_rows, seg_query, seg_keys, place_query, first_pair):
    key_heads = head_pairs(key_rows, first_pair)
    value_heads = head_pairs(value_rows, first_pair)
    scores = jnp.einsum(
        "qhd,hkd->hqk", queries, key_heads, preferred_element_type=jnp.float32
    ) * HD ** (-0.5)
    allowed = allowed_of(seg_query, seg_keys, place_query)[None]
    masked = jnp.where(allowed, scores, -1e30)
    highest = jnp.max(masked, axis=-1, keepdims=True)
    exponent = jnp.where(allowed, jnp.exp(masked - highest), 0.0)
    row_total = jnp.sum(exponent, axis=-1, keepdims=True)
    live_rows = row_total > 0.0
    safe_total = jnp.where(live_rows, row_total, 1.0)
    probability = (exponent / safe_total).astype(jnp.bfloat16)
    mixed = jnp.einsum("hqk,hkd->qhd", probability, value_heads, preferred_element_type=jnp.float32)
    merged = jnp.where(live_rows, highest + jnp.log(safe_total), 0.0)
    return (mixed, merged[..., 0])


def attend_back(
    queries, key_rows, value_rows, grad_mixed, merged, seg_query, seg_keys, place_query, first_pair
):
    key_heads = head_pairs(key_rows, first_pair)
    value_heads = head_pairs(value_rows, first_pair)
    scores = jnp.einsum(
        "qhd,hkd->hqk", queries, key_heads, preferred_element_type=jnp.float32
    ) * HD ** (-0.5)
    allowed = allowed_of(seg_query, seg_keys, place_query)[None]
    probability = jnp.where(allowed, jnp.exp(scores - merged[..., None]), 0.0)
    grad_value_heads = jnp.einsum(
        "hqk,qhd->hkd",
        probability.astype(jnp.bfloat16),
        grad_mixed,
        preferred_element_type=jnp.float32,
    )
    grad_prob = jnp.einsum(
        "qhd,hkd->hqk", grad_mixed, value_heads, preferred_element_type=jnp.float32
    )
    row_delta = jnp.sum(probability * grad_prob, axis=-1, keepdims=True)
    grad_scores = (probability * (grad_prob - row_delta)).astype(jnp.bfloat16)
    grad_queries = jnp.einsum(
        "hqk,hkd->qhd", grad_scores, key_heads, preferred_element_type=jnp.float32
    ) * HD ** (-0.5)
    grad_key_heads = jnp.einsum(
        "hqk,qhd->hkd", grad_scores, queries, preferred_element_type=jnp.float32
    ) * HD ** (-0.5)
    weight_first = first_pair.astype(jnp.float32)[:, None, None]
    grad_keys = jnp.stack(
        [
            jnp.sum(grad_key_heads * weight_first, axis=0),
            jnp.sum(grad_key_heads * (1.0 - weight_first), axis=0),
        ],
        axis=1,
    )
    grad_values = jnp.stack(
        [
            jnp.sum(grad_value_heads * weight_first, axis=0),
            jnp.sum(grad_value_heads * (1.0 - weight_first), axis=0),
        ],
        axis=1,
    )
    return (grad_queries, grad_keys, grad_values)


def local(
    tokens, doc_lengths, w_query, w_key, w_value, w_out, w_gate, w_up, w_down, norm_gains, cotangent
):
    micro_count, sequences, half_rows, model_width = tokens.shape
    length = half_rows * lax.axis_size("ctx")
    row_count = sequences * half_rows
    head_count = w_query.shape[2] // HD
    group_size = HQ // HK
    tensor_rank = lax.axis_index("tensor")
    pair_start = tensor_rank * head_count // group_size
    first_pair = (
        tensor_rank * head_count + jnp.arange(head_count, dtype=jnp.int32)
    ) // group_size == pair_start
    offset = lax.axis_index("ctx") * half_rows
    place_query = offset + jnp.arange(half_rows, dtype=jnp.int32)
    segment, position = layout(doc_lengths, length)
    seg_query_all = lax.dynamic_slice_in_dim(segment, offset, half_rows, axis=2)
    pos_query_all = lax.dynamic_slice_in_dim(position, offset, half_rows, axis=2)
    fetched = []
    for layer_index in range(LAYERS):
        fetched.append(
            (
                lax.all_gather(w_query[layer_index], ("dp", "ctx"), axis=0, tiled=True),
                lax.all_gather(w_key[layer_index], ("dp", "ctx"), axis=0, tiled=True),
                lax.all_gather(w_value[layer_index], ("dp", "ctx"), axis=0, tiled=True),
                lax.all_gather(w_out[layer_index], ("dp", "ctx"), axis=1, tiled=True),
                lax.all_gather(w_gate[layer_index], ("dp", "ctx"), axis=0, tiled=True),
                lax.all_gather(w_up[layer_index], ("dp", "ctx"), axis=0, tiled=True),
                lax.all_gather(w_down[layer_index], ("dp", "ctx"), axis=1, tiled=True),
                lax.all_gather(norm_gains[layer_index], ("dp", "ctx"), axis=0, tiled=True),
            )
        )

    def split_gains(gain_low):
        gain_all = gain_low.astype(jnp.float32)
        return (
            gain_all[:model_width],
            gain_all[model_width : 2 * model_width],
            gain_all[2 * model_width : 2 * model_width + HD],
            gain_all[2 * model_width + HD :],
        )

    def widen(layer_grads):
        grad_q, grad_k, grad_v, grad_o, grad_g, grad_u, grad_d, grad_n = layer_grads
        empty_block = jnp.zeros((model_width, HK * HD), jnp.float32)
        full_key = lax.dynamic_update_slice_in_dim(empty_block, grad_k, pair_start * HD, axis=1)
        full_value = lax.dynamic_update_slice_in_dim(empty_block, grad_v, pair_start * HD, axis=1)
        return (grad_q, full_key, full_value, grad_o, grad_g, grad_u, grad_d, grad_n)

    totals = [None] * LAYERS
    outputs = []
    input_grads = []
    for micro_step in range(micro_count):
        seg_query = seg_query_all[micro_step]
        seg_keys = segment[micro_step]
        cosine, sine_value = rotation(pos_query_all[micro_step].reshape(row_count))
        state = tokens[micro_step].reshape(row_count, model_width).astype(jnp.float32)
        stored_all = []
        for layer_index in range(LAYERS):
            (
                forward_w_q,
                forward_w_k,
                forward_w_v,
                forward_w_o,
                forward_w_g,
                forward_w_u,
                forward_w_d,
                forward_gain_low,
            ) = fetched[layer_index]
            forward_g_attn, forward_g_ffn, forward_g_query, forward_g_key = split_gains(
                forward_gain_low
            )
            forward_key_cols = lax.dynamic_slice_in_dim(
                forward_w_k, pair_start * HD, 2 * HD, axis=1
            )
            forward_value_cols = lax.dynamic_slice_in_dim(
                forward_w_v, pair_start * HD, 2 * HD, axis=1
            )
            forward_scale_in = scale_of(state)
            forward_normed = (state * forward_scale_in * forward_g_attn).astype(jnp.bfloat16)
            forward_queries = product(forward_normed, forward_w_q, ((1,), (0,))).reshape(
                row_count, head_count, HD
            )
            forward_query_scale = scale_of(forward_queries)
            forward_query_low = rotate(
                forward_queries * forward_query_scale * forward_g_query, cosine, sine_value
            ).astype(jnp.bfloat16)
            forward_key_rows = product(forward_normed, forward_key_cols, ((1,), (0,))).reshape(
                row_count, 2, HD
            )
            forward_key_scale = scale_of(forward_key_rows)
            key_low = rotate(
                forward_key_rows * forward_key_scale * forward_g_key, cosine, sine_value
            ).astype(jnp.bfloat16)
            value_low = product(forward_normed, forward_value_cols, ((1,), (0,))).astype(
                jnp.bfloat16
            )
            forward_all_keys = lax.all_gather(
                key_low.reshape(sequences, half_rows, 2 * HD), "ctx", axis=1, tiled=True
            )
            forward_all_values = lax.all_gather(
                value_low.reshape(sequences, half_rows, 2 * HD), "ctx", axis=1, tiled=True
            )
            forward_all_keys = forward_all_keys.reshape(sequences, length, 2, HD)
            forward_all_values = forward_all_values.reshape(sequences, length, 2, HD)

            def attend_one(inputs):
                query_part, key_part, value_part, seg_part, seg_key_part = inputs
                return attend(
                    query_part,
                    key_part,
                    value_part,
                    seg_part,
                    seg_key_part,
                    place_query,
                    first_pair,
                )

            mixed, forward_merged = lax.map(
                attend_one,
                (
                    forward_query_low.reshape(sequences, half_rows, head_count, HD),
                    forward_all_keys,
                    forward_all_values,
                    seg_query,
                    seg_keys,
                ),
            )
            forward_mixed_low = mixed.reshape(row_count, head_count * HD).astype(jnp.bfloat16)
            attn = lax.psum(
                product(forward_mixed_low, forward_w_o, ((1,), (0,))).astype(jnp.bfloat16), "tensor"
            ).astype(jnp.float32)
            forward_middle = state + attn
            forward_scale_mid = scale_of(forward_middle)
            forward_normed2 = (forward_middle * forward_scale_mid * forward_g_ffn).astype(
                jnp.bfloat16
            )
            forward_gate_value = product(forward_normed2, forward_w_g, ((1,), (0,)))
            forward_up_value = product(forward_normed2, forward_w_u, ((1,), (0,)))
            forward_hidden = (jax.nn.silu(forward_gate_value) * forward_up_value).astype(
                jnp.bfloat16
            )
            ffn = lax.psum(
                product(forward_hidden, forward_w_d, ((1,), (0,))).astype(jnp.bfloat16), "tensor"
            ).astype(jnp.float32)
            forward_stored = (
                state,
                forward_scale_in,
                forward_normed,
                forward_queries,
                forward_query_scale,
                forward_query_low,
                forward_key_rows,
                forward_key_scale,
                forward_all_keys,
                forward_all_values,
                forward_merged,
                forward_mixed_low,
                forward_middle,
                forward_scale_mid,
                forward_normed2,
                forward_gate_value,
                forward_up_value,
                forward_hidden,
            )
            state = forward_middle + ffn
            stored_all.append(forward_stored)
        outputs.append(state.astype(jnp.bfloat16).reshape(sequences, half_rows, model_width))
        live_rows = (seg_query >= 0).astype(jnp.float32).reshape(row_count, 1)
        gradient = (
            cotangent[micro_step].reshape(row_count, model_width).astype(jnp.float32) * live_rows
        )
        for layer_index in reversed(range(LAYERS)):
            w_q, w_k, w_v, w_o, w_g, w_u, w_d, backward_gain_low = fetched[layer_index]
            g_attn, g_ffn, g_query, g_key = split_gains(backward_gain_low)
            key_cols = lax.dynamic_slice_in_dim(w_k, pair_start * HD, 2 * HD, axis=1)
            value_cols = lax.dynamic_slice_in_dim(w_v, pair_start * HD, 2 * HD, axis=1)
            (
                backward_state,
                scale_in,
                normed,
                queries,
                query_scale,
                query_low,
                key_rows,
                key_scale,
                all_keys,
                all_values,
                merged,
                mixed_low,
                middle,
                scale_mid,
                normed2,
                gate_value,
                up_value,
                hidden,
            ) = stored_all[layer_index]
            grad_ffn = gradient.astype(jnp.bfloat16)
            grad_hidden = product(grad_ffn, w_d, ((1,), (1,)))
            grad_w_down = product(hidden, grad_ffn, ((0,), (0,)))
            sigmoid_gate = jax.nn.sigmoid(gate_value)
            grad_gate = (
                grad_hidden * up_value * sigmoid_gate * (1.0 + gate_value * (1.0 - sigmoid_gate))
            ).astype(jnp.bfloat16)
            grad_up = (grad_hidden * jax.nn.silu(gate_value)).astype(jnp.bfloat16)
            grad_w_gate = product(normed2, grad_gate, ((0,), (0,)))
            grad_w_up = product(normed2, grad_up, ((0,), (0,)))
            term_mid = product(grad_gate, w_g, ((1,), (1,))) + product(grad_up, w_u, ((1,), (1,)))
            term_mid = lax.optimization_barrier(term_mid.astype(jnp.bfloat16)).astype(jnp.float32)
            grad_g_ffn = jnp.sum(term_mid * middle * scale_mid, axis=0)
            summed_mid = lax.psum(term_mid.astype(jnp.bfloat16), "tensor").astype(jnp.float32)
            grad_mid = gradient + norm_back(summed_mid, middle, scale_mid, g_ffn)
            grad_attn = grad_mid.astype(jnp.bfloat16)
            grad_mixed = product(grad_attn, w_o, ((1,), (1,))).astype(jnp.bfloat16)
            grad_w_out = product(mixed_low, grad_attn, ((0,), (0,)))

            def attend_back_one(inputs):
                query_part, key_part, value_part, grad_part, merged_part, seg_part, seg_key_part = (
                    inputs
                )
                return attend_back(
                    query_part,
                    key_part,
                    value_part,
                    grad_part,
                    merged_part,
                    seg_part,
                    seg_key_part,
                    place_query,
                    first_pair,
                )

            grad_query_rot, grad_all_keys, grad_all_values = lax.map(
                attend_back_one,
                (
                    query_low.reshape(sequences, half_rows, head_count, HD),
                    all_keys,
                    all_values,
                    grad_mixed.reshape(sequences, half_rows, head_count, HD),
                    merged,
                    seg_query,
                    seg_keys,
                ),
            )
            own_keys = lax.psum_scatter(
                grad_all_keys.reshape(sequences, length, 2 * HD).astype(jnp.bfloat16),
                "ctx",
                scatter_dimension=1,
                tiled=True,
            ).astype(jnp.float32)
            own_values = lax.psum_scatter(
                grad_all_values.reshape(sequences, length, 2 * HD).astype(jnp.bfloat16),
                "ctx",
                scatter_dimension=1,
                tiled=True,
            ).astype(jnp.float32)
            grad_query_norm = rotate(
                grad_query_rot.reshape(row_count, head_count, HD), cosine, -sine_value
            )
            grad_g_query = jnp.sum(grad_query_norm * queries * query_scale, axis=(0, 1))
            grad_queries = (
                norm_back(grad_query_norm, queries, query_scale, g_query)
                .reshape(row_count, head_count * HD)
                .astype(jnp.bfloat16)
            )
            grad_key_norm = rotate(own_keys.reshape(row_count, 2, HD), cosine, -sine_value)
            grad_g_key = jnp.sum(grad_key_norm * key_rows * key_scale, axis=(0, 1))
            grad_keys = (
                norm_back(grad_key_norm, key_rows, key_scale, g_key)
                .reshape(row_count, 2 * HD)
                .astype(jnp.bfloat16)
            )
            grad_values = own_values.reshape(row_count, 2 * HD).astype(jnp.bfloat16)
            grad_w_query = product(normed, grad_queries, ((0,), (0,)))
            grad_w_key = product(normed, grad_keys, ((0,), (0,)))
            grad_w_value = product(normed, grad_values, ((0,), (0,)))
            term_in = (
                product(grad_queries, w_q, ((1,), (1,)))
                + product(grad_keys, key_cols, ((1,), (1,)))
                + product(grad_values, value_cols, ((1,), (1,)))
            )
            term_in = lax.optimization_barrier(term_in.astype(jnp.bfloat16)).astype(jnp.float32)
            grad_g_attn = jnp.sum(term_in * backward_state * scale_in, axis=0)
            summed_in = lax.psum(term_in.astype(jnp.bfloat16), "tensor").astype(jnp.float32)
            grad_state = grad_mid + norm_back(summed_in, backward_state, scale_in, g_attn)
            grad_gain_all = jnp.concatenate([grad_g_attn, grad_g_ffn, grad_g_query, grad_g_key])
            gradient = grad_state
            layer_grads = (
                grad_w_query,
                grad_w_key,
                grad_w_value,
                grad_w_out,
                grad_w_gate,
                grad_w_up,
                grad_w_down,
                grad_gain_all,
            )
            if totals[layer_index] is None:
                totals[layer_index] = layer_grads
            else:
                totals[layer_index] = jax.tree.map(jnp.add, totals[layer_index], layer_grads)
        input_grads.append(gradient.reshape(sequences, half_rows, model_width))
    widened = [widen(totals[layer_index]) for layer_index in range(LAYERS)]
    stacked = [
        jnp.stack([widened[layer_index][member] for layer_index in range(LAYERS)])
        for member in range(8)
    ]
    reduced = (
        lax.psum_scatter(
            stacked[0].astype(jnp.bfloat16), ("dp", "ctx"), scatter_dimension=1, tiled=True
        ).astype(jnp.float32),
        lax.psum_scatter(
            stacked[1].astype(jnp.bfloat16), ("dp", "ctx"), scatter_dimension=1, tiled=True
        ).astype(jnp.float32),
        lax.psum_scatter(
            stacked[2].astype(jnp.bfloat16), ("dp", "ctx"), scatter_dimension=1, tiled=True
        ).astype(jnp.float32),
        lax.psum_scatter(
            stacked[3].astype(jnp.bfloat16), ("dp", "ctx"), scatter_dimension=2, tiled=True
        ).astype(jnp.float32),
        lax.psum_scatter(
            stacked[4].astype(jnp.bfloat16), ("dp", "ctx"), scatter_dimension=1, tiled=True
        ).astype(jnp.float32),
        lax.psum_scatter(
            stacked[5].astype(jnp.bfloat16), ("dp", "ctx"), scatter_dimension=1, tiled=True
        ).astype(jnp.float32),
        lax.psum_scatter(
            stacked[6].astype(jnp.bfloat16), ("dp", "ctx"), scatter_dimension=2, tiled=True
        ).astype(jnp.float32),
        lax.psum_scatter(
            stacked[7].astype(jnp.bfloat16), ("dp", "ctx"), scatter_dimension=1, tiled=True
        ).astype(jnp.float32),
    )
    shared = (
        lax.psum(reduced[1].astype(jnp.bfloat16), "tensor").astype(jnp.float32),
        lax.psum(reduced[2].astype(jnp.bfloat16), "tensor").astype(jnp.float32),
        lax.psum(reduced[7].astype(jnp.bfloat16), "tensor").astype(jnp.float32),
    )
    results = (
        reduced[0],
        shared[0],
        shared[1],
        reduced[3],
        reduced[4],
        reduced[5],
        reduced[6],
        shared[2],
    )
    return (
        jnp.stack(outputs),
        jnp.stack(input_grads),
        results[0],
        results[1],
        results[2],
        results[3],
        results[4],
        results[5],
        results[6],
        results[7],
    )


def solution(mesh):
    placed = (
        P(None, "dp", "ctx", None),
        P(None, "dp", None),
        P(None, ("dp", "ctx"), "tensor"),
        P(None, ("dp", "ctx"), None),
        P(None, ("dp", "ctx"), None),
        P(None, "tensor", ("dp", "ctx")),
        P(None, ("dp", "ctx"), "tensor"),
        P(None, ("dp", "ctx"), "tensor"),
        P(None, "tensor", ("dp", "ctx")),
        P(None, ("dp", "ctx")),
        P(None, "dp", "ctx", None),
    )
    return jax.shard_map(
        local,
        mesh=mesh,
        in_specs=placed,
        out_specs=(
            P(None, "dp", "ctx", None),
            P(None, "dp", "ctx", None),
            P(None, ("dp", "ctx"), "tensor"),
            P(None, ("dp", "ctx"), None),
            P(None, ("dp", "ctx"), None),
            P(None, "tensor", ("dp", "ctx")),
            P(None, ("dp", "ctx"), "tensor"),
            P(None, ("dp", "ctx"), "tensor"),
            P(None, "tensor", ("dp", "ctx")),
            P(None, ("dp", "ctx")),
        ),
        check_vma=False,
    )
```

profile of v0, /device:TPU:1, one launch (start us, length us, event | category | flops | bytes accessed | tf_op | source)
XLA Modules:
  0.0 2416.1 jit_solution(16440520713134625952)
XLA Ops:
  15.5 32.0 %all-reduce.2 = (bf16[4224]{0:T(1024)(128)(2,1)S(1)}, bf16[4224]{0:T(1024)(128)(2,1)}) all-reduce(bf16[4224]{0:T(1024)(128)(2,1)S(1)} %dynamic-update-slice, bf16[4224]{0:T(1024)(128)(2,1)S(1)} %dynamic-update-slice.1), channel_id=2, replica_groups=mesh['dp'=4,'ctx'=2,'tensor'=4] {'dp','ctx'}, use_global_device_ids=true, to_apply=%add | all-reduce | flops 8448 | bytes 33792
  52.6 4.1 all-gather.39.cloned.1.call-done
  59.1 37.2 %all-gather.37.cloned.1.call-done = bf16[1,2048,320]{1,2,0:T(8,128)(2,1)} async-done(((bf16[1,256,320]{1,2,0:T(8,128)(2,1)}), bf16[1,2048,320]{1,2,0:T(8,128)(2,1)}) %all-gather.37.cloned.1.call-update) | async-done | bytes 1310736 | tf_op jit(solution)/shard_map/all_gather | solution.py:161
  100.9 6.0 all_gather.93
  109.7 30.3 %all-gather.35.cloned.1.call-done = bf16[1,2048,320]{1,2,0:T(8,128)(2,1)} async-done(((bf16[1,256,320]{1,2,0:T(8,128)(2,1)}), bf16[1,2048,320]{1,2,0:T(8,128)(2,1)}) %all-gather.35.cloned.1.call-update) | async-done | bytes 1310736 | tf_op jit(solution)/shard_map/all_gather | solution.py:163
  141.5 6.0 all-gather.18
  153.8 4.1 all-gather.2
  166.3 17.2 all-gather.41.cloned.1.call-done
  194.0 47.4 %all-reduce.30.cloned.1.call-done = (bf16[256,2048]{1,0:T(8,128)(2,1)}, bf16[256,2048]{1,0:T(8,128)(2,1)}) async-done(((bf16[256,2048]{1,0:T(8,128)(2,1)}, bf16[256,2048]{1,0:T(8,128)(2,1)}), (bf16[256,2048]{1,0:T(8,128)(2,1)}, bf16[256,2048]{1,0:T(8,128)(2,1)})) %all-reduce.30.cloned.1.call-update) | async-done | bytes 2097168 | tf_op jit(solution)/shard_map/psum | solution.py:268
  247.4 82.4 %all-gather.43.cloned.1.call-done = bf16[1,2048,1280]{2,1,0:T(8,128)(2,1)} async-done(((bf16[1,256,1280]{2,1,0:T(8,128)(2,1)}), bf16[1,2048,1280]{2,1,0:T(8,128)(2,1)}) %all-gather.43.cloned.1.call-update) | async-done | bytes 5242896 | tf_op jit(solution)/shard_map/all_gather | solution.py:165
  329.9 5.5 fusion.50
  338.0 79.3 %all-gather.45.cloned.1.call-done = bf16[1,2048,1280]{2,1,0:T(8,128)(2,1)} async-done(((bf16[1,256,1280]{2,1,0:T(8,128)(2,1)}), bf16[1,2048,1280]{2,1,0:T(8,128)(2,1)}) %all-gather.45.cloned.1.call-update) | async-done | bytes 5242896 | tf_op jit(solution)/shard_map/all_gather | solution.py:166
  417.3 6.1 multiply_convert_fusion.19
  426.3 79.6 %all-gather.47.cloned.1.call-done = bf16[1,1280,2048]{2,1,0:T(8,128)(2,1)} async-done(((bf16[1,1280,256]{2,1,0:T(8,128)(2,1)}), bf16[1,1280,2048]{2,1,0:T(8,128)(2,1)}) %all-gather.47.cloned.1.call-update) | async-done | bytes 5242896 | tf_op jit(solution)/shard_map/all_gather | solution.py:167
  506.0 5.3 fusion.105
  517.7 46.4 %all-reduce.28.cloned.1.call-done = (bf16[256,2048]{1,0:T(8,128)(2,1)}, bf16[256,2048]{1,0:T(8,128)(2,1)}) async-done(((bf16[256,2048]{1,0:T(8,128)(2,1)}, bf16[256,2048]{1,0:T(8,128)(2,1)}), (bf16[256,2048]{1,0:T(8,128)(2,1)}, bf16[256,2048]{1,0:T(8,128)(2,1)})) %all-reduce.28.cloned.1.call-update) | async-done | bytes 2097168 | tf_op jit(solution)/shard_map/psum | solution.py:281
  570.4 35.4 %all-gather.49.cloned.1.call-done = bf16[1,2048,320]{1,2,0:T(8,128)(2,1)} async-done(((bf16[1,256,320]{1,2,0:T(8,128)(2,1)}), bf16[1,2048,320]{1,2,0:T(8,128)(2,1)}) %all-gather.49.cloned.1.call-update) | async-done | bytes 1310736 | tf_op jit(solution)/shard_map/all_gather | solution.py:163
  607.2 6.2 all-gather.19
  615.9 4.4 all-gather.11
  621.1 28.4 %all-gather.53.cloned.1.call-done = bf16[1,2048,320]{1,2,0:T(8,128)(2,1)} async-done(((bf16[1,256,320]{1,2,0:T(8,128)(2,1)}), bf16[1,2048,320]{1,2,0:T(8,128)(2,1)}) %all-gather.53.cloned.1.call-update) | async-done | bytes 1310736 | tf_op jit(solution)/shard_map/all_gather | solution.py:162
  655.0 6.1 all_gather.95
  661.1 5.1 all_gather.87
  666.2 27.0 %all-gather.51.cloned.1.call-done = bf16[1,2048,320]{1,2,0:T(8,128)(2,1)} async-done(((bf16[1,256,320]{1,2,0:T(8,128)(2,1)}), bf16[1,2048,320]{1,2,0:T(8,128)(2,1)}) %all-gather.51.cloned.1.call-update) | async-done | bytes 1310736 | tf_op jit(solution)/shard_map/all_gather | solution.py:161
  707.5 28.7 %all-gather.55.cloned.1.call-done = bf16[1,320,2048]{2,1,0:T(8,128)(2,1)} async-done(((bf16[1,320,256]{2,1,0:T(8,128)(2,1)}), bf16[1,320,2048]{2,1,0:T(8,128)(2,1)}) %all-gather.55.cloned.1.call-update) | async-done | bytes 1310736 | tf_op jit(solution)/shard_map/all_gather | solution.py:164
  746.1 80.2 %all-gather.61.cloned.1.call-done = bf16[1,1280,2048]{2,1,0:T(8,128)(2,1)} async-done(((bf16[1,1280,256]{2,1,0:T(8,128)(2,1)}), bf16[1,1280,2048]{2,1,0:T(8,128)(2,1)}) %all-gather.61.cloned.1.call-update) | async-done | bytes 5242896 | tf_op jit(solution)/shard_map/all_gather | solution.py:167
  826.3 5.7 fusion.6
  834.6 44.2 %all-reduce.26.cloned.1.call-done = (bf16[256,2048]{1,0:T(8,128)(2,1)}, bf16[256,2048]{1,0:T(8,128)(2,1)}) async-done(((bf16[256,2048]{1,0:T(8,128)(2,1)}, bf16[256,2048]{1,0:T(8,128)(2,1)}), (bf16[256,2048]{1,0:T(8,128)(2,1)}, bf16[256,2048]{1,0:T(8,128)(2,1)})) %all-reduce.26.cloned.1.call-update) | async-done | bytes 2097168 | tf_op jit(solution)/shard_map/psum | solution.py:268
  885.2 82.0 %all-gather.59.cloned.1.call-done = bf16[1,2048,1280]{2,1,0:T(8,128)(2,1)} async-done(((bf16[1,256,1280]{2,1,0:T(8,128)(2,1)}), bf16[1,2048,1280]{2,1,0:T(8,128)(2,1)}) %all-gather.59.cloned.1.call-update) | async-done | bytes 5242896 | tf_op jit(solution)/shard_map/all_gather | solution.py:166
  967.2 5.4 fusion.18
  972.6 81.9 %all-gather.57.cloned.1.call-done = bf16[1,2048,1280]{2,1,0:T(8,128)(2,1)} async-done(((bf16[1,256,1280]{2,1,0:T(8,128)(2,1)}), bf16[1,2048,1280]{2,1,0:T(8,128)(2,1)}) %all-gather.57.cloned.1.call-update) | async-done | bytes 5242896 | tf_op jit(solution)/shard_map/all_gather | solution.py:165
  1054.5 6.4 multiply_convert_fusion.13
  1083.1 43.2 %all-reduce.24.cloned.1.call-done = (bf16[256,2048]{1,0:T(8,128)(2,1)}, bf16[256,2048]{1,0:T(8,128)(2,1)}) async-done(((bf16[256,2048]{1,0:T(8,128)(2,1)}, bf16[256,2048]{1,0:T(8,128)(2,1)}), (bf16[256,2048]{1,0:T(8,128)(2,1)}, bf16[256,2048]{1,0:T(8,128)(2,1)})) %all-reduce.24.cloned.1.call-update) | async-done | bytes 2097168 | tf_op jit(solution)/shard_map/psum | solution.py:349
  1126.3 5.5 multiply_reduce_fusion.6
  1177.9 7.1 reduce-scatter.29.cloned.1.call-done
  1190.6 6.9 reduce-scatter.21.cloned.1.call-done
  1202.5 51.7 %all-reduce.22.cloned.1.call-done = (bf16[256,2048]{1,0:T(8,128)(2,1)}, bf16[256,2048]{1,0:T(8,128)(2,1)}) async-done(((bf16[256,2048]{1,0:T(8,128)(2,1)}, bf16[256,2048]{1,0:T(8,128)(2,1)}), (bf16[256,2048]{1,0:T(8,128)(2,1)}, bf16[256,2048]{1,0:T(8,128)(2,1)})) %all-reduce.22.cloned.1.call-update) | async-done | bytes 2097168 | tf_op jit(solution)/shard_map/psum | solution.py:422
  1254.2 5.4 multiply_reduce_fusion.7
  1262.9 5.9 multiply_convert_fusion.11
  1268.9 4.5 fusion.38
  1285.3 48.8 %all-reduce.20.cloned.1.call-done = (bf16[256,2048]{1,0:T(8,128)(2,1)}, bf16[256,2048]{1,0:T(8,128)(2,1)}) async-done(((bf16[256,2048]{1,0:T(8,128)(2,1)}, bf16[256,2048]{1,0:T(8,128)(2,1)}), (bf16[256,2048]{1,0:T(8,128)(2,1)}, bf16[256,2048]{1,0:T(8,128)(2,1)})) %all-reduce.20.cloned.1.call-update) | async-done | bytes 2097168 | tf_op jit(solution)/shard_map/psum | solution.py:349
  1334.2 5.2 multiply_reduce_fusion.9
  1368.5 7.8 reduce-scatter.31.cloned.1.call-done
  1391.9 9.8 reduce-scatter.33.cloned.1.call-done
  1406.8 5.2 fusion.111
  1412.0 5.4 fusion.108
  1426.9 48.9 %reduce-scatter.37.cloned.1.call-done = bf16[2,256,320]{1,2,0:T(8,128)(2,1)} async-done(((bf16[2,2048,320]{1,2,0:T(8,128)(2,1)}), bf16[2,256,320]{1,2,0:T(8,128)(2,1)}) %reduce-scatter.37.cloned.1.call-update) | async-done | bytes 327696 | tf_op jit(solution)/shard_map/reduce_scatter | solution.py:450
  1475.8 73.6 %reduce-scatter.39.cloned.1.call-done = bf16[2,256,320]{1,2,0:T(8,128)(2,1)} async-done(((bf16[2,2048,320]{1,2,0:T(8,128)(2,1)}), bf16[2,256,320]{1,2,0:T(8,128)(2,1)}) %reduce-scatter.39.cloned.1.call-update) | async-done | bytes 327696 | tf_op jit(solution)/shard_map/reduce_scatter | solution.py:453
  1557.6 7.0 fusion.486
  1572.9 8.2 fusion.1
  1585.6 3.9 fusion
  1589.5 60.1 %all-reduce.18.cloned.1.call-done = (bf16[256,2048]{1,0:T(8,128)(2,1)}, bf16[256,2048]{1,0:T(8,128)(2,1)}, bf16[256,2048]{1,0:T(8,128)(2,1)}, bf16[256,2048]{1,0...) async-done(((bf16[256,2048]{1,0:T(8,128)(2,1)}, bf16[256,2048]{1,0:T(8,128)(2,1)}, bf16[256,2048]{1,0:T(8,128)(2,1)}, ...) | async-done | bytes 4849680 | tf_op jit(solution)/shard_map/psum | solution.py:281
  1655.5 9.0 pad_maximum_fusion
  1667.7 4.0 fusion.3
  1673.3 3.9 fusion.2
  1677.2 9.0 pad_maximum_fusion.1
  1690.3 4.0 fusion.5
  1699.8 8.9 pad_maximum_fusion.2
  1708.8 15.4 reduce-scatter.35.cloned.1.call-done
  1726.0 71.9 %reduce-scatter.41.cloned.1.call-done = bf16[2,320,256]{2,1,0:T(8,128)(2,1)} async-done(((bf16[2,320,2048]{2,1,0:T(8,128)(2,1)}), bf16[2,320,256]{2,1,0:T(8,128)(2,1)}) %reduce-scatter.41.cloned.1.call-update) | async-done | bytes 327696 | tf_op jit(solution)/shard_map/reduce_scatter | solution.py:456
  1812.0 50.0 %reduce-scatter.49.cloned.1.call-done = bf16[528,2]{1,0:T(8,128)(2,1)} async-done(((bf16[4224,2]{1,0:T(8,128)(2,1)}), bf16[528,2]{1,0:T(8,128)(2,1)}) %reduce-scatter.49.cloned.1.call-update) | async-done | bytes 2128
  1863.0 7.4 psum.151
  1871.0 173.4 %reduce-scatter.43.cloned.1.call-done = bf16[2,256,1280]{2,1,0:T(8,128)(2,1)} async-done(((bf16[2,2048,1280]{2,1,0:T(8,128)(2,1)}), bf16[2,256,1280]{2,1,0:T(8,128)(2,1)}) %reduce-scatter.43.cloned.1.call-update) | async-done | bytes 1310736 | tf_op jit(solution)/shard_map/reduce_scatter | solution.py:459
  2047.3 177.7 %reduce-scatter.45.cloned.1.call-done = bf16[2,256,1280]{2,1,0:T(8,128)(2,1)} async-done(((bf16[2,2048,1280]{2,1,0:T(8,128)(2,1)}), bf16[2,256,1280]{2,1,0:T(8,128)(2,1)}) %reduce-scatter.45.cloned.1.call-update) | async-done | bytes 1310736 | tf_op jit(solution)/shard_map/reduce_scatter | solution.py:462
  2228.0 178.0 %reduce-scatter.47.cloned.1.call-done = bf16[2,1280,256]{2,1,0:T(8,128)(2,1)} async-done(((bf16[2,1280,2048]{2,1,0:T(8,128)(2,1)}), bf16[2,1280,256]{2,1,0:T(8,128)(2,1)}) %reduce-scatter.47.cloned.1.call-update) | async-done | bytes 1310736 | tf_op jit(solution)/shard_map/reduce_scatter | solution.py:465
  (1026 shorter events, 334.5 us)
Async XLA Ops:
  7.2 41.0 %copy-start.296 = (s32[2,1,6]{2,1,0:T(1,128)S(1)}, s32[2,1,6]{2,1,0:T(1,128)}, u32[]{:S(2)}) copy-start(s32[2,1,6]{2,1,0:T(1,128)} %param.12) | copy-start | bytes 148
  7.2 42.2 %copy-start = (bf16[2,1,256,2048]{3,2,1,0:T(8,128)(2,1)S(1)}, bf16[2,1,256,2048]{3,2,1,0:T(8,128)(2,1)}, u32[]{:S(2)}) copy-start(bf16[2,1,256,2048]{3,2,1,0:T(8,128)(2,1)} %param.11) | copy-start | bytes 6291460
  7.2 49.4 %all-gather.39.cloned.1.call-start = ((), (), s32[]{:S(2)}) async-start(), calls=%async_computation.33 | async-start | bytes 1474560 | tf_op jit(solution)/shard_map/all_gather | solution.py:162
  9.2 87.1 %all-gather.37.cloned.1.call-start = ((), (), s32[]{:S(2)}) async-start(), calls=%async_computation.32 | async-start | bytes 1474560 | tf_op jit(solution)/shard_map/all_gather | solution.py:161
  11.0 128.9 %all-gather.35.cloned.1.call-start = ((), (), s32[]{:S(2)}) async-start(), calls=%async_computation.31 | async-start | bytes 1474560 | tf_op jit(solution)/shard_map/all_gather | solution.py:163
  12.9 170.7 %all-gather.41.cloned.1.call-start = ((), (), s32[]{:S(2)}) async-start(), calls=%async_computation.34 | async-start | bytes 1474560 | tf_op jit(solution)/shard_map/all_gather | solution.py:164
  13.7 227.8 %all-reduce.30.cloned.1.call-start = ((), (), s32[]{:S(2)}) async-start(), calls=%async_computation.52 | async-start | bytes 4194304 | tf_op jit(solution)/shard_map/psum | solution.py:268
  47.5 104.6 %copy-start.158 = (f32[1,2048]{1,0:T(1,128)}, f32[1,2048]{1,0:T(1,128)S(1)}, u32[]{:S(2)}) copy-start(f32[1,2048]{1,0:T(1,128)S(1)} %get-tuple-element.481) | copy-start | bytes 24580
  47.6 197.5 %copy-start.217 = (f32[1,2048]{1,0:T(1,128)}, f32[1,2048]{1,0:T(1,128)S(1)}, u32[]{:S(2)}) copy-start(f32[1,2048]{1,0:T(1,128)S(1)} %get-tuple-element.480) | copy-start | bytes 24580
  48.1 52.2 %copy-start.282 = (f32[64]{0:T(128)}, f32[64]{0:T(128)S(1)}, u32[]{:S(2)}) copy-start(f32[64]{0:T(128)S(1)} %get-tuple-element.483) | copy-start | bytes 772
  51.3 45.0 %copy-start.268 = (f32[256]{0:T(256)}, f32[256]{0:T(256)S(1)}, u32[]{:S(2)}) copy-start(f32[256]{0:T(256)S(1)} %get-tuple-element.603) | copy-start | bytes 3076
  51.3 47.0 %copy-start.236 = (f32[256]{0:T(256)}, f32[256]{0:T(256)S(1)}, u32[]{:S(2)}) copy-start(f32[256]{0:T(256)S(1)} %get-tuple-element.533) | copy-start | bytes 3076
  52.3 602.7 %copy-start.124 = (f32[256,32]{0,1:T(8,128)}, f32[256,32]{0,1:T(8,128)S(1)}, u32[]{:S(2)}) copy-start(f32[256,32]{0,1:T(8,128)S(1)} %get-tuple-element.556) | copy-start | bytes 98308
  52.3 608.8 %copy-start.122 = (f32[256,32]{0,1:T(8,128)}, f32[256,32]{0,1:T(8,128)S(1)}, u32[]{:S(2)}) copy-start(f32[256,32]{0,1:T(8,128)S(1)} %get-tuple-element.525) | copy-start | bytes 98308
  52.6 110.9 %copy-start.68 = (pred[256,512]{1,0:T(8,128)(4,1)}, pred[256,512]{1,0:T(8,128)(4,1)S(1)}, u32[]{:S(2)}) copy-start(pred[256,512]{1,0:T(8,128)(4,1)S(1)} %get-tuple-element.547) | copy-start | bytes 393220
  52.6 112.0 %copy-start.72 = (pred[256,512]{1,0:T(8,128)(4,1)}, pred[256,512]{1,0:T(8,128)(4,1)S(1)}, u32[]{:S(2)}) copy-start(pred[256,512]{1,0:T(8,128)(4,1)S(1)} %get-tuple-element.546) | copy-start | bytes 393220
  58.3 42.0 %copy-start.106 = (f32[256,2,64]{0,2,1:T(8,128)}, f32[256,2,64]{0,2,1:T(8,128)S(1)}, u32[]{:S(2)}) copy-start(f32[256,2,64]{0,2,1:T(8,128)S(1)} %get-tuple-element.570) | copy-start | bytes 393220
  59.1 41.2 %copy-start.108 = (f32[256,2,64]{0,2,1:T(8,128)}, f32[256,2,64]{0,2,1:T(8,128)S(1)}, u32[]{:S(2)}) copy-start(f32[256,2,64]{0,2,1:T(8,128)S(1)} %get-tuple-element.572) | copy-start | bytes 393220
  100.9 39.0 %copy-start.237 = (f32[256]{0:T(256)S(1)}, f32[256]{0:T(256)}, u32[]{:S(2)}) copy-start(f32[256]{0:T(256)} %copy-done.236) | copy-start | bytes 3076
  108.2 33.3 %copy-start.213 = (f32[256,5]{0,1:T(8,128)}, f32[256,5]{0,1:T(8,128)S(1)}, u32[]{:S(2)}) copy-start(f32[256,5]{0,1:T(8,128)S(1)} %get-tuple-element.485) | copy-start | bytes 15364
  108.8 32.7 %copy-start.215 = (f32[256,5]{0,1:T(8,128)}, f32[256,5]{0,1:T(8,128)S(1)}, u32[]{:S(2)}) copy-start(f32[256,5]{0,1:T(8,128)S(1)} %get-tuple-element.487) | copy-start | bytes 15364
  164.6 19.0 copy-start.138
  188.4 141.4 %all-gather.43.cloned.1.call-start = ((), (), s32[]{:S(2)}) async-start(), calls=%async_computation.35 | async-start | bytes 5898240 | tf_op jit(solution)/shard_map/all_gather | solution.py:165
  189.6 227.7 %all-gather.45.cloned.1.call-start = ((), (), s32[]{:S(2)}) async-start(), calls=%async_computation.36 | async-start | bytes 5898240 | tf_op jit(solution)/shard_map/all_gather | solution.py:166
  192.2 313.7 %all-gather.47.cloned.1.call-start = ((), (), s32[]{:S(2)}) async-start(), calls=%async_computation.37 | async-start | bytes 5898240 | tf_op jit(solution)/shard_map/all_gather | solution.py:167
  193.4 370.7 %all-reduce.28.cloned.1.call-start = ((), (), s32[]{:S(2)}) async-start(), calls=%async_computation.51 | async-start | bytes 4194304 | tf_op jit(solution)/shard_map/psum | solution.py:281
  513.8 91.9 %all-gather.49.cloned.1.call-start = ((), (), s32[]{:S(2)}) async-start(), calls=%async_computation.38 | async-start | bytes 1474560 | tf_op jit(solution)/shard_map/all_gather | solution.py:163
  514.4 135.1 %all-gather.53.cloned.1.call-start = ((), (), s32[]{:S(2)}) async-start(), calls=%async_computation.40 | async-start | bytes 1474560 | tf_op jit(solution)/shard_map/all_gather | solution.py:162
  515.1 178.0 %all-gather.51.cloned.1.call-start = ((), (), s32[]{:S(2)}) async-start(), calls=%async_computation.39 | async-start | bytes 1474560 | tf_op jit(solution)/shard_map/all_gather | solution.py:161
  515.7 220.5 %all-gather.55.cloned.1.call-start = ((), (), s32[]{:S(2)}) async-start(), calls=%async_computation.41 | async-start | bytes 1474560 | tf_op jit(solution)/shard_map/all_gather | solution.py:164
  516.5 309.8 %all-gather.61.cloned.1.call-start = ((), (), s32[]{:S(2)}) async-start(), calls=%async_computation.44 | async-start | bytes 5898240 | tf_op jit(solution)/shard_map/all_gather | solution.py:167
  517.0 361.7 %all-reduce.26.cloned.1.call-start = ((), (), s32[]{:S(2)}) async-start(), calls=%async_computation.50 | async-start | bytes 4194304 | tf_op jit(solution)/shard_map/psum | solution.py:268
  651.4 14.8 copy-start.93
  744.7 222.5 %all-gather.59.cloned.1.call-start = ((), (), s32[]{:S(2)}) async-start(), calls=%async_computation.43 | async-start | bytes 5898240 | tf_op jit(solution)/shard_map/all_gather | solution.py:166
  745.3 309.2 %all-gather.57.cloned.1.call-start = ((), (), s32[]{:S(2)}) async-start(), calls=%async_computation.42 | async-start | bytes 5898240 | tf_op jit(solution)/shard_map/all_gather | solution.py:165
  745.9 380.4 %all-reduce.24.cloned.1.call-start = ((), (), s32[]{:S(2)}) async-start(), calls=%async_computation.49 | async-start | bytes 4194304 | tf_op jit(solution)/shard_map/psum | solution.py:349
  1075.6 93.7 %reduce-scatter.19.cloned.1.call-start = ((), (), s32[]{:S(2)}) async-start(), calls=%async_computation.16 | async-start | bytes 196608 | tf_op jit(solution)/shard_map/reduce_scatter | solution.py:383
  1149.7 22.8 reduce-scatter.27.cloned.1.call-start
  1153.9 31.1 %reduce-scatter.29.cloned.1.call-start = ((), (), s32[]{:S(2)}) async-start(), calls=%async_computation.21 | async-start | bytes 196608 | tf_op jit(solution)/shard_map/reduce_scatter | solution.py:389
  1162.4 35.2 %reduce-scatter.21.cloned.1.call-start = ((), (), s32[]{:S(2)}) async-start(), calls=%async_computation.17 | async-start | bytes 196608 | tf_op jit(solution)/shard_map/reduce_scatter | solution.py:389
  1165.4 88.7 %all-reduce.22.cloned.1.call-start = ((), (), s32[]{:S(2)}) async-start(), calls=%async_computation.48 | async-start | bytes 4194304 | tf_op jit(solution)/shard_map/psum | solution.py:422
  1202.4 51.7 %copy-start.261 = (f32[256]{0:T(256)S(1)}, f32[256]{0:T(256)}, u32[]{:S(2)}) copy-start(f32[256]{0:T(256)} %copy-done.260) | copy-start | bytes 3076
  1202.4 51.7 %copy-start.263 = (f32[256]{0:T(256)S(1)}, f32[256]{0:T(256)}, u32[]{:S(2)}) copy-start(f32[256]{0:T(256)} %copy-done.262) | copy-start | bytes 3076
  1202.4 131.7 %all-reduce.20.cloned.1.call-start = ((), (), s32[]{:S(2)}) async-start(), calls=%async_computation.47 | async-start | bytes 4194304 | tf_op jit(solution)/shard_map/psum | solution.py:349
  1282.3 51.8 %copy-start.218 = (f32[1,2048]{1,0:T(1,128)S(1)}, f32[1,2048]{1,0:T(1,128)}, u32[]{:S(2)}) copy-start(f32[1,2048]{1,0:T(1,128)} %copy-done.217) | copy-start | bytes 24580
  1282.3 51.8 %copy-start.257 = (f32[256]{0:T(256)S(1)}, f32[256]{0:T(256)}, u32[]{:S(2)}) copy-start(f32[256]{0:T(256)} %copy-done.256) | copy-start | bytes 3076
  1282.3 51.8 %copy-start.259 = (f32[256]{0:T(256)S(1)}, f32[256]{0:T(256)}, u32[]{:S(2)}) copy-start(f32[256]{0:T(256)} %copy-done.258) | copy-start | bytes 3076
  1282.3 84.6 %reduce-scatter.23.cloned.1.call-start = ((), (), s32[]{:S(2)}) async-start(), calls=%async_computation.18 | async-start | bytes 196608 | tf_op jit(solution)/shard_map/reduce_scatter | solution.py:383
  1353.4 22.8 reduce-scatter.31.cloned.1.call-start
  1358.3 31.3 %reduce-scatter.25.cloned.1.call-start = ((), (), s32[]{:S(2)}) async-start(), calls=%async_computation.19 | async-start | bytes 196608 | tf_op jit(solution)/shard_map/reduce_scatter | solution.py:389
  1362.5 39.2 %reduce-scatter.33.cloned.1.call-start = ((), (), s32[]{:S(2)}) async-start(), calls=%async_computation.23 | async-start | bytes 196608 | tf_op jit(solution)/shard_map/reduce_scatter | solution.py:389
  1363.8 13.4 copy-start.109
  1366.2 13.7 copy-start.159
  1366.9 109.0 %reduce-scatter.37.cloned.1.call-start = ((), (), s32[]{:S(2)}) async-start(), calls=%async_computation.25 | async-start | bytes 2949120 | tf_op jit(solution)/shard_map/reduce_scatter | solution.py:450
  1384.9 164.6 %reduce-scatter.39.cloned.1.call-start = ((), (), s32[]{:S(2)}) async-start(), calls=%async_computation.26 | async-start | bytes 2949120 | tf_op jit(solution)/shard_map/reduce_scatter | solution.py:453
  1406.7 242.9 %all-reduce.18.cloned.1.call-start = ((), (), s32[]{:S(2)}) async-start(), calls=%async_computation.46 | async-start | bytes 9699328 | tf_op jit(solution)/shard_map/psum | solution.py:281
  1549.5 174.6 %reduce-scatter.35.cloned.1.call-start = ((), (), s32[]{:S(2)}) async-start(), calls=%async_computation.24 | async-start | bytes 2949120 | tf_op jit(solution)/shard_map/reduce_scatter | solution.py:447
  1556.4 241.5 %reduce-scatter.41.cloned.1.call-start = ((), (), s32[]{:S(2)}) async-start(), calls=%async_computation.27 | async-start | bytes 2949120 | tf_op jit(solution)/shard_map/reduce_scatter | solution.py:456
  1571.8 290.2 %reduce-scatter.49.cloned.1.call-start = ((), (), s32[]{:S(2)}) async-start(), calls=%async_computation.45 | async-start | bytes 1216512
  1655.1 389.3 %reduce-scatter.43.cloned.1.call-start = ((), (), s32[]{:S(2)}) async-start(), calls=%async_computation.28 | async-start | bytes 11796480 | tf_op jit(solution)/shard_map/reduce_scatter | solution.py:459
  1664.5 560.5 %reduce-scatter.45.cloned.1.call-start = ((), (), s32[]{:S(2)}) async-start(), calls=%async_computation.29 | async-start | bytes 11796480 | tf_op jit(solution)/shard_map/reduce_scatter | solution.py:462
  1686.2 719.8 %reduce-scatter.47.cloned.1.call-start = ((), (), s32[]{:S(2)}) async-start(), calls=%async_computation.30 | async-start | bytes 11796480 | tf_op jit(solution)/shard_map/reduce_scatter | solution.py:465
  1708.7 93.0 %copy-start.177 = (bf16[2,256,320]{1,2,0:T(8,128)(2,1)S(1)}, bf16[2,256,320]{1,2,0:T(8,128)(2,1)}, u32[]{:S(2)}) copy-start(bf16[2,256,320]{1,2,0:T(8,128)(2,1)} %get-tuple-element.342) | copy-start | bytes 983044
  1708.8 93.9 %copy-start.111 = (bf16[256,2048]{1,0:T(8,128)(2,1)S(1)}, bf16[256,2048]{1,0:T(8,128)(2,1)}, u32[]{:S(2)}) copy-start(bf16[256,2048]{1,0:T(8,128)(2,1)} %get-tuple-element.324) | copy-start | bytes 3145732
  (299 other events, 1092.6 us)
Sparse Core Ops, SparseCore 0:
  10.7 45.9 all-gather.38
  59.3 37.0 all-gather.36
  99.0 40.9 all-gather.34
  142.4 41.0 all-gather.40
  188.5 52.8 all-reduce.29
  244.3 85.5 all-gather.42
  332.8 84.4 all-gather.44
  420.1 85.7 all-gather.46
  513.9 50.1 all-reduce.27
  566.0 39.6 all-gather.48
  607.8 41.7 all-gather.52
  651.4 41.7 all-gather.50
  695.2 40.9 all-gather.54
  738.1 88.1 all-gather.60
  828.6 50.1 all-reduce.25
  881.6 85.5 all-gather.58
  970.0 84.4 all-gather.56
  1075.7 50.5 all-reduce.23
  1149.8 10.3 reduce-scatter.18
  1162.2 10.2 reduce-scatter.26
  1174.7 10.2 reduce-scatter.28
  1187.2 10.2 reduce-scatter.20
  1202.5 51.5 all-reduce.21
  1282.4 51.6 all-reduce.19
  1353.5 10.3 reduce-scatter.22
  1366.0 10.2 reduce-scatter.30
  1378.3 10.2 reduce-scatter.24
  1391.4 10.2 reduce-scatter.32
  1405.8 69.9 reduce-scatter.36
  1479.8 69.6 reduce-scatter.38
  1552.8 96.7 all-reduce.17
  1653.7 70.3 reduce-scatter.34
  1728.1 69.7 reduce-scatter.40
  1801.9 59.9 reduce-scatter.48
  1865.5 178.7 reduce-scatter.42
  2047.8 177.1 reduce-scatter.44
  2228.4 177.5 reduce-scatter.46
where the time goes:
time: 2420 us
  waiting for transfers between devices  1860 us (77%)
  matrix products  232 us (10%)
  other arithmetic  156 us (6%)
  blocking collectives  81 us (3%)
  local copies, waits for them, and re-layouts  62.4 us (3%)
    dot_general x84, matrix products, product(): lax.dot_general(left_side, right_side, (contract, ((), ())), preferred_el...  197 us
    reduce_scatter x1, waiting for transfers between devices, local(): lax.psum_scatter(stacked[6].astype(jnp.bfloat16), ('dp', 'ctx'), scatter_...  178 us
    reduce_scatter x1, waiting for transfers between devices, local(): lax.psum_scatter(stacked[5].astype(jnp.bfloat16), ('dp', 'ctx'), scatter_...  178 us
    reduce_scatter x1, waiting for transfers between devices, local(): lax.psum_scatter(stacked[4].astype(jnp.bfloat16), ('dp', 'ctx'), scatter_...  173 us
    all_gather x2, waiting for transfers between devices, local(): lax.all_gather(w_gate[layer_index], ('dp', 'ctx'), axis=0, tiled=True)  164 us
    all_gather x2, waiting for transfers between devices, local(): lax.all_gather(w_up[layer_index], ('dp', 'ctx'), axis=0, tiled=True)  161 us
    all_gather x2, waiting for transfers between devices, local(): lax.all_gather(w_down[layer_index], ('dp', 'ctx'), axis=1, tiled=True)  160 us
    psum x2, waiting for transfers between devices, local(): lax.psum(product(forward_hidden, forward_w_d, ((1,), (0,))).astype(jnp.bf...  106 us
  transfers between devices with their start and end apart: 37, of which 34 were waited for; matrix products, arithmetic and copies ran while one was open for 13% of the time, Pallas kernels for 0%

commit v1 on v0

v1 whole, which is shorter than its diff:
```python
import jax
import jax.numpy as jnp
from jax import lax
from jax.sharding import PartitionSpec as P

HQ = 20
HK = 5
HD = 64
LAYERS = 2
GROUP_SIZE = HQ // HK

epsilon = 1e-05
rope_base = 10000.0

f32 = jnp.float32
bf16 = jnp.bfloat16


def product(left_side, right_side, contract):
    return lax.dot_general(
        left_side, right_side, (contract, ((), ())), preferred_element_type=f32
    )


def rotate(values, cosine, sine_value):
    half_size = values.shape[-1] // 2
    first_half = values[..., :half_size]
    second_half = values[..., half_size:]
    return jnp.concatenate(
        [
            first_half * cosine - second_half * sine_value,
            second_half * cosine + first_half * sine_value,
        ],
        axis=-1,
    )


def scale_of(values):
    return lax.rsqrt(jnp.mean(values * values, axis=-1, keepdims=True) + epsilon)


def norm_back(gradient, values, scaling, gain_vector):
    scaled = gradient * gain_vector
    cubed = scaling * scaling * scaling
    return scaling * scaled - values * cubed * jnp.mean(scaled * values, axis=-1, keepdims=True)


class Plan:
    def __init__(self):
        self.n = lax.axis_size("dp")
        self.nt = lax.axis_size("tensor")
        assert lax.axis_size("ctx") == 2 and self.nt == 4
        self.z = lax.axis_index("dp")
        self.x = lax.axis_index("ctx")
        self.t = lax.axis_index("tensor")
        self.y = self.t // 2
        self.c = self.t % 2
        nt = self.nt
        places = [(a, b, d) for a in range(2) for b in range(2) for d in range(2)]
        self.peers = {}
        for j in range(1, 4):
            self.peers[j] = [
                (a * nt + 2 * b + d, (a ^ (j // 2)) * nt + 2 * (b ^ (j % 2)) + d)
                for a, b, d in places
            ]
        self.swap_pairs = [(a * nt + 2 * b + d, d * nt + 2 * b + a) for a, b, d in places]
        self.core_pairs = [(i, i ^ 1) for i in range(nt)]
        self.up = [(i, (i + 1) % self.n) for i in range(self.n)]
        self.down = [(i, (i - 1) % self.n) for i in range(self.n)]

    def peer(self, value, j):
        return lax.ppermute(value, ("ctx", "tensor"), self.peers[j])

    def swap(self, value):
        return lax.ppermute(value, ("ctx", "tensor"), self.swap_pairs)

    def core(self, value):
        return lax.ppermute(value, "tensor", self.core_pairs)

    def fetch(self, shard):
        own = [self.swap(shard)]
        for _ in range(1, self.n):
            own.append(lax.ppermute(own[-1], "dp", self.down))
        other = [self.core(piece) for piece in own]
        return jnp.concatenate(own + other, axis=0)

    def scatter(self, grad):
        half = grad.shape[0] // 2
        w = half // self.n
        both = grad[:half].astype(f32) + self.core(grad[half:]).astype(f32)
        total = both[(self.n - 1) * w :]
        for s in reversed(range(self.n - 1)):
            moved = lax.ppermute(total.astype(bf16), "dp", self.up)
            total = both[s * w : (s + 1) * w] + moved.astype(f32)
        return self.swap(total.astype(bf16))

    def spread(self, rows):
        return jnp.concatenate([rows] + [self.peer(rows, j) for j in range(1, 4)], axis=0)

    def gather_sum(self, terms):
        rows = terms.shape[0] // 4
        total = terms[:rows].astype(f32)
        for j in range(1, 4):
            total = total + self.peer(terms[j * rows : (j + 1) * rows], j).astype(f32)
        return total

    def inward(self, array):
        lead = array.shape[:-1]
        d = array.shape[-1]
        w = d // (2 * self.n)
        parts = array.reshape(lead + (self.n, 2, w))
        axis = len(lead)
        twice = jnp.concatenate([parts, parts], axis=axis)
        rolled = lax.dynamic_slice_in_dim(twice, self.z, self.n, axis=axis)
        rolled = jnp.where(self.c == 0, rolled, jnp.flip(rolled, axis + 1))
        return jnp.swapaxes(rolled, axis, axis + 1).reshape(lead + (d,))

    def outward(self, array):
        lead = array.shape[:-1]
        d = array.shape[-1]
        w = d // (2 * self.n)
        axis = len(lead)
        parts = jnp.swapaxes(array.reshape(lead + (2, self.n, w)), axis, axis + 1)
        parts = jnp.where(self.c == 0, parts, jnp.flip(parts, axis + 1))
        twice = jnp.concatenate([parts, parts], axis=axis)
        rolled = lax.dynamic_slice_in_dim(twice, (self.n - self.z) % self.n, self.n, axis=axis)
        return rolled.reshape(lead + (d,))

    def replicate(self, rows):
        beside = self.peer(rows, 1)
        half = jnp.where(
            self.y == 0,
            jnp.concatenate([rows, beside], axis=0),
            jnp.concatenate([beside, rows], axis=0),
        )
        other = self.core(half)
        return jnp.where(self.c == 0, jnp.stack([half, other]), jnp.stack([other, half]))


def pairs_of(rows, first_pair):
    return jnp.where(first_pair[:, None, None], rows[None, :, 0], rows[None, :, 1])


def attend(queries, key_heads, value_heads, allowed):
    scores = (
        jnp.einsum("hqd,hkd->hqk", queries, key_heads, preferred_element_type=f32) * HD ** (-0.5)
    )
    masked = jnp.where(allowed, scores, -1e30)
    highest = jnp.max(masked, axis=-1, keepdims=True)
    exponent = jnp.where(allowed, jnp.exp(masked - highest), 0.0)
    row_total = jnp.sum(exponent, axis=-1, keepdims=True)
    live_rows = row_total > 0.0
    safe_total = jnp.where(live_rows, row_total, 1.0)
    probability = (exponent / safe_total).astype(bf16)
    mixed = jnp.einsum("hqk,hkd->hqd", probability, value_heads, preferred_element_type=f32)
    merged = jnp.where(live_rows, highest + jnp.log(safe_total), 0.0)
    return mixed, merged


def attend_back(queries, key_heads, value_heads, grad_mixed, merged, allowed):
    scores = (
        jnp.einsum("hqd,hkd->hqk", queries, key_heads, preferred_element_type=f32) * HD ** (-0.5)
    )
    probability = jnp.where(allowed, jnp.exp(scores - merged), 0.0)
    grad_value_heads = jnp.einsum(
        "hqk,hqd->hkd", probability.astype(bf16), grad_mixed, preferred_element_type=f32
    )
    grad_prob = jnp.einsum("hqd,hkd->hqk", grad_mixed, value_heads, preferred_element_type=f32)
    row_delta = jnp.sum(probability * grad_prob, axis=-1, keepdims=True)
    grad_scores = (probability * (grad_prob - row_delta)).astype(bf16)
    grad_queries = jnp.einsum(
        "hqk,hkd->hqd", grad_scores, key_heads, preferred_element_type=f32
    ) * HD ** (-0.5)
    grad_key_heads = jnp.einsum(
        "hqk,hqd->hkd", grad_scores, queries, preferred_element_type=f32
    ) * HD ** (-0.5)
    return grad_queries, grad_key_heads, grad_value_heads


def local(
    tokens, doc_lengths, w_query, w_key, w_value, w_out, w_gate, w_up, w_down, norm_gains, cotangent
):
    plan = Plan()
    micro_count, sequences, half_rows, width = tokens.shape
    assert micro_count == 2 and sequences == 1
    quarter = half_rows // 2
    heads = w_query.shape[2] // HD
    n = plan.n
    group = 2 * plan.y + plan.x
    qw, kw = heads * HD, 2 * HD

    kv_at = plan.t * heads // GROUP_SIZE * HD
    fetched = []
    for layer in range(LAYERS):
        keys = lax.dynamic_slice_in_dim(w_key[layer], kv_at, kw, axis=1)
        values = lax.dynamic_slice_in_dim(w_value[layer], kv_at, kw, axis=1)
        attn_shard = jnp.concatenate([w_query[layer], keys, values, w_out[layer].T], axis=1)
        attn_w = plan.fetch(attn_shard)
        fetched.append(
            (
                attn_w[:, : qw + 2 * kw],
                attn_w[:, qw + 2 * kw :],
                plan.fetch(w_gate[layer]),
                plan.fetch(w_up[layer]),
                plan.fetch(w_down[layer].T),
            )
        )

    side = lax.ppermute(norm_gains, "ctx", [(0, 1), (1, 0)])
    pair = jnp.where(
        plan.x == 0,
        jnp.concatenate([norm_gains, side], axis=1),
        jnp.concatenate([side, norm_gains], axis=1),
    )
    gain_pieces = [pair]
    for _ in range(1, n):
        gain_pieces.append(lax.ppermute(gain_pieces[-1], "dp", plan.down))
    ring = jnp.concatenate(gain_pieces + gain_pieces, axis=1)
    gain_width = pair.shape[1]
    gains = lax.dynamic_slice_in_dim(
        ring, (n - plan.z) % n * gain_width, n * gain_width, axis=1
    ).astype(f32)
    gain_attn = plan.inward(gains[:, :width])
    gain_ffn = plan.inward(gains[:, width : 2 * width])
    gain_query = gains[:, 2 * width : 2 * width + HD]
    gain_key = gains[:, 2 * width + HD :]

    blocks = jnp.arange(4, dtype=jnp.int32) ^ (2 * plan.x + plan.y).astype(jnp.int32)
    places = (blocks[:, None] * quarter + jnp.arange(quarter, dtype=jnp.int32)[None, :]).reshape(-1)
    lengths = lax.dynamic_index_in_dim(doc_lengths, plan.c, axis=0, keepdims=False)[0]
    docs = lengths.shape[0]
    ends = jnp.cumsum(lengths, dtype=jnp.int32)
    starts = ends - lengths
    document = jnp.sum((places[:, None] >= ends[None, :]).astype(jnp.int32), axis=-1)
    chosen = document[:, None] == jnp.arange(docs, dtype=jnp.int32)[None, :]
    position = places - jnp.sum(jnp.where(chosen, starts[None, :], 0), axis=-1)
    segment = jnp.where(document < docs, document, -1)
    allowed = (
        (segment[:, None] == segment[None, :])
        & (segment[:, None] >= 0)
        & (places[None, :] <= places[:, None])
    )[None]
    frequency = rope_base ** (-jnp.arange(HD // 2, dtype=f32) * (2.0 / HD))
    angle = position.astype(f32)[:, None] * frequency
    cosine, sine_value = jnp.cos(angle), jnp.sin(angle)
    pair_start = group * heads // GROUP_SIZE
    first_pair = (
        group * heads + jnp.arange(heads, dtype=jnp.int32)
    ) // GROUP_SIZE == pair_start
    weight_first = first_pair.astype(f32)[:, None, None]

    def own_half(array):
        rows = lax.dynamic_index_in_dim(array, plan.c, axis=0, keepdims=False)[0]
        rows = jnp.where(plan.y == 0, rows, jnp.roll(rows, quarter, axis=0))
        return plan.inward(rows)

    def by_head(array, count):
        return jnp.swapaxes(array.reshape(array.shape[0], count, HD), 0, 1)

    def flat(array):
        return jnp.swapaxes(array, 0, 1).reshape(array.shape[1], -1)

    first_half = own_half(tokens)
    cot_half = own_half(cotangent)
    cot_all = jnp.concatenate([cot_half, plan.peer(cot_half, 2)], axis=0)
    tokens_all = jnp.concatenate([first_half, plan.peer(first_half, 2)], axis=0).astype(f32)
    start_grad = jnp.where(segment[:, None] >= 0, cot_all, jnp.zeros_like(cot_all))

    state = tokens_all[:quarter]
    stored = []
    output = None
    for layer in range(LAYERS):
        w_qkv, w_o, w_g, w_u, w_d = fetched[layer]
        if layer == 0:
            scale_in = scale_of(tokens_all)
            normed = (tokens_all * scale_in * gain_attn[layer]).astype(bf16)
            scale_in = scale_in[:quarter]
        else:
            scale_in = scale_of(state)
            normed = plan.spread((state * scale_in * gain_attn[layer]).astype(bf16))
        qkv = product(normed, w_qkv, ((1,), (0,)))
        queries = by_head(qkv[:, :qw], heads)
        query_scale = scale_of(queries)
        query_low = rotate(queries * query_scale * gain_query[layer], cosine, sine_value).astype(
            bf16
        )
        keys = by_head(qkv[:, qw : qw + kw], 2)
        key_scale = scale_of(keys)
        key_low = rotate(keys * key_scale * gain_key[layer], cosine, sine_value).astype(bf16)
        value_low = by_head(qkv[:, qw + kw :].astype(bf16), 2)
        key_heads = jnp.where(first_pair[:, None, None], key_low[0][None], key_low[1][None])
        value_heads = jnp.where(first_pair[:, None, None], value_low[0][None], value_low[1][None])
        mixed, merged = attend(query_low, key_heads, value_heads, allowed)
        mixed_low = flat(mixed.astype(bf16))
        attn = plan.gather_sum(product(mixed_low, w_o, ((1,), (1,))).astype(bf16))
        middle = state + attn
        scale_mid = scale_of(middle)
        normed2 = plan.spread((middle * scale_mid * gain_ffn[layer]).astype(bf16))
        gate = product(normed2, w_g, ((1,), (0,)))
        up = product(normed2, w_u, ((1,), (0,)))
        hidden = (jax.nn.silu(gate) * up).astype(bf16)
        ffn = plan.gather_sum(product(hidden, w_d, ((1,), (1,))).astype(bf16))
        stored.append(
            (
                state,
                scale_in,
                normed,
                queries,
                query_scale,
                query_low,
                keys,
                key_scale,
                key_heads,
                value_heads,
                merged,
                mixed_low,
                middle,
                scale_mid,
                normed2,
                gate,
                up,
                hidden,
            )
        )
        state = middle + ffn
    output = plan.replicate(plan.outward(state.astype(bf16)))

    gradient = start_grad[:quarter].astype(f32)
    grad_ffn = start_grad
    results = [None] * LAYERS
    gain_grads = [None] * LAYERS
    for layer in reversed(range(LAYERS)):
        w_qkv, w_o, w_g, w_u, w_d = fetched[layer]
        (
            state,
            scale_in,
            normed,
            queries,
            query_scale,
            query_low,
            keys,
            key_scale,
            key_heads,
            value_heads,
            merged,
            mixed_low,
            middle,
            scale_mid,
            normed2,
            gate,
            up,
            hidden,
        ) = stored[layer]
        if grad_ffn is None:
            grad_ffn = plan.spread(gradient.astype(bf16))
        grad_w_d = plan.scatter(product(grad_ffn, hidden, ((0,), (0,))).astype(bf16))
        grad_hidden = product(grad_ffn, w_d, ((1,), (0,)))
        sigmoid_gate = jax.nn.sigmoid(gate)
        grad_gate = (
            grad_hidden * up * sigmoid_gate * (1.0 + gate * (1.0 - sigmoid_gate))
        ).astype(bf16)
        grad_up = (grad_hidden * (gate * sigmoid_gate)).astype(bf16)
        grad_w_g = plan.scatter(product(normed2, grad_gate, ((0,), (0,))).astype(bf16))
        grad_w_u = plan.scatter(product(normed2, grad_up, ((0,), (0,))).astype(bf16))
        term_mid = product(grad_gate, w_g, ((1,), (1,))) + product(grad_up, w_u, ((1,), (1,)))
        summed_mid = plan.gather_sum(term_mid.astype(bf16))
        grad_g_ffn = jnp.sum(summed_mid * middle * scale_mid, axis=0)
        grad_mid = gradient + norm_back(summed_mid, middle, scale_mid, gain_ffn[layer])
        grad_attn = plan.spread(grad_mid.astype(bf16))
        grad_mixed = by_head(product(grad_attn, w_o, ((1,), (0,))).astype(bf16), heads)
        grad_w_o = product(grad_attn, mixed_low, ((0,), (0,))).astype(bf16)
        grad_query_rot, grad_key_heads, grad_value_heads = attend_back(
            query_low, key_heads, value_heads, grad_mixed, merged, allowed
        )
        grad_key_rot = jnp.stack(
            [
                jnp.sum(grad_key_heads * weight_first, axis=0),
                jnp.sum(grad_key_heads * (1.0 - weight_first), axis=0),
            ]
        )
        grad_values = jnp.concatenate(
            [
                jnp.sum(grad_value_heads * weight_first, axis=0),
                jnp.sum(grad_value_heads * (1.0 - weight_first), axis=0),
            ],
            axis=1,
        ).astype(bf16)
        grad_query_norm = rotate(grad_query_rot, cosine, -sine_value)
        grad_g_query = jnp.sum(grad_query_norm * queries * query_scale, axis=(0, 1))
        grad_queries = flat(
            norm_back(grad_query_norm, queries, query_scale, gain_query[layer]).astype(bf16)
        )
        grad_key_norm = rotate(grad_key_rot, cosine, -sine_value)
        grad_g_key = jnp.sum(grad_key_norm * keys * key_scale, axis=(0, 1))
        grad_keys = flat(norm_back(grad_key_norm, keys, key_scale, gain_key[layer]).astype(bf16))
        grad_qkv = jnp.concatenate([grad_queries, grad_keys, grad_values], axis=1)
        grad_w_qkv = product(normed, grad_qkv, ((0,), (0,))).astype(bf16)
        grad_w_attn = plan.scatter(jnp.concatenate([grad_w_qkv, grad_w_o], axis=1))
        summed_in = plan.gather_sum(product(grad_qkv, w_qkv, ((1,), (1,))).astype(bf16))
        grad_g_attn = jnp.sum(summed_in * state * scale_in, axis=0)
        gradient = grad_mid + norm_back(summed_in, state, scale_in, gain_attn[layer])
        grad_ffn = None
        results[layer] = (grad_w_attn, grad_w_g, grad_w_u, grad_w_d)
        gain_grads[layer] = jnp.concatenate(
            [plan.outward(grad_g_attn), plan.outward(grad_g_ffn), grad_g_query, grad_g_key]
        )
    grad_input = plan.replicate(plan.outward(gradient.astype(bf16))).astype(f32)

    def stack(pick):
        return jnp.stack([pick(results[layer]) for layer in range(LAYERS)])

    slice_width = w_query.shape[1]
    shared = jnp.stack(
        [
            jnp.stack(
                [results[layer][0][:, qw : qw + kw], results[layer][0][:, qw + kw : qw + 2 * kw]]
            )
            for layer in range(LAYERS)
        ]
    )
    wide = jnp.zeros(shared.shape[:-1] + (w_key.shape[2],), bf16)
    wide = lax.dynamic_update_slice_in_dim(wide, shared, kv_at, axis=3)
    wide = lax.psum(wide, "tensor").astype(f32)
    all_gains = lax.psum(jnp.stack(gain_grads), ("dp", "ctx", "tensor"))
    share = norm_gains.shape[1]
    grad_gains = lax.dynamic_slice_in_dim(
        all_gains, (2 * plan.z + plan.x) * share, share, axis=1
    )
    return (
        output[:, None],
        grad_input[:, None],
        stack(lambda r: r[0][:, :qw]).astype(f32),
        wide[:, 0],
        wide[:, 1],
        stack(lambda r: r[0][:, qw + 2 * kw :].T).astype(f32),
        stack(lambda r: r[1]).astype(f32),
        stack(lambda r: r[2]).astype(f32),
        stack(lambda r: r[3].T).astype(f32),
        grad_gains,
    )


def solution(mesh):
    placed = (
        P(None, "dp", "ctx", None),
        P(None, "dp", None),
        P(None, ("dp", "ctx"), "tensor"),
        P(None, ("dp", "ctx"), None),
        P(None, ("dp", "ctx"), None),
        P(None, "tensor", ("dp", "ctx")),
        P(None, ("dp", "ctx"), "tensor"),
        P(None, ("dp", "ctx"), "tensor"),
        P(None, "tensor", ("dp", "ctx")),
        P(None, ("dp", "ctx")),
        P(None, "dp", "ctx", None),
    )
    return jax.shard_map(
        local,
        mesh=mesh,
        in_specs=placed,
        out_specs=(
            P(None, "dp", "ctx", None),
            P(None, "dp", "ctx", None),
            P(None, ("dp", "ctx"), "tensor"),
            P(None, ("dp", "ctx"), None),
            P(None, ("dp", "ctx"), None),
            P(None, "tensor", ("dp", "ctx")),
            P(None, ("dp", "ctx"), "tensor"),
            P(None, ("dp", "ctx"), "tensor"),
            P(None, "tensor", ("dp", "ctx")),
            P(None, ("dp", "ctx")),
        ),
        check_vma=False,
    )
```

time: 2420 us -> 1290 us (0.53)
  waiting for transfers between devices: 1860 us -> 604 us
  starting transfers between devices: 3.8 us -> 286 us
  matrix products: 232 us -> 117 us
  other arithmetic: 156 us -> 111 us
  blocking collectives: 81 us -> 40.7 us
  local copies, waits for them, and re-layouts: 62.4 us -> 100 us
    reduce_scatter x15 -> x0, waiting for transfers between devices: 772 us -> none  [the longest x1 178 us: local(): lax.psum_scatter(stacked[6].astype(jnp.bfloat16), ('dp', 'ctx'), scatter_...]
    all_gather x14 -> x0, waiting for transfers between devices: 694 us -> none  [the longest x2 164 us: local(): lax.all_gather(w_gate[layer_index], ('dp', 'ctx'), axis=0, tiled=True)]
    ppermute x0 -> x156, waiting for transfers between devices: none -> 577 us  [the longest x24 201 us: scatter(): moved = lax.ppermute(total.astype(bf16), 'dp', self.up)]
    psum x7 -> x1, waiting for transfers between devices: 342 us -> 27.6 us  [local(): wide = lax.psum(wide, 'tensor').astype(f32)]
    ppermute x0 -> x156, starting transfers between devices: none -> 286 us  [the longest x42 84.1 us: core(): return lax.ppermute(value, 'tensor', self.core_pairs)]
    dot_general x84 -> x30, matrix products: 197 us -> 102 us  [product(): lax.dot_general(left_side, right_side, (contract, ((), ())), preferred_el...]
    unnamed x38 -> x1, waiting for transfers between devices: 54.5 us -> 0.02 us
    another operation x32 -> x9, other arithmetic: 51.5 us -> 1.03 us  [the longest x2 0.51 us: replicate(): jnp.stack([half, other])]
  transfers between devices with their start and end apart: 37 -> 157, of which waited for: 34 -> 69; matrix products, arithmetic and copies ran while one was open for 13% -> 23% of each run, Pallas kernels for 0% -> 0%
where the time goes in v1:
time: 1290 us; the launch traced here: 1280 us
  waiting for transfers between devices  604 us (47%)
  starting transfers between devices  286 us (22%)
  matrix products  117 us (9%)
  other arithmetic  111 us (9%)
  local copies, waits for them, and re-layouts  100 us (8%)
  blocking collectives  40.7 us (3%)
  between operations  18.7 us (1%)
    ppermute x24, waiting for transfers between devices, scatter(): moved = lax.ppermute(total.astype(bf16), 'dp', self.up)  201 us
    ppermute x46, waiting for transfers between devices, peer(): return lax.ppermute(value, ('ctx', 'tensor'), self.peers[j])  188 us
    ppermute x24, waiting for transfers between devices, fetch(): own.append(lax.ppermute(own[-1], 'dp', self.down))  159 us
    dot_general x30, matrix products, product(): lax.dot_general(left_side, right_side, (contract, ((), ())), preferred_el...  102 us
    ppermute x42, starting transfers between devices, core(): return lax.ppermute(value, 'tensor', self.core_pairs)  84.1 us
    ppermute x24, starting transfers between devices, fetch(): own.append(lax.ppermute(own[-1], 'dp', self.down))  64.1 us
    ppermute x46, starting transfers between devices, peer(): return lax.ppermute(value, ('ctx', 'tensor'), self.peers[j])  59.6 us
    ppermute x16, starting transfers between devices, swap(): return lax.ppermute(value, ('ctx', 'tensor'), self.swap_pairs)  59.1 us
  transfers between devices with their start and end apart: 157, of which 69 were waited for; matrix products, arithmetic and copies ran while one was open for 23% of the time, Pallas kernels for 0%

profile of v1, /device:TPU:1, one launch (start us, length us, event | category | flops | bytes accessed | tf_op | source)
XLA Modules:
  0.0 1278.4 jit_solution(9152590695670052272)
XLA Ops:
  72.8 6.6 collective-permute-start.71
  89.9 17.7 %collective-permute-done.71 = bf16[256,1280]{1,0:T(8,128)(2,1)S(1)} collective-permute-done((bf16[256,1280]{1,0:T(8,128)(2,1)}, bf16[256,1280]{1,0:T(8,128)(2,1)S(1)}, u32[]{:S(2)}, u32[]{:S(2)}) %collective-permute-start.71) | collective-permute-done | bytes 655392 | tf_op jit(solution)/shard_map/ppermute | solution.py:75
  109.2 5.4 collective-permute-done.19
  116.3 5.4 collective-permute-done.63
  130.2 36.4 %collective-permute-done.36 = bf16[256,1280]{0,1:T(8,128)(2,1)S(1)} collective-permute-done((bf16[256,1280]{0,1:T(8,128)(2,1)}, bf16[256,1280]{0,1:T(8,128)(2,1)S(1)}, u32[]{:S(2)}, u32[]{:S(2)}) %collective-permute-start.36) | collective-permute-done | bytes 655392 | tf_op jit(solution)/shard_map/ppermute | solution.py:83
  173.3 9.9 collective-permute-done.72
  188.1 9.1 collective-permute-done.20
  202.1 9.2 collective-permute-done.64
  215.4 5.7 collective-permute-done.51
  225.2 5.7 collective-permute-done.7
  235.2 5.6 collective-permute-done.52
  257.1 6.3 collective-permute-start.23
  271.3 9.1 collective-permute-done.81
  285.3 9.1 collective-permute-done.29
  299.3 9.1 collective-permute-done.73
  308.5 6.0 collective-permute-start.40
  315.4 7.1 collective-permute-done.21
  322.5 6.0 collective-permute-start.12
  329.4 7.1 collective-permute-done.65
  367.1 10.8 collective-permute-done.82
  385.8 9.4 collective-permute-done.30
  406.3 10.0 collective-permute-done.22
  416.3 5.1 collective-permute-start.15
  426.6 6.4 collective-permute-done.15
  433.0 10.3 collective-permute-done.14
  462.0 6.9 collective-permute-done.17
  470.6 5.6 fusion.148
  495.3 12.7 collective-permute-done.43
  518.0 6.2 collective-permute-done.48
  528.0 7.4 collective-permute-done.47
  551.0 19.4 %collective-permute-done.57 = bf16[128,2048]{1,0:T(8,128)(2,1)S(1)} collective-permute-done((bf16[128,2048]{1,0:T(8,128)(2,1)S(1)}, bf16[128,2048]{1,0:T(8,128)(2,1)S(1)}, u32[]{:S(2)}, u32[]{:S(2)}) %collective-permute-start.57) | collective-permute-done | bytes 524320 | tf_op jit(solution)/shard_map/ppermute | solution.py:72
  577.1 8.7 collective-permute-done.62
  585.8 11.3 collective-permute-done.61
  605.9 5.7 multiply_convert_fusion.6
  630.4 14.8 %collective-permute-done.93 = bf16[128,2048]{1,0:T(8,128)(2,1)S(1)} collective-permute-done((bf16[128,2048]{1,0:T(8,128)(2,1)S(1)}, bf16[128,2048]{1,0:T(8,128)(2,1)S(1)}, u32[]{:S(2)}, u32[]{:S(2)}) %collective-permute-start.93) | collective-permute-done | bytes 524320 | tf_op jit(solution)/shard_map/ppermute | solution.py:72
  656.6 11.1 collective-permute-done.87
  688.9 6.3 collective-permute-done.97
  716.8 18.2 %collective-permute-done.99 = bf16[128,2048]{1,0:T(8,128)(2,1)S(1)} collective-permute-done((bf16[128,2048]{1,0:T(8,128)(2,1)S(1)}, bf16[128,2048]{1,0:T(8,128)(2,1)S(1)}, u32[]{:S(2)}, u32[]{:S(2)}) %collective-permute-start.99) | collective-permute-done | bytes 524320 | tf_op jit(solution)/shard_map/ppermute | solution.py:72
  755.7 6.8 collective-permute-done.103
  764.3 7.9 multiply_convert_fusion.4
  777.2 5.8 add_convert_fusion
  810.3 5.2 collective-permute-done.106
  832.2 7.0 collective-permute-done.109
  874.6 6.7 collective-permute-done.122
  905.5 40.7 %psum.15 = f32[2,4224]{1,0:T(2,128)S(1)} all-reduce(f32[2,4224]{1,0:T(2,128)S(1)} %pad_maximum_fusion.39), channel_id=1, replica_groups=mesh['dp'=4,'ctx'=2,'tensor'=4] {'dp','ctx','tensor'}, use_global_device_ids=true, to_apply=%region_42.43 | all-reduce | flops 8448 | bytes 67584 | tf_op jit(solution)/shard_map/psum | solution.py:424
  950.0 13.7 %collective-permute-done.133 = bf16[256,1280]{1,0:T(8,128)(2,1)S(1)} collective-permute-done((bf16[256,1280]{1,0:T(8,128)(2,1)}, bf16[256,1280]{1,0:T(8,128)(2,1)S(1)}, u32[]{:S(2)}, u32[]{:S(2)}) %collective-permute-start.133) | collective-permute-done | bytes 655392 | tf_op jit(solution)/shard_map/ppermute | solution.py:93
  965.4 12.3 collective-permute-done.143
  979.8 8.9 collective-permute-done.114
  992.2 12.6 collective-permute-done.154
  1007.1 11.7 collective-permute-done.134
  1018.8 6.8 collective-permute-start.116
  1064.7 5.7 collective-permute-done.147
  1070.5 13.9 %collective-permute-done.127 = bf16[256,1280]{1,0:T(8,128)(2,1)S(1)} collective-permute-done((bf16[256,1280]{1,0:T(8,128)(2,1)S(1)}, bf16[256,1280]{1,0:T(8,128)(2,1)S(1)}, u32[]{:S(2)}, u32[]{:S(2)}) %collective-permute-start.127) | collective-permute-done | bytes 655392 | tf_op jit(solution)/shard_map/ppermute | solution.py:93
  1084.6 23.7 %collective-permute-done.117 = bf16[256,896]{0,1:T(8,128)(2,1)S(1)} collective-permute-done((bf16[256,896]{0,1:T(8,128)(2,1)S(1)}, bf16[256,896]{0,1:T(8,128)(2,1)S(1)}, u32[]{:S(2)}, u32[]{:S(2)}) %collective-permute-start.117) | collective-permute-done | bytes 458784 | tf_op jit(solution)/shard_map/ppermute | solution.py:93
  1108.7 22.6 %collective-permute-done.118 = bf16[256,896]{0,1:T(8,128)(2,1)S(1)} collective-permute-done((bf16[256,896]{0,1:T(8,128)(2,1)S(1)}, bf16[256,896]{0,1:T(8,128)(2,1)S(1)}, u32[]{:S(2)}, u32[]{:S(2)}) %collective-permute-start.118) | collective-permute-done | bytes 458784 | tf_op jit(solution)/shard_map/ppermute | solution.py:93
  1131.7 13.1 %collective-permute-done.128 = bf16[256,1280]{1,0:T(8,128)(2,1)S(1)} collective-permute-done((bf16[256,1280]{1,0:T(8,128)(2,1)S(1)}, bf16[256,1280]{1,0:T(8,128)(2,1)S(1)}, u32[]{:S(2)}, u32[]{:S(2)}) %collective-permute-start.128) | collective-permute-done | bytes 655392 | tf_op jit(solution)/shard_map/ppermute | solution.py:93
  1144.9 13.6 %collective-permute-done.138 = bf16[256,1280]{1,0:T(8,128)(2,1)S(1)} collective-permute-done((bf16[256,1280]{1,0:T(8,128)(2,1)S(1)}, bf16[256,1280]{1,0:T(8,128)(2,1)S(1)}, u32[]{:S(2)}, u32[]{:S(2)}) %collective-permute-start.138) | collective-permute-done | bytes 655392 | tf_op jit(solution)/shard_map/ppermute | solution.py:93
  1158.7 9.7 collective-permute-done.119
  1168.6 13.9 %collective-permute-done.149 = bf16[256,1280]{1,0:T(8,128)(2,1)S(1)} collective-permute-done((bf16[256,1280]{1,0:T(8,128)(2,1)S(1)}, bf16[256,1280]{1,0:T(8,128)(2,1)S(1)}, u32[]{:S(2)}, u32[]{:S(2)}) %collective-permute-start.149) | collective-permute-done | bytes 655392 | tf_op jit(solution)/shard_map/ppermute | solution.py:93
  1182.6 13.9 %collective-permute-done.129 = bf16[256,1280]{1,0:T(8,128)(2,1)S(1)} collective-permute-done((bf16[256,1280]{1,0:T(8,128)(2,1)S(1)}, bf16[256,1280]{1,0:T(8,128)(2,1)S(1)}, u32[]{:S(2)}, u32[]{:S(2)}) %collective-permute-start.129) | collective-permute-done | bytes 655392 | tf_op jit(solution)/shard_map/ppermute | solution.py:93
  1196.5 5.8 collective-permute-start.120
  1202.4 8.1 collective-permute-done.139
  1210.5 5.8 collective-permute-start.150
  1224.0 27.6 %all-reduce.2.cloned.1.call-done = bf16[2,2,256,320]{2,3,0,1:T(8,128)(2,1)} async-done(((bf16[2,2,256,320]{2,3,0,1:T(8,128)(2,1)}), bf16[2,2,256,320]{2,3,0,1:T(8,128)(2,1)}) %all-reduce.2.cloned.1.call-update) | async-done | bytes 655376 | tf_op jit(solution)/shard_map/psum | solution.py:423
  (1004 shorter events, 573.6 us)
Async XLA Ops:
  7.2 1244.4 %all-reduce.2.cloned.1.call-start = ((), (), s32[]{:S(2)}) async-start(), calls=%async_computation | async-start | bytes 1310720 | tf_op jit(solution)/shard_map/psum | solution.py:423
  7.2 34.2 %collective-permute-start.1 = (bf16[2,528]{1,0:T(2,128)(2,1)}, bf16[2,528]{1,0:T(2,128)(2,1)S(1)}, u32[]{:S(2)}, u32[]{:S(2)}) collective-permute-start(bf16[2,528]{1,0:T(2,128)(2,1)} %param.20), channel_id=1, source_target_pairs={{0,4},{4,0},{1,5},{5,1},{2,6},{6,2},{3,7},{7,3},{8,12},{12,8},{9,1... | collective-permute-start | bytes 6344 | tf_op jit(solution)/shard_map/ppermute | solution.py:209
  14.3 52.8 %collective-permute-start.5 = (bf16[256,896]{0,1:T(8,128)(2,1)}, bf16[256,896]{0,1:T(8,128)(2,1)}, u32[]{:S(2)}, u32[]{:S(2)}) collective-permute-start(bf16[256,896]{0,1:T(8,128)(2,1)} %pad_maximum_fusion.12), channel_id=1, source_target_pairs={{0,0},{1,4},{2,2},{3,6},{4,1},{5,5},{6,3},{7,7},{8,8},{9,12},{10,1... | collective-permute-start | bytes 1376264 | tf_op jit(solution)/shard_map/ppermute | solution.py:75
  17.8 46.4 %collective-permute-start.49 = (bf16[256,896]{0,1:T(8,128)(2,1)}, bf16[256,896]{0,1:T(8,128)(2,1)}, u32[]{:S(2)}, u32[]{:S(2)}) collective-permute-start(bf16[256,896]{0,1:T(8,128)(2,1)} %pad_maximum_fusion.13), channel_id=1, source_target_pairs={{0,0},{1,4},{2,2},{3,6},{4,1},{5,5},{6,3},{7,7},{8,8},{9,12},{10,1... | collective-permute-start | bytes 1376264 | tf_op jit(solution)/shard_map/ppermute | solution.py:75
  24.2 100.7 %collective-permute-start = (bf16[256,2048]{1,0:T(8,128)(2,1)S(1)}, bf16[256,2048]{1,0:T(8,128)(2,1)}, u32[]{:S(2)}, u32[]{:S(2)}) collective-permute-start(bf16[256,2048]{1,0:T(8,128)(2,1)S(1)} %reshape.957), channel_id=1, source_target_pairs={{0,4},{1,5},{2,6},{3,7},{4,0},{5,1},{6,2},{7,3},{8,12},{9,13},{10,... | collective-permute-start | bytes 3145736 | tf_op jit(solution)/shard_map/ppermute | solution.py:72
  30.0 51.4 %collective-permute-start.79 = (bf16[256,1280]{0,1:T(8,128)(2,1)}, bf16[256,1280]{0,1:T(8,128)(2,1)}, u32[]{:S(2)}, u32[]{:S(2)}) collective-permute-start(bf16[256,1280]{0,1:T(8,128)(2,1)} %get-tuple-element.119), channel_id=1, source_target_pairs={{0,0},{1,4},{2,2},{3,6},{4,1},{5,5},{6,3},{7,7},{8,8},{9,12},{10,1... | collective-permute-start | bytes 1966088 | tf_op jit(solution)/shard_map/ppermute | solution.py:75
  67.1 59.6 %collective-permute-start.92 = (bf16[256,2048]{1,0:T(8,128)(2,1)S(1)}, bf16[256,2048]{1,0:T(8,128)(2,1)S(1)}, u32[]{:S(2)}, u32[]{:S(2)}) collective-permute-start(bf16[256,2048]{1,0:T(8,128)(2,1)S(1)} %reshape.972), channel_id=1, source_target_pairs={{0,4},{1,5},{2,6},{3,7},{4,0},{5,1},{6,2},{7,3},{8,12},{9,13},{10,... | collective-permute-start | bytes 3145736 | tf_op jit(solution)/shard_map/ppermute | solution.py:72
  72.8 34.9 %collective-permute-start.71 = (bf16[256,1280]{1,0:T(8,128)(2,1)}, bf16[256,1280]{1,0:T(8,128)(2,1)S(1)}, u32[]{:S(2)}, u32[]{:S(2)}) collective-permute-start(bf16[256,1280]{1,0:T(8,128)(2,1)} %get-tuple-element.123), channel_id=1, source_target_pairs={{0,0},{1,4},{2,2},{3,6},{4,1},{5,5},{6,3},{7,7},{8,8},{9,12},{10,1... | collective-permute-start | bytes 1966088 | tf_op jit(solution)/shard_map/ppermute | solution.py:75
  81.5 33.2 %collective-permute-start.19 = (bf16[256,1280]{1,0:T(8,128)(2,1)}, bf16[256,1280]{1,0:T(8,128)(2,1)S(1)}, u32[]{:S(2)}, u32[]{:S(2)}) collective-permute-start(bf16[256,1280]{1,0:T(8,128)(2,1)} %get-tuple-element.122), channel_id=1, source_target_pairs={{0,0},{1,4},{2,2},{3,6},{4,1},{5,5},{6,3},{7,7},{8,8},{9,12},{10,1... | collective-permute-start | bytes 1966088 | tf_op jit(solution)/shard_map/ppermute | solution.py:75
  85.4 36.3 %collective-permute-start.63 = (bf16[256,1280]{1,0:T(8,128)(2,1)}, bf16[256,1280]{1,0:T(8,128)(2,1)S(1)}, u32[]{:S(2)}, u32[]{:S(2)}) collective-permute-start(bf16[256,1280]{1,0:T(8,128)(2,1)} %get-tuple-element.121), channel_id=1, source_target_pairs={{0,0},{1,4},{2,2},{3,6},{4,1},{5,5},{6,3},{7,7},{8,8},{9,12},{10,1... | collective-permute-start | bytes 1966088 | tf_op jit(solution)/shard_map/ppermute | solution.py:75
  121.7 135.5 %collective-permute-start.9 = (bf16[256,896]{0,1:T(8,128)(2,1)}, bf16[256,896]{0,1:T(8,128)(2,1)S(1)}, u32[]{:S(2)}, u32[]{:S(2)}) collective-permute-start(bf16[256,896]{0,1:T(8,128)(2,1)} %collective-permute-done.5), channel_id=1, source_target_pairs={{0,1},{1,0},{2,3},{3,2},{4,5},{5,4},{6,7},{7,6},{8,9},{9,8},{10,11... | collective-permute-start | bytes 1376264 | tf_op jit(solution)/shard_map/ppermute | solution.py:78
  122.2 122.6 %collective-permute-start.53 = (bf16[256,896]{0,1:T(8,128)(2,1)}, bf16[256,896]{0,1:T(8,128)(2,1)S(1)}, u32[]{:S(2)}, u32[]{:S(2)}) collective-permute-start(bf16[256,896]{0,1:T(8,128)(2,1)} %collective-permute-done.49), channel_id=1, source_target_pairs={{0,1},{1,0},{2,3},{3,2},{4,5},{5,4},{6,7},{7,6},{8,9},{9,8},{10,11... | collective-permute-start | bytes 1376264 | tf_op jit(solution)/shard_map/ppermute | solution.py:78
  122.4 50.0 %collective-permute-start.28 = (bf16[256,1280]{1,0:T(8,128)(2,1)S(1)}, bf16[256,1280]{1,0:T(8,128)(2,1)S(1)}, u32[]{:S(2)}, u32[]{:S(2)}) collective-permute-start(bf16[256,1280]{1,0:T(8,128)(2,1)S(1)} %collective-permute-done.27), channel_id=1, source_target_pairs={{0,24},{8,0},{16,8},{24,16},{1,25},{9,1},{17,9},{25,17},{2,26},{10... | collective-permute-start | bytes 1966088 | tf_op jit(solution)/shard_map/ppermute | solution.py:83
  124.9 46.5 %collective-permute-start.80 = (bf16[256,1280]{0,1:T(8,128)(2,1)}, bf16[256,1280]{0,1:T(8,128)(2,1)S(1)}, u32[]{:S(2)}, u32[]{:S(2)}) collective-permute-start(bf16[256,1280]{0,1:T(8,128)(2,1)} %collective-permute-done.79), channel_id=1, source_target_pairs={{0,24},{8,0},{16,8},{24,16},{1,25},{9,1},{17,9},{25,17},{2,26},{10... | collective-permute-start | bytes 1966088 | tf_op jit(solution)/shard_map/ppermute | solution.py:83
  126.7 39.9 %collective-permute-start.36 = (bf16[256,1280]{0,1:T(8,128)(2,1)}, bf16[256,1280]{0,1:T(8,128)(2,1)S(1)}, u32[]{:S(2)}, u32[]{:S(2)}) collective-permute-start(bf16[256,1280]{0,1:T(8,128)(2,1)} %collective-permute-done.35), channel_id=1, source_target_pairs={{0,24},{8,0},{16,8},{24,16},{1,25},{9,1},{17,9},{25,17},{2,26},{10... | collective-permute-start | bytes 1966088 | tf_op jit(solution)/shard_map/ppermute | solution.py:83
  172.4 38.8 %collective-permute-start.64 = (bf16[256,1280]{1,0:T(8,128)(2,1)S(1)}, bf16[256,1280]{1,0:T(8,128)(2,1)S(1)}, u32[]{:S(2)}, u32[]{:S(2)}) collective-permute-start(bf16[256,1280]{1,0:T(8,128)(2,1)S(1)} %collective-permute-done.63), channel_id=1, source_target_pairs={{0,24},{8,0},{16,8},{24,16},{1,25},{9,1},{17,9},{25,17},{2,26},{10... | collective-permute-start | bytes 1966088 | tf_op jit(solution)/shard_map/ppermute | solution.py:83
  183.2 37.9 %collective-permute-start.51 = (bf16[256,896]{0,1:T(8,128)(2,1)S(1)}, bf16[256,896]{0,1:T(8,128)(2,1)S(1)}, u32[]{:S(2)}, u32[]{:S(2)}) collective-permute-start(bf16[256,896]{0,1:T(8,128)(2,1)S(1)} %collective-permute-done.50), channel_id=1, source_target_pairs={{0,24},{8,0},{16,8},{24,16},{1,25},{9,1},{17,9},{25,17},{2,26},{10... | collective-permute-start | bytes 1376264 | tf_op jit(solution)/shard_map/ppermute | solution.py:83
  197.2 33.7 %collective-permute-start.7 = (bf16[256,896]{0,1:T(8,128)(2,1)S(1)}, bf16[256,896]{0,1:T(8,128)(2,1)S(1)}, u32[]{:S(2)}, u32[]{:S(2)}) collective-permute-start(bf16[256,896]{0,1:T(8,128)(2,1)S(1)} %collective-permute-done.6), channel_id=1, source_target_pairs={{0,24},{8,0},{16,8},{24,16},{1,25},{9,1},{17,9},{25,17},{2,26},{10... | collective-permute-start | bytes 1376264 | tf_op jit(solution)/shard_map/ppermute | solution.py:83
  211.3 36.3 %collective-permute-start.54 = (bf16[256,896]{0,1:T(8,128)(2,1)S(1)}, bf16[256,896]{0,1:T(8,128)(2,1)S(1)}, u32[]{:S(2)}, u32[]{:S(2)}) collective-permute-start(bf16[256,896]{0,1:T(8,128)(2,1)S(1)} %collective-permute-done.50), channel_id=1, source_target_pairs={{0,1},{1,0},{2,3},{3,2},{4,5},{5,4},{6,7},{7,6},{8,9},{9,8},{10,11... | collective-permute-start | bytes 1376264 | tf_op jit(solution)/shard_map/ppermute | solution.py:78
  252.3 28.1 %collective-permute-start.81 = (bf16[256,1280]{0,1:T(8,128)(2,1)S(1)}, bf16[256,1280]{0,1:T(8,128)(2,1)S(1)}, u32[]{:S(2)}, u32[]{:S(2)}) collective-permute-start(bf16[256,1280]{0,1:T(8,128)(2,1)S(1)} %collective-permute-done.80), channel_id=1, source_target_pairs={{0,24},{8,0},{16,8},{24,16},{1,25},{9,1},{17,9},{25,17},{2,26},{10... | collective-permute-start | bytes 1966088 | tf_op jit(solution)/shard_map/ppermute | solution.py:83
  257.1 165.2 %collective-permute-start.23 = (bf16[256,1280]{1,0:T(8,128)(2,1)S(1)}, bf16[256,1280]{1,0:T(8,128)(2,1)S(1)}, u32[]{:S(2)}, u32[]{:S(2)}) collective-permute-start(bf16[256,1280]{1,0:T(8,128)(2,1)S(1)} %collective-permute-done.19), channel_id=1, source_target_pairs={{0,1},{1,0},{2,3},{3,2},{4,5},{5,4},{6,7},{7,6},{8,9},{9,8},{10,11... | collective-permute-start | bytes 1966088 | tf_op jit(solution)/shard_map/ppermute | solution.py:78
  264.3 30.2 %collective-permute-start.29 = (bf16[256,1280]{1,0:T(8,128)(2,1)S(1)}, bf16[256,1280]{1,0:T(8,128)(2,1)S(1)}, u32[]{:S(2)}, u32[]{:S(2)}) collective-permute-start(bf16[256,1280]{1,0:T(8,128)(2,1)S(1)} %collective-permute-done.28), channel_id=1, source_target_pairs={{0,24},{8,0},{16,8},{24,16},{1,25},{9,1},{17,9},{25,17},{2,26},{10... | collective-permute-start | bytes 1966088 | tf_op jit(solution)/shard_map/ppermute | solution.py:83
  265.1 95.3 %collective-permute-start.39 = (bf16[256,1280]{0,1:T(8,128)(2,1)}, bf16[256,1280]{0,1:T(8,128)(2,1)S(1)}, u32[]{:S(2)}, u32[]{:S(2)}) collective-permute-start(bf16[256,1280]{0,1:T(8,128)(2,1)} %collective-permute-done.35), channel_id=1, source_target_pairs={{0,1},{1,0},{2,3},{3,2},{4,5},{5,4},{6,7},{7,6},{8,9},{9,8},{10,11... | collective-permute-start | bytes 1966088 | tf_op jit(solution)/shard_map/ppermute | solution.py:78
  266.3 42.1 %collective-permute-start.73 = (bf16[256,1280]{1,0:T(8,128)(2,1)S(1)}, bf16[256,1280]{1,0:T(8,128)(2,1)S(1)}, u32[]{:S(2)}, u32[]{:S(2)}) collective-permute-start(bf16[256,1280]{1,0:T(8,128)(2,1)S(1)} %collective-permute-done.72), channel_id=1, source_target_pairs={{0,24},{8,0},{16,8},{24,16},{1,25},{9,1},{17,9},{25,17},{2,26},{10... | collective-permute-start | bytes 1966088 | tf_op jit(solution)/shard_map/ppermute | solution.py:83
  280.4 42.1 %collective-permute-start.21 = (bf16[256,1280]{1,0:T(8,128)(2,1)S(1)}, bf16[256,1280]{1,0:T(8,128)(2,1)S(1)}, u32[]{:S(2)}, u32[]{:S(2)}) collective-permute-start(bf16[256,1280]{1,0:T(8,128)(2,1)S(1)} %collective-permute-done.20), channel_id=1, source_target_pairs={{0,24},{8,0},{16,8},{24,16},{1,25},{9,1},{17,9},{25,17},{2,26},{10... | collective-permute-start | bytes 1966088 | tf_op jit(solution)/shard_map/ppermute | solution.py:83
  294.4 42.1 %collective-permute-start.65 = (bf16[256,1280]{1,0:T(8,128)(2,1)S(1)}, bf16[256,1280]{1,0:T(8,128)(2,1)S(1)}, u32[]{:S(2)}, u32[]{:S(2)}) collective-permute-start(bf16[256,1280]{1,0:T(8,128)(2,1)S(1)} %collective-permute-done.64), channel_id=1, source_target_pairs={{0,24},{8,0},{16,8},{24,16},{1,25},{9,1},{17,9},{25,17},{2,26},{10... | collective-permute-start | bytes 1966088 | tf_op jit(solution)/shard_map/ppermute | solution.py:83
  308.5 56.2 %collective-permute-start.40 = (bf16[256,1280]{0,1:T(8,128)(2,1)S(1)}, bf16[256,1280]{0,1:T(8,128)(2,1)S(1)}, u32[]{:S(2)}, u32[]{:S(2)}) collective-permute-start(bf16[256,1280]{0,1:T(8,128)(2,1)S(1)} %collective-permute-done.36), channel_id=1, source_target_pairs={{0,1},{1,0},{2,3},{3,2},{4,5},{5,4},{6,7},{7,6},{8,9},{9,8},{10,11... | collective-permute-start | bytes 1966088 | tf_op jit(solution)/shard_map/ppermute | solution.py:78
  358.5 39.2 %collective-permute-start.31 = (bf16[256,1280]{1,0:T(8,128)(2,1)S(1)}, bf16[256,1280]{1,0:T(8,128)(2,1)S(1)}, u32[]{:S(2)}, u32[]{:S(2)}) collective-permute-start(bf16[256,1280]{1,0:T(8,128)(2,1)S(1)} %collective-permute-done.27), channel_id=1, source_target_pairs={{0,1},{1,0},{2,3},{3,2},{4,5},{5,4},{6,7},{7,6},{8,9},{9,8},{10,11... | collective-permute-start | bytes 1966088 | tf_op jit(solution)/shard_map/ppermute | solution.py:78
  382.9 40.4 %collective-permute-start.24 = (bf16[256,1280]{1,0:T(8,128)(2,1)S(1)}, bf16[256,1280]{1,0:T(8,128)(2,1)S(1)}, u32[]{:S(2)}, u32[]{:S(2)}) collective-permute-start(bf16[256,1280]{1,0:T(8,128)(2,1)S(1)} %collective-permute-done.20), channel_id=1, source_target_pairs={{0,1},{1,0},{2,3},{3,2},{4,5},{5,4},{6,7},{7,6},{8,9},{9,8},{10,11... | collective-permute-start | bytes 1966088 | tf_op jit(solution)/shard_map/ppermute | solution.py:78
  423.2 28.7 %collective-permute-start.26 = (bf16[256,1280]{1,0:T(8,128)(2,1)S(1)}, bf16[256,1280]{1,0:T(8,128)(2,1)S(1)}, u32[]{:S(2)}, u32[]{:S(2)}) collective-permute-start(bf16[256,1280]{1,0:T(8,128)(2,1)S(1)} %collective-permute-done.22), channel_id=1, source_target_pairs={{0,1},{1,0},{2,3},{3,2},{4,5},{5,4},{6,7},{7,6},{8,9},{9,8},{10,11... | collective-permute-start | bytes 1966088 | tf_op jit(solution)/shard_map/ppermute | solution.py:78
  448.8 41.4 %collective-permute-start.75 = (bf16[256,1280]{1,0:T(8,128)(2,1)S(1)}, bf16[256,1280]{1,0:T(8,128)(2,1)S(1)}, u32[]{:S(2)}, u32[]{:S(2)}) collective-permute-start(bf16[256,1280]{1,0:T(8,128)(2,1)S(1)} %collective-permute-done.71), channel_id=1, source_target_pairs={{0,1},{1,0},{2,3},{3,2},{4,5},{5,4},{6,7},{7,6},{8,9},{9,8},{10,11... | collective-permute-start | bytes 1966088 | tf_op jit(solution)/shard_map/ppermute | solution.py:78
  452.0 36.3 %collective-permute-start.74 = (bf16[256,1280]{1,0:T(8,128)(2,1)S(1)}, bf16[256,1280]{1,0:T(8,128)(2,1)S(1)}, u32[]{:S(2)}, u32[]{:S(2)}) collective-permute-start(bf16[256,1280]{1,0:T(8,128)(2,1)S(1)} %collective-permute-done.73), channel_id=1, source_target_pairs={{0,24},{8,0},{16,8},{24,16},{1,25},{9,1},{17,9},{25,17},{2,26},{10... | collective-permute-start | bytes 1966088 | tf_op jit(solution)/shard_map/ppermute | solution.py:83
  457.4 30.0 %collective-permute-start.85 = (bf16[256,1280]{0,1:T(8,128)(2,1)S(1)}, bf16[256,1280]{0,1:T(8,128)(2,1)S(1)}, u32[]{:S(2)}, u32[]{:S(2)}) collective-permute-start(bf16[256,1280]{0,1:T(8,128)(2,1)S(1)} %collective-permute-done.81), channel_id=1, source_target_pairs={{0,1},{1,0},{2,3},{3,2},{4,5},{5,4},{6,7},{7,6},{8,9},{9,8},{10,11... | collective-permute-start | bytes 1966088 | tf_op jit(solution)/shard_map/ppermute | solution.py:78
  490.3 27.6 %collective-permute-start.66 = (bf16[256,1280]{1,0:T(8,128)(2,1)S(1)}, bf16[256,1280]{1,0:T(8,128)(2,1)S(1)}, u32[]{:S(2)}, u32[]{:S(2)}) collective-permute-start(bf16[256,1280]{1,0:T(8,128)(2,1)S(1)} %collective-permute-done.65), channel_id=1, source_target_pairs={{0,24},{8,0},{16,8},{24,16},{1,25},{9,1},{17,9},{25,17},{2,26},{10... | collective-permute-start | bytes 1966088 | tf_op jit(solution)/shard_map/ppermute | solution.py:83
  515.2 34.5 %collective-permute-start.67 = (bf16[256,1280]{1,0:T(8,128)(2,1)S(1)}, bf16[256,1280]{1,0:T(8,128)(2,1)S(1)}, u32[]{:S(2)}, u32[]{:S(2)}) collective-permute-start(bf16[256,1280]{1,0:T(8,128)(2,1)S(1)} %collective-permute-done.63), channel_id=1, source_target_pairs={{0,1},{1,0},{2,3},{3,2},{4,5},{5,4},{6,7},{7,6},{8,9},{9,8},{10,11... | collective-permute-start | bytes 1966088 | tf_op jit(solution)/shard_map/ppermute | solution.py:78
  517.9 31.8 %collective-permute-start.68 = (bf16[256,1280]{1,0:T(8,128)(2,1)S(1)}, bf16[256,1280]{1,0:T(8,128)(2,1)S(1)}, u32[]{:S(2)}, u32[]{:S(2)}) collective-permute-start(bf16[256,1280]{1,0:T(8,128)(2,1)S(1)} %collective-permute-done.64), channel_id=1, source_target_pairs={{0,1},{1,0},{2,3},{3,2},{4,5},{5,4},{6,7},{7,6},{8,9},{9,8},{10,11... | collective-permute-start | bytes 1966088 | tf_op jit(solution)/shard_map/ppermute | solution.py:78
  622.3 30.0 %collective-permute-start.95 = (bf16[128,2048]{1,0:T(8,128)(2,1)S(1)}, bf16[128,2048]{1,0:T(8,128)(2,1)S(1)}, u32[]{:S(2)}, u32[]{:S(2)}) collective-permute-start(bf16[128,2048]{1,0:T(8,128)(2,1)S(1)} %get-tuple-element.103), channel_id=1, source_target_pairs={{0,6},{1,7},{2,4},{3,5},{4,2},{5,3},{6,0},{7,1},{8,14},{9,15},{10,... | collective-permute-start | bytes 1572872 | tf_op jit(solution)/shard_map/ppermute | solution.py:72
  624.3 31.7 %collective-permute-start.94 = (bf16[128,2048]{1,0:T(8,128)(2,1)S(1)}, bf16[128,2048]{1,0:T(8,128)(2,1)S(1)}, u32[]{:S(2)}, u32[]{:S(2)}) collective-permute-start(bf16[128,2048]{1,0:T(8,128)(2,1)S(1)} %get-tuple-element.104), channel_id=1, source_target_pairs={{0,4},{1,5},{2,6},{3,7},{4,0},{5,1},{6,2},{7,3},{8,12},{9,13},{10,... | collective-permute-start | bytes 1572872 | tf_op jit(solution)/shard_map/ppermute | solution.py:72
  624.5 43.1 %collective-permute-start.87 = (bf16[128,2048]{1,0:T(8,128)(2,1)S(1)}, bf16[128,2048]{1,0:T(8,128)(2,1)S(1)}, u32[]{:S(2)}, u32[]{:S(2)}) collective-permute-start(bf16[128,2048]{1,0:T(8,128)(2,1)S(1)} %get-tuple-element.105), channel_id=1, source_target_pairs={{0,2},{1,3},{2,0},{3,1},{4,6},{5,7},{6,4},{7,5},{8,10},{9,11},{10,... | collective-permute-start | bytes 1572872 | tf_op jit(solution)/shard_map/ppermute | solution.py:72
  625.2 42.5 %collective-permute-start.89 = (bf16[128,2048]{1,0:T(8,128)(2,1)S(1)}, bf16[128,2048]{1,0:T(8,128)(2,1)S(1)}, u32[]{:S(2)}, u32[]{:S(2)}) collective-permute-start(bf16[128,2048]{1,0:T(8,128)(2,1)S(1)} %get-tuple-element.106), channel_id=1, source_target_pairs={{0,6},{1,7},{2,4},{3,5},{4,2},{5,3},{6,0},{7,1},{8,14},{9,15},{10,... | collective-permute-start | bytes 1572872 | tf_op jit(solution)/shard_map/ppermute | solution.py:72
  652.4 150.7 %collective-permute-start.151 = (bf16[1024,1280]{1,0:T(8,128)(2,1)}, bf16[1024,1280]{1,0:T(8,128)(2,1)}, u32[]{:S(2)}, u32[]{:S(2)}) collective-permute-start(bf16[1024,1280]{1,0:T(8,128)(2,1)} %slice.793), channel_id=1, source_target_pairs={{0,1},{1,0},{2,3},{3,2},{4,5},{5,4},{6,7},{7,6},{8,9},{9,8},{10,11... | collective-permute-start | bytes 7864328 | tf_op jit(solution)/shard_map/ppermute | solution.py:78
  681.5 136.9 %collective-permute-start.131 = (bf16[1024,1280]{1,0:T(8,128)(2,1)}, bf16[1024,1280]{1,0:T(8,128)(2,1)}, u32[]{:S(2)}, u32[]{:S(2)}) collective-permute-start(bf16[1024,1280]{1,0:T(8,128)(2,1)} %slice.769), channel_id=1, source_target_pairs={{0,1},{1,0},{2,3},{3,2},{4,5},{5,4},{6,7},{7,6},{8,9},{9,8},{10,11... | collective-permute-start | bytes 7864328 | tf_op jit(solution)/shard_map/ppermute | solution.py:78
  751.0 71.4 %collective-permute-start.141 = (bf16[1024,1280]{1,0:T(8,128)(2,1)}, bf16[1024,1280]{1,0:T(8,128)(2,1)S(1)}, u32[]{:S(2)}, u32[]{:S(2)}) collective-permute-start(bf16[1024,1280]{1,0:T(8,128)(2,1)} %slice.781), channel_id=1, source_target_pairs={{0,1},{1,0},{2,3},{3,2},{4,5},{5,4},{6,7},{7,6},{8,9},{9,8},{10,11... | collective-permute-start | bytes 7864328 | tf_op jit(solution)/shard_map/ppermute | solution.py:78
  810.2 228.7 %collective-permute-start.146 = (bf16[1024,1280]{1,0:T(8,128)(2,1)}, bf16[1024,1280]{1,0:T(8,128)(2,1)}, u32[]{:S(2)}, u32[]{:S(2)}) collective-permute-start(bf16[1024,1280]{1,0:T(8,128)(2,1)} %slice.787), channel_id=1, source_target_pairs={{0,1},{1,0},{2,3},{3,2},{4,5},{5,4},{6,7},{7,6},{8,9},{9,8},{10,11... | collective-permute-start | bytes 7864328 | tf_op jit(solution)/shard_map/ppermute | solution.py:78
  826.8 38.1 %collective-permute-start.152 = (bf16[256,1280]{1,0:T(8,128)(2,1)}, bf16[256,1280]{1,0:T(8,128)(2,1)S(1)}, u32[]{:S(2)}, u32[]{:S(2)}) collective-permute-start(bf16[256,1280]{1,0:T(8,128)(2,1)} %slice.1064), channel_id=1, source_target_pairs={{0,8},{8,16},{16,24},{24,0},{1,9},{9,17},{17,25},{25,1},{2,10},{10... | collective-permute-start | bytes 1966088 | tf_op jit(solution)/shard_map/ppermute | solution.py:93
  830.4 36.8 %collective-permute-start.132 = (bf16[256,1280]{1,0:T(8,128)(2,1)}, bf16[256,1280]{1,0:T(8,128)(2,1)S(1)}, u32[]{:S(2)}, u32[]{:S(2)}) collective-permute-start(bf16[256,1280]{1,0:T(8,128)(2,1)} %slice.1068), channel_id=1, source_target_pairs={{0,8},{8,16},{16,24},{24,0},{1,9},{9,17},{17,25},{25,1},{2,10},{10... | collective-permute-start | bytes 1966088 | tf_op jit(solution)/shard_map/ppermute | solution.py:93
  839.2 32.1 %collective-permute-start.142 = (bf16[256,1280]{1,0:T(8,128)(2,1)}, bf16[256,1280]{1,0:T(8,128)(2,1)S(1)}, u32[]{:S(2)}, u32[]{:S(2)}) collective-permute-start(bf16[256,1280]{1,0:T(8,128)(2,1)} %slice.1066), channel_id=1, source_target_pairs={{0,8},{8,16},{16,24},{24,0},{1,9},{9,17},{17,25},{25,1},{2,10},{10... | collective-permute-start | bytes 1966088 | tf_op jit(solution)/shard_map/ppermute | solution.py:93
  843.7 37.6 %collective-permute-start.122 = (bf16[256,896]{0,1:T(8,128)(2,1)}, bf16[256,896]{0,1:T(8,128)(2,1)}, u32[]{:S(2)}, u32[]{:S(2)}) collective-permute-start(bf16[256,896]{0,1:T(8,128)(2,1)} %slice.1070), channel_id=1, source_target_pairs={{0,8},{8,16},{16,24},{24,0},{1,9},{9,17},{17,25},{25,1},{2,10},{10... | collective-permute-start | bytes 1376264 | tf_op jit(solution)/shard_map/ppermute | solution.py:93
  881.3 160.2 %collective-permute-start.126 = (bf16[1024,1280]{1,0:T(8,128)(2,1)}, bf16[1024,1280]{1,0:T(8,128)(2,1)}, u32[]{:S(2)}, u32[]{:S(2)}) collective-permute-start(bf16[1024,1280]{1,0:T(8,128)(2,1)} %slice.763), channel_id=1, source_target_pairs={{0,1},{1,0},{2,3},{3,2},{4,5},{5,4},{6,7},{7,6},{8,9},{9,8},{10,11... | collective-permute-start | bytes 7864328 | tf_op jit(solution)/shard_map/ppermute | solution.py:78
  888.2 160.2 %collective-permute-start.136 = (bf16[1024,1280]{1,0:T(8,128)(2,1)}, bf16[1024,1280]{1,0:T(8,128)(2,1)}, u32[]{:S(2)}, u32[]{:S(2)}) collective-permute-start(bf16[1024,1280]{1,0:T(8,128)(2,1)} %slice.775), channel_id=1, source_target_pairs={{0,1},{1,0},{2,3},{3,2},{4,5},{5,4},{6,7},{7,6},{8,9},{9,8},{10,11... | collective-permute-start | bytes 7864328 | tf_op jit(solution)/shard_map/ppermute | solution.py:78
  890.5 57.8 %collective-permute-start.153 = (bf16[256,1280]{1,0:T(8,128)(2,1)}, bf16[256,1280]{1,0:T(8,128)(2,1)}, u32[]{:S(2)}, u32[]{:S(2)}) collective-permute-start(bf16[256,1280]{1,0:T(8,128)(2,1)} %fusion.23), channel_id=1, source_target_pairs={{0,8},{8,16},{16,24},{24,0},{1,9},{9,17},{17,25},{25,1},{2,10},{10... | collective-permute-start | bytes 1966088 | tf_op jit(solution)/shard_map/ppermute | solution.py:93
  892.3 54.6 %collective-permute-start.123 = (bf16[256,896]{0,1:T(8,128)(2,1)}, bf16[256,896]{0,1:T(8,128)(2,1)}, u32[]{:S(2)}, u32[]{:S(2)}) collective-permute-start(bf16[256,896]{0,1:T(8,128)(2,1)} %fusion.53), channel_id=1, source_target_pairs={{0,8},{8,16},{16,24},{24,0},{1,9},{9,17},{17,25},{25,1},{2,10},{10... | collective-permute-start | bytes 1376264 | tf_op jit(solution)/shard_map/ppermute | solution.py:93
  948.3 29.4 %collective-permute-start.143 = (bf16[256,1280]{1,0:T(8,128)(2,1)}, bf16[256,1280]{1,0:T(8,128)(2,1)S(1)}, u32[]{:S(2)}, u32[]{:S(2)}) collective-permute-start(bf16[256,1280]{1,0:T(8,128)(2,1)} %fusion.29), channel_id=1, source_target_pairs={{0,8},{8,16},{16,24},{24,0},{1,9},{9,17},{17,25},{25,1},{2,10},{10... | collective-permute-start | bytes 1966088 | tf_op jit(solution)/shard_map/ppermute | solution.py:93
  989.9 28.9 %collective-permute-start.134 = (bf16[256,1280]{1,0:T(8,128)(2,1)S(1)}, bf16[256,1280]{1,0:T(8,128)(2,1)S(1)}, u32[]{:S(2)}, u32[]{:S(2)}) collective-permute-start(bf16[256,1280]{1,0:T(8,128)(2,1)S(1)} %fusion.36), channel_id=1, source_target_pairs={{0,8},{8,16},{16,24},{24,0},{1,9},{9,17},{17,25},{25,1},{2,10},{10... | collective-permute-start | bytes 1966088 | tf_op jit(solution)/shard_map/ppermute | solution.py:93
  1004.8 28.1 %collective-permute-start.144 = (bf16[256,1280]{1,0:T(8,128)(2,1)S(1)}, bf16[256,1280]{1,0:T(8,128)(2,1)S(1)}, u32[]{:S(2)}, u32[]{:S(2)}) collective-permute-start(bf16[256,1280]{1,0:T(8,128)(2,1)S(1)} %fusion.30), channel_id=1, source_target_pairs={{0,8},{8,16},{16,24},{24,0},{1,9},{9,17},{17,25},{25,1},{2,10},{10... | collective-permute-start | bytes 1966088 | tf_op jit(solution)/shard_map/ppermute | solution.py:93
  1018.8 38.9 %collective-permute-start.116 = (bf16[1024,896]{0,1:T(8,128)(2,1)S(1)}, bf16[1024,896]{0,1:T(8,128)(2,1)S(1)}, u32[]{:S(2)}, u32[]{:S(2)}) collective-permute-start(bf16[1024,896]{0,1:T(8,128)(2,1)S(1)} %copy-done.42), channel_id=1, source_target_pairs={{0,1},{1,0},{2,3},{3,2},{4,5},{5,4},{6,7},{7,6},{8,9},{9,8},{10,11... | collective-permute-start | bytes 5505032 | tf_op jit(solution)/shard_map/ppermute | solution.py:78
  1048.3 205.7 %collective-permute-start.155 = (bf16[256,1280]{1,0:T(8,128)(2,1)}, bf16[256,1280]{1,0:T(8,128)(2,1)}, u32[]{:S(2)}, u32[]{:S(2)}) collective-permute-start(bf16[256,1280]{1,0:T(8,128)(2,1)} %fusion.25), channel_id=1, source_target_pairs={{0,0},{1,4},{2,2},{3,6},{4,1},{5,5},{6,3},{7,7},{8,8},{9,12},{10,1... | collective-permute-start | bytes 1966088 | tf_op jit(solution)/shard_map/ppermute | solution.py:75
  1053.2 211.9 %collective-permute-start.135 = (bf16[256,1280]{1,0:T(8,128)(2,1)}, bf16[256,1280]{1,0:T(8,128)(2,1)}, u32[]{:S(2)}, u32[]{:S(2)}) collective-permute-start(bf16[256,1280]{1,0:T(8,128)(2,1)} %fusion.37), channel_id=1, source_target_pairs={{0,0},{1,4},{2,2},{3,6},{4,1},{5,5},{6,3},{7,7},{8,8},{9,12},{10,1... | collective-permute-start | bytes 1966088 | tf_op jit(solution)/shard_map/ppermute | solution.py:75
  1058.7 209.5 %collective-permute-start.145 = (bf16[256,1280]{1,0:T(8,128)(2,1)}, bf16[256,1280]{1,0:T(8,128)(2,1)}, u32[]{:S(2)}, u32[]{:S(2)}) collective-permute-start(bf16[256,1280]{1,0:T(8,128)(2,1)} %fusion.31), channel_id=1, source_target_pairs={{0,0},{1,4},{2,2},{3,6},{4,1},{5,5},{6,3},{7,7},{8,8},{9,12},{10,1... | collective-permute-start | bytes 1966088 | tf_op jit(solution)/shard_map/ppermute | solution.py:75
  1070.4 38.1 %collective-permute-start.137 = (bf16[256,1280]{1,0:T(8,128)(2,1)S(1)}, bf16[256,1280]{1,0:T(8,128)(2,1)S(1)}, u32[]{:S(2)}, u32[]{:S(2)}) collective-permute-start(bf16[256,1280]{1,0:T(8,128)(2,1)S(1)} %slice.1067), channel_id=1, source_target_pairs={{0,8},{8,16},{16,24},{24,0},{1,9},{9,17},{17,25},{25,1},{2,10},{10... | collective-permute-start | bytes 1966088 | tf_op jit(solution)/shard_map/ppermute | solution.py:93
  1168.4 28.1 %collective-permute-start.129 = (bf16[256,1280]{1,0:T(8,128)(2,1)S(1)}, bf16[256,1280]{1,0:T(8,128)(2,1)S(1)}, u32[]{:S(2)}, u32[]{:S(2)}) collective-permute-start(bf16[256,1280]{1,0:T(8,128)(2,1)S(1)} %fusion.39), channel_id=1, source_target_pairs={{0,8},{8,16},{16,24},{24,0},{1,9},{9,17},{17,25},{25,1},{2,10},{10... | collective-permute-start | bytes 1966088 | tf_op jit(solution)/shard_map/ppermute | solution.py:93
  1182.4 28.1 %collective-permute-start.139 = (bf16[256,1280]{1,0:T(8,128)(2,1)S(1)}, bf16[256,1280]{1,0:T(8,128)(2,1)S(1)}, u32[]{:S(2)}, u32[]{:S(2)}) collective-permute-start(bf16[256,1280]{1,0:T(8,128)(2,1)S(1)} %fusion.33), channel_id=1, source_target_pairs={{0,8},{8,16},{16,24},{24,0},{1,9},{9,17},{17,25},{25,1},{2,10},{10... | collective-permute-start | bytes 1966088 | tf_op jit(solution)/shard_map/ppermute | solution.py:93
  1210.5 48.4 %collective-permute-start.150 = (bf16[256,1280]{1,0:T(8,128)(2,1)S(1)}, bf16[256,1280]{1,0:T(8,128)(2,1)}, u32[]{:S(2)}, u32[]{:S(2)}) collective-permute-start(bf16[256,1280]{1,0:T(8,128)(2,1)S(1)} %fusion.28), channel_id=1, source_target_pairs={{0,0},{1,4},{2,2},{3,6},{4,1},{5,5},{6,3},{7,7},{8,8},{9,12},{10,1... | collective-permute-start | bytes 1966088 | tf_op jit(solution)/shard_map/ppermute | solution.py:75
  1216.5 48.6 %collective-permute-start.130 = (bf16[256,1280]{1,0:T(8,128)(2,1)S(1)}, bf16[256,1280]{1,0:T(8,128)(2,1)}, u32[]{:S(2)}, u32[]{:S(2)}) collective-permute-start(bf16[256,1280]{1,0:T(8,128)(2,1)S(1)} %fusion.40), channel_id=1, source_target_pairs={{0,0},{1,4},{2,2},{3,6},{4,1},{5,5},{6,3},{7,7},{8,8},{9,12},{10,1... | collective-permute-start | bytes 1966088 | tf_op jit(solution)/shard_map/ppermute | solution.py:75
  (285 other events, 7496.0 us)
Sparse Core Ops, SparseCore 0:
  1219.5 32.0 all-reduce.1

commit v2 on v1

--- a/solution.py
+++ b/solution.py
@@ -64,6 +64,8 @@
                 for a, b, d in places
             ]
         self.swap_pairs = [(a * nt + 2 * b + d, d * nt + 2 * b + a) for a, b, d in places]
+        assert self.n & (self.n - 1) == 0
+        self.core_all = [(i, i ^ 1) for i in range(2 * nt)]
         self.core_pairs = [(i, i ^ 1) for i in range(nt)]
         self.up = [(i, (i + 1) % self.n) for i in range(self.n)]
         self.down = [(i, (i - 1) % self.n) for i in range(self.n)]
@@ -77,54 +79,70 @@
     def core(self, value):
         return lax.ppermute(value, "tensor", self.core_pairs)
 
-    def fetch(self, shard):
-        own = [self.swap(shard)]
-        for _ in range(1, self.n):
-            own.append(lax.ppermute(own[-1], "dp", self.down))
-        other = [self.core(piece) for piece in own]
-        return jnp.concatenate(own + other, axis=0)
-
-    def scatter(self, grad):
-        half = grad.shape[0] // 2
-        w = half // self.n
-        both = grad[:half].astype(f32) + self.core(grad[half:]).astype(f32)
-        total = both[(self.n - 1) * w :]
-        for s in reversed(range(self.n - 1)):
-            moved = lax.ppermute(total.astype(bf16), "dp", self.up)
-            total = both[s * w : (s + 1) * w] + moved.astype(f32)
-        return self.swap(total.astype(bf16))
+    def total(self, value):
+        for pairs in self.peers[1], self.peers[2], self.core_all:
+            value = value + lax.ppermute(value, ("ctx", "tensor"), pairs)
+        step = 1
+        while step < self.n:
+            value = value + lax.ppermute(value, "dp", [(i, i ^ step) for i in range(self.n)])
+            step *= 2
+        return value
+
+    def weight_term(self, left, right):
+        half = left.shape[1] // 2
+        away = self.core(product(left[:, half:], right, ((0,), (0,))).astype(bf16))
+        return (product(left[:, :half], right, ((0,), (0,))) + away.astype(f32)).astype(bf16)
+
+    def scatter(self, term):
+        return lax.psum_scatter(term, "dp", scatter_dimension=0, tiled=True)
+
+    def into(self, rows, halves):
+        half = rows.shape[1] // 2
+        return product(rows[:, :half], halves[0], ((1,), (0,))) + product(
+            rows[:, half:], halves[1], ((1,), (0,))
+        )
+
+    def out_of(self, rows, halves):
+        return jnp.concatenate(
+            [product(rows, part, ((1,), (1,))).astype(bf16) for part in halves], axis=1
+        )
 
     def spread(self, rows):
         return jnp.concatenate([rows] + [self.peer(rows, j) for j in range(1, 4)], axis=0)
 
-    def gather_sum(self, terms):
+    def gather_sum(self, terms, beside=()):
         rows = terms.shape[0] // 4
+        moved = [self.peer(terms[j * rows : (j + 1) * rows], j) for j in range(1, 4)]
+        moved, beside = lax.optimization_barrier((moved, beside))
         total = terms[:rows].astype(f32)
-        for j in range(1, 4):
-            total = total + self.peer(terms[j * rows : (j + 1) * rows], j).astype(f32)
-        return total
+        for piece in moved:
+            total = total + piece.astype(f32)
+        return total, beside
 
     def inward(self, array):
         lead = array.shape[:-1]
         d = array.shape[-1]
         w = d // (2 * self.n)
         parts = array.reshape(lead + (self.n, 2, w))
-        axis = len(lead)
-        twice = jnp.concatenate([parts, parts], axis=axis)
-        rolled = lax.dynamic_slice_in_dim(twice, self.z, self.n, axis=axis)
-        rolled = jnp.where(self.c == 0, rolled, jnp.flip(rolled, axis + 1))
-        return jnp.swapaxes(rolled, axis, axis + 1).reshape(lead + (d,))
+        even = parts[..., 0, :].reshape(lead + (d // 2,))
+        odd = parts[..., 1, :].reshape(lead + (d // 2,))
+        return jnp.where(
+            self.c == 0,
+            jnp.concatenate([even, odd], axis=-1),
+            jnp.concatenate([odd, even], axis=-1),
+        )
 
     def outward(self, array):
         lead = array.shape[:-1]
         d = array.shape[-1]
         w = d // (2 * self.n)
-        axis = len(lead)
-        parts = jnp.swapaxes(array.reshape(lead + (2, self.n, w)), axis, axis + 1)
-        parts = jnp.where(self.c == 0, parts, jnp.flip(parts, axis + 1))
-        twice = jnp.concatenate([parts, parts], axis=axis)
-        rolled = lax.dynamic_slice_in_dim(twice, (self.n - self.z) % self.n, self.n, axis=axis)
-        return rolled.reshape(lead + (d,))
+        own = array[..., : d // 2].reshape(lead + (self.n, w))
+        other = array[..., d // 2 :].reshape(lead + (self.n, w))
+        return jnp.where(
+            self.c == 0,
+            jnp.stack([own, other], axis=-2),
+            jnp.stack([other, own], axis=-2),
+        ).reshape(lead + (d,))
 
     def replicate(self, rows):
         beside = self.peer(rows, 1)
@@ -190,21 +208,36 @@
     qw, kw = heads * HD, 2 * HD
 
     kv_at = plan.t * heads // GROUP_SIZE * HD
-    fetched = []
+    hidden_units = w_gate.shape[2]
+    shards = []
     for layer in range(LAYERS):
         keys = lax.dynamic_slice_in_dim(w_key[layer], kv_at, kw, axis=1)
         values = lax.dynamic_slice_in_dim(w_value[layer], kv_at, kw, axis=1)
-        attn_shard = jnp.concatenate([w_query[layer], keys, values, w_out[layer].T], axis=1)
-        attn_w = plan.fetch(attn_shard)
-        fetched.append(
-            (
-                attn_w[:, : qw + 2 * kw],
-                attn_w[:, qw + 2 * kw :],
-                plan.fetch(w_gate[layer]),
-                plan.fetch(w_up[layer]),
-                plan.fetch(w_down[layer].T),
-            )
-        )
+        shards.append(jnp.concatenate([w_query[layer], keys, values, w_out[layer].T], axis=1))
+        ffn_parts = [w_gate[layer], w_up[layer], w_down[layer].T]
+        if layer + 1 < LAYERS:
+            shards.append(jnp.concatenate(ffn_parts, axis=1))
+        else:
+            shards.append(jnp.concatenate(ffn_parts[:2], axis=1))
+            shards.append(ffn_parts[2])
+    swapped = []
+    for shard in shards:
+        if swapped:
+            shard, swapped[-1] = lax.optimization_barrier((shard, swapped[-1]))
+        swapped.append(plan.swap(shard))
+    owned = []
+    for shard in swapped:
+        if owned:
+            shard, owned[-1] = lax.optimization_barrier((shard, owned[-1]))
+        owned.append(lax.all_gather(shard, "dp", axis=0, tiled=True))
+
+    def columns(halves, start, stop):
+        return tuple(part[:, start:stop] for part in halves)
+
+    def both_parities(own, after=None):
+        if after is not None:
+            own, after = lax.optimization_barrier((own, after))
+        return (own, plan.core(own)), after
 
     side = lax.ppermute(norm_gains, "ctx", [(0, 1), (1, 0)])
     pair = jnp.where(
@@ -268,9 +301,11 @@
 
     state = tokens_all[:quarter]
     stored = []
-    output = None
+    fetched = []
+    attn_w, _ = both_parities(owned[0])
     for layer in range(LAYERS):
-        w_qkv, w_o, w_g, w_u, w_d = fetched[layer]
+        w_qkv = columns(attn_w, 0, qw + 2 * kw)
+        w_o = columns(attn_w, qw + 2 * kw, None)
         if layer == 0:
             scale_in = scale_of(tokens_all)
             normed = (tokens_all * scale_in * gain_attn[layer]).astype(bf16)
@@ -278,7 +313,7 @@
         else:
             scale_in = scale_of(state)
             normed = plan.spread((state * scale_in * gain_attn[layer]).astype(bf16))
-        qkv = product(normed, w_qkv, ((1,), (0,)))
+        qkv = plan.into(normed, w_qkv)
         queries = by_head(qkv[:, :qw], heads)
         query_scale = scale_of(queries)
         query_low = rotate(queries * query_scale * gain_query[layer], cosine, sine_value).astype(
@@ -292,14 +327,27 @@
         value_heads = jnp.where(first_pair[:, None, None], value_low[0][None], value_low[1][None])
         mixed, merged = attend(query_low, key_heads, value_heads, allowed)
         mixed_low = flat(mixed.astype(bf16))
-        attn = plan.gather_sum(product(mixed_low, w_o, ((1,), (1,))).astype(bf16))
+        attn_terms = plan.out_of(mixed_low, w_o)
+        attn, _ = plan.gather_sum(attn_terms)
         middle = state + attn
+        ffn_w, later_middle = both_parities(owned[2 * layer + 1], middle)
+        w_g = columns(ffn_w, 0, hidden_units)
+        w_u = columns(ffn_w, hidden_units, 2 * hidden_units)
+        w_gu = columns(ffn_w, 0, 2 * hidden_units)
         scale_mid = scale_of(middle)
         normed2 = plan.spread((middle * scale_mid * gain_ffn[layer]).astype(bf16))
-        gate = product(normed2, w_g, ((1,), (0,)))
-        up = product(normed2, w_u, ((1,), (0,)))
+        gate = plan.into(normed2, w_g)
+        up = plan.into(normed2, w_u)
         hidden = (jax.nn.silu(gate) * up).astype(bf16)
-        ffn = plan.gather_sum(product(hidden, w_d, ((1,), (1,))).astype(bf16))
+        if layer + 1 < LAYERS:
+            w_d = columns(ffn_w, 2 * hidden_units, None)
+            ffn_terms = plan.out_of(hidden, w_d)
+            attn_next, hidden = both_parities(owned[2 * layer + 2], hidden)
+        else:
+            w_d, normed2 = both_parities(owned[-1], normed2)
+            ffn_terms = plan.out_of(hidden, w_d)
+        fetched.append((w_qkv, w_o, w_d, w_gu))
+        ffn, _ = plan.gather_sum(ffn_terms)
         stored.append(
             (
                 state,
@@ -322,15 +370,25 @@
                 hidden,
             )
         )
-        state = middle + ffn
+        state = later_middle + ffn
+        attn_w = attn_next
     output = plan.replicate(plan.outward(state.astype(bf16)))
 
     gradient = start_grad[:quarter].astype(f32)
     grad_ffn = start_grad
-    results = [None] * LAYERS
+    results = [[None] * 3 for _ in range(LAYERS)]
+    last = []
+
+    def scatter_next(layer, member, term):
+        if last:
+            at, part = last[-1]
+            term, results[at][part] = lax.optimization_barrier((term, results[at][part]))
+        results[layer][member] = plan.scatter(term)
+        last.append((layer, member))
+
     gain_grads = [None] * LAYERS
     for layer in reversed(range(LAYERS)):
-        w_qkv, w_o, w_g, w_u, w_d = fetched[layer]
+        w_qkv, w_o, w_d, w_gu = fetched[layer]
         (
             state,
             scale_in,
@@ -353,22 +411,31 @@
         ) = stored[layer]
         if grad_ffn is None:
             grad_ffn = plan.spread(gradient.astype(bf16))
-        grad_w_d = plan.scatter(product(grad_ffn, hidden, ((0,), (0,))).astype(bf16))
-        grad_hidden = product(grad_ffn, w_d, ((1,), (0,)))
+        term_d = plan.weight_term(grad_ffn, hidden)
+        if layer + 1 == LAYERS:
+            w_d, term_d = lax.optimization_barrier((w_d, term_d))
+        grad_hidden = plan.into(grad_ffn, w_d)
         sigmoid_gate = jax.nn.sigmoid(gate)
         grad_gate = (
             grad_hidden * up * sigmoid_gate * (1.0 + gate * (1.0 - sigmoid_gate))
         ).astype(bf16)
         grad_up = (grad_hidden * (gate * sigmoid_gate)).astype(bf16)
-        grad_w_g = plan.scatter(product(normed2, grad_gate, ((0,), (0,))).astype(bf16))
-        grad_w_u = plan.scatter(product(normed2, grad_up, ((0,), (0,))).astype(bf16))
-        term_mid = product(grad_gate, w_g, ((1,), (1,))) + product(grad_up, w_u, ((1,), (1,)))
-        summed_mid = plan.gather_sum(term_mid.astype(bf16))
+        grad_gu = jnp.concatenate([grad_gate, grad_up], axis=1)
+        term_gu = plan.weight_term(normed2, grad_gu)
+        if layer + 1 == LAYERS:
+            scatter_next(layer, 2, term_d)
+            summed_mid, term_gu = plan.gather_sum(plan.out_of(grad_gu, w_gu), term_gu)
+        else:
+            summed_mid, (term_d, term_gu) = plan.gather_sum(
+                plan.out_of(grad_gu, w_gu), (term_d, term_gu)
+            )
+            scatter_next(layer, 2, term_d)
+        scatter_next(layer, 1, term_gu)
         grad_g_ffn = jnp.sum(summed_mid * middle * scale_mid, axis=0)
         grad_mid = gradient + norm_back(summed_mid, middle, scale_mid, gain_ffn[layer])
         grad_attn = plan.spread(grad_mid.astype(bf16))
-        grad_mixed = by_head(product(grad_attn, w_o, ((1,), (0,))).astype(bf16), heads)
-        grad_w_o = product(grad_attn, mixed_low, ((0,), (0,))).astype(bf16)
+        grad_mixed = by_head(plan.into(grad_attn, w_o).astype(bf16), heads)
+        term_o = plan.weight_term(grad_attn, mixed_low)
         grad_query_rot, grad_key_heads, grad_value_heads = attend_back(
             query_low, key_heads, value_heads, grad_mixed, merged, allowed
         )
@@ -394,34 +461,38 @@
         grad_g_key = jnp.sum(grad_key_norm * keys * key_scale, axis=(0, 1))
         grad_keys = flat(norm_back(grad_key_norm, keys, key_scale, gain_key[layer]).astype(bf16))
         grad_qkv = jnp.concatenate([grad_queries, grad_keys, grad_values], axis=1)
-        grad_w_qkv = product(normed, grad_qkv, ((0,), (0,))).astype(bf16)
-        grad_w_attn = plan.scatter(jnp.concatenate([grad_w_qkv, grad_w_o], axis=1))
-        summed_in = plan.gather_sum(product(grad_qkv, w_qkv, ((1,), (1,))).astype(bf16))
+        term_qkv = plan.weight_term(normed, grad_qkv)
+        summed_in, (term_o, term_qkv) = plan.gather_sum(
+            plan.out_of(grad_qkv, w_qkv), (term_o, term_qkv)
+        )
+        scatter_next(layer, 0, jnp.concatenate([term_qkv, term_o], axis=1))
         grad_g_attn = jnp.sum(summed_in * state * scale_in, axis=0)
         gradient = grad_mid + norm_back(summed_in, state, scale_in, gain_attn[layer])
         grad_ffn = None
-        results[layer] = (grad_w_attn, grad_w_g, grad_w_u, grad_w_d)
         gain_grads[layer] = jnp.concatenate(
             [plan.outward(grad_g_attn), plan.outward(grad_g_ffn), grad_g_query, grad_g_key]
         )
     grad_input = plan.replicate(plan.outward(gradient.astype(bf16))).astype(f32)
 
+    for layer in range(LAYERS):
+        results[layer] = [plan.swap(term) for term in results[layer]]
+
     def stack(pick):
         return jnp.stack([pick(results[layer]) for layer in range(LAYERS)])
 
-    slice_width = w_query.shape[1]
-    shared = jnp.stack(
-        [
-            jnp.stack(
-                [results[layer][0][:, qw : qw + kw], results[layer][0][:, qw + kw : qw + 2 * kw]]
-            )
-            for layer in range(LAYERS)
-        ]
-    )
-    wide = jnp.zeros(shared.shape[:-1] + (w_key.shape[2],), bf16)
-    wide = lax.dynamic_update_slice_in_dim(wide, shared, kv_at, axis=3)
-    wide = lax.psum(wide, "tensor").astype(f32)
-    all_gains = lax.psum(jnp.stack(gain_grads), ("dp", "ctx", "tensor"))
+    shared = stack(lambda r: r[0][:, qw : qw + 2 * kw])
+    wide_keys = jnp.zeros(shared.shape[:-1] + (w_key.shape[2],), f32)
+    wide_values = wide_keys
+    for j in range(plan.nt):
+        part = shared
+        if j:
+            part = lax.ppermute(shared, "tensor", [(i, i ^ j) for i in range(plan.nt)])
+        part = part.astype(f32)
+        at = (plan.t ^ j) * heads // GROUP_SIZE * HD
+        zeros = jnp.zeros_like(wide_keys)
+        wide_keys += lax.dynamic_update_slice_in_dim(zeros, part[..., :kw], at, axis=2)
+        wide_values += lax.dynamic_update_slice_in_dim(zeros, part[..., kw:], at, axis=2)
+    all_gains = plan.total(jnp.stack(gain_grads))
     share = norm_gains.shape[1]
     grad_gains = lax.dynamic_slice_in_dim(
         all_gains, (2 * plan.z + plan.x) * share, share, axis=1
@@ -430,12 +501,12 @@
         output[:, None],
         grad_input[:, None],
         stack(lambda r: r[0][:, :qw]).astype(f32),
-        wide[:, 0],
-        wide[:, 1],
+        wide_keys,
+        wide_values,
         stack(lambda r: r[0][:, qw + 2 * kw :].T).astype(f32),
-        stack(lambda r: r[1]).astype(f32),
-        stack(lambda r: r[2]).astype(f32),
-        stack(lambda r: r[3].T).astype(f32),
+        stack(lambda r: r[1][:, :hidden_units]).astype(f32),
+        stack(lambda r: r[1][:, hidden_units:]).astype(f32),
+        stack(lambda r: r[2].T).astype(f32),
         grad_gains,
     )
 

time: 1290 us -> 939 us (0.73)
  starting transfers between devices: 286 us -> 134 us
  waiting for transfers between devices: 604 us -> 479 us
  local copies, waits for them, and re-layouts: 100 us -> 48.1 us
  matrix products: 117 us -> 168 us
  blocking collectives: 40.7 us -> 0 us
  other arithmetic: 111 us -> 82.1 us
    ppermute x48 -> x8, waiting for transfers between devices: 359 us -> 19.2 us  [the longest x3 9.33 us: local(): part = lax.ppermute(shared, 'tensor', [(i, i ^ j) for i in range(plan.nt)])]
    all_gather x0 -> x5, waiting for transfers between devices: none -> 116 us  [local(): owned.append(lax.all_gather(shard, 'dp', axis=0, tiled=True))]
    ppermute x46, waiting for transfers between devices: 188 us -> 289 us  [peer(): return lax.ppermute(value, ('ctx', 'tensor'), self.peers[j])]
    ppermute x42 -> x15, starting transfers between devices: 84.1 us -> 16 us  [core(): return lax.ppermute(value, 'tensor', self.core_pairs)]
    ppermute x48 -> x8, starting transfers between devices: 71.1 us -> 12.9 us  [the longest x3 9.99 us: total(): value = value + lax.ppermute(value, ('ctx', 'tensor'), pairs)]
    dot_general x30 -> x52, matrix products: 102 us -> 148 us  [product(): lax.dot_general(left_side, right_side, (contract, ((), ())), preferred_el...]
    psum x1 -> x0, blocking collectives: 40.7 us -> none  [local(): all_gains = lax.psum(jnp.stack(gain_grads), ('dp', 'ctx', 'tensor'))]
    unnamed x449 -> x267, local copies, waits for them, and re-layouts: 52.3 us -> 16 us
  transfers between devices with their start and end apart: 157 -> 95, of which waited for: 69 -> 59; matrix products, arithmetic and copies ran while one was open for 23% -> 29% of each run, Pallas kernels for 0% -> 0%
where the time goes in v2:
time: 939 us; the launch traced here: 929 us
  waiting for transfers between devices  479 us (51%)
  matrix products  168 us (18%)
  starting transfers between devices  134 us (14%)
  other arithmetic  82.1 us (9%)
  local copies, waits for them, and re-layouts  48.1 us (5%)
  between operations  17.4 us (2%)
    ppermute x46, waiting for transfers between devices, peer(): return lax.ppermute(value, ('ctx', 'tensor'), self.peers[j])  289 us
    dot_general x52, matrix products, product(): lax.dot_general(left_side, right_side, (contract, ((), ())), preferred_el...  148 us
    all_gather x5, waiting for transfers between devices, local(): owned.append(lax.all_gather(shard, 'dp', axis=0, tiled=True))  116 us
    ppermute x46, starting transfers between devices, peer(): return lax.ppermute(value, ('ctx', 'tensor'), self.peers[j])  58.3 us
    ppermute x11, waiting for transfers between devices, swap(): return lax.ppermute(value, ('ctx', 'tensor'), self.swap_pairs)  42.8 us
    ppermute x11, starting transfers between devices, swap(): return lax.ppermute(value, ('ctx', 'tensor'), self.swap_pairs)  33.2 us
  transfers between devices with their start and end apart: 95, of which 59 were waited for; matrix products, arithmetic and copies ran while one was open for 29% of the time, Pallas kernels for 0%

profile of v2, /device:TPU:1, one launch (start us, length us, event | category | flops | bytes accessed | tf_op | source)
XLA Modules:
  0.0 928.8 jit_solution(14198012647824308196)
XLA Ops:
  17.1 4.5 collective-permute-start
  36.3 14.5 %collective-permute-start.5 = (bf16[256,2048]{1,0:T(8,128)(2,1)S(1)}, bf16[256,2048]{1,0:T(8,128)(2,1)S(1)}, u32[]{:S(2)}, u32[]{:S(2)}) collective-permute-start(bf16[256,2048]{1,0:T(8,128)(2,1)S(1)} %maximum_select_fusion.4), channel_id=1, source_target_pairs={{0,4},{1,5},{2,6},{3,7},{4,0},{5,1},{6,2},{7,3},{8,12},{9,13},{10,... | collective-permute-start | bytes 3145736 | tf_op jit(solution)/shard_map/ppermute | solution.py:74
  52.6 13.2 %collective-permute-done.1 = bf16[256,3840]{0,1:T(8,128)(2,1)} collective-permute-done((bf16[256,3840]{0,1:T(8,128)(2,1)}, bf16[256,3840]{0,1:T(8,128)(2,1)}, u32[]{:S(2)}, u32[]{:S(2)}) %collective-permute-start.1) | collective-permute-done | bytes 1966112 | tf_op jit(solution)/shard_map/ppermute | solution.py:77
  65.8 7.1 all-gather.6.cloned.1.call-done
  116.7 6.4 collective-permute-done.12
  123.1 10.6 %collective-permute-done.13 = bf16[128,2048]{1,0:T(8,128)(2,1)} collective-permute-done((bf16[128,2048]{1,0:T(8,128)(2,1)}, bf16[128,2048]{1,0:T(8,128)(2,1)}, u32[]{:S(2)}, u32[]{:S(2)}) %collective-permute-start.13) | collective-permute-done | bytes 524320 | tf_op jit(solution)/shard_map/ppermute | solution.py:74
  136.0 78.4 %all-gather.8.cloned.1.call-done = bf16[1024,3840]{0,1:T(8,128)(2,1)} async-done(((bf16[256,3840]{0,1:T(8,128)(2,1)}), bf16[1024,3840]{0,1:T(8,128)(2,1)}) %all-gather.8.cloned.1.call-update) | async-done | bytes 7864336 | tf_op jit(solution)/shard_map/all_gather | solution.py:232
  218.4 3.9 collective-permute-start.3
  222.4 7.9 collective-permute-done.16
  230.3 11.2 %collective-permute-done.15 = bf16[128,2048]{1,0:T(8,128)(2,1)S(1)} collective-permute-done((bf16[128,2048]{1,0:T(8,128)(2,1)S(1)}, bf16[128,2048]{1,0:T(8,128)(2,1)S(1)}, u32[]{:S(2)}, u32[]{:S(2)}) %collective-permute-start.15) | collective-permute-done | bytes 524320 | tf_op jit(solution)/shard_map/ppermute | solution.py:74
  251.0 4.3 fusion.12
  267.9 14.7 %all-gather.10.cloned.1.call-done = bf16[1024,896]{0,1:T(8,128)(2,1)} async-done(((bf16[256,896]{0,1:T(8,128)(2,1)}), bf16[1024,896]{0,1:T(8,128)(2,1)}) %all-gather.10.cloned.1.call-update) | async-done | bytes 1835024 | tf_op jit(solution)/shard_map/all_gather | solution.py:232
  285.3 5.2 collective-permute-done.20
  295.6 10.1 %collective-permute-done.23 = bf16[128,2048]{1,0:T(8,128)(2,1)S(1)} collective-permute-done((bf16[128,2048]{1,0:T(8,128)(2,1)S(1)}, bf16[128,2048]{1,0:T(8,128)(2,1)S(1)}, u32[]{:S(2)}, u32[]{:S(2)}) %collective-permute-start.23) | collective-permute-done | bytes 524320 | tf_op jit(solution)/shard_map/ppermute | solution.py:74
  305.7 11.3 %collective-permute-done.22 = bf16[128,2048]{1,0:T(8,128)(2,1)S(1)} collective-permute-done((bf16[128,2048]{1,0:T(8,128)(2,1)S(1)}, bf16[128,2048]{1,0:T(8,128)(2,1)S(1)}, u32[]{:S(2)}, u32[]{:S(2)}) %collective-permute-start.22) | collective-permute-done | bytes 524320 | tf_op jit(solution)/shard_map/ppermute | solution.py:74
  334.8 4.5 collective-permute-start.4
  339.3 5.9 collective-permute-done.25
  346.2 11.1 %collective-permute-done.27 = bf16[128,2048]{1,0:T(8,128)(2,1)S(1)} collective-permute-done((bf16[128,2048]{1,0:T(8,128)(2,1)S(1)}, bf16[128,2048]{1,0:T(8,128)(2,1)S(1)}, u32[]{:S(2)}, u32[]{:S(2)}) %collective-permute-start.27) | collective-permute-done | bytes 524320 | tf_op jit(solution)/shard_map/ppermute | solution.py:74
  357.8 7.8 collective-permute-done.4
  365.7 15.8 %all-gather.12.cloned.1.call-done = bf16[1024,2560]{1,0:T(8,128)(2,1)} async-done(((bf16[256,2560]{1,0:T(8,128)(2,1)}), bf16[1024,2560]{1,0:T(8,128)(2,1)}) %all-gather.12.cloned.1.call-update) | async-done | bytes 5242896 | tf_op jit(solution)/shard_map/all_gather | solution.py:232
  400.9 20.5 %collective-permute-done.38 = bf16[256,2048]{1,0:T(8,128)(2,1)} collective-permute-done((bf16[256,2048]{1,0:T(8,128)(2,1)}, bf16[256,2048]{1,0:T(8,128)(2,1)}, u32[]{:S(2)}, u32[]{:S(2)}) %collective-permute-start.38) | collective-permute-done | bytes 1048608 | tf_op jit(solution)/shard_map/ppermute | solution.py:74
  423.5 10.2 %collective-permute-done.30 = bf16[128,2048]{1,0:T(8,128)(2,1)S(1)} collective-permute-done((bf16[128,2048]{1,0:T(8,128)(2,1)S(1)}, bf16[128,2048]{1,0:T(8,128)(2,1)S(1)}, u32[]{:S(2)}, u32[]{:S(2)}) %collective-permute-start.30) | collective-permute-done | bytes 524320 | tf_op jit(solution)/shard_map/ppermute | solution.py:74
  433.6 10.3 %collective-permute-done.29 = bf16[128,2048]{1,0:T(8,128)(2,1)S(1)} collective-permute-done((bf16[128,2048]{1,0:T(8,128)(2,1)S(1)}, bf16[128,2048]{1,0:T(8,128)(2,1)S(1)}, u32[]{:S(2)}, u32[]{:S(2)}) %collective-permute-start.29) | collective-permute-done | bytes 524320 | tf_op jit(solution)/shard_map/ppermute | solution.py:74
  444.2 4.0 fusion.10
  460.1 4.8 collective-permute-done.39
  464.9 5.5 add_convert_fusion.3
  474.7 4.5 multiply_convert_fusion.6
  479.2 4.9 convolution_convert_fusion.1
  484.6 6.3 convolution_convert_fusion.7
  490.9 5.8 convolution_convert_fusion.6
  500.8 6.6 add_convert_fusion.1
  507.4 4.4 collective-permute-done.40
  512.8 11.2 %collective-permute-done.42 = bf16[128,2048]{1,0:T(8,128)(2,1)} collective-permute-done((bf16[128,2048]{1,0:T(8,128)(2,1)}, bf16[128,2048]{1,0:T(8,128)(2,1)}, u32[]{:S(2)}, u32[]{:S(2)}) %collective-permute-start.42) | collective-permute-done | bytes 524320 | tf_op jit(solution)/shard_map/ppermute | solution.py:74
  534.8 7.3 collective-permute-done.46
  542.1 11.3 %collective-permute-done.45 = bf16[128,2048]{1,0:T(8,128)(2,1)} collective-permute-done((bf16[128,2048]{1,0:T(8,128)(2,1)}, bf16[128,2048]{1,0:T(8,128)(2,1)}, u32[]{:S(2)}, u32[]{:S(2)}) %collective-permute-start.45) | collective-permute-done | bytes 524320 | tf_op jit(solution)/shard_map/ppermute | solution.py:74
  559.1 4.6 multiply_reduce_fusion.1
  579.4 9.2 collective-permute-done.47
  589.4 11.2 %collective-permute-done.49 = bf16[128,2048]{1,0:T(8,128)(2,1)S(1)} collective-permute-done((bf16[128,2048]{1,0:T(8,128)(2,1)S(1)}, bf16[128,2048]{1,0:T(8,128)(2,1)S(1)}, u32[]{:S(2)}, u32[]{:S(2)}) %collective-permute-start.49) | collective-permute-done | bytes 524320 | tf_op jit(solution)/shard_map/ppermute | solution.py:74
  605.3 10.2 %collective-permute-done.54 = bf16[128,2048]{1,0:T(8,128)(2,1)S(1)} collective-permute-done((bf16[128,2048]{1,0:T(8,128)(2,1)S(1)}, bf16[128,2048]{1,0:T(8,128)(2,1)S(1)}, u32[]{:S(2)}, u32[]{:S(2)}) %collective-permute-start.54) | collective-permute-done | bytes 524320 | tf_op jit(solution)/shard_map/ppermute | solution.py:74
  615.4 11.3 %collective-permute-done.53 = bf16[128,2048]{1,0:T(8,128)(2,1)S(1)} collective-permute-done((bf16[128,2048]{1,0:T(8,128)(2,1)S(1)}, bf16[128,2048]{1,0:T(8,128)(2,1)S(1)}, u32[]{:S(2)}, u32[]{:S(2)}) %collective-permute-start.53) | collective-permute-done | bytes 524320 | tf_op jit(solution)/shard_map/ppermute | solution.py:74
  629.3 4.1 fusion.30
  633.4 4.3 multiply_convert_fusion.4
  637.8 4.9 convolution_convert_fusion
  648.0 6.3 fusion.38
  654.3 5.4 fusion.41
  664.6 4.8 add_convert_fusion.2
  669.4 8.9 add_convert_fusion
  678.3 9.1 collective-permute-done.57
  697.7 8.9 collective-permute-done.33
  707.7 10.9 %collective-permute-done.35 = bf16[128,2048]{1,0:T(8,128)(2,1)S(1)} collective-permute-done((bf16[128,2048]{1,0:T(8,128)(2,1)S(1)}, bf16[128,2048]{1,0:T(8,128)(2,1)S(1)}, u32[]{:S(2)}, u32[]{:S(2)}) %collective-permute-start.35) | collective-permute-done | bytes 524320 | tf_op jit(solution)/shard_map/ppermute | solution.py:74
  723.2 9.1 collective-permute-done.36
  735.0 4.0 collective-permute-start.37
  745.5 11.6 %collective-permute-done.62 = bf16[128,2048]{1,0:T(8,128)(2,1)S(1)} collective-permute-done((bf16[128,2048]{1,0:T(8,128)(2,1)}, bf16[128,2048]{1,0:T(8,128)(2,1)S(1)}, u32[]{:S(2)}, u32[]{:S(2)}) %collective-permute-start.62) | collective-permute-done | bytes 524320 | tf_op jit(solution)/shard_map/ppermute | solution.py:74
  757.1 11.4 %collective-permute-done.61 = bf16[128,2048]{1,0:T(8,128)(2,1)S(1)} collective-permute-done((bf16[128,2048]{1,0:T(8,128)(2,1)}, bf16[128,2048]{1,0:T(8,128)(2,1)S(1)}, u32[]{:S(2)}, u32[]{:S(2)}) %collective-permute-start.61) | collective-permute-done | bytes 524320 | tf_op jit(solution)/shard_map/ppermute | solution.py:74
  772.7 4.5 multiply_reduce_fusion
  794.3 7.8 collective-permute-done.63
  803.0 11.2 %collective-permute-done.65 = bf16[128,2048]{1,0:T(8,128)(2,1)S(1)} collective-permute-done((bf16[128,2048]{1,0:T(8,128)(2,1)S(1)}, bf16[128,2048]{1,0:T(8,128)(2,1)S(1)}, u32[]{:S(2)}, u32[]{:S(2)}) %collective-permute-start.65) | collective-permute-done | bytes 524320 | tf_op jit(solution)/shard_map/ppermute | solution.py:74
  822.1 8.6 collective-permute-done.79
  838.8 8.4 collective-permute-start.81
  860.3 4.0 fusion.37
  874.6 7.0 collective-permute-done.77
  886.4 8.9 collective-permute-done.75
  902.0 4.7 collective-permute-done.70
  914.6 6.1 collective-permute-done.74
  (681 shorter events, 324.0 us)
Async XLA Ops:
  7.2 65.7 %all-gather.6.cloned.1.call-start = ((), (), s32[]{:S(2)}) async-start(), calls=%async_computation.6 | async-start | bytes 2293760 | tf_op jit(solution)/shard_map/all_gather | solution.py:232
  29.7 184.8 %all-gather.8.cloned.1.call-start = ((), (), s32[]{:S(2)}) async-start(), calls=%async_computation.7 | async-start | bytes 9830400 | tf_op jit(solution)/shard_map/all_gather | solution.py:232
  29.7 43.9 %collective-permute-start.6 = (bf16[2,528]{1,0:T(2,128)(2,1)S(1)}, bf16[2,528]{1,0:T(2,128)(2,1)S(1)}, u32[]{:S(2)}, u32[]{:S(2)}) collective-permute-start(bf16[2,528]{1,0:T(2,128)(2,1)S(1)} %copy-done.85), channel_id=1, source_target_pairs={{0,4},{4,0},{1,5},{5,1},{2,6},{6,2},{3,7},{7,3},{8,12},{12,8},{9,1... | collective-permute-start | bytes 6344 | tf_op jit(solution)/shard_map/ppermute | solution.py:242
  32.4 33.4 %collective-permute-start.1 = (bf16[256,3840]{0,1:T(8,128)(2,1)}, bf16[256,3840]{0,1:T(8,128)(2,1)}, u32[]{:S(2)}, u32[]{:S(2)}) collective-permute-start(bf16[256,3840]{0,1:T(8,128)(2,1)} %pad_maximum_fusion.8), channel_id=1, source_target_pairs={{0,0},{1,4},{2,2},{3,6},{4,1},{5,5},{6,3},{7,7},{8,8},{9,12},{10,1... | collective-permute-start | bytes 5898248 | tf_op jit(solution)/shard_map/ppermute | solution.py:77
  36.3 53.4 %collective-permute-start.5 = (bf16[256,2048]{1,0:T(8,128)(2,1)S(1)}, bf16[256,2048]{1,0:T(8,128)(2,1)S(1)}, u32[]{:S(2)}, u32[]{:S(2)}) collective-permute-start(bf16[256,2048]{1,0:T(8,128)(2,1)S(1)} %maximum_select_fusion.4), channel_id=1, source_target_pairs={{0,4},{1,5},{2,6},{3,7},{4,0},{5,1},{6,2},{7,3},{8,12},{9,13},{10,... | collective-permute-start | bytes 3145736 | tf_op jit(solution)/shard_map/ppermute | solution.py:74
  72.9 209.6 %all-gather.10.cloned.1.call-start = ((), (), s32[]{:S(2)}) async-start(), calls=%async_computation.8 | async-start | bytes 2293760 | tf_op jit(solution)/shard_map/all_gather | solution.py:232
  90.7 24.0 %collective-permute-start.2 = (bf16[256,896]{0,1:T(8,128)(2,1)}, bf16[256,896]{0,1:T(8,128)(2,1)}, u32[]{:S(2)}, u32[]{:S(2)}) collective-permute-start(bf16[256,896]{0,1:T(8,128)(2,1)} %pad_maximum_fusion.24), channel_id=1, source_target_pairs={{0,0},{1,4},{2,2},{3,6},{4,1},{5,5},{6,3},{7,7},{8,8},{9,12},{10,1... | collective-permute-start | bytes 1376264 | tf_op jit(solution)/shard_map/ppermute | solution.py:77
  107.4 15.7 %collective-permute-start.12 = (bf16[128,2048]{1,0:T(8,128)(2,1)}, bf16[128,2048]{1,0:T(8,128)(2,1)}, u32[]{:S(2)}, u32[]{:S(2)}) collective-permute-start(bf16[128,2048]{1,0:T(8,128)(2,1)} %get-tuple-element.249), channel_id=1, source_target_pairs={{0,4},{1,5},{2,6},{3,7},{4,0},{5,1},{6,2},{7,3},{8,12},{9,13},{10,... | collective-permute-start | bytes 1572872 | tf_op jit(solution)/shard_map/ppermute | solution.py:74
  111.1 22.6 %collective-permute-start.13 = (bf16[128,2048]{1,0:T(8,128)(2,1)}, bf16[128,2048]{1,0:T(8,128)(2,1)}, u32[]{:S(2)}, u32[]{:S(2)}) collective-permute-start(bf16[128,2048]{1,0:T(8,128)(2,1)} %get-tuple-element.247), channel_id=1, source_target_pairs={{0,6},{1,7},{2,4},{3,5},{4,2},{5,3},{6,0},{7,1},{8,14},{9,15},{10,... | collective-permute-start | bytes 1572872 | tf_op jit(solution)/shard_map/ppermute | solution.py:74
  214.5 29.1 %collective-permute-start.17 = (bf16[1024,3840]{0,1:T(8,128)(2,1)}, bf16[1024,3840]{0,1:T(8,128)(2,1)}, u32[]{:S(2)}, u32[]{:S(2)}) collective-permute-start(bf16[1024,3840]{0,1:T(8,128)(2,1)} %all-gather.8.cloned.1.call-done), channel_id=1, source_target_pairs={{0,1},{1,0},{2,3},{3,2},{4,5},{5,4},{6,7},{7,6},{8,9},{9,8},{10,11... | collective-permute-start | bytes 23592968 | tf_op jit(solution)/shard_map/ppermute | solution.py:80
  215.7 14.6 %collective-permute-start.16 = (bf16[128,2048]{1,0:T(8,128)(2,1)S(1)}, bf16[128,2048]{1,0:T(8,128)(2,1)S(1)}, u32[]{:S(2)}, u32[]{:S(2)}) collective-permute-start(bf16[128,2048]{1,0:T(8,128)(2,1)S(1)} %multiply_convert_fusion.11), channel_id=1, source_target_pairs={{0,6},{1,7},{2,4},{3,5},{4,2},{5,3},{6,0},{7,1},{8,14},{9,15},{10,... | collective-permute-start | bytes 1572872 | tf_op jit(solution)/shard_map/ppermute | solution.py:74
  217.9 23.6 %collective-permute-start.15 = (bf16[128,2048]{1,0:T(8,128)(2,1)S(1)}, bf16[128,2048]{1,0:T(8,128)(2,1)S(1)}, u32[]{:S(2)}, u32[]{:S(2)}) collective-permute-start(bf16[128,2048]{1,0:T(8,128)(2,1)S(1)} %multiply_convert_fusion.11), channel_id=1, source_target_pairs={{0,4},{1,5},{2,6},{3,7},{4,0},{5,1},{6,2},{7,3},{8,12},{9,13},{10,... | collective-permute-start | bytes 1572872 | tf_op jit(solution)/shard_map/ppermute | solution.py:74
  218.2 23.6 %collective-permute-start.14 = (bf16[128,2048]{1,0:T(8,128)(2,1)S(1)}, bf16[128,2048]{1,0:T(8,128)(2,1)S(1)}, u32[]{:S(2)}, u32[]{:S(2)}) collective-permute-start(bf16[128,2048]{1,0:T(8,128)(2,1)S(1)} %multiply_convert_fusion.11), channel_id=1, source_target_pairs={{0,2},{1,3},{2,0},{3,1},{4,6},{5,7},{6,4},{7,5},{8,10},{9,11},{10,... | collective-permute-start | bytes 1572872 | tf_op jit(solution)/shard_map/ppermute | solution.py:74
  218.4 49.4 %collective-permute-start.3 = (bf16[256,2560]{1,0:T(8,128)(2,1)}, bf16[256,2560]{1,0:T(8,128)(2,1)}, u32[]{:S(2)}, u32[]{:S(2)}) collective-permute-start(bf16[256,2560]{1,0:T(8,128)(2,1)} %pad_maximum_fusion.11), channel_id=1, source_target_pairs={{0,0},{1,4},{2,2},{3,6},{4,1},{5,5},{6,3},{7,7},{8,8},{9,12},{10,1... | collective-permute-start | bytes 3932168 | tf_op jit(solution)/shard_map/ppermute | solution.py:77
  243.4 138.1 %all-gather.12.cloned.1.call-start = ((), (), s32[]{:S(2)}) async-start(), calls=%async_computation.9 | async-start | bytes 6553600 | tf_op jit(solution)/shard_map/all_gather | solution.py:232
  265.2 19.3 %collective-permute-start.18 = (bf16[128,2048]{1,0:T(8,128)(2,1)}, bf16[128,2048]{1,0:T(8,128)(2,1)S(1)}, u32[]{:S(2)}, u32[]{:S(2)}) collective-permute-start(bf16[128,2048]{1,0:T(8,128)(2,1)} %get-tuple-element.245), channel_id=1, source_target_pairs={{0,2},{1,3},{2,0},{3,1},{4,6},{5,7},{6,4},{7,5},{8,10},{9,11},{10,... | collective-permute-start | bytes 1572872 | tf_op jit(solution)/shard_map/ppermute | solution.py:74
  266.4 18.1 %collective-permute-start.19 = (bf16[128,2048]{1,0:T(8,128)(2,1)}, bf16[128,2048]{1,0:T(8,128)(2,1)S(1)}, u32[]{:S(2)}, u32[]{:S(2)}) collective-permute-start(bf16[128,2048]{1,0:T(8,128)(2,1)} %get-tuple-element.246), channel_id=1, source_target_pairs={{0,4},{1,5},{2,6},{3,7},{4,0},{5,1},{6,2},{7,3},{8,12},{9,13},{10,... | collective-permute-start | bytes 1572872 | tf_op jit(solution)/shard_map/ppermute | solution.py:74
  267.7 22.8 %collective-permute-start.20 = (bf16[128,2048]{1,0:T(8,128)(2,1)S(1)}, bf16[128,2048]{1,0:T(8,128)(2,1)}, u32[]{:S(2)}, u32[]{:S(2)}) collective-permute-start(bf16[128,2048]{1,0:T(8,128)(2,1)S(1)} %get-tuple-element.244), channel_id=1, source_target_pairs={{0,6},{1,7},{2,4},{3,5},{4,2},{5,3},{6,0},{7,1},{8,14},{9,15},{10,... | collective-permute-start | bytes 1572872 | tf_op jit(solution)/shard_map/ppermute | solution.py:74
  282.5 36.7 %collective-permute-start.24 = (bf16[1024,896]{0,1:T(8,128)(2,1)}, bf16[1024,896]{0,1:T(8,128)(2,1)}, u32[]{:S(2)}, u32[]{:S(2)}) collective-permute-start(bf16[1024,896]{0,1:T(8,128)(2,1)} %all-gather.10.cloned.1.call-done), channel_id=1, source_target_pairs={{0,1},{1,0},{2,3},{3,2},{4,5},{5,4},{6,7},{7,6},{8,9},{9,8},{10,11... | collective-permute-start | bytes 5505032 | tf_op jit(solution)/shard_map/ppermute | solution.py:80
  284.2 175.8 %all-gather.14.cloned.1.call-start = ((), (), s32[]{:S(2)}) async-start(), calls=%async_computation.10 | async-start | bytes 3276800 | tf_op jit(solution)/shard_map/all_gather | solution.py:232
  295.2 21.8 %collective-permute-start.22 = (bf16[128,2048]{1,0:T(8,128)(2,1)S(1)}, bf16[128,2048]{1,0:T(8,128)(2,1)S(1)}, u32[]{:S(2)}, u32[]{:S(2)}) collective-permute-start(bf16[128,2048]{1,0:T(8,128)(2,1)S(1)} %multiply_convert_fusion.10), channel_id=1, source_target_pairs={{0,4},{1,5},{2,6},{3,7},{4,0},{5,1},{6,2},{7,3},{8,12},{9,13},{10,... | collective-permute-start | bytes 1572872 | tf_op jit(solution)/shard_map/ppermute | solution.py:74
  295.2 23.7 %collective-permute-start.21 = (bf16[128,2048]{1,0:T(8,128)(2,1)S(1)}, bf16[128,2048]{1,0:T(8,128)(2,1)S(1)}, u32[]{:S(2)}, u32[]{:S(2)}) collective-permute-start(bf16[128,2048]{1,0:T(8,128)(2,1)S(1)} %multiply_convert_fusion.10), channel_id=1, source_target_pairs={{0,2},{1,3},{2,0},{3,1},{4,6},{5,7},{6,4},{7,5},{8,10},{9,11},{10,... | collective-permute-start | bytes 1572872 | tf_op jit(solution)/shard_map/ppermute | solution.py:74
  334.8 22.6 %collective-permute-start.27 = (bf16[128,2048]{1,0:T(8,128)(2,1)S(1)}, bf16[128,2048]{1,0:T(8,128)(2,1)S(1)}, u32[]{:S(2)}, u32[]{:S(2)}) collective-permute-start(bf16[128,2048]{1,0:T(8,128)(2,1)S(1)} %get-tuple-element.241), channel_id=1, source_target_pairs={{0,6},{1,7},{2,4},{3,5},{4,2},{5,3},{6,0},{7,1},{8,14},{9,15},{10,... | collective-permute-start | bytes 1572872 | tf_op jit(solution)/shard_map/ppermute | solution.py:74
  334.8 30.9 %collective-permute-start.4 = (bf16[256,1280]{0,1:T(8,128)(2,1)S(1)}, bf16[256,1280]{0,1:T(8,128)(2,1)}, u32[]{:S(2)}, u32[]{:S(2)}) collective-permute-start(bf16[256,1280]{0,1:T(8,128)(2,1)S(1)} %copy-done.44), channel_id=1, source_target_pairs={{0,0},{1,4},{2,2},{3,6},{4,1},{5,5},{6,3},{7,7},{8,8},{9,12},{10,1... | collective-permute-start | bytes 1966088 | tf_op jit(solution)/shard_map/ppermute | solution.py:77
  381.5 62.7 %collective-permute-start.31 = (bf16[1024,2560]{1,0:T(8,128)(2,1)}, bf16[1024,2560]{1,0:T(8,128)(2,1)}, u32[]{:S(2)}, u32[]{:S(2)}) collective-permute-start(bf16[1024,2560]{1,0:T(8,128)(2,1)} %all-gather.12.cloned.1.call-done), channel_id=1, source_target_pairs={{0,1},{1,0},{2,3},{3,2},{4,5},{5,4},{6,7},{7,6},{8,9},{9,8},{10,11... | collective-permute-start | bytes 15728648 | tf_op jit(solution)/shard_map/ppermute | solution.py:80
  396.4 25.1 %collective-permute-start.38 = (bf16[256,2048]{1,0:T(8,128)(2,1)}, bf16[256,2048]{1,0:T(8,128)(2,1)}, u32[]{:S(2)}, u32[]{:S(2)}) collective-permute-start(bf16[256,2048]{1,0:T(8,128)(2,1)} %maximum_select_fusion.8), channel_id=1, source_target_pairs={{0,4},{1,5},{2,6},{3,7},{4,0},{5,1},{6,2},{7,3},{8,12},{9,13},{10,... | collective-permute-start | bytes 3145736 | tf_op jit(solution)/shard_map/ppermute | solution.py:74
  397.6 136.9 %reduce-scatter.7.cloned.1.call-start = ((), (), s32[]{:S(2)}) async-start(), calls=%async_computation.11 | async-start | bytes 3276800 | tf_op jit(solution)/shard_map/reduce_scatter | solution.py:97
  398.2 35.4 %collective-permute-start.30 = (bf16[128,2048]{1,0:T(8,128)(2,1)S(1)}, bf16[128,2048]{1,0:T(8,128)(2,1)S(1)}, u32[]{:S(2)}, u32[]{:S(2)}) collective-permute-start(bf16[128,2048]{1,0:T(8,128)(2,1)S(1)} %multiply_convert_fusion.9), channel_id=1, source_target_pairs={{0,6},{1,7},{2,4},{3,5},{4,2},{5,3},{6,0},{7,1},{8,14},{9,15},{10,... | collective-permute-start | bytes 1572872 | tf_op jit(solution)/shard_map/ppermute | solution.py:74
  399.5 44.5 %collective-permute-start.29 = (bf16[128,2048]{1,0:T(8,128)(2,1)S(1)}, bf16[128,2048]{1,0:T(8,128)(2,1)S(1)}, u32[]{:S(2)}, u32[]{:S(2)}) collective-permute-start(bf16[128,2048]{1,0:T(8,128)(2,1)S(1)} %multiply_convert_fusion.9), channel_id=1, source_target_pairs={{0,4},{1,5},{2,6},{3,7},{4,0},{5,1},{6,2},{7,3},{8,12},{9,13},{10,... | collective-permute-start | bytes 1572872 | tf_op jit(solution)/shard_map/ppermute | solution.py:74
  400.6 43.3 %collective-permute-start.28 = (bf16[128,2048]{1,0:T(8,128)(2,1)S(1)}, bf16[128,2048]{1,0:T(8,128)(2,1)S(1)}, u32[]{:S(2)}, u32[]{:S(2)}) collective-permute-start(bf16[128,2048]{1,0:T(8,128)(2,1)S(1)} %multiply_convert_fusion.9), channel_id=1, source_target_pairs={{0,2},{1,3},{2,0},{3,1},{4,6},{5,7},{6,4},{7,5},{8,10},{9,11},{10,... | collective-permute-start | bytes 1572872 | tf_op jit(solution)/shard_map/ppermute | solution.py:74
  484.1 16.7 %collective-permute-start.43 = (bf16[1024,2560]{1,0:T(8,128)(2,1)}, bf16[1024,2560]{1,0:T(8,128)(2,1)}, u32[]{:S(2)}, u32[]{:S(2)}) collective-permute-start(bf16[1024,2560]{1,0:T(8,128)(2,1)} %convolution_convert_fusion.1), channel_id=1, source_target_pairs={{0,1},{1,0},{2,3},{3,2},{4,5},{5,4},{6,7},{7,6},{8,9},{9,8},{10,11... | collective-permute-start | bytes 15728648 | tf_op jit(solution)/shard_map/ppermute | solution.py:80
  484.5 163.3 %reduce-scatter.9.cloned.1.call-start = ((), (), s32[]{:S(2)}) async-start(), calls=%async_computation.12 | async-start | bytes 6553600 | tf_op jit(solution)/shard_map/reduce_scatter | solution.py:97
  498.2 13.7 %collective-permute-start.40 = (bf16[128,2048]{1,0:T(8,128)(2,1)}, bf16[128,2048]{1,0:T(8,128)(2,1)}, u32[]{:S(2)}, u32[]{:S(2)}) collective-permute-start(bf16[128,2048]{1,0:T(8,128)(2,1)} %get-tuple-element.236), channel_id=1, source_target_pairs={{0,2},{1,3},{2,0},{3,1},{4,6},{5,7},{6,4},{7,5},{8,10},{9,11},{10,... | collective-permute-start | bytes 1572872 | tf_op jit(solution)/shard_map/ppermute | solution.py:74
  499.4 13.4 %collective-permute-start.41 = (bf16[128,2048]{1,0:T(8,128)(2,1)}, bf16[128,2048]{1,0:T(8,128)(2,1)}, u32[]{:S(2)}, u32[]{:S(2)}) collective-permute-start(bf16[128,2048]{1,0:T(8,128)(2,1)} %get-tuple-element.237), channel_id=1, source_target_pairs={{0,4},{1,5},{2,6},{3,7},{4,0},{5,1},{6,2},{7,3},{8,12},{9,13},{10,... | collective-permute-start | bytes 1572872 | tf_op jit(solution)/shard_map/ppermute | solution.py:74
  500.6 23.4 %collective-permute-start.42 = (bf16[128,2048]{1,0:T(8,128)(2,1)}, bf16[128,2048]{1,0:T(8,128)(2,1)}, u32[]{:S(2)}, u32[]{:S(2)}) collective-permute-start(bf16[128,2048]{1,0:T(8,128)(2,1)} %get-tuple-element.235), channel_id=1, source_target_pairs={{0,6},{1,7},{2,4},{3,5},{4,2},{5,3},{6,0},{7,1},{8,14},{9,15},{10,... | collective-permute-start | bytes 1572872 | tf_op jit(solution)/shard_map/ppermute | solution.py:74
  528.7 13.4 %collective-permute-start.46 = (bf16[128,2048]{1,0:T(8,128)(2,1)}, bf16[128,2048]{1,0:T(8,128)(2,1)}, u32[]{:S(2)}, u32[]{:S(2)}) collective-permute-start(bf16[128,2048]{1,0:T(8,128)(2,1)} %get-tuple-element.213), channel_id=1, source_target_pairs={{0,6},{1,7},{2,4},{3,5},{4,2},{5,3},{6,0},{7,1},{8,14},{9,15},{10,... | collective-permute-start | bytes 1572872 | tf_op jit(solution)/shard_map/ppermute | solution.py:74
  530.8 22.6 %collective-permute-start.45 = (bf16[128,2048]{1,0:T(8,128)(2,1)}, bf16[128,2048]{1,0:T(8,128)(2,1)}, u32[]{:S(2)}, u32[]{:S(2)}) collective-permute-start(bf16[128,2048]{1,0:T(8,128)(2,1)} %get-tuple-element.213), channel_id=1, source_target_pairs={{0,4},{1,5},{2,6},{3,7},{4,0},{5,1},{6,2},{7,3},{8,12},{9,13},{10,... | collective-permute-start | bytes 1572872 | tf_op jit(solution)/shard_map/ppermute | solution.py:74
  531.1 23.9 %collective-permute-start.44 = (bf16[128,2048]{1,0:T(8,128)(2,1)}, bf16[128,2048]{1,0:T(8,128)(2,1)}, u32[]{:S(2)}, u32[]{:S(2)}) collective-permute-start(bf16[128,2048]{1,0:T(8,128)(2,1)} %get-tuple-element.213), channel_id=1, source_target_pairs={{0,2},{1,3},{2,0},{3,1},{4,6},{5,7},{6,4},{7,5},{8,10},{9,11},{10,... | collective-permute-start | bytes 1572872 | tf_op jit(solution)/shard_map/ppermute | solution.py:74
  534.5 153.0 %reduce-scatter.11.cloned.1.call-start = ((), (), s32[]{:S(2)}) async-start(), calls=%async_computation.13 | async-start | bytes 2293760 | tf_op jit(solution)/shard_map/reduce_scatter | solution.py:97
  575.4 13.3 %collective-permute-start.47 = (bf16[128,2048]{1,0:T(8,128)(2,1)S(1)}, bf16[128,2048]{1,0:T(8,128)(2,1)S(1)}, u32[]{:S(2)}, u32[]{:S(2)}) collective-permute-start(bf16[128,2048]{1,0:T(8,128)(2,1)S(1)} %get-tuple-element.233), channel_id=1, source_target_pairs={{0,2},{1,3},{2,0},{3,1},{4,6},{5,7},{6,4},{7,5},{8,10},{9,11},{10,... | collective-permute-start | bytes 1572872 | tf_op jit(solution)/shard_map/ppermute | solution.py:74
  577.7 22.9 %collective-permute-start.49 = (bf16[128,2048]{1,0:T(8,128)(2,1)S(1)}, bf16[128,2048]{1,0:T(8,128)(2,1)S(1)}, u32[]{:S(2)}, u32[]{:S(2)}) collective-permute-start(bf16[128,2048]{1,0:T(8,128)(2,1)S(1)} %get-tuple-element.232), channel_id=1, source_target_pairs={{0,6},{1,7},{2,4},{3,5},{4,2},{5,3},{6,0},{7,1},{8,14},{9,15},{10,... | collective-permute-start | bytes 1572872 | tf_op jit(solution)/shard_map/ppermute | solution.py:74
  604.7 22.1 %collective-permute-start.53 = (bf16[128,2048]{1,0:T(8,128)(2,1)S(1)}, bf16[128,2048]{1,0:T(8,128)(2,1)S(1)}, u32[]{:S(2)}, u32[]{:S(2)}) collective-permute-start(bf16[128,2048]{1,0:T(8,128)(2,1)S(1)} %get-tuple-element.208), channel_id=1, source_target_pairs={{0,4},{1,5},{2,6},{3,7},{4,0},{5,1},{6,2},{7,3},{8,12},{9,13},{10,... | collective-permute-start | bytes 1572872 | tf_op jit(solution)/shard_map/ppermute | solution.py:74
  604.9 23.8 %collective-permute-start.52 = (bf16[128,2048]{1,0:T(8,128)(2,1)S(1)}, bf16[128,2048]{1,0:T(8,128)(2,1)S(1)}, u32[]{:S(2)}, u32[]{:S(2)}) collective-permute-start(bf16[128,2048]{1,0:T(8,128)(2,1)S(1)} %get-tuple-element.208), channel_id=1, source_target_pairs={{0,2},{1,3},{2,0},{3,1},{4,6},{5,7},{6,4},{7,5},{8,10},{9,11},{10,... | collective-permute-start | bytes 1572872 | tf_op jit(solution)/shard_map/ppermute | solution.py:74
  642.7 26.7 %collective-permute-start.59 = (bf16[1024,2560]{1,0:T(8,128)(2,1)}, bf16[1024,2560]{1,0:T(8,128)(2,1)}, u32[]{:S(2)}, u32[]{:S(2)}) collective-permute-start(bf16[1024,2560]{1,0:T(8,128)(2,1)} %convolution_convert_fusion), channel_id=1, source_target_pairs={{0,1},{1,0},{2,3},{3,2},{4,5},{5,4},{6,7},{7,6},{8,9},{9,8},{10,11... | collective-permute-start | bytes 15728648 | tf_op jit(solution)/shard_map/ppermute | solution.py:80
  646.2 18.4 %collective-permute-start.58 = (bf16[1024,1280]{1,0:T(8,128)(2,1)}, bf16[1024,1280]{1,0:T(8,128)(2,1)}, u32[]{:S(2)}, u32[]{:S(2)}) collective-permute-start(bf16[1024,1280]{1,0:T(8,128)(2,1)} %convolution_convert_fusion.2), channel_id=1, source_target_pairs={{0,1},{1,0},{2,3},{3,2},{4,5},{5,4},{6,7},{7,6},{8,9},{9,8},{10,11... | collective-permute-start | bytes 7864328 | tf_op jit(solution)/shard_map/ppermute | solution.py:80
  647.8 97.3 %reduce-scatter.13.cloned.1.call-start = ((), (), s32[]{:S(2)}) async-start(), calls=%async_computation.14 | async-start | bytes 3276800 | tf_op jit(solution)/shard_map/reduce_scatter | solution.py:97
  661.9 16.4 %collective-permute-start.55 = (bf16[128,2048]{1,0:T(8,128)(2,1)}, bf16[128,2048]{1,0:T(8,128)(2,1)S(1)}, u32[]{:S(2)}, u32[]{:S(2)}) collective-permute-start(bf16[128,2048]{1,0:T(8,128)(2,1)} %get-tuple-element.230), channel_id=1, source_target_pairs={{0,2},{1,3},{2,0},{3,1},{4,6},{5,7},{6,4},{7,5},{8,10},{9,11},{10,... | collective-permute-start | bytes 1572872 | tf_op jit(solution)/shard_map/ppermute | solution.py:74
  663.1 15.2 %collective-permute-start.56 = (bf16[128,2048]{1,0:T(8,128)(2,1)}, bf16[128,2048]{1,0:T(8,128)(2,1)}, u32[]{:S(2)}, u32[]{:S(2)}) collective-permute-start(bf16[128,2048]{1,0:T(8,128)(2,1)} %get-tuple-element.231), channel_id=1, source_target_pairs={{0,4},{1,5},{2,6},{3,7},{4,0},{5,1},{6,2},{7,3},{8,12},{9,13},{10,... | collective-permute-start | bytes 1572872 | tf_op jit(solution)/shard_map/ppermute | solution.py:74
  664.3 23.2 %collective-permute-start.57 = (bf16[128,2048]{1,0:T(8,128)(2,1)}, bf16[128,2048]{1,0:T(8,128)(2,1)}, u32[]{:S(2)}, u32[]{:S(2)}) collective-permute-start(bf16[128,2048]{1,0:T(8,128)(2,1)} %get-tuple-element.229), channel_id=1, source_target_pairs={{0,6},{1,7},{2,4},{3,5},{4,2},{5,3},{6,0},{7,1},{8,14},{9,15},{10,... | collective-permute-start | bytes 1572872 | tf_op jit(solution)/shard_map/ppermute | solution.py:74
  687.5 151.2 %reduce-scatter.15.cloned.1.call-start = ((), (), s32[]{:S(2)}) async-start(), calls=%async_computation.15 | async-start | bytes 6553600 | tf_op jit(solution)/shard_map/reduce_scatter | solution.py:97
  697.3 21.2 %collective-permute-start.35 = (bf16[128,2048]{1,0:T(8,128)(2,1)S(1)}, bf16[128,2048]{1,0:T(8,128)(2,1)S(1)}, u32[]{:S(2)}, u32[]{:S(2)}) collective-permute-start(bf16[128,2048]{1,0:T(8,128)(2,1)S(1)} %get-tuple-element.238), channel_id=1, source_target_pairs={{0,6},{1,7},{2,4},{3,5},{4,2},{5,3},{6,0},{7,1},{8,14},{9,15},{10,... | collective-permute-start | bytes 1572872 | tf_op jit(solution)/shard_map/ppermute | solution.py:74
  735.0 116.8 %collective-permute-start.37 = (bf16[256,2048]{1,0:T(8,128)(2,1)}, bf16[256,2048]{1,0:T(8,128)(2,1)}, u32[]{:S(2)}, u32[]{:S(2)}) collective-permute-start(bf16[256,2048]{1,0:T(8,128)(2,1)} %maximum_select_fusion.6), channel_id=1, source_target_pairs={{0,1},{1,0},{2,3},{3,2},{4,5},{5,4},{6,7},{7,6},{8,9},{9,8},{10,11... | collective-permute-start | bytes 3145736 | tf_op jit(solution)/shard_map/ppermute | solution.py:80
  742.3 14.8 %collective-permute-start.62 = (bf16[128,2048]{1,0:T(8,128)(2,1)}, bf16[128,2048]{1,0:T(8,128)(2,1)S(1)}, u32[]{:S(2)}, u32[]{:S(2)}) collective-permute-start(bf16[128,2048]{1,0:T(8,128)(2,1)} %get-tuple-element.205), channel_id=1, source_target_pairs={{0,6},{1,7},{2,4},{3,5},{4,2},{5,3},{6,0},{7,1},{8,14},{9,15},{10,... | collective-permute-start | bytes 1572872 | tf_op jit(solution)/shard_map/ppermute | solution.py:74
  744.6 23.9 %collective-permute-start.61 = (bf16[128,2048]{1,0:T(8,128)(2,1)}, bf16[128,2048]{1,0:T(8,128)(2,1)S(1)}, u32[]{:S(2)}, u32[]{:S(2)}) collective-permute-start(bf16[128,2048]{1,0:T(8,128)(2,1)} %get-tuple-element.205), channel_id=1, source_target_pairs={{0,4},{1,5},{2,6},{3,7},{4,0},{5,1},{6,2},{7,3},{8,12},{9,13},{10,... | collective-permute-start | bytes 1572872 | tf_op jit(solution)/shard_map/ppermute | solution.py:74
  744.9 23.7 %collective-permute-start.60 = (bf16[128,2048]{1,0:T(8,128)(2,1)}, bf16[128,2048]{1,0:T(8,128)(2,1)}, u32[]{:S(2)}, u32[]{:S(2)}) collective-permute-start(bf16[128,2048]{1,0:T(8,128)(2,1)} %get-tuple-element.205), channel_id=1, source_target_pairs={{0,2},{1,3},{2,0},{3,1},{4,6},{5,7},{6,4},{7,5},{8,10},{9,11},{10,... | collective-permute-start | bytes 1572872 | tf_op jit(solution)/shard_map/ppermute | solution.py:74
  745.2 151.6 %reduce-scatter.17.cloned.1.call-start = ((), (), s32[]{:S(2)}) async-start(), calls=%async_computation.16 | async-start | bytes 2293760 | tf_op jit(solution)/shard_map/reduce_scatter | solution.py:97
  788.4 13.7 %collective-permute-start.63 = (bf16[128,2048]{1,0:T(8,128)(2,1)S(1)}, bf16[128,2048]{1,0:T(8,128)(2,1)S(1)}, u32[]{:S(2)}, u32[]{:S(2)}) collective-permute-start(bf16[128,2048]{1,0:T(8,128)(2,1)S(1)} %get-tuple-element.227), channel_id=1, source_target_pairs={{0,2},{1,3},{2,0},{3,1},{4,6},{5,7},{6,4},{7,5},{8,10},{9,11},{10,... | collective-permute-start | bytes 1572872 | tf_op jit(solution)/shard_map/ppermute | solution.py:74
  790.9 23.2 %collective-permute-start.65 = (bf16[128,2048]{1,0:T(8,128)(2,1)S(1)}, bf16[128,2048]{1,0:T(8,128)(2,1)S(1)}, u32[]{:S(2)}, u32[]{:S(2)}) collective-permute-start(bf16[128,2048]{1,0:T(8,128)(2,1)S(1)} %get-tuple-element.226), channel_id=1, source_target_pairs={{0,6},{1,7},{2,4},{3,5},{4,2},{5,3},{6,0},{7,1},{8,14},{9,15},{10,... | collective-permute-start | bytes 1572872 | tf_op jit(solution)/shard_map/ppermute | solution.py:74
  817.5 14.6 %collective-permute-start.68 = (bf16[128,2048]{1,0:T(8,128)(2,1)S(1)}, bf16[128,2048]{1,0:T(8,128)(2,1)S(1)}, u32[]{:S(2)}, u32[]{:S(2)}) collective-permute-start(bf16[128,2048]{1,0:T(8,128)(2,1)S(1)} %select_n.412), channel_id=1, source_target_pairs={{0,2},{1,3},{2,0},{3,1},{4,6},{5,7},{6,4},{7,5},{8,10},{9,11},{10,... | collective-permute-start | bytes 1572872 | tf_op jit(solution)/shard_map/ppermute | solution.py:74
  833.3 27.0 %collective-permute-start.69 = (bf16[256,2048]{1,0:T(8,128)(2,1)}, bf16[256,2048]{1,0:T(8,128)(2,1)}, u32[]{:S(2)}, u32[]{:S(2)}) collective-permute-start(bf16[256,2048]{1,0:T(8,128)(2,1)} %maximum_select_fusion.10), channel_id=1, source_target_pairs={{0,1},{1,0},{2,3},{3,2},{4,5},{5,4},{6,7},{7,6},{8,9},{9,8},{10,11... | collective-permute-start | bytes 3145736 | tf_op jit(solution)/shard_map/ppermute | solution.py:80
  835.5 36.4 %collective-permute-start.76 = (bf16[256,2560]{1,0:T(8,128)(2,1)}, bf16[256,2560]{1,0:T(8,128)(2,1)}, u32[]{:S(2)}, u32[]{:S(2)}) collective-permute-start(bf16[256,2560]{1,0:T(8,128)(2,1)} %reduce-scatter.9.cloned.1.call-done), channel_id=1, source_target_pairs={{0,0},{1,4},{2,2},{3,6},{4,1},{5,5},{6,3},{7,7},{8,8},{9,12},{10,1... | collective-permute-start | bytes 3932168 | tf_op jit(solution)/shard_map/ppermute | solution.py:77
  855.1 19.5 %collective-permute-start.78 = (bf16[256,1280]{1,0:T(8,128)(2,1)}, bf16[256,1280]{1,0:T(8,128)(2,1)S(1)}, u32[]{:S(2)}, u32[]{:S(2)}) collective-permute-start(bf16[256,1280]{1,0:T(8,128)(2,1)} %reduce-scatter.7.cloned.1.call-done), channel_id=1, source_target_pairs={{0,0},{1,4},{2,2},{3,6},{4,1},{5,5},{6,3},{7,7},{8,8},{9,12},{10,1... | collective-permute-start | bytes 1966088 | tf_op jit(solution)/shard_map/ppermute | solution.py:77
  866.3 15.3 %collective-permute-start.77 = (bf16[256,1280]{1,0:T(8,128)(2,1)S(1)}, bf16[256,1280]{1,0:T(8,128)(2,1)S(1)}, u32[]{:S(2)}, u32[]{:S(2)}) collective-permute-start(bf16[256,1280]{1,0:T(8,128)(2,1)S(1)} %copy-done.95), channel_id=1, source_target_pairs={{0,0},{1,4},{2,2},{3,6},{4,1},{5,5},{6,3},{7,7},{8,8},{9,12},{10,1... | collective-permute-start | bytes 1966088 | tf_op jit(solution)/shard_map/ppermute | solution.py:77
  869.9 25.4 %collective-permute-start.75 = (bf16[256,2560]{1,0:T(8,128)(2,1)}, bf16[256,2560]{1,0:T(8,128)(2,1)}, u32[]{:S(2)}, u32[]{:S(2)}) collective-permute-start(bf16[256,2560]{1,0:T(8,128)(2,1)} %reduce-scatter.15.cloned.1.call-done), channel_id=1, source_target_pairs={{0,0},{1,4},{2,2},{3,6},{4,1},{5,5},{6,3},{7,7},{8,8},{9,12},{10,1... | collective-permute-start | bytes 3932168 | tf_op jit(solution)/shard_map/ppermute | solution.py:77
  (160 other events, 1156.0 us)
Sparse Core Ops, SparseCore 0:
  29.8 43.0 all-gather.5
  74.5 139.9 all-gather.7
  243.5 38.9 all-gather.9
  284.4 97.0 all-gather.11
  397.7 51.9 all-gather.13
  484.6 49.8 reduce-scatter.6
  536.8 93.6 reduce-scatter.8
  647.9 37.4 reduce-scatter.10
  688.3 51.2 reduce-scatter.12
  745.3 93.3 reduce-scatter.14
  841.6 43.2 reduce-scatter.16

commit v3 on v2

--- a/solution.py
+++ b/solution.py
@@ -1,6 +1,8 @@
 import jax
 import jax.numpy as jnp
 from jax import lax
+from jax.experimental import pallas as pl
+from jax.experimental.pallas import tpu as pltpu
 from jax.sharding import PartitionSpec as P
 
 HQ = 20
@@ -43,6 +45,86 @@
     scaled = gradient * gain_vector
     cubed = scaling * scaling * scaling
     return scaling * scaled - values * cubed * jnp.mean(scaled * values, axis=-1, keepdims=True)
+
+
+PARTS = 2
+
+
+def join_kernel(terms, state, gain, middle, normed, inbox, sum_send, sum_recv, row_send, row_recv):
+    x, t = lax.axis_index("ctx"), lax.axis_index("tensor")
+    other_x, other_t = 1 - x, t + 2 - 4 * (t // 2)
+    peers = [
+        {"ctx": x, "tensor": other_t},
+        {"ctx": other_x, "tensor": t},
+        {"ctx": other_x, "tensor": other_t},
+    ]
+    rows = state.shape[0]
+    step = rows // PARTS
+    barrier = pltpu.get_barrier_semaphore()
+    for peer in peers:
+        pl.semaphore_signal(barrier, inc=1, device_id=peer, device_id_type=pl.DeviceIdType.MESH)
+    pl.semaphore_wait(barrier, len(peers))
+
+    def sum_copy(part, j):
+        return pltpu.make_async_remote_copy(
+            src_ref=terms.at[pl.ds((j + 1) * rows + part * step, step)],
+            dst_ref=inbox.at[part, j],
+            send_sem=sum_send.at[part, j],
+            recv_sem=sum_recv.at[part, j],
+            device_id=peers[j],
+            device_id_type=pl.DeviceIdType.MESH,
+        )
+
+    def row_copy(part, j):
+        return pltpu.make_async_remote_copy(
+            src_ref=normed.at[pl.ds(part * step, step)],
+            dst_ref=normed.at[pl.ds((j + 1) * rows + part * step, step)],
+            send_sem=row_send.at[part, j],
+            recv_sem=row_recv.at[part, j],
+            device_id=peers[j],
+            device_id_type=pl.DeviceIdType.MESH,
+        )
+
+    for part in range(PARTS):
+        for j in (2, 1, 0):
+            sum_copy(part, j).start()
+    for part in range(PARTS):
+        here = pl.ds(part * step, step)
+        total = terms[here].astype(f32)
+        for j in range(3):
+            sum_copy(part, j).wait_recv()
+            total = total + inbox[part, j].astype(f32)
+        total = state[here] + total
+        middle[here] = total
+        normed[here] = (total * scale_of(total) * gain[...]).astype(bf16)
+        for j in (2, 1, 0):
+            row_copy(part, j).start()
+    for part in range(PARTS):
+        for j in range(3):
+            sum_copy(part, j).wait_send()
+            row_copy(part, j).wait_send()
+            row_copy(part, j).wait_recv()
+
+
+def join(terms, state, gain):
+    rows, width = state.shape
+    whole = pl.BlockSpec(memory_space=pltpu.VMEM)
+    return pl.pallas_call(
+        join_kernel,
+        out_shape=(
+            jax.ShapeDtypeStruct((rows, width), f32),
+            jax.ShapeDtypeStruct((4 * rows, width), bf16),
+        ),
+        in_specs=[whole] * 3,
+        out_specs=(whole, whole),
+        scratch_shapes=[pltpu.VMEM((PARTS, 3, rows // PARTS, width), bf16)]
+        + [pltpu.SemaphoreType.DMA((PARTS, 3))] * 4,
+        compiler_params=pltpu.CompilerParams(
+            collective_id=0, has_side_effects=True, vmem_limit_bytes=32 * 2**20
+        ),
+        cost_estimate=pl.CostEstimate(flops=1000, bytes_accessed=1000, transcendentals=0),
+        name="join",
+    )(terms, state, gain[None])
 
 
 class Plan:
@@ -63,7 +145,16 @@
                 (a * nt + 2 * b + d, (a ^ (j // 2)) * nt + 2 * (b ^ (j % 2)) + d)
                 for a, b, d in places
             ]
-        self.swap_pairs = [(a * nt + 2 * b + d, d * nt + 2 * b + a) for a, b, d in places]
+        self.swap_pairs = [
+            (a * nt + 2 * b + d, d * nt + 2 * b + a) for a, b, d in places if a != d
+        ]
+        self.cross_pairs = {
+            j: [
+                (a * nt + 2 * b + d, d * nt + 2 * (b ^ (j // 2)) + (a ^ (j % 2)))
+                for a, b, d in places
+            ]
+            for j in range(1, 4)
+        }
         assert self.n & (self.n - 1) == 0
         self.core_all = [(i, i ^ 1) for i in range(2 * nt)]
         self.core_pairs = [(i, i ^ 1) for i in range(nt)]
@@ -74,7 +165,11 @@
         return lax.ppermute(value, ("ctx", "tensor"), self.peers[j])
 
     def swap(self, value):
-        return lax.ppermute(value, ("ctx", "tensor"), self.swap_pairs)
+        moved = lax.ppermute(value, ("ctx", "tensor"), self.swap_pairs)
+        return jnp.where(self.x == self.c, value, moved)
+
+    def cross(self, value, j):
+        return lax.ppermute(value, ("ctx", "tensor"), self.cross_pairs[j])
 
     def core(self, value):
         return lax.ppermute(value, "tensor", self.core_pairs)
@@ -109,6 +204,11 @@
 
     def spread(self, rows):
         return jnp.concatenate([rows] + [self.peer(rows, j) for j in range(1, 4)], axis=0)
+
+    def spread_beside(self, rows, beside):
+        moved = [self.peer(rows, j) for j in range(1, 4)]
+        moved, beside = lax.optimization_barrier((moved, beside))
+        return jnp.concatenate([rows] + moved, axis=0), beside
 
     def gather_sum(self, terms, beside=()):
         rows = terms.shape[0] // 4
@@ -144,19 +244,16 @@
             jnp.stack([other, own], axis=-2),
         ).reshape(lead + (d,))
 
-    def replicate(self, rows):
+    def both_quarters(self, rows):
         beside = self.peer(rows, 1)
-        half = jnp.where(
+        return jnp.where(
             self.y == 0,
             jnp.concatenate([rows, beside], axis=0),
             jnp.concatenate([beside, rows], axis=0),
         )
-        other = self.core(half)
+
+    def both_micro(self, half, other):
         return jnp.where(self.c == 0, jnp.stack([half, other]), jnp.stack([other, half]))
-
-
-def pairs_of(rows, first_pair):
-    return jnp.where(first_pair[:, None, None], rows[None, :, 0], rows[None, :, 1])
 
 
 def attend(queries, key_heads, value_heads, allowed):
@@ -209,25 +306,24 @@
 
     kv_at = plan.t * heads // GROUP_SIZE * HD
     hidden_units = w_gate.shape[2]
-    shards = []
+    attn_width = qw + 2 * kw + qw
+    attn_shards = []
     for layer in range(LAYERS):
         keys = lax.dynamic_slice_in_dim(w_key[layer], kv_at, kw, axis=1)
         values = lax.dynamic_slice_in_dim(w_value[layer], kv_at, kw, axis=1)
-        shards.append(jnp.concatenate([w_query[layer], keys, values, w_out[layer].T], axis=1))
-        ffn_parts = [w_gate[layer], w_up[layer], w_down[layer].T]
-        if layer + 1 < LAYERS:
-            shards.append(jnp.concatenate(ffn_parts, axis=1))
-        else:
-            shards.append(jnp.concatenate(ffn_parts[:2], axis=1))
-            shards.append(ffn_parts[2])
-    swapped = []
-    for shard in shards:
-        if swapped:
+        attn_shards += [w_query[layer], keys, values, w_out[layer].T]
+    swapped = [plan.swap(jnp.concatenate(attn_shards, axis=1))]
+    swapped[-1], w_gate, w_up, w_down, tokens, cotangent, norm_gains = lax.optimization_barrier(
+        (swapped[-1], w_gate, w_up, w_down, tokens, cotangent, norm_gains)
+    )
+    for layer in range(LAYERS):
+        shard = jnp.concatenate([w_gate[layer], w_up[layer], w_down[layer].T], axis=1)
+        if layer:
             shard, swapped[-1] = lax.optimization_barrier((shard, swapped[-1]))
         swapped.append(plan.swap(shard))
     owned = []
-    for shard in swapped:
-        if owned:
+    for index, shard in enumerate(swapped):
+        if index > 1:
             shard, owned[-1] = lax.optimization_barrier((shard, owned[-1]))
         owned.append(lax.all_gather(shard, "dp", axis=0, tiled=True))
 
@@ -302,17 +398,19 @@
     state = tokens_all[:quarter]
     stored = []
     fetched = []
-    attn_w, _ = both_parities(owned[0])
+    attn_all, _ = both_parities(owned[0])
     for layer in range(LAYERS):
+        attn_w = columns(attn_all, layer * attn_width, (layer + 1) * attn_width)
         w_qkv = columns(attn_w, 0, qw + 2 * kw)
         w_o = columns(attn_w, qw + 2 * kw, None)
         if layer == 0:
             scale_in = scale_of(tokens_all)
             normed = (tokens_all * scale_in * gain_attn[layer]).astype(bf16)
+            normed, start_grad = lax.optimization_barrier((normed, start_grad))
             scale_in = scale_in[:quarter]
         else:
             scale_in = scale_of(state)
-            normed = plan.spread((state * scale_in * gain_attn[layer]).astype(bf16))
+            normed = next_normed
         qkv = plan.into(normed, w_qkv)
         queries = by_head(qkv[:, :qw], heads)
         query_scale = scale_of(queries)
@@ -328,26 +426,18 @@
         mixed, merged = attend(query_low, key_heads, value_heads, allowed)
         mixed_low = flat(mixed.astype(bf16))
         attn_terms = plan.out_of(mixed_low, w_o)
-        attn, _ = plan.gather_sum(attn_terms)
-        middle = state + attn
-        ffn_w, later_middle = both_parities(owned[2 * layer + 1], middle)
+        middle, normed2 = join(attn_terms, state, gain_ffn[layer])
+        ffn_w, later_middle = both_parities(owned[layer + 1], middle)
         w_g = columns(ffn_w, 0, hidden_units)
         w_u = columns(ffn_w, hidden_units, 2 * hidden_units)
         w_gu = columns(ffn_w, 0, 2 * hidden_units)
         scale_mid = scale_of(middle)
-        normed2 = plan.spread((middle * scale_mid * gain_ffn[layer]).astype(bf16))
         gate = plan.into(normed2, w_g)
         up = plan.into(normed2, w_u)
         hidden = (jax.nn.silu(gate) * up).astype(bf16)
-        if layer + 1 < LAYERS:
-            w_d = columns(ffn_w, 2 * hidden_units, None)
-            ffn_terms = plan.out_of(hidden, w_d)
-            attn_next, hidden = both_parities(owned[2 * layer + 2], hidden)
-        else:
-            w_d, normed2 = both_parities(owned[-1], normed2)
-            ffn_terms = plan.out_of(hidden, w_d)
+        w_d = columns(ffn_w, 2 * hidden_units, None)
+        ffn_terms = plan.out_of(hidden, w_d)
         fetched.append((w_qkv, w_o, w_d, w_gu))
-        ffn, _ = plan.gather_sum(ffn_terms)
         stored.append(
             (
                 state,
@@ -370,14 +460,29 @@
                 hidden,
             )
         )
-        state = later_middle + ffn
-        attn_w = attn_next
-    output = plan.replicate(plan.outward(state.astype(bf16)))
+        if layer + 1 < LAYERS:
+            state, next_normed = join(ffn_terms, later_middle, gain_attn[layer + 1])
 
     gradient = start_grad[:quarter].astype(f32)
     grad_ffn = start_grad
     results = [[None] * 3 for _ in range(LAYERS)]
     last = []
+
+    def finish(term):
+        moved = plan.swap(term)
+        keys = jnp.zeros((term.shape[0], w_key.shape[2]), f32)
+        values = keys
+        for j in range(plan.nt):
+            part = moved[:, qw : qw + 2 * kw] if j == 0 else plan.cross(term[:, qw : qw + 2 * kw], j)
+            part = part.astype(f32)
+            sender = 2 * (plan.y ^ (j // 2)) + (plan.c ^ (j % 2))
+            at = sender * heads // GROUP_SIZE * HD
+            zeros = jnp.zeros_like(keys)
+            keys += lax.dynamic_update_slice_in_dim(zeros, part[:, :kw], at, axis=1)
+            values += lax.dynamic_update_slice_in_dim(zeros, part[:, kw:], at, axis=1)
+        query = moved[:, :qw].astype(f32)
+        out = moved[:, qw + 2 * kw :].T.astype(f32)
+        return query, keys, values, out
 
     def scatter_next(layer, member, term):
         if last:
@@ -410,10 +515,12 @@
             hidden,
         ) = stored[layer]
         if grad_ffn is None:
-            grad_ffn = plan.spread(gradient.astype(bf16))
+            grad_ffn, results[layer + 1][1] = plan.spread_beside(
+                gradient.astype(bf16), results[layer + 1][1]
+            )
         term_d = plan.weight_term(grad_ffn, hidden)
         if layer + 1 == LAYERS:
-            w_d, term_d = lax.optimization_barrier((w_d, term_d))
+            scatter_next(layer, 2, term_d)
         grad_hidden = plan.into(grad_ffn, w_d)
         sigmoid_gate = jax.nn.sigmoid(gate)
         grad_gate = (
@@ -421,15 +528,21 @@
         ).astype(bf16)
         grad_up = (grad_hidden * (gate * sigmoid_gate)).astype(bf16)
         grad_gu = jnp.concatenate([grad_gate, grad_up], axis=1)
+        if layer + 1 < LAYERS:
+            above = results[layer + 1]
+            ffn_high = plan.swap(jnp.concatenate([above[1], above[2]], axis=1))
+            grad_gu, ffn_high, above[0], term_d = lax.optimization_barrier(
+                (grad_gu, ffn_high, above[0], term_d)
+            )
         term_gu = plan.weight_term(normed2, grad_gu)
+        mid_terms = plan.out_of(grad_gu, w_gu)
         if layer + 1 == LAYERS:
+            summed_mid, term_gu = plan.gather_sum(mid_terms, term_gu)
+        else:
             scatter_next(layer, 2, term_d)
-            summed_mid, term_gu = plan.gather_sum(plan.out_of(grad_gu, w_gu), term_gu)
-        else:
-            summed_mid, (term_d, term_gu) = plan.gather_sum(
-                plan.out_of(grad_gu, w_gu), (term_d, term_gu)
+            summed_mid, (results[layer][2], term_gu) = plan.gather_sum(
+                mid_terms, (results[layer][2], term_gu)
             )
-            scatter_next(layer, 2, term_d)
         scatter_next(layer, 1, term_gu)
         grad_g_ffn = jnp.sum(summed_mid * middle * scale_mid, axis=0)
         grad_mid = gradient + norm_back(summed_mid, middle, scale_mid, gain_ffn[layer])
@@ -461,6 +574,9 @@
         grad_g_key = jnp.sum(grad_key_norm * keys * key_scale, axis=(0, 1))
         grad_keys = flat(norm_back(grad_key_norm, keys, key_scale, gain_key[layer]).astype(bf16))
         grad_qkv = jnp.concatenate([grad_queries, grad_keys, grad_values], axis=1)
+        if layer + 1 < LAYERS:
+            attn_high = finish(results[layer + 1][0])
+            grad_qkv, attn_high = lax.optimization_barrier((grad_qkv, attn_high))
         term_qkv = plan.weight_term(normed, grad_qkv)
         summed_in, (term_o, term_qkv) = plan.gather_sum(
             plan.out_of(grad_qkv, w_qkv), (term_o, term_qkv)
@@ -472,27 +588,26 @@
         gain_grads[layer] = jnp.concatenate(
             [plan.outward(grad_g_attn), plan.outward(grad_g_ffn), grad_g_query, grad_g_key]
         )
-    grad_input = plan.replicate(plan.outward(gradient.astype(bf16))).astype(f32)
-
-    for layer in range(LAYERS):
-        results[layer] = [plan.swap(term) for term in results[layer]]
-
-    def stack(pick):
-        return jnp.stack([pick(results[layer]) for layer in range(LAYERS)])
-
-    shared = stack(lambda r: r[0][:, qw : qw + 2 * kw])
-    wide_keys = jnp.zeros(shared.shape[:-1] + (w_key.shape[2],), f32)
-    wide_values = wide_keys
-    for j in range(plan.nt):
-        part = shared
-        if j:
-            part = lax.ppermute(shared, "tensor", [(i, i ^ j) for i in range(plan.nt)])
-        part = part.astype(f32)
-        at = (plan.t ^ j) * heads // GROUP_SIZE * HD
-        zeros = jnp.zeros_like(wide_keys)
-        wide_keys += lax.dynamic_update_slice_in_dim(zeros, part[..., :kw], at, axis=2)
-        wide_values += lax.dynamic_update_slice_in_dim(zeros, part[..., kw:], at, axis=2)
+    ffn_terms, gradient = lax.optimization_barrier((ffn_terms, gradient))
+    ffn, _ = plan.gather_sum(ffn_terms)
+    output = plan.both_quarters(plan.outward((later_middle + ffn).astype(bf16)))
+    output = (output, plan.core(output))
+    grad_input = plan.both_quarters(plan.outward(gradient.astype(bf16)))
+    grad_input = (grad_input, plan.core(grad_input))
     all_gains = plan.total(jnp.stack(gain_grads))
+
+    ffn_low = plan.swap(jnp.concatenate([results[0][1], results[0][2]], axis=1))
+    grad_down = jnp.stack([ffn[:, 2 * hidden_units :].T for ffn in (ffn_low, ffn_high)])
+    attn_low, ffn_low, grad_down, output, grad_input, all_gains = lax.optimization_barrier(
+        (results[0][0], ffn_low, grad_down.astype(f32), output, grad_input, all_gains)
+    )
+    grad_gate = jnp.stack([ffn[:, :hidden_units] for ffn in (ffn_low, ffn_high)])
+    grad_up = jnp.stack([ffn[:, hidden_units : 2 * hidden_units] for ffn in (ffn_low, ffn_high)])
+    output = plan.both_micro(*output)
+    grad_input = plan.both_micro(*grad_input).astype(f32)
+    grad_query, grad_key, grad_value, grad_out = (
+        jnp.stack(pair) for pair in zip(finish(attn_low), attn_high)
+    )
     share = norm_gains.shape[1]
     grad_gains = lax.dynamic_slice_in_dim(
         all_gains, (2 * plan.z + plan.x) * share, share, axis=1
@@ -500,13 +615,13 @@
     return (
         output[:, None],
         grad_input[:, None],
-        stack(lambda r: r[0][:, :qw]).astype(f32),
-        wide_keys,
-        wide_values,
-        stack(lambda r: r[0][:, qw + 2 * kw :].T).astype(f32),
-        stack(lambda r: r[1][:, :hidden_units]).astype(f32),
-        stack(lambda r: r[1][:, hidden_units:]).astype(f32),
-        stack(lambda r: r[2].T).astype(f32),
+        grad_query,
+        grad_key,
+        grad_value,
+        grad_out,
+        grad_gate.astype(f32),
+        grad_up.astype(f32),
+        grad_down,
         grad_gains,
     )
 

time: 939 us -> 867 us (0.923)
  waiting for transfers between devices: 479 us -> 297 us
  Pallas kernels: 0 us -> 147 us
  starting transfers between devices: 134 us -> 79.4 us
  other arithmetic: 82.1 us -> 93.2 us
  local copies, waits for them, and re-layouts: 48.1 us -> 58 us
    pallas_call x0 -> x3, Pallas kernels: none -> 147 us  [join(): pl.pallas_call(join_kernel, out_shape=(jax.ShapeDtypeStruct((rows, width)...]
    ppermute x46 -> x28, waiting for transfers between devices: 289 us -> 157 us  [peer(): return lax.ppermute(value, ('ctx', 'tensor'), self.peers[j])]
    all_gather x5 -> x3, waiting for transfers between devices: 116 us -> 33 us  [local(): owned.append(lax.all_gather(shard, 'dp', axis=0, tiled=True))]
    ppermute x46 -> x28, starting transfers between devices: 58.3 us -> 23.3 us  [peer(): return lax.ppermute(value, ('ctx', 'tensor'), self.peers[j])]
    reduce_scatter x6, waiting for transfers between devices: 4.24 us -> 32 us  [scatter(): return lax.psum_scatter(term, 'dp', scatter_dimension=0, tiled=True)]
    ppermute x14 -> x13, waiting for transfers between devices: 52.2 us -> 66.8 us  [the longest x7 66.8 us: swap(): moved = lax.ppermute(value, ('ctx', 'tensor'), self.swap_pairs)]
    ppermute x15 -> x13, starting transfers between devices: 16 us -> 4.48 us  [core(): return lax.ppermute(value, 'tensor', self.core_pairs)]
    select_n x3 -> x10, other arithmetic: 7.19 us -> 18.2 us  [the longest x7 11.8 us: swap(): return jnp.where(self.x == self.c, value, moved)]
  transfers between devices with their start and end apart: 95 -> 72, of which waited for: 59 -> 35; matrix products, arithmetic and copies ran while one was open for 29% -> 32% of each run, Pallas kernels for 0% -> 17%
where the time goes in v3:
time: 867 us; the launch traced here: 859 us
  waiting for transfers between devices  297 us (34%)
  matrix products  166 us (19%)
  Pallas kernels  147 us (17%)
  other arithmetic  93.2 us (11%)
  starting transfers between devices  79.4 us (9%)
  local copies, waits for them, and re-layouts  58 us (7%)
  between operations  17.8 us (2%)
    ppermute x28, waiting for transfers between devices, peer(): return lax.ppermute(value, ('ctx', 'tensor'), self.peers[j])  157 us
    dot_general x52, matrix products, product(): lax.dot_general(left_side, right_side, (contract, ((), ())), preferred_el...  148 us
    pallas_call x3, Pallas kernels, join(): pl.pallas_call(join_kernel, out_shape=(jax.ShapeDtypeStruct((rows, width)...  147 us
    ppermute x7, waiting for transfers between devices, swap(): moved = lax.ppermute(value, ('ctx', 'tensor'), self.swap_pairs)  66.8 us
    all_gather x3, waiting for transfers between devices, local(): owned.append(lax.all_gather(shard, 'dp', axis=0, tiled=True))  33 us
    reduce_scatter x6, waiting for transfers between devices, scatter(): return lax.psum_scatter(term, 'dp', scatter_dimension=0, tiled=True)  32 us
    ppermute x7, starting transfers between devices, swap(): moved = lax.ppermute(value, ('ctx', 'tensor'), self.swap_pairs)  28.4 us
    ppermute x28, starting transfers between devices, peer(): return lax.ppermute(value, ('ctx', 'tensor'), self.peers[j])  23.3 us
  transfers between devices with their start and end apart: 72, of which 35 were waited for; matrix products, arithmetic and copies ran while one was open for 32% of the time, Pallas kernels for 17%

profile of v3, /device:TPU:1, one launch (start us, length us, event | category | flops | bytes accessed | tf_op | source)
XLA Modules:
  0.0 859.2 jit_solution(16386151205833807571)
XLA Ops:
  12.4 4.5 collective-permute-start
  18.0 9.9 %collective-permute-done = bf16[256,1792]{0,1:T(8,128)(2,1)S(1)} collective-permute-done((bf16[256,1792]{0,1:T(8,128)(2,1)S(1)}, bf16[256,1792]{0,1:T(8,128)(2,1)S(1)}, u32[]{:S(2)}, u32[]{:S(2)}) %collective-permute-start) | collective-permute-done | bytes 917536 | tf_op jit(solution)/shard_map/ppermute | solution.py:168
  40.0 3.6 collective-permute-start.8
  45.0 3.9 copy.70
  53.0 24.7 %collective-permute-done.8 = bf16[256,3840]{1,0:T(8,128)(2,1)} collective-permute-done((bf16[256,3840]{1,0:T(8,128)(2,1)}, bf16[256,3840]{1,0:T(8,128)(2,1)}, u32[]{:S(2)}, u32[]{:S(2)}) %collective-permute-start.8) | collective-permute-done | bytes 1966112 | tf_op jit(solution)/shard_map/ppermute | solution.py:168
  77.8 3.4 broadcast_select_fusion.3
  81.3 3.3 collective-permute-start.3
  95.4 8.1 collective-permute-start.9
  104.9 12.6 %collective-permute-done.6 = bf16[256,2048]{1,0:T(8,128)(2,1)} collective-permute-done((bf16[256,2048]{1,0:T(8,128)(2,1)}, bf16[256,2048]{1,0:T(8,128)(2,1)}, u32[]{:S(2)}, u32[]{:S(2)}) %collective-permute-start.6) | collective-permute-done | bytes 1048608 | tf_op jit(solution)/shard_map/ppermute | solution.py:165
  117.5 3.3 maximum_select_fusion
  122.7 18.7 %collective-permute-done.9 = bf16[256,3840]{1,0:T(8,128)(2,1)} collective-permute-done((bf16[256,3840]{1,0:T(8,128)(2,1)}, bf16[256,3840]{1,0:T(8,128)(2,1)}, u32[]{:S(2)}, u32[]{:S(2)}) %collective-permute-start.9) | collective-permute-done | bytes 1966112 | tf_op jit(solution)/shard_map/ppermute | solution.py:168
  161.1 50.2 %join.3 = (f32[128,2048]{1,0:T(8,128)S(1)}, bf16[512,2048]{1,0:T(8,128)(2,1)S(1)}) custom-call(bf16[512,2048]{1,0:T(8,128)(2,1)S(1)} %pad_maximum_fusion.2.terms, f32[128,2048]{1,0:T(8,128)S(1)} %slice.859.state, f32[1,2048]{1,0:T(1,128)S(1)} %get-tuple-element.338.gain), custom_call_target="tpu_custom_call" | custom-call | flops 1000 | bytes 1000 | tf_op jit(solution)/shard_map/join/pallas_call | solution.py:112
  212.7 31.6 %all-gather.6.cloned.1.call-done = bf16[1024,3840]{1,0:T(8,128)(2,1)} async-done(((bf16[256,3840]{1,0:T(8,128)(2,1)}), bf16[1024,3840]{1,0:T(8,128)(2,1)}) %all-gather.6.cloned.1.call-update) | async-done | bytes 7864336 | tf_op jit(solution)/shard_map/all_gather | solution.py:328
  245.1 3.7 fusion.21
  248.8 3.3 fusion.24
  252.1 5.1 collective-permute-done.10
  257.2 3.5 convolution_add_fusion.5
  260.6 5.8 multiply_convert_fusion.8
  266.4 3.8 fusion.61
  270.2 3.3 fusion.67
  273.7 48.9 %join.4 = (f32[128,2048]{1,0:T(8,128)S(1)}, bf16[512,2048]{1,0:T(8,128)(2,1)S(1)}) custom-call(bf16[512,2048]{1,0:T(8,128)(2,1)S(1)} %pad_maximum_fusion.3.terms, f32[128,2048]{1,0:T(8,128)S(1)} %get-tuple-element.103.state, f32[1,2048]{1,0:T(1,128)S(1)} %get-tuple-element.339.gain), custom_call_target="tpu_custom_call" | custom-call | flops 1000 | bytes 1000 | tf_op jit(solution)/shard_map/join/pallas_call | solution.py:112
  334.8 48.3 %join.5 = (f32[128,2048]{1,0:T(8,128)S(1)}, bf16[512,2048]{1,0:T(8,128)(2,1)S(1)}) custom-call(bf16[512,2048]{1,0:T(8,128)(2,1)S(1)} %pad_maximum_fusion.4.terms, f32[128,2048]{1,0:T(8,128)S(1)} %get-tuple-element.105.state, f32[1,2048]{1,0:T(1,128)S(1)} %get-tuple-element.337.gain), custom_call_target="tpu_custom_call" | custom-call | flops 1000 | bytes 1000 | tf_op jit(solution)/shard_map/join/pallas_call | solution.py:112
  386.3 3.7 fusion.17
  390.0 3.4 fusion.19
  393.5 3.3 fusion.42
  406.7 4.8 convolution_convert_fusion.1
  411.6 3.1 add_convert_fusion.3
  417.2 6.8 fusion.49
  424.0 5.8 fusion.55
  434.0 6.6 add_convert_fusion.1
  440.6 5.2 collective-permute-done.14
  445.8 11.9 %collective-permute-done.12 = bf16[128,2048]{1,0:T(8,128)(2,1)} collective-permute-done((bf16[128,2048]{1,0:T(8,128)(2,1)}, bf16[128,2048]{1,0:T(8,128)(2,1)}, u32[]{:S(2)}, u32[]{:S(2)}) %collective-permute-start.12) | collective-permute-done | bytes 524320 | tf_op jit(solution)/shard_map/ppermute | solution.py:165
  457.7 7.2 reduce-scatter.7.cloned.1.call-done
  473.2 9.5 %collective-permute-done.18 = bf16[128,2048]{1,0:T(8,128)(2,1)S(1)} collective-permute-done((bf16[128,2048]{1,0:T(8,128)(2,1)S(1)}, bf16[128,2048]{1,0:T(8,128)(2,1)S(1)}, u32[]{:S(2)}, u32[]{:S(2)}) %collective-permute-start.18) | collective-permute-done | bytes 524320 | tf_op jit(solution)/shard_map/ppermute | solution.py:165
  482.7 11.4 %collective-permute-done.17 = bf16[128,2048]{1,0:T(8,128)(2,1)S(1)} collective-permute-done((bf16[128,2048]{1,0:T(8,128)(2,1)S(1)}, bf16[128,2048]{1,0:T(8,128)(2,1)S(1)}, u32[]{:S(2)}, u32[]{:S(2)}) %collective-permute-start.17) | collective-permute-done | bytes 524320 | tf_op jit(solution)/shard_map/ppermute | solution.py:165
  519.2 9.9 %collective-permute-done.21 = bf16[128,2048]{1,0:T(8,128)(2,1)S(1)} collective-permute-done((bf16[128,2048]{1,0:T(8,128)(2,1)S(1)}, bf16[128,2048]{1,0:T(8,128)(2,1)S(1)}, u32[]{:S(2)}, u32[]{:S(2)}) %collective-permute-start.21) | collective-permute-done | bytes 524320 | tf_op jit(solution)/shard_map/ppermute | solution.py:165
  529.1 12.0 %collective-permute-done.19 = bf16[128,2048]{1,0:T(8,128)(2,1)S(1)} collective-permute-done((bf16[128,2048]{1,0:T(8,128)(2,1)S(1)}, bf16[128,2048]{1,0:T(8,128)(2,1)S(1)}, u32[]{:S(2)}, u32[]{:S(2)}) %collective-permute-start.19) | collective-permute-done | bytes 524320 | tf_op jit(solution)/shard_map/ppermute | solution.py:165
  547.5 13.1 %reduce-scatter.9.cloned.1.call-done = bf16[256,2560]{1,0:T(8,128)(2,1)} async-done(((bf16[1024,2560]{1,0:T(8,128)(2,1)}), bf16[256,2560]{1,0:T(8,128)(2,1)}) %reduce-scatter.9.cloned.1.call-update) | async-done | bytes 1310736 | tf_op jit(solution)/shard_map/reduce_scatter | solution.py:192
  560.7 8.3 collective-permute-done.25
  571.2 3.6 collective-permute-start.28
  578.3 3.4 fusion.44
  581.7 4.0 multiply_convert_fusion.4
  587.4 10.2 %collective-permute-done.28 = bf16[256,3840]{1,0:T(8,128)(2,1)S(1)} collective-permute-done((bf16[256,3840]{1,0:T(8,128)(2,1)S(1)}, bf16[256,3840]{1,0:T(8,128)(2,1)S(1)}, u32[]{:S(2)}, u32[]{:S(2)}) %collective-permute-start.28) | collective-permute-done | bytes 1966112 | tf_op jit(solution)/shard_map/ppermute | solution.py:168
  602.2 5.7 reduce-scatter.11.cloned.1.call-done
  607.9 7.3 convolution_convert_fusion
  616.1 3.3 fusion.64
  619.4 4.3 fusion.70
  630.3 3.4 collective-permute-start.37
  633.7 6.2 fusion.52
  640.0 5.4 fusion.58
  652.2 6.4 add_convert_fusion
  658.6 3.2 collective-permute-done.32
  661.8 10.4 %collective-permute-done.30 = bf16[128,2048]{1,0:T(8,128)(2,1)} collective-permute-done((bf16[128,2048]{1,0:T(8,128)(2,1)}, bf16[128,2048]{1,0:T(8,128)(2,1)}, u32[]{:S(2)}, u32[]{:S(2)}) %collective-permute-start.30) | collective-permute-done | bytes 524320 | tf_op jit(solution)/shard_map/ppermute | solution.py:165
  682.0 9.9 %collective-permute-done.36 = bf16[128,2048]{1,0:T(8,128)(2,1)S(1)} collective-permute-done((bf16[128,2048]{1,0:T(8,128)(2,1)}, bf16[128,2048]{1,0:T(8,128)(2,1)S(1)}, u32[]{:S(2)}, u32[]{:S(2)}) %collective-permute-start.36) | collective-permute-done | bytes 524320 | tf_op jit(solution)/shard_map/ppermute | solution.py:165
  691.9 11.3 %collective-permute-done.35 = bf16[128,2048]{1,0:T(8,128)(2,1)S(1)} collective-permute-done((bf16[128,2048]{1,0:T(8,128)(2,1)}, bf16[128,2048]{1,0:T(8,128)(2,1)S(1)}, u32[]{:S(2)}, u32[]{:S(2)}) %collective-permute-start.35) | collective-permute-done | bytes 524320 | tf_op jit(solution)/shard_map/ppermute | solution.py:165
  708.2 4.6 multiply_reduce_fusion
  730.6 8.1 collective-permute-done.43
  738.7 12.1 %collective-permute-done.41 = bf16[128,2048]{1,0:T(8,128)(2,1)S(1)} collective-permute-done((bf16[128,2048]{1,0:T(8,128)(2,1)S(1)}, bf16[128,2048]{1,0:T(8,128)(2,1)S(1)}, u32[]{:S(2)}, u32[]{:S(2)}) %collective-permute-start.41) | collective-permute-done | bytes 524320 | tf_op jit(solution)/shard_map/ppermute | solution.py:165
  778.5 5.7 collective-permute-done.48
  784.3 3.5 collective-permute-done.47
  803.1 9.3 %collective-permute-done.50 = bf16[128,2048]{1,0:T(8,128)(2,1)S(1)} collective-permute-done((bf16[128,2048]{1,0:T(8,128)(2,1)}, bf16[128,2048]{1,0:T(8,128)(2,1)S(1)}, u32[]{:S(2)}, u32[]{:S(2)}) %collective-permute-start.50) | collective-permute-done | bytes 524320 | tf_op jit(solution)/shard_map/ppermute | solution.py:165
  822.3 3.8 reduce-scatter.17.cloned.1.call-done
  838.9 3.2 maximum_select_fusion.1
  842.1 3.3 copy.87
  (711 shorter events, 260.0 us)
Async XLA Ops:
  7.2 96.3 %all-gather.4.cloned.1.call-start = ((), (), s32[]{:S(2)}) async-start(), calls=%async_computation.6 | async-start | bytes 4587520 | tf_op jit(solution)/shard_map/all_gather | solution.py:328
  12.4 15.6 %collective-permute-start = (bf16[256,1792]{0,1:T(8,128)(2,1)S(1)}, bf16[256,1792]{0,1:T(8,128)(2,1)S(1)}, u32[]{:S(2)}, u32[]{:S(2)}) collective-permute-start(bf16[256,1792]{0,1:T(8,128)(2,1)S(1)} %bitcast_dynamic-update-slice_fusion), channel_id=1, source_target_pairs={{1,4},{3,6},{4,1},{6,3},{9,12},{11,14},{12,9},{14,11},{17,20},{19,... | collective-permute-start | bytes 2752520 | tf_op jit(solution)/shard_map/ppermute | solution.py:168
  29.0 215.3 %all-gather.6.cloned.1.call-start = ((), (), s32[]{:S(2)}) async-start(), calls=%async_computation.7 | async-start | bytes 9830400 | tf_op jit(solution)/shard_map/all_gather | solution.py:328
  30.4 50.8 %collective-permute-start.2 = (bf16[2,528]{1,0:T(2,128)(2,1)S(1)}, bf16[2,528]{1,0:T(2,128)(2,1)S(1)}, u32[]{:S(2)}, u32[]{:S(2)}) collective-permute-start(bf16[2,528]{1,0:T(2,128)(2,1)S(1)} %copy-done.118), channel_id=1, source_target_pairs={{0,4},{4,0},{1,5},{5,1},{2,6},{6,2},{3,7},{7,3},{8,12},{12,8},{9,1... | collective-permute-start | bytes 6344 | tf_op jit(solution)/shard_map/ppermute | solution.py:338
  40.0 37.8 %collective-permute-start.8 = (bf16[256,3840]{1,0:T(8,128)(2,1)}, bf16[256,3840]{1,0:T(8,128)(2,1)}, u32[]{:S(2)}, u32[]{:S(2)}) collective-permute-start(bf16[256,3840]{1,0:T(8,128)(2,1)} %pad_maximum_fusion.10), channel_id=1, source_target_pairs={{1,4},{3,6},{4,1},{6,3},{9,12},{11,14},{12,9},{14,11},{17,20},{19,... | collective-permute-start | bytes 5898248 | tf_op jit(solution)/shard_map/ppermute | solution.py:168
  45.0 58.8 %collective-permute-start.1 = (bf16[256,2048]{1,0:T(8,128)(2,1)S(1)}, bf16[256,2048]{1,0:T(8,128)(2,1)S(1)}, u32[]{:S(2)}, u32[]{:S(2)}) collective-permute-start(bf16[256,2048]{1,0:T(8,128)(2,1)S(1)} %maximum_select_fusion.4), channel_id=1, source_target_pairs={{0,4},{1,5},{2,6},{3,7},{4,0},{5,1},{6,2},{7,3},{8,12},{9,13},{10,... | collective-permute-start | bytes 3145736 | tf_op jit(solution)/shard_map/ppermute | solution.py:165
  81.1 304.7 %all-gather.8.cloned.1.call-start = ((), (), s32[]{:S(2)}) async-start(), calls=%async_computation.8 | async-start | bytes 9830400 | tf_op jit(solution)/shard_map/all_gather | solution.py:328
  94.8 22.7 %collective-permute-start.6 = (bf16[256,2048]{1,0:T(8,128)(2,1)}, bf16[256,2048]{1,0:T(8,128)(2,1)}, u32[]{:S(2)}, u32[]{:S(2)}) collective-permute-start(bf16[256,2048]{1,0:T(8,128)(2,1)} %maximum_select_fusion.6), channel_id=1, source_target_pairs={{0,4},{1,5},{2,6},{3,7},{4,0},{5,1},{6,2},{7,3},{8,12},{9,13},{10,... | collective-permute-start | bytes 3145736 | tf_op jit(solution)/shard_map/ppermute | solution.py:165
  95.4 46.0 %collective-permute-start.9 = (bf16[256,3840]{1,0:T(8,128)(2,1)}, bf16[256,3840]{1,0:T(8,128)(2,1)}, u32[]{:S(2)}, u32[]{:S(2)}) collective-permute-start(bf16[256,3840]{1,0:T(8,128)(2,1)} %pad_maximum_fusion.9), channel_id=1, source_target_pairs={{1,4},{3,6},{4,1},{6,3},{9,12},{11,14},{12,9},{14,11},{17,20},{19,... | collective-permute-start | bytes 5898248 | tf_op jit(solution)/shard_map/ppermute | solution.py:168
  103.5 43.3 %collective-permute-start.7 = (bf16[1024,1792]{0,1:T(8,128)(2,1)}, bf16[1024,1792]{0,1:T(8,128)(2,1)}, u32[]{:S(2)}, u32[]{:S(2)}) collective-permute-start(bf16[1024,1792]{0,1:T(8,128)(2,1)} %all-gather.4.cloned.1.call-done), channel_id=1, source_target_pairs={{0,1},{1,0},{2,3},{3,2},{4,5},{5,4},{6,7},{7,6},{8,9},{9,8},{10,11... | collective-permute-start | bytes 11010056 | tf_op jit(solution)/shard_map/ppermute | solution.py:175
  244.3 12.8 %collective-permute-start.10 = (bf16[1024,3840]{1,0:T(8,128)(2,1)}, bf16[1024,3840]{1,0:T(8,128)(2,1)}, u32[]{:S(2)}, u32[]{:S(2)}) collective-permute-start(bf16[1024,3840]{1,0:T(8,128)(2,1)} %all-gather.6.cloned.1.call-done), channel_id=1, source_target_pairs={{0,1},{1,0},{2,3},{3,2},{4,5},{5,4},{6,7},{7,6},{8,9},{9,8},{10,11... | collective-permute-start | bytes 23592968 | tf_op jit(solution)/shard_map/ppermute | solution.py:175
  244.8 220.0 %reduce-scatter.7.cloned.1.call-start = ((), (), s32[]{:S(2)}) async-start(), calls=%async_computation.9 | async-start | bytes 3276800 | tf_op jit(solution)/shard_map/reduce_scatter | solution.py:192
  385.8 12.7 %collective-permute-start.11 = (bf16[1024,3840]{1,0:T(8,128)(2,1)}, bf16[1024,3840]{1,0:T(8,128)(2,1)S(1)}, u32[]{:S(2)}, u32[]{:S(2)}) collective-permute-start(bf16[1024,3840]{1,0:T(8,128)(2,1)} %all-gather.8.cloned.1.call-done), channel_id=1, source_target_pairs={{0,1},{1,0},{2,3},{3,2},{4,5},{5,4},{6,7},{7,6},{8,9},{9,8},{10,11... | collective-permute-start | bytes 23592968 | tf_op jit(solution)/shard_map/ppermute | solution.py:175
  411.5 22.5 %collective-permute-start.15 = (bf16[1024,2560]{1,0:T(8,128)(2,1)}, bf16[1024,2560]{1,0:T(8,128)(2,1)}, u32[]{:S(2)}, u32[]{:S(2)}) collective-permute-start(bf16[1024,2560]{1,0:T(8,128)(2,1)} %convolution_convert_fusion.1), channel_id=1, source_target_pairs={{0,1},{1,0},{2,3},{3,2},{4,5},{5,4},{6,7},{7,6},{8,9},{9,8},{10,11... | collective-permute-start | bytes 15728648 | tf_op jit(solution)/shard_map/ppermute | solution.py:175
  414.8 145.9 %reduce-scatter.9.cloned.1.call-start = ((), (), s32[]{:S(2)}) async-start(), calls=%async_computation.10 | async-start | bytes 6553600 | tf_op jit(solution)/shard_map/reduce_scatter | solution.py:192
  431.4 14.4 %collective-permute-start.14 = (bf16[128,2048]{1,0:T(8,128)(2,1)}, bf16[128,2048]{1,0:T(8,128)(2,1)}, u32[]{:S(2)}, u32[]{:S(2)}) collective-permute-start(bf16[128,2048]{1,0:T(8,128)(2,1)} %get-tuple-element.253), channel_id=1, source_target_pairs={{0,6},{1,7},{2,4},{3,5},{4,2},{5,3},{6,0},{7,1},{8,14},{9,15},{10,... | collective-permute-start | bytes 1572872 | tf_op jit(solution)/shard_map/ppermute | solution.py:165
  433.5 24.2 %collective-permute-start.12 = (bf16[128,2048]{1,0:T(8,128)(2,1)}, bf16[128,2048]{1,0:T(8,128)(2,1)}, u32[]{:S(2)}, u32[]{:S(2)}) collective-permute-start(bf16[128,2048]{1,0:T(8,128)(2,1)} %get-tuple-element.254), channel_id=1, source_target_pairs={{0,2},{1,3},{2,0},{3,1},{4,6},{5,7},{6,4},{7,5},{8,10},{9,11},{10,... | collective-permute-start | bytes 1572872 | tf_op jit(solution)/shard_map/ppermute | solution.py:165
  433.7 23.9 %collective-permute-start.13 = (bf16[128,2048]{1,0:T(8,128)(2,1)}, bf16[128,2048]{1,0:T(8,128)(2,1)}, u32[]{:S(2)}, u32[]{:S(2)}) collective-permute-start(bf16[128,2048]{1,0:T(8,128)(2,1)} %get-tuple-element.255), channel_id=1, source_target_pairs={{0,4},{1,5},{2,6},{3,7},{4,0},{5,1},{6,2},{7,3},{8,12},{9,13},{10,... | collective-permute-start | bytes 1572872 | tf_op jit(solution)/shard_map/ppermute | solution.py:165
  464.8 143.1 %reduce-scatter.11.cloned.1.call-start = ((), (), s32[]{:S(2)}) async-start(), calls=%async_computation.11 | async-start | bytes 2293760 | tf_op jit(solution)/shard_map/reduce_scatter | solution.py:192
  469.2 13.6 %collective-permute-start.18 = (bf16[128,2048]{1,0:T(8,128)(2,1)S(1)}, bf16[128,2048]{1,0:T(8,128)(2,1)S(1)}, u32[]{:S(2)}, u32[]{:S(2)}) collective-permute-start(bf16[128,2048]{1,0:T(8,128)(2,1)S(1)} %get-tuple-element.233), channel_id=1, source_target_pairs={{0,6},{1,7},{2,4},{3,5},{4,2},{5,3},{6,0},{7,1},{8,14},{9,15},{10,... | collective-permute-start | bytes 1572872 | tf_op jit(solution)/shard_map/ppermute | solution.py:165
  471.3 22.8 %collective-permute-start.17 = (bf16[128,2048]{1,0:T(8,128)(2,1)S(1)}, bf16[128,2048]{1,0:T(8,128)(2,1)S(1)}, u32[]{:S(2)}, u32[]{:S(2)}) collective-permute-start(bf16[128,2048]{1,0:T(8,128)(2,1)S(1)} %get-tuple-element.233), channel_id=1, source_target_pairs={{0,4},{1,5},{2,6},{3,7},{4,0},{5,1},{6,2},{7,3},{8,12},{9,13},{10,... | collective-permute-start | bytes 1572872 | tf_op jit(solution)/shard_map/ppermute | solution.py:165
  471.6 23.7 %collective-permute-start.16 = (bf16[128,2048]{1,0:T(8,128)(2,1)S(1)}, bf16[128,2048]{1,0:T(8,128)(2,1)S(1)}, u32[]{:S(2)}, u32[]{:S(2)}) collective-permute-start(bf16[128,2048]{1,0:T(8,128)(2,1)S(1)} %get-tuple-element.233), channel_id=1, source_target_pairs={{0,2},{1,3},{2,0},{3,1},{4,6},{5,7},{6,4},{7,5},{8,10},{9,11},{10,... | collective-permute-start | bytes 1572872 | tf_op jit(solution)/shard_map/ppermute | solution.py:165
  509.1 9.1 %collective-permute-start.23 = (bf16[1024,576]{0,1:T(8,128)(2,1)S(1)}, bf16[1024,576]{0,1:T(8,128)(2,1)S(1)}, u32[]{:S(2)}, u32[]{:S(2)}) collective-permute-start(bf16[1024,576]{0,1:T(8,128)(2,1)S(1)} %convolution_convert_fusion.5), channel_id=1, source_target_pairs={{0,1},{1,0},{2,3},{3,2},{4,5},{5,4},{6,7},{7,6},{8,9},{9,8},{10,11... | collective-permute-start | bytes 3538952 | tf_op jit(solution)/shard_map/ppermute | solution.py:175
  515.0 14.1 %collective-permute-start.21 = (bf16[128,2048]{1,0:T(8,128)(2,1)S(1)}, bf16[128,2048]{1,0:T(8,128)(2,1)S(1)}, u32[]{:S(2)}, u32[]{:S(2)}) collective-permute-start(bf16[128,2048]{1,0:T(8,128)(2,1)S(1)} %get-tuple-element.250), channel_id=1, source_target_pairs={{0,6},{1,7},{2,4},{3,5},{4,2},{5,3},{6,0},{7,1},{8,14},{9,15},{10,... | collective-permute-start | bytes 1572872 | tf_op jit(solution)/shard_map/ppermute | solution.py:165
  517.2 24.0 %collective-permute-start.19 = (bf16[128,2048]{1,0:T(8,128)(2,1)S(1)}, bf16[128,2048]{1,0:T(8,128)(2,1)S(1)}, u32[]{:S(2)}, u32[]{:S(2)}) collective-permute-start(bf16[128,2048]{1,0:T(8,128)(2,1)S(1)} %get-tuple-element.251), channel_id=1, source_target_pairs={{0,2},{1,3},{2,0},{3,1},{4,6},{5,7},{6,4},{7,5},{8,10},{9,11},{10,... | collective-permute-start | bytes 1572872 | tf_op jit(solution)/shard_map/ppermute | solution.py:165
  517.5 23.7 %collective-permute-start.20 = (bf16[128,2048]{1,0:T(8,128)(2,1)S(1)}, bf16[128,2048]{1,0:T(8,128)(2,1)S(1)}, u32[]{:S(2)}, u32[]{:S(2)}) collective-permute-start(bf16[128,2048]{1,0:T(8,128)(2,1)S(1)} %get-tuple-element.252), channel_id=1, source_target_pairs={{0,4},{1,5},{2,6},{3,7},{4,0},{5,1},{6,2},{7,3},{8,12},{9,13},{10,... | collective-permute-start | bytes 1572872 | tf_op jit(solution)/shard_map/ppermute | solution.py:165
  543.3 17.3 %collective-permute-start.26 = (bf16[128,2048]{1,0:T(8,128)(2,1)}, bf16[128,2048]{1,0:T(8,128)(2,1)}, u32[]{:S(2)}, u32[]{:S(2)}) collective-permute-start(bf16[128,2048]{1,0:T(8,128)(2,1)} %get-tuple-element.228), channel_id=1, source_target_pairs={{0,6},{1,7},{2,4},{3,5},{4,2},{5,3},{6,0},{7,1},{8,14},{9,15},{10,... | collective-permute-start | bytes 1572872 | tf_op jit(solution)/shard_map/ppermute | solution.py:165
  544.1 24.8 %collective-permute-start.25 = (bf16[128,2048]{1,0:T(8,128)(2,1)}, bf16[128,2048]{1,0:T(8,128)(2,1)}, u32[]{:S(2)}, u32[]{:S(2)}) collective-permute-start(bf16[128,2048]{1,0:T(8,128)(2,1)} %get-tuple-element.228), channel_id=1, source_target_pairs={{0,4},{1,5},{2,6},{3,7},{4,0},{5,1},{6,2},{7,3},{8,12},{9,13},{10,... | collective-permute-start | bytes 1572872 | tf_op jit(solution)/shard_map/ppermute | solution.py:165
  545.7 23.9 %collective-permute-start.24 = (bf16[128,2048]{1,0:T(8,128)(2,1)}, bf16[128,2048]{1,0:T(8,128)(2,1)}, u32[]{:S(2)}, u32[]{:S(2)}) collective-permute-start(bf16[128,2048]{1,0:T(8,128)(2,1)} %get-tuple-element.228), channel_id=1, source_target_pairs={{0,2},{1,3},{2,0},{3,1},{4,6},{5,7},{6,4},{7,5},{8,10},{9,11},{10,... | collective-permute-start | bytes 1572872 | tf_op jit(solution)/shard_map/ppermute | solution.py:165
  569.7 104.8 %reduce-scatter.13.cloned.1.call-start = ((), (), s32[]{:S(2)}) async-start(), calls=%async_computation.12 | async-start | bytes 3276800 | tf_op jit(solution)/shard_map/reduce_scatter | solution.py:192
  571.2 26.5 %collective-permute-start.28 = (bf16[256,3840]{1,0:T(8,128)(2,1)S(1)}, bf16[256,3840]{1,0:T(8,128)(2,1)S(1)}, u32[]{:S(2)}, u32[]{:S(2)}) collective-permute-start(bf16[256,3840]{1,0:T(8,128)(2,1)S(1)} %constant_dynamic-update-slice_fusion), channel_id=1, source_target_pairs={{1,4},{3,6},{4,1},{6,3},{9,12},{11,14},{12,9},{14,11},{17,20},{19,... | collective-permute-start | bytes 5898248 | tf_op jit(solution)/shard_map/ppermute | solution.py:168
  578.2 20.9 %collective-permute-start.29 = (bf16[1024,1280]{1,0:T(8,128)(2,1)S(1)}, bf16[1024,1280]{1,0:T(8,128)(2,1)S(1)}, u32[]{:S(2)}, u32[]{:S(2)}) collective-permute-start(bf16[1024,1280]{1,0:T(8,128)(2,1)S(1)} %convolution_convert_fusion.2), channel_id=1, source_target_pairs={{0,1},{1,0},{2,3},{3,2},{4,5},{5,4},{6,7},{7,6},{8,9},{9,8},{10,11... | collective-permute-start | bytes 7864328 | tf_op jit(solution)/shard_map/ppermute | solution.py:175
  615.3 36.9 %collective-permute-start.33 = (bf16[1024,2560]{1,0:T(8,128)(2,1)}, bf16[1024,2560]{1,0:T(8,128)(2,1)}, u32[]{:S(2)}, u32[]{:S(2)}) collective-permute-start(bf16[1024,2560]{1,0:T(8,128)(2,1)} %convolution_convert_fusion), channel_id=1, source_target_pairs={{0,1},{1,0},{2,3},{3,2},{4,5},{5,4},{6,7},{7,6},{8,9},{9,8},{10,11... | collective-permute-start | bytes 15728648 | tf_op jit(solution)/shard_map/ppermute | solution.py:175
  623.8 164.0 %reduce-scatter.15.cloned.1.call-start = ((), (), s32[]{:S(2)}) async-start(), calls=%async_computation.13 | async-start | bytes 6553600 | tf_op jit(solution)/shard_map/reduce_scatter | solution.py:192
  627.7 18.9 %collective-permute-start.40 = (bf16[256,256]{0,1:T(8,128)(2,1)S(1)}, bf16[256,256]{0,1:T(8,128)(2,1)S(1)}, u32[]{:S(2)}, u32[]{:S(2)}) collective-permute-start(bf16[256,256]{0,1:T(8,128)(2,1)S(1)} %slice.777), channel_id=1, source_target_pairs={{0,3},{1,7},{2,1},{3,5},{4,2},{5,6},{6,0},{7,4},{8,11},{9,15},{10,... | collective-permute-start | bytes 393224 | tf_op jit(solution)/shard_map/ppermute | solution.py:172
  629.9 17.5 %collective-permute-start.39 = (bf16[256,256]{0,1:T(8,128)(2,1)S(1)}, bf16[256,256]{0,1:T(8,128)(2,1)S(1)}, u32[]{:S(2)}, u32[]{:S(2)}) collective-permute-start(bf16[256,256]{0,1:T(8,128)(2,1)S(1)} %slice.777), channel_id=1, source_target_pairs={{0,2},{1,6},{2,0},{3,4},{4,3},{5,7},{6,1},{7,5},{8,10},{9,14},{10,... | collective-permute-start | bytes 393224 | tf_op jit(solution)/shard_map/ppermute | solution.py:172
  630.3 18.2 %collective-permute-start.38 = (bf16[256,256]{0,1:T(8,128)(2,1)S(1)}, bf16[256,256]{0,1:T(8,128)(2,1)S(1)}, u32[]{:S(2)}, u32[]{:S(2)}) collective-permute-start(bf16[256,256]{0,1:T(8,128)(2,1)S(1)} %slice.777), channel_id=1, source_target_pairs={{0,1},{1,5},{2,3},{3,7},{4,0},{5,4},{6,2},{7,6},{8,9},{9,13},{10,1... | collective-permute-start | bytes 393224 | tf_op jit(solution)/shard_map/ppermute | solution.py:172
  630.3 19.8 %collective-permute-start.37 = (bf16[256,896]{0,1:T(8,128)(2,1)}, bf16[256,896]{0,1:T(8,128)(2,1)S(1)}, u32[]{:S(2)}, u32[]{:S(2)}) collective-permute-start(bf16[256,896]{0,1:T(8,128)(2,1)} %reduce-scatter.11.cloned.1.call-done), channel_id=1, source_target_pairs={{1,4},{3,6},{4,1},{6,3},{9,12},{11,14},{12,9},{14,11},{17,20},{19,... | collective-permute-start | bytes 1376264 | tf_op jit(solution)/shard_map/ppermute | solution.py:168
  646.6 15.2 %collective-permute-start.32 = (bf16[128,2048]{1,0:T(8,128)(2,1)}, bf16[128,2048]{1,0:T(8,128)(2,1)}, u32[]{:S(2)}, u32[]{:S(2)}) collective-permute-start(bf16[128,2048]{1,0:T(8,128)(2,1)} %get-tuple-element.247), channel_id=1, source_target_pairs={{0,6},{1,7},{2,4},{3,5},{4,2},{5,3},{6,0},{7,1},{8,14},{9,15},{10,... | collective-permute-start | bytes 1572872 | tf_op jit(solution)/shard_map/ppermute | solution.py:165
  647.3 24.8 %collective-permute-start.30 = (bf16[128,2048]{1,0:T(8,128)(2,1)}, bf16[128,2048]{1,0:T(8,128)(2,1)}, u32[]{:S(2)}, u32[]{:S(2)}) collective-permute-start(bf16[128,2048]{1,0:T(8,128)(2,1)} %get-tuple-element.248), channel_id=1, source_target_pairs={{0,2},{1,3},{2,0},{3,1},{4,6},{5,7},{6,4},{7,5},{8,10},{9,11},{10,... | collective-permute-start | bytes 1572872 | tf_op jit(solution)/shard_map/ppermute | solution.py:165
  648.6 23.6 %collective-permute-start.31 = (bf16[128,2048]{1,0:T(8,128)(2,1)}, bf16[128,2048]{1,0:T(8,128)(2,1)}, u32[]{:S(2)}, u32[]{:S(2)}) collective-permute-start(bf16[128,2048]{1,0:T(8,128)(2,1)} %get-tuple-element.249), channel_id=1, source_target_pairs={{0,4},{1,5},{2,6},{3,7},{4,0},{5,1},{6,2},{7,3},{8,12},{9,13},{10,... | collective-permute-start | bytes 1572872 | tf_op jit(solution)/shard_map/ppermute | solution.py:165
  678.1 13.8 %collective-permute-start.36 = (bf16[128,2048]{1,0:T(8,128)(2,1)}, bf16[128,2048]{1,0:T(8,128)(2,1)S(1)}, u32[]{:S(2)}, u32[]{:S(2)}) collective-permute-start(bf16[128,2048]{1,0:T(8,128)(2,1)} %get-tuple-element.225), channel_id=1, source_target_pairs={{0,6},{1,7},{2,4},{3,5},{4,2},{5,3},{6,0},{7,1},{8,14},{9,15},{10,... | collective-permute-start | bytes 1572872 | tf_op jit(solution)/shard_map/ppermute | solution.py:165
  680.2 23.0 %collective-permute-start.35 = (bf16[128,2048]{1,0:T(8,128)(2,1)}, bf16[128,2048]{1,0:T(8,128)(2,1)S(1)}, u32[]{:S(2)}, u32[]{:S(2)}) collective-permute-start(bf16[128,2048]{1,0:T(8,128)(2,1)} %get-tuple-element.225), channel_id=1, source_target_pairs={{0,4},{1,5},{2,6},{3,7},{4,0},{5,1},{6,2},{7,3},{8,12},{9,13},{10,... | collective-permute-start | bytes 1572872 | tf_op jit(solution)/shard_map/ppermute | solution.py:165
  680.5 23.9 %collective-permute-start.34 = (bf16[128,2048]{1,0:T(8,128)(2,1)}, bf16[128,2048]{1,0:T(8,128)(2,1)}, u32[]{:S(2)}, u32[]{:S(2)}) collective-permute-start(bf16[128,2048]{1,0:T(8,128)(2,1)} %get-tuple-element.225), channel_id=1, source_target_pairs={{0,2},{1,3},{2,0},{3,1},{4,6},{5,7},{6,4},{7,5},{8,10},{9,11},{10,... | collective-permute-start | bytes 1572872 | tf_op jit(solution)/shard_map/ppermute | solution.py:165
  681.5 144.5 %reduce-scatter.17.cloned.1.call-start = ((), (), s32[]{:S(2)}) async-start(), calls=%async_computation.14 | async-start | bytes 2293760 | tf_op jit(solution)/shard_map/reduce_scatter | solution.py:192
  720.1 8.7 %collective-permute-start.45 = (bf16[1024,576]{0,1:T(8,128)(2,1)S(1)}, bf16[1024,576]{0,1:T(8,128)(2,1)S(1)}, u32[]{:S(2)}, u32[]{:S(2)}) collective-permute-start(bf16[1024,576]{0,1:T(8,128)(2,1)S(1)} %convolution_convert_fusion.4), channel_id=1, source_target_pairs={{0,1},{1,0},{2,3},{3,2},{4,5},{5,4},{6,7},{7,6},{8,9},{9,8},{10,11... | collective-permute-start | bytes 3538952 | tf_op jit(solution)/shard_map/ppermute | solution.py:175
  724.7 14.0 %collective-permute-start.43 = (bf16[128,2048]{1,0:T(8,128)(2,1)S(1)}, bf16[128,2048]{1,0:T(8,128)(2,1)S(1)}, u32[]{:S(2)}, u32[]{:S(2)}) collective-permute-start(bf16[128,2048]{1,0:T(8,128)(2,1)S(1)} %get-tuple-element.244), channel_id=1, source_target_pairs={{0,6},{1,7},{2,4},{3,5},{4,2},{5,3},{6,0},{7,1},{8,14},{9,15},{10,... | collective-permute-start | bytes 1572872 | tf_op jit(solution)/shard_map/ppermute | solution.py:165
  726.8 24.0 %collective-permute-start.41 = (bf16[128,2048]{1,0:T(8,128)(2,1)S(1)}, bf16[128,2048]{1,0:T(8,128)(2,1)S(1)}, u32[]{:S(2)}, u32[]{:S(2)}) collective-permute-start(bf16[128,2048]{1,0:T(8,128)(2,1)S(1)} %get-tuple-element.245), channel_id=1, source_target_pairs={{0,2},{1,3},{2,0},{3,1},{4,6},{5,7},{6,4},{7,5},{8,10},{9,11},{10,... | collective-permute-start | bytes 1572872 | tf_op jit(solution)/shard_map/ppermute | solution.py:165
  727.1 23.7 %collective-permute-start.42 = (bf16[128,2048]{1,0:T(8,128)(2,1)S(1)}, bf16[128,2048]{1,0:T(8,128)(2,1)S(1)}, u32[]{:S(2)}, u32[]{:S(2)}) collective-permute-start(bf16[128,2048]{1,0:T(8,128)(2,1)S(1)} %get-tuple-element.246), channel_id=1, source_target_pairs={{0,4},{1,5},{2,6},{3,7},{4,0},{5,1},{6,2},{7,3},{8,12},{9,13},{10,... | collective-permute-start | bytes 1572872 | tf_op jit(solution)/shard_map/ppermute | solution.py:165
  756.3 7.7 collective-permute-start.55
  761.4 17.1 %collective-permute-start.49 = (bf16[128,2048]{1,0:T(8,128)(2,1)}, bf16[128,2048]{1,0:T(8,128)(2,1)}, u32[]{:S(2)}, u32[]{:S(2)}) collective-permute-start(bf16[128,2048]{1,0:T(8,128)(2,1)} %get-tuple-element.241), channel_id=1, source_target_pairs={{0,6},{1,7},{2,4},{3,5},{4,2},{5,3},{6,0},{7,1},{8,14},{9,15},{10,... | collective-permute-start | bytes 1572872 | tf_op jit(solution)/shard_map/ppermute | solution.py:165
  762.6 21.6 %collective-permute-start.48 = (bf16[128,2048]{1,0:T(8,128)(2,1)}, bf16[128,2048]{1,0:T(8,128)(2,1)}, u32[]{:S(2)}, u32[]{:S(2)}) collective-permute-start(bf16[128,2048]{1,0:T(8,128)(2,1)} %get-tuple-element.242), channel_id=1, source_target_pairs={{0,4},{1,5},{2,6},{3,7},{4,0},{5,1},{6,2},{7,3},{8,12},{9,13},{10,... | collective-permute-start | bytes 1572872 | tf_op jit(solution)/shard_map/ppermute | solution.py:165
  762.6 25.1 %collective-permute-start.47 = (bf16[128,2048]{1,0:T(8,128)(2,1)}, bf16[128,2048]{1,0:T(8,128)(2,1)}, u32[]{:S(2)}, u32[]{:S(2)}) collective-permute-start(bf16[128,2048]{1,0:T(8,128)(2,1)} %get-tuple-element.243), channel_id=1, source_target_pairs={{0,2},{1,3},{2,0},{3,1},{4,6},{5,7},{6,4},{7,5},{8,10},{9,11},{10,... | collective-permute-start | bytes 1572872 | tf_op jit(solution)/shard_map/ppermute | solution.py:165
  764.9 8.2 collective-permute-start.56
  772.6 28.8 %collective-permute-start.52 = (bf16[128,2048]{1,0:T(8,128)(2,1)}, bf16[128,2048]{1,0:T(8,128)(2,1)}, u32[]{:S(2)}, u32[]{:S(2)}) collective-permute-start(bf16[128,2048]{1,0:T(8,128)(2,1)} %select_n.426), channel_id=1, source_target_pairs={{0,2},{1,3},{2,0},{3,1},{4,6},{5,7},{6,4},{7,5},{8,10},{9,11},{10,... | collective-permute-start | bytes 1572872 | tf_op jit(solution)/shard_map/ppermute | solution.py:165
  776.6 24.2 %collective-permute-start.58 = (f32[2,4224]{1,0:T(2,128)S(1)}, f32[2,4224]{1,0:T(2,128)S(1)}, u32[]{:S(2)}, u32[]{:S(2)}) collective-permute-start(f32[2,4224]{1,0:T(2,128)S(1)} %add.585), channel_id=1, source_target_pairs={{0,16},{8,24},{16,0},{24,8},{1,17},{9,25},{17,1},{25,9},{2,18},{10... | collective-permute-start | bytes 101384 | tf_op jit(solution)/shard_map/ppermute | solution.py:182
  791.2 26.5 %collective-permute-start.46 = (bf16[256,3840]{1,0:T(8,128)(2,1)}, bf16[256,3840]{1,0:T(8,128)(2,1)}, u32[]{:S(2)}, u32[]{:S(2)}) collective-permute-start(bf16[256,3840]{1,0:T(8,128)(2,1)} %constant_dynamic-update-slice_fusion.2), channel_id=1, source_target_pairs={{1,4},{3,6},{4,1},{6,3},{9,12},{11,14},{12,9},{14,11},{17,20},{19,... | collective-permute-start | bytes 5898248 | tf_op jit(solution)/shard_map/ppermute | solution.py:168
  798.4 14.0 %collective-permute-start.50 = (bf16[128,2048]{1,0:T(8,128)(2,1)}, bf16[128,2048]{1,0:T(8,128)(2,1)S(1)}, u32[]{:S(2)}, u32[]{:S(2)}) collective-permute-start(bf16[128,2048]{1,0:T(8,128)(2,1)} %select_n.423), channel_id=1, source_target_pairs={{0,2},{1,3},{2,0},{3,1},{4,6},{5,7},{6,4},{7,5},{8,10},{9,11},{10,... | collective-permute-start | bytes 1572872 | tf_op jit(solution)/shard_map/ppermute | solution.py:165
  803.0 18.3 %collective-permute-start.53 = (bf16[256,2048]{1,0:T(8,128)(2,1)S(1)}, bf16[256,2048]{1,0:T(8,128)(2,1)S(1)}, u32[]{:S(2)}, u32[]{:S(2)}) collective-permute-start(bf16[256,2048]{1,0:T(8,128)(2,1)S(1)} %maximum_select_fusion.8), channel_id=1, source_target_pairs={{0,1},{1,0},{2,3},{3,2},{4,5},{5,4},{6,7},{7,6},{8,9},{9,8},{10,11... | collective-permute-start | bytes 3145736 | tf_op jit(solution)/shard_map/ppermute | solution.py:175
  814.0 8.3 collective-permute-start.51
  827.0 19.7 %collective-permute-start.62 = (bf16[256,256]{0,1:T(8,128)(2,1)S(1)}, bf16[256,256]{0,1:T(8,128)(2,1)S(1)}, u32[]{:S(2)}, u32[]{:S(2)}) collective-permute-start(bf16[256,256]{0,1:T(8,128)(2,1)S(1)} %slice.821), channel_id=1, source_target_pairs={{0,3},{1,7},{2,1},{3,5},{4,2},{5,6},{6,0},{7,4},{8,11},{9,15},{10,... | collective-permute-start | bytes 393224 | tf_op jit(solution)/shard_map/ppermute | solution.py:172
  829.2 17.6 %collective-permute-start.61 = (bf16[256,256]{0,1:T(8,128)(2,1)S(1)}, bf16[256,256]{0,1:T(8,128)(2,1)S(1)}, u32[]{:S(2)}, u32[]{:S(2)}) collective-permute-start(bf16[256,256]{0,1:T(8,128)(2,1)S(1)} %slice.821), channel_id=1, source_target_pairs={{0,2},{1,6},{2,0},{3,4},{4,3},{5,7},{6,1},{7,5},{8,10},{9,14},{10,... | collective-permute-start | bytes 393224 | tf_op jit(solution)/shard_map/ppermute | solution.py:172
  830.5 16.3 %collective-permute-start.60 = (bf16[256,256]{0,1:T(8,128)(2,1)S(1)}, bf16[256,256]{0,1:T(8,128)(2,1)S(1)}, u32[]{:S(2)}, u32[]{:S(2)}) collective-permute-start(bf16[256,256]{0,1:T(8,128)(2,1)S(1)} %slice.821), channel_id=1, source_target_pairs={{0,1},{1,5},{2,3},{3,7},{4,0},{5,4},{6,2},{7,6},{8,9},{9,13},{10,1... | collective-permute-start | bytes 393224 | tf_op jit(solution)/shard_map/ppermute | solution.py:172
  830.5 16.3 %collective-permute-start.59 = (bf16[256,896]{0,1:T(8,128)(2,1)}, bf16[256,896]{0,1:T(8,128)(2,1)}, u32[]{:S(2)}, u32[]{:S(2)}) collective-permute-start(bf16[256,896]{0,1:T(8,128)(2,1)} %reduce-scatter.17.cloned.1.call-done), channel_id=1, source_target_pairs={{1,4},{3,6},{4,1},{6,3},{9,12},{11,14},{12,9},{14,11},{17,20},{19,... | collective-permute-start | bytes 1376264 | tf_op jit(solution)/shard_map/ppermute | solution.py:168
  (164 other events, 1901.1 us)
Sparse Core Ops, SparseCore 0:
  29.1 73.5 all-gather.3
  104.9 139.3 all-gather.5
  246.5 139.2 all-gather.7
  414.9 49.8 reduce-scatter.6
  467.0 93.6 reduce-scatter.8
  569.8 38.0 reduce-scatter.10
  623.9 50.5 reduce-scatter.12
  681.0 94.4 reduce-scatter.14
  787.9 38.1 reduce-scatter.16

commit v4 on v3

--- a/solution.py
+++ b/solution.py
@@ -485,8 +485,8 @@
         return query, keys, values, out
 
     def scatter_next(layer, member, term):
-        if last:
-            at, part = last[-1]
+        if len(last) > 1:
+            at, part = last[-2]
             term, results[at][part] = lax.optimization_barrier((term, results[at][part]))
         results[layer][member] = plan.scatter(term)
         last.append((layer, member))
@@ -540,8 +540,9 @@
             summed_mid, term_gu = plan.gather_sum(mid_terms, term_gu)
         else:
             scatter_next(layer, 2, term_d)
-            summed_mid, (results[layer][2], term_gu) = plan.gather_sum(
-                mid_terms, (results[layer][2], term_gu)
+            summed_mid, term_gu = plan.gather_sum(mid_terms, term_gu)
+            summed_mid, results[layer][2] = lax.optimization_barrier(
+                (summed_mid, results[layer][2])
             )
         scatter_next(layer, 1, term_gu)
         grad_g_ffn = jnp.sum(summed_mid * middle * scale_mid, axis=0)

time: 867 us -> 854 us (0.985)
  waiting for transfers between devices: 297 us -> 284 us
  local copies, waits for them, and re-layouts: 58 us -> 66.8 us
    reduce_scatter x6, waiting for transfers between devices: 32 us -> 10.1 us  [scatter(): return lax.psum_scatter(term, 'dp', scatter_dimension=0, tiled=True)]
    ppermute x28, waiting for transfers between devices: 157 us -> 168 us  [peer(): return lax.ppermute(value, ('ctx', 'tensor'), self.peers[j])]
    unnamed x328 -> x330, local copies, waits for them, and re-layouts: 19.7 us -> 23.5 us
  transfers between devices with their start and end apart: 72 -> 72, of which waited for: 35 -> 35; matrix products, arithmetic and copies ran while one was open for 32% -> 33% of each run, Pallas kernels for 17% -> 17%
where the time goes in v4:
time: 854 us; the launch traced here: 846 us
  waiting for transfers between devices  284 us (33%)
  matrix products  166 us (19%)
  Pallas kernels  148 us (17%)
  other arithmetic  88.7 us (10%)
  starting transfers between devices  75.1 us (9%)
  local copies, waits for them, and re-layouts  66.8 us (8%)
  between operations  17.8 us (2%)
    ppermute x28, waiting for transfers between devices, peer(): return lax.ppermute(value, ('ctx', 'tensor'), self.peers[j])  168 us
    dot_general x52, matrix products, product(): lax.dot_general(left_side, right_side, (contract, ((), ())), preferred_el...  151 us
    pallas_call x3, Pallas kernels, join(): pl.pallas_call(join_kernel, out_shape=(jax.ShapeDtypeStruct((rows, width)...  148 us
    ppermute x7, waiting for transfers between devices, swap(): moved = lax.ppermute(value, ('ctx', 'tensor'), self.swap_pairs)  63.6 us
    all_gather x3, waiting for transfers between devices, local(): owned.append(lax.all_gather(shard, 'dp', axis=0, tiled=True))  33.2 us
    ppermute x7, starting transfers between devices, swap(): moved = lax.ppermute(value, ('ctx', 'tensor'), self.swap_pairs)  28.5 us
    unnamed x330, local copies, waits for them, and re-layouts  23.5 us
    ppermute x28, starting transfers between devices, peer(): return lax.ppermute(value, ('ctx', 'tensor'), self.peers[j])  23 us
  transfers between devices with their start and end apart: 72, of which 35 were waited for; matrix products, arithmetic and copies ran while one was open for 33% of the time, Pallas kernels for 17%

profile of v4, /device:TPU:1, one launch (start us, length us, event | category | flops | bytes accessed | tf_op | source)
XLA Modules:
  0.0 846.1 jit_solution(5647110457421374687)
XLA Ops:
  12.4 4.5 collective-permute-start
  18.1 9.9 %collective-permute-done = bf16[256,1792]{0,1:T(8,128)(2,1)S(1)} collective-permute-done((bf16[256,1792]{0,1:T(8,128)(2,1)S(1)}, bf16[256,1792]{0,1:T(8,128)(2,1)S(1)}, u32[]{:S(2)}, u32[]{:S(2)}) %collective-permute-start) | collective-permute-done | bytes 917536 | tf_op jit(solution)/shard_map/ppermute | solution.py:168
  31.9 2.8 copy.65
  39.9 3.6 collective-permute-start.8
  46.8 3.9 copy.70
  55.6 22.0 %collective-permute-done.8 = bf16[256,3840]{1,0:T(8,128)(2,1)} collective-permute-done((bf16[256,3840]{1,0:T(8,128)(2,1)}, bf16[256,3840]{1,0:T(8,128)(2,1)}, u32[]{:S(2)}, u32[]{:S(2)}) %collective-permute-start.8) | collective-permute-done | bytes 1966112 | tf_op jit(solution)/shard_map/ppermute | solution.py:168
  77.7 3.3 broadcast_select_fusion.3
  81.2 3.3 collective-permute-start.3
  96.0 7.5 collective-permute-start.9
  107.7 9.7 %collective-permute-done.6 = bf16[256,2048]{1,0:T(8,128)(2,1)} collective-permute-done((bf16[256,2048]{1,0:T(8,128)(2,1)}, bf16[256,2048]{1,0:T(8,128)(2,1)}, u32[]{:S(2)}, u32[]{:S(2)}) %collective-permute-start.6) | collective-permute-done | bytes 1048608 | tf_op jit(solution)/shard_map/ppermute | solution.py:165
  117.4 3.3 maximum_select_fusion
  122.6 18.7 %collective-permute-done.9 = bf16[256,3840]{1,0:T(8,128)(2,1)} collective-permute-done((bf16[256,3840]{1,0:T(8,128)(2,1)}, bf16[256,3840]{1,0:T(8,128)(2,1)}, u32[]{:S(2)}, u32[]{:S(2)}) %collective-permute-start.9) | collective-permute-done | bytes 1966112 | tf_op jit(solution)/shard_map/ppermute | solution.py:168
  141.3 3.0 broadcast_select_fusion.2
  160.6 50.3 %join.3 = (f32[128,2048]{1,0:T(8,128)S(1)}, bf16[512,2048]{1,0:T(8,128)(2,1)S(1)}) custom-call(bf16[512,2048]{1,0:T(8,128)(2,1)S(1)} %pad_maximum_fusion.2.terms, f32[128,2048]{1,0:T(8,128)S(1)} %slice.859.state, f32[1,2048]{1,0:T(1,128)S(1)} %get-tuple-element.333.gain), custom_call_target="tpu_custom_call" | custom-call | flops 1000 | bytes 1000 | tf_op jit(solution)/shard_map/join/pallas_call | solution.py:112
  212.3 32.1 %all-gather.6.cloned.1.call-done = bf16[1024,3840]{1,0:T(8,128)(2,1)} async-done(((bf16[256,3840]{1,0:T(8,128)(2,1)}), bf16[1024,3840]{1,0:T(8,128)(2,1)}) %all-gather.6.cloned.1.call-update) | async-done | bytes 7864336 | tf_op jit(solution)/shard_map/all_gather | solution.py:328
  245.1 3.7 fusion.21
  248.8 3.3 fusion.24
  252.1 5.1 collective-permute-done.10
  257.2 3.5 convolution_add_fusion.5
  260.6 5.8 multiply_convert_fusion.8
  266.4 3.8 fusion.61
  270.2 3.3 fusion.67
  273.7 48.9 %join.4 = (f32[128,2048]{1,0:T(8,128)S(1)}, bf16[512,2048]{1,0:T(8,128)(2,1)S(1)}) custom-call(bf16[512,2048]{1,0:T(8,128)(2,1)S(1)} %pad_maximum_fusion.3.terms, f32[128,2048]{1,0:T(8,128)S(1)} %get-tuple-element.101.state, f32[1,2048]{1,0:T(1,128)S(1)} %get-tuple-element.334.gain), custom_call_target="tpu_custom_call" | custom-call | flops 1000 | bytes 1000 | tf_op jit(solution)/shard_map/join/pallas_call | solution.py:112
  335.0 48.3 %join.5 = (f32[128,2048]{1,0:T(8,128)S(1)}, bf16[512,2048]{1,0:T(8,128)(2,1)S(1)}) custom-call(bf16[512,2048]{1,0:T(8,128)(2,1)S(1)} %pad_maximum_fusion.4.terms, f32[128,2048]{1,0:T(8,128)S(1)} %get-tuple-element.103.state, f32[1,2048]{1,0:T(1,128)S(1)} %get-tuple-element.332.gain), custom_call_target="tpu_custom_call" | custom-call | flops 1000 | bytes 1000 | tf_op jit(solution)/shard_map/join/pallas_call | solution.py:112
  386.3 3.7 fusion.17
  390.0 3.4 fusion.19
  393.4 3.3 fusion.42
  401.6 3.0 multiply_convert_fusion.3
  406.7 4.8 convolution_convert_fusion.1
  411.6 3.1 add_convert_fusion.3
  415.4 6.3 fusion.49
  421.7 5.8 fusion.55
  431.7 6.6 add_convert_fusion.1
  438.3 5.1 collective-permute-done.14
  443.4 11.9 %collective-permute-done.12 = bf16[128,2048]{1,0:T(8,128)(2,1)} collective-permute-done((bf16[128,2048]{1,0:T(8,128)(2,1)}, bf16[128,2048]{1,0:T(8,128)(2,1)}, u32[]{:S(2)}, u32[]{:S(2)}) %collective-permute-start.12) | collective-permute-done | bytes 524320 | tf_op jit(solution)/shard_map/ppermute | solution.py:165
  462.4 11.0 %collective-permute-done.18 = bf16[128,2048]{1,0:T(8,128)(2,1)S(1)} collective-permute-done((bf16[128,2048]{1,0:T(8,128)(2,1)S(1)}, bf16[128,2048]{1,0:T(8,128)(2,1)S(1)}, u32[]{:S(2)}, u32[]{:S(2)}) %collective-permute-start.18) | collective-permute-done | bytes 524320 | tf_op jit(solution)/shard_map/ppermute | solution.py:165
  473.4 11.4 %collective-permute-done.17 = bf16[128,2048]{1,0:T(8,128)(2,1)S(1)} collective-permute-done((bf16[128,2048]{1,0:T(8,128)(2,1)S(1)}, bf16[128,2048]{1,0:T(8,128)(2,1)S(1)}, u32[]{:S(2)}, u32[]{:S(2)}) %collective-permute-start.17) | collective-permute-done | bytes 524320 | tf_op jit(solution)/shard_map/ppermute | solution.py:165
  509.8 9.6 %collective-permute-done.21 = bf16[128,2048]{1,0:T(8,128)(2,1)S(1)} collective-permute-done((bf16[128,2048]{1,0:T(8,128)(2,1)S(1)}, bf16[128,2048]{1,0:T(8,128)(2,1)S(1)}, u32[]{:S(2)}, u32[]{:S(2)}) %collective-permute-start.21) | collective-permute-done | bytes 524320 | tf_op jit(solution)/shard_map/ppermute | solution.py:165
  519.4 12.1 %collective-permute-done.19 = bf16[128,2048]{1,0:T(8,128)(2,1)S(1)} collective-permute-done((bf16[128,2048]{1,0:T(8,128)(2,1)S(1)}, bf16[128,2048]{1,0:T(8,128)(2,1)S(1)}, u32[]{:S(2)}, u32[]{:S(2)}) %collective-permute-start.19) | collective-permute-done | bytes 524320 | tf_op jit(solution)/shard_map/ppermute | solution.py:165
  537.8 10.2 %collective-permute-done.26 = bf16[128,2048]{1,0:T(8,128)(2,1)} collective-permute-done((bf16[128,2048]{1,0:T(8,128)(2,1)}, bf16[128,2048]{1,0:T(8,128)(2,1)}, u32[]{:S(2)}, u32[]{:S(2)}) %collective-permute-start.26) | collective-permute-done | bytes 524320 | tf_op jit(solution)/shard_map/ppermute | solution.py:165
  548.0 11.3 %collective-permute-done.25 = bf16[128,2048]{1,0:T(8,128)(2,1)} collective-permute-done((bf16[128,2048]{1,0:T(8,128)(2,1)}, bf16[128,2048]{1,0:T(8,128)(2,1)}, u32[]{:S(2)}, u32[]{:S(2)}) %collective-permute-start.25) | collective-permute-done | bytes 524320 | tf_op jit(solution)/shard_map/ppermute | solution.py:165
  562.2 3.7 collective-permute-start.28
  569.3 3.5 fusion.44
  572.8 4.0 multiply_convert_fusion.5
  578.5 10.1 %collective-permute-done.28 = bf16[256,3840]{1,0:T(8,128)(2,1)S(1)} collective-permute-done((bf16[256,3840]{1,0:T(8,128)(2,1)S(1)}, bf16[256,3840]{1,0:T(8,128)(2,1)S(1)}, u32[]{:S(2)}, u32[]{:S(2)}) %collective-permute-start.28) | collective-permute-done | bytes 1966112 | tf_op jit(solution)/shard_map/ppermute | solution.py:168
  590.1 3.1 add_convert_fusion.2
  593.2 9.3 %reduce-scatter.11.cloned.1.call-done = bf16[256,896]{0,1:T(8,128)(2,1)} async-done(((bf16[1024,896]{0,1:T(8,128)(2,1)}), bf16[256,896]{0,1:T(8,128)(2,1)}) %reduce-scatter.11.cloned.1.call-update) | async-done | bytes 458768 | tf_op jit(solution)/shard_map/reduce_scatter | solution.py:192
  602.5 7.2 convolution_convert_fusion
  611.1 3.8 fusion.64
  614.9 3.7 fusion.70
  620.4 6.4 fusion.52
  626.8 5.8 fusion.58
  636.8 6.5 add_convert_fusion
  643.2 5.7 collective-permute-done.32
  649.0 11.5 %collective-permute-done.30 = bf16[128,2048]{1,0:T(8,128)(2,1)S(1)} collective-permute-done((bf16[128,2048]{1,0:T(8,128)(2,1)}, bf16[128,2048]{1,0:T(8,128)(2,1)S(1)}, u32[]{:S(2)}, u32[]{:S(2)}) %collective-permute-start.30) | collective-permute-done | bytes 524320 | tf_op jit(solution)/shard_map/ppermute | solution.py:165
  679.8 7.0 collective-permute-done.36
  686.8 11.1 %collective-permute-done.35 = bf16[128,2048]{1,0:T(8,128)(2,1)S(1)} collective-permute-done((bf16[128,2048]{1,0:T(8,128)(2,1)S(1)}, bf16[128,2048]{1,0:T(8,128)(2,1)S(1)}, u32[]{:S(2)}, u32[]{:S(2)}) %collective-permute-start.35) | collective-permute-done | bytes 524320 | tf_op jit(solution)/shard_map/ppermute | solution.py:165
  723.8 8.1 collective-permute-done.43
  731.8 10.8 %collective-permute-done.41 = bf16[128,2048]{1,0:T(8,128)(2,1)S(1)} collective-permute-done((bf16[128,2048]{1,0:T(8,128)(2,1)S(1)}, bf16[128,2048]{1,0:T(8,128)(2,1)S(1)}, u32[]{:S(2)}, u32[]{:S(2)}) %collective-permute-start.41) | collective-permute-done | bytes 524320 | tf_op jit(solution)/shard_map/ppermute | solution.py:165
  766.8 7.7 collective-permute-done.48
  791.4 9.6 %collective-permute-done.50 = bf16[128,2048]{1,0:T(8,128)(2,1)S(1)} collective-permute-done((bf16[128,2048]{1,0:T(8,128)(2,1)}, bf16[128,2048]{1,0:T(8,128)(2,1)S(1)}, u32[]{:S(2)}, u32[]{:S(2)}) %collective-permute-start.50) | collective-permute-done | bytes 524320 | tf_op jit(solution)/shard_map/ppermute | solution.py:165
  803.4 2.8 collective-permute-done.46
  814.0 3.8 collective-permute-start.59
  825.8 3.2 maximum_select_fusion.1
  (714 shorter events, 253.3 us)
Async XLA Ops:
  7.2 96.3 %all-gather.4.cloned.1.call-start = ((), (), s32[]{:S(2)}) async-start(), calls=%async_computation.6 | async-start | bytes 4587520 | tf_op jit(solution)/shard_map/all_gather | solution.py:328
  12.4 15.6 %collective-permute-start = (bf16[256,1792]{0,1:T(8,128)(2,1)S(1)}, bf16[256,1792]{0,1:T(8,128)(2,1)S(1)}, u32[]{:S(2)}, u32[]{:S(2)}) collective-permute-start(bf16[256,1792]{0,1:T(8,128)(2,1)S(1)} %bitcast_dynamic-update-slice_fusion), channel_id=1, source_target_pairs={{1,4},{3,6},{4,1},{6,3},{9,12},{11,14},{12,9},{14,11},{17,20},{19,... | collective-permute-start | bytes 2752520 | tf_op jit(solution)/shard_map/ppermute | solution.py:168
  29.0 215.3 %all-gather.6.cloned.1.call-start = ((), (), s32[]{:S(2)}) async-start(), calls=%async_computation.7 | async-start | bytes 9830400 | tf_op jit(solution)/shard_map/all_gather | solution.py:328
  30.4 50.7 %collective-permute-start.2 = (bf16[2,528]{1,0:T(2,128)(2,1)S(1)}, bf16[2,528]{1,0:T(2,128)(2,1)S(1)}, u32[]{:S(2)}, u32[]{:S(2)}) collective-permute-start(bf16[2,528]{1,0:T(2,128)(2,1)S(1)} %copy-done.122), channel_id=1, source_target_pairs={{0,4},{4,0},{1,5},{5,1},{2,6},{6,2},{3,7},{7,3},{8,12},{12,8},{9,1... | collective-permute-start | bytes 6344 | tf_op jit(solution)/shard_map/ppermute | solution.py:338
  39.9 37.8 %collective-permute-start.8 = (bf16[256,3840]{1,0:T(8,128)(2,1)}, bf16[256,3840]{1,0:T(8,128)(2,1)}, u32[]{:S(2)}, u32[]{:S(2)}) collective-permute-start(bf16[256,3840]{1,0:T(8,128)(2,1)} %pad_maximum_fusion.10), channel_id=1, source_target_pairs={{1,4},{3,6},{4,1},{6,3},{9,12},{11,14},{12,9},{14,11},{17,20},{19,... | collective-permute-start | bytes 5898248 | tf_op jit(solution)/shard_map/ppermute | solution.py:168
  46.7 57.0 %collective-permute-start.1 = (bf16[256,2048]{1,0:T(8,128)(2,1)S(1)}, bf16[256,2048]{1,0:T(8,128)(2,1)S(1)}, u32[]{:S(2)}, u32[]{:S(2)}) collective-permute-start(bf16[256,2048]{1,0:T(8,128)(2,1)S(1)} %maximum_select_fusion.4), channel_id=1, source_target_pairs={{0,4},{1,5},{2,6},{3,7},{4,0},{5,1},{6,2},{7,3},{8,12},{9,13},{10,... | collective-permute-start | bytes 3145736 | tf_op jit(solution)/shard_map/ppermute | solution.py:165
  81.0 304.8 %all-gather.8.cloned.1.call-start = ((), (), s32[]{:S(2)}) async-start(), calls=%async_computation.8 | async-start | bytes 9830400 | tf_op jit(solution)/shard_map/all_gather | solution.py:328
  94.7 22.7 %collective-permute-start.6 = (bf16[256,2048]{1,0:T(8,128)(2,1)}, bf16[256,2048]{1,0:T(8,128)(2,1)}, u32[]{:S(2)}, u32[]{:S(2)}) collective-permute-start(bf16[256,2048]{1,0:T(8,128)(2,1)} %maximum_select_fusion.6), channel_id=1, source_target_pairs={{0,4},{1,5},{2,6},{3,7},{4,0},{5,1},{6,2},{7,3},{8,12},{9,13},{10,... | collective-permute-start | bytes 3145736 | tf_op jit(solution)/shard_map/ppermute | solution.py:165
  96.0 45.3 %collective-permute-start.9 = (bf16[256,3840]{1,0:T(8,128)(2,1)}, bf16[256,3840]{1,0:T(8,128)(2,1)}, u32[]{:S(2)}, u32[]{:S(2)}) collective-permute-start(bf16[256,3840]{1,0:T(8,128)(2,1)} %pad_maximum_fusion.9), channel_id=1, source_target_pairs={{1,4},{3,6},{4,1},{6,3},{9,12},{11,14},{12,9},{14,11},{17,20},{19,... | collective-permute-start | bytes 5898248 | tf_op jit(solution)/shard_map/ppermute | solution.py:168
  103.5 43.1 %collective-permute-start.7 = (bf16[1024,1792]{0,1:T(8,128)(2,1)}, bf16[1024,1792]{0,1:T(8,128)(2,1)}, u32[]{:S(2)}, u32[]{:S(2)}) collective-permute-start(bf16[1024,1792]{0,1:T(8,128)(2,1)} %all-gather.4.cloned.1.call-done), channel_id=1, source_target_pairs={{0,1},{1,0},{2,3},{3,2},{4,5},{5,4},{6,7},{7,6},{8,9},{9,8},{10,11... | collective-permute-start | bytes 11010056 | tf_op jit(solution)/shard_map/ppermute | solution.py:175
  244.3 12.8 %collective-permute-start.10 = (bf16[1024,3840]{1,0:T(8,128)(2,1)}, bf16[1024,3840]{1,0:T(8,128)(2,1)}, u32[]{:S(2)}, u32[]{:S(2)}) collective-permute-start(bf16[1024,3840]{1,0:T(8,128)(2,1)} %all-gather.6.cloned.1.call-done), channel_id=1, source_target_pairs={{0,1},{1,0},{2,3},{3,2},{4,5},{5,4},{6,7},{7,6},{8,9},{9,8},{10,11... | collective-permute-start | bytes 23592968 | tf_op jit(solution)/shard_map/ppermute | solution.py:175
  244.8 292.9 %reduce-scatter.9.cloned.1.call-start = ((), (), s32[]{:S(2)}) async-start(), calls=%async_computation.10 | async-start | bytes 3276800 | tf_op jit(solution)/shard_map/reduce_scatter | solution.py:192
  385.8 12.7 %collective-permute-start.11 = (bf16[1024,3840]{1,0:T(8,128)(2,1)}, bf16[1024,3840]{1,0:T(8,128)(2,1)S(1)}, u32[]{:S(2)}, u32[]{:S(2)}) collective-permute-start(bf16[1024,3840]{1,0:T(8,128)(2,1)} %all-gather.8.cloned.1.call-done), channel_id=1, source_target_pairs={{0,1},{1,0},{2,3},{3,2},{4,5},{5,4},{6,7},{7,6},{8,9},{9,8},{10,11... | collective-permute-start | bytes 23592968 | tf_op jit(solution)/shard_map/ppermute | solution.py:175
  411.5 20.2 %collective-permute-start.15 = (bf16[1024,2560]{1,0:T(8,128)(2,1)}, bf16[1024,2560]{1,0:T(8,128)(2,1)}, u32[]{:S(2)}, u32[]{:S(2)}) collective-permute-start(bf16[1024,2560]{1,0:T(8,128)(2,1)} %convolution_convert_fusion.1), channel_id=1, source_target_pairs={{0,1},{1,0},{2,3},{3,2},{4,5},{5,4},{6,7},{7,6},{8,9},{9,8},{10,11... | collective-permute-start | bytes 15728648 | tf_op jit(solution)/shard_map/ppermute | solution.py:175
  414.8 145.9 %reduce-scatter.7.cloned.1.call-start = ((), (), s32[]{:S(2)}) async-start(), calls=%async_computation.9 | async-start | bytes 6553600 | tf_op jit(solution)/shard_map/reduce_scatter | solution.py:192
  429.0 14.4 %collective-permute-start.14 = (bf16[128,2048]{1,0:T(8,128)(2,1)}, bf16[128,2048]{1,0:T(8,128)(2,1)}, u32[]{:S(2)}, u32[]{:S(2)}) collective-permute-start(bf16[128,2048]{1,0:T(8,128)(2,1)} %get-tuple-element.248), channel_id=1, source_target_pairs={{0,6},{1,7},{2,4},{3,5},{4,2},{5,3},{6,0},{7,1},{8,14},{9,15},{10,... | collective-permute-start | bytes 1572872 | tf_op jit(solution)/shard_map/ppermute | solution.py:165
  431.1 24.2 %collective-permute-start.12 = (bf16[128,2048]{1,0:T(8,128)(2,1)}, bf16[128,2048]{1,0:T(8,128)(2,1)}, u32[]{:S(2)}, u32[]{:S(2)}) collective-permute-start(bf16[128,2048]{1,0:T(8,128)(2,1)} %get-tuple-element.249), channel_id=1, source_target_pairs={{0,2},{1,3},{2,0},{3,1},{4,6},{5,7},{6,4},{7,5},{8,10},{9,11},{10,... | collective-permute-start | bytes 1572872 | tf_op jit(solution)/shard_map/ppermute | solution.py:165
  431.4 23.9 %collective-permute-start.13 = (bf16[128,2048]{1,0:T(8,128)(2,1)}, bf16[128,2048]{1,0:T(8,128)(2,1)}, u32[]{:S(2)}, u32[]{:S(2)}) collective-permute-start(bf16[128,2048]{1,0:T(8,128)(2,1)} %get-tuple-element.250), channel_id=1, source_target_pairs={{0,4},{1,5},{2,6},{3,7},{4,0},{5,1},{6,2},{7,3},{8,12},{9,13},{10,... | collective-permute-start | bytes 1572872 | tf_op jit(solution)/shard_map/ppermute | solution.py:165
  455.4 147.2 %reduce-scatter.11.cloned.1.call-start = ((), (), s32[]{:S(2)}) async-start(), calls=%async_computation.11 | async-start | bytes 2293760 | tf_op jit(solution)/shard_map/reduce_scatter | solution.py:192
  459.5 14.0 %collective-permute-start.18 = (bf16[128,2048]{1,0:T(8,128)(2,1)S(1)}, bf16[128,2048]{1,0:T(8,128)(2,1)S(1)}, u32[]{:S(2)}, u32[]{:S(2)}) collective-permute-start(bf16[128,2048]{1,0:T(8,128)(2,1)S(1)} %get-tuple-element.228), channel_id=1, source_target_pairs={{0,6},{1,7},{2,4},{3,5},{4,2},{5,3},{6,0},{7,1},{8,14},{9,15},{10,... | collective-permute-start | bytes 1572872 | tf_op jit(solution)/shard_map/ppermute | solution.py:165
  460.4 24.5 %collective-permute-start.17 = (bf16[128,2048]{1,0:T(8,128)(2,1)S(1)}, bf16[128,2048]{1,0:T(8,128)(2,1)S(1)}, u32[]{:S(2)}, u32[]{:S(2)}) collective-permute-start(bf16[128,2048]{1,0:T(8,128)(2,1)S(1)} %get-tuple-element.228), channel_id=1, source_target_pairs={{0,4},{1,5},{2,6},{3,7},{4,0},{5,1},{6,2},{7,3},{8,12},{9,13},{10,... | collective-permute-start | bytes 1572872 | tf_op jit(solution)/shard_map/ppermute | solution.py:165
  461.9 23.7 %collective-permute-start.16 = (bf16[128,2048]{1,0:T(8,128)(2,1)S(1)}, bf16[128,2048]{1,0:T(8,128)(2,1)S(1)}, u32[]{:S(2)}, u32[]{:S(2)}) collective-permute-start(bf16[128,2048]{1,0:T(8,128)(2,1)S(1)} %get-tuple-element.228), channel_id=1, source_target_pairs={{0,2},{1,3},{2,0},{3,1},{4,6},{5,7},{6,4},{7,5},{8,10},{9,11},{10,... | collective-permute-start | bytes 1572872 | tf_op jit(solution)/shard_map/ppermute | solution.py:165
  499.5 9.1 %collective-permute-start.23 = (bf16[1024,576]{0,1:T(8,128)(2,1)S(1)}, bf16[1024,576]{0,1:T(8,128)(2,1)S(1)}, u32[]{:S(2)}, u32[]{:S(2)}) collective-permute-start(bf16[1024,576]{0,1:T(8,128)(2,1)S(1)} %convolution_convert_fusion.5), channel_id=1, source_target_pairs={{0,1},{1,0},{2,3},{3,2},{4,5},{5,4},{6,7},{7,6},{8,9},{9,8},{10,11... | collective-permute-start | bytes 3538952 | tf_op jit(solution)/shard_map/ppermute | solution.py:175
  500.5 7.6 collective-permute-start.22
  505.3 14.0 %collective-permute-start.21 = (bf16[128,2048]{1,0:T(8,128)(2,1)S(1)}, bf16[128,2048]{1,0:T(8,128)(2,1)S(1)}, u32[]{:S(2)}, u32[]{:S(2)}) collective-permute-start(bf16[128,2048]{1,0:T(8,128)(2,1)S(1)} %get-tuple-element.245), channel_id=1, source_target_pairs={{0,6},{1,7},{2,4},{3,5},{4,2},{5,3},{6,0},{7,1},{8,14},{9,15},{10,... | collective-permute-start | bytes 1572872 | tf_op jit(solution)/shard_map/ppermute | solution.py:165
  506.5 25.0 %collective-permute-start.19 = (bf16[128,2048]{1,0:T(8,128)(2,1)S(1)}, bf16[128,2048]{1,0:T(8,128)(2,1)S(1)}, u32[]{:S(2)}, u32[]{:S(2)}) collective-permute-start(bf16[128,2048]{1,0:T(8,128)(2,1)S(1)} %get-tuple-element.246), channel_id=1, source_target_pairs={{0,2},{1,3},{2,0},{3,1},{4,6},{5,7},{6,4},{7,5},{8,10},{9,11},{10,... | collective-permute-start | bytes 1572872 | tf_op jit(solution)/shard_map/ppermute | solution.py:165
  507.8 23.7 %collective-permute-start.20 = (bf16[128,2048]{1,0:T(8,128)(2,1)S(1)}, bf16[128,2048]{1,0:T(8,128)(2,1)S(1)}, u32[]{:S(2)}, u32[]{:S(2)}) collective-permute-start(bf16[128,2048]{1,0:T(8,128)(2,1)S(1)} %get-tuple-element.247), channel_id=1, source_target_pairs={{0,4},{1,5},{2,6},{3,7},{4,0},{5,1},{6,2},{7,3},{8,12},{9,13},{10,... | collective-permute-start | bytes 1572872 | tf_op jit(solution)/shard_map/ppermute | solution.py:165
  533.7 14.3 %collective-permute-start.26 = (bf16[128,2048]{1,0:T(8,128)(2,1)}, bf16[128,2048]{1,0:T(8,128)(2,1)}, u32[]{:S(2)}, u32[]{:S(2)}) collective-permute-start(bf16[128,2048]{1,0:T(8,128)(2,1)} %get-tuple-element.223), channel_id=1, source_target_pairs={{0,6},{1,7},{2,4},{3,5},{4,2},{5,3},{6,0},{7,1},{8,14},{9,15},{10,... | collective-permute-start | bytes 1572872 | tf_op jit(solution)/shard_map/ppermute | solution.py:165
  534.7 24.5 %collective-permute-start.25 = (bf16[128,2048]{1,0:T(8,128)(2,1)}, bf16[128,2048]{1,0:T(8,128)(2,1)}, u32[]{:S(2)}, u32[]{:S(2)}) collective-permute-start(bf16[128,2048]{1,0:T(8,128)(2,1)} %get-tuple-element.223), channel_id=1, source_target_pairs={{0,4},{1,5},{2,6},{3,7},{4,0},{5,1},{6,2},{7,3},{8,12},{9,13},{10,... | collective-permute-start | bytes 1572872 | tf_op jit(solution)/shard_map/ppermute | solution.py:165
  536.0 23.9 %collective-permute-start.24 = (bf16[128,2048]{1,0:T(8,128)(2,1)}, bf16[128,2048]{1,0:T(8,128)(2,1)}, u32[]{:S(2)}, u32[]{:S(2)}) collective-permute-start(bf16[128,2048]{1,0:T(8,128)(2,1)} %get-tuple-element.223), channel_id=1, source_target_pairs={{0,2},{1,3},{2,0},{3,1},{4,6},{5,7},{6,4},{7,5},{8,10},{9,11},{10,... | collective-permute-start | bytes 1572872 | tf_op jit(solution)/shard_map/ppermute | solution.py:165
  537.7 132.0 %reduce-scatter.13.cloned.1.call-start = ((), (), s32[]{:S(2)}) async-start(), calls=%async_computation.12 | async-start | bytes 3276800 | tf_op jit(solution)/shard_map/reduce_scatter | solution.py:192
  562.2 26.5 %collective-permute-start.28 = (bf16[256,3840]{1,0:T(8,128)(2,1)S(1)}, bf16[256,3840]{1,0:T(8,128)(2,1)S(1)}, u32[]{:S(2)}, u32[]{:S(2)}) collective-permute-start(bf16[256,3840]{1,0:T(8,128)(2,1)S(1)} %constant_dynamic-update-slice_fusion), channel_id=1, source_target_pairs={{1,4},{3,6},{4,1},{6,3},{9,12},{11,14},{12,9},{14,11},{17,20},{19,... | collective-permute-start | bytes 5898248 | tf_op jit(solution)/shard_map/ppermute | solution.py:168
  569.2 20.9 %collective-permute-start.29 = (bf16[1024,1280]{1,0:T(8,128)(2,1)S(1)}, bf16[1024,1280]{1,0:T(8,128)(2,1)S(1)}, u32[]{:S(2)}, u32[]{:S(2)}) collective-permute-start(bf16[1024,1280]{1,0:T(8,128)(2,1)S(1)} %convolution_convert_fusion.2), channel_id=1, source_target_pairs={{0,1},{1,0},{2,3},{3,2},{4,5},{5,4},{6,7},{7,6},{8,9},{9,8},{10,11... | collective-permute-start | bytes 7864328 | tf_op jit(solution)/shard_map/ppermute | solution.py:175
  609.8 27.0 %collective-permute-start.33 = (bf16[1024,2560]{1,0:T(8,128)(2,1)}, bf16[1024,2560]{1,0:T(8,128)(2,1)}, u32[]{:S(2)}, u32[]{:S(2)}) collective-permute-start(bf16[1024,2560]{1,0:T(8,128)(2,1)} %convolution_convert_fusion), channel_id=1, source_target_pairs={{0,1},{1,0},{2,3},{3,2},{4,5},{5,4},{6,7},{7,6},{8,9},{9,8},{10,11... | collective-permute-start | bytes 15728648 | tf_op jit(solution)/shard_map/ppermute | solution.py:175
  610.8 165.7 %reduce-scatter.17.cloned.1.call-start = ((), (), s32[]{:S(2)}) async-start(), calls=%async_computation.14 | async-start | bytes 6553600 | tf_op jit(solution)/shard_map/reduce_scatter | solution.py:192
  634.1 14.9 %collective-permute-start.32 = (bf16[128,2048]{1,0:T(8,128)(2,1)}, bf16[128,2048]{1,0:T(8,128)(2,1)S(1)}, u32[]{:S(2)}, u32[]{:S(2)}) collective-permute-start(bf16[128,2048]{1,0:T(8,128)(2,1)} %get-tuple-element.242), channel_id=1, source_target_pairs={{0,6},{1,7},{2,4},{3,5},{4,2},{5,3},{6,0},{7,1},{8,14},{9,15},{10,... | collective-permute-start | bytes 1572872 | tf_op jit(solution)/shard_map/ppermute | solution.py:165
  636.1 24.4 %collective-permute-start.30 = (bf16[128,2048]{1,0:T(8,128)(2,1)}, bf16[128,2048]{1,0:T(8,128)(2,1)S(1)}, u32[]{:S(2)}, u32[]{:S(2)}) collective-permute-start(bf16[128,2048]{1,0:T(8,128)(2,1)} %get-tuple-element.243), channel_id=1, source_target_pairs={{0,2},{1,3},{2,0},{3,1},{4,6},{5,7},{6,4},{7,5},{8,10},{9,11},{10,... | collective-permute-start | bytes 1572872 | tf_op jit(solution)/shard_map/ppermute | solution.py:165
  636.3 24.2 %collective-permute-start.31 = (bf16[128,2048]{1,0:T(8,128)(2,1)}, bf16[128,2048]{1,0:T(8,128)(2,1)}, u32[]{:S(2)}, u32[]{:S(2)}) collective-permute-start(bf16[128,2048]{1,0:T(8,128)(2,1)} %get-tuple-element.244), channel_id=1, source_target_pairs={{0,4},{1,5},{2,6},{3,7},{4,0},{5,1},{6,2},{7,3},{8,12},{9,13},{10,... | collective-permute-start | bytes 1572872 | tf_op jit(solution)/shard_map/ppermute | solution.py:165
  662.2 9.6 %collective-permute-start.40 = (bf16[256,256]{0,1:T(8,128)(2,1)}, bf16[256,256]{0,1:T(8,128)(2,1)}, u32[]{:S(2)}, u32[]{:S(2)}) collective-permute-start(bf16[256,256]{0,1:T(8,128)(2,1)} %slice.777), channel_id=1, source_target_pairs={{0,3},{1,7},{2,1},{3,5},{4,2},{5,6},{6,0},{7,4},{8,11},{9,15},{10,... | collective-permute-start | bytes 393224 | tf_op jit(solution)/shard_map/ppermute | solution.py:172
  663.1 11.8 %collective-permute-start.39 = (bf16[256,256]{0,1:T(8,128)(2,1)}, bf16[256,256]{0,1:T(8,128)(2,1)}, u32[]{:S(2)}, u32[]{:S(2)}) collective-permute-start(bf16[256,256]{0,1:T(8,128)(2,1)} %slice.777), channel_id=1, source_target_pairs={{0,2},{1,6},{2,0},{3,4},{4,3},{5,7},{6,1},{7,5},{8,10},{9,14},{10,... | collective-permute-start | bytes 393224 | tf_op jit(solution)/shard_map/ppermute | solution.py:172
  665.1 11.2 %collective-permute-start.38 = (bf16[256,256]{0,1:T(8,128)(2,1)}, bf16[256,256]{0,1:T(8,128)(2,1)}, u32[]{:S(2)}, u32[]{:S(2)}) collective-permute-start(bf16[256,256]{0,1:T(8,128)(2,1)} %slice.777), channel_id=1, source_target_pairs={{0,1},{1,5},{2,3},{3,7},{4,0},{5,4},{6,2},{7,6},{8,9},{9,13},{10,1... | collective-permute-start | bytes 393224 | tf_op jit(solution)/shard_map/ppermute | solution.py:172
  665.1 12.2 %collective-permute-start.37 = (bf16[256,896]{0,1:T(8,128)(2,1)}, bf16[256,896]{0,1:T(8,128)(2,1)}, u32[]{:S(2)}, u32[]{:S(2)}) collective-permute-start(bf16[256,896]{0,1:T(8,128)(2,1)} %reduce-scatter.11.cloned.1.call-done), channel_id=1, source_target_pairs={{1,4},{3,6},{4,1},{6,3},{9,12},{11,14},{12,9},{14,11},{17,20},{19,... | collective-permute-start | bytes 1376264 | tf_op jit(solution)/shard_map/ppermute | solution.py:168
  669.8 140.4 %reduce-scatter.15.cloned.1.call-start = ((), (), s32[]{:S(2)}) async-start(), calls=%async_computation.13 | async-start | bytes 2293760 | tf_op jit(solution)/shard_map/reduce_scatter | solution.py:192
  671.7 15.1 %collective-permute-start.36 = (bf16[128,2048]{1,0:T(8,128)(2,1)S(1)}, bf16[128,2048]{1,0:T(8,128)(2,1)S(1)}, u32[]{:S(2)}, u32[]{:S(2)}) collective-permute-start(bf16[128,2048]{1,0:T(8,128)(2,1)S(1)} %get-tuple-element.221), channel_id=1, source_target_pairs={{0,6},{1,7},{2,4},{3,5},{4,2},{5,3},{6,0},{7,1},{8,14},{9,15},{10,... | collective-permute-start | bytes 1572872 | tf_op jit(solution)/shard_map/ppermute | solution.py:165
  671.7 26.1 %collective-permute-start.35 = (bf16[128,2048]{1,0:T(8,128)(2,1)S(1)}, bf16[128,2048]{1,0:T(8,128)(2,1)S(1)}, u32[]{:S(2)}, u32[]{:S(2)}) collective-permute-start(bf16[128,2048]{1,0:T(8,128)(2,1)S(1)} %get-tuple-element.221), channel_id=1, source_target_pairs={{0,4},{1,5},{2,6},{3,7},{4,0},{5,1},{6,2},{7,3},{8,12},{9,13},{10,... | collective-permute-start | bytes 1572872 | tf_op jit(solution)/shard_map/ppermute | solution.py:165
  675.0 23.7 %collective-permute-start.34 = (bf16[128,2048]{1,0:T(8,128)(2,1)S(1)}, bf16[128,2048]{1,0:T(8,128)(2,1)S(1)}, u32[]{:S(2)}, u32[]{:S(2)}) collective-permute-start(bf16[128,2048]{1,0:T(8,128)(2,1)S(1)} %get-tuple-element.221), channel_id=1, source_target_pairs={{0,2},{1,3},{2,0},{3,1},{4,6},{5,7},{6,4},{7,5},{8,10},{9,11},{10,... | collective-permute-start | bytes 1572872 | tf_op jit(solution)/shard_map/ppermute | solution.py:165
  711.7 10.0 %collective-permute-start.45 = (bf16[1024,576]{0,1:T(8,128)(2,1)S(1)}, bf16[1024,576]{0,1:T(8,128)(2,1)S(1)}, u32[]{:S(2)}, u32[]{:S(2)}) collective-permute-start(bf16[1024,576]{0,1:T(8,128)(2,1)S(1)} %convolution_convert_fusion.4), channel_id=1, source_target_pairs={{0,1},{1,0},{2,3},{3,2},{4,5},{5,4},{6,7},{7,6},{8,9},{9,8},{10,11... | collective-permute-start | bytes 3538952 | tf_op jit(solution)/shard_map/ppermute | solution.py:175
  712.6 7.7 collective-permute-start.44
  717.6 14.2 %collective-permute-start.43 = (bf16[128,2048]{1,0:T(8,128)(2,1)S(1)}, bf16[128,2048]{1,0:T(8,128)(2,1)S(1)}, u32[]{:S(2)}, u32[]{:S(2)}) collective-permute-start(bf16[128,2048]{1,0:T(8,128)(2,1)S(1)} %get-tuple-element.239), channel_id=1, source_target_pairs={{0,6},{1,7},{2,4},{3,5},{4,2},{5,3},{6,0},{7,1},{8,14},{9,15},{10,... | collective-permute-start | bytes 1572872 | tf_op jit(solution)/shard_map/ppermute | solution.py:165
  718.0 24.6 %collective-permute-start.41 = (bf16[128,2048]{1,0:T(8,128)(2,1)S(1)}, bf16[128,2048]{1,0:T(8,128)(2,1)S(1)}, u32[]{:S(2)}, u32[]{:S(2)}) collective-permute-start(bf16[128,2048]{1,0:T(8,128)(2,1)S(1)} %get-tuple-element.240), channel_id=1, source_target_pairs={{0,2},{1,3},{2,0},{3,1},{4,6},{5,7},{6,4},{7,5},{8,10},{9,11},{10,... | collective-permute-start | bytes 1572872 | tf_op jit(solution)/shard_map/ppermute | solution.py:165
  719.1 23.8 %collective-permute-start.42 = (bf16[128,2048]{1,0:T(8,128)(2,1)S(1)}, bf16[128,2048]{1,0:T(8,128)(2,1)S(1)}, u32[]{:S(2)}, u32[]{:S(2)}) collective-permute-start(bf16[128,2048]{1,0:T(8,128)(2,1)S(1)} %get-tuple-element.241), channel_id=1, source_target_pairs={{0,4},{1,5},{2,6},{3,7},{4,0},{5,1},{6,2},{7,3},{8,12},{9,13},{10,... | collective-permute-start | bytes 1572872 | tf_op jit(solution)/shard_map/ppermute | solution.py:165
  750.1 16.7 %collective-permute-start.49 = (bf16[128,2048]{1,0:T(8,128)(2,1)}, bf16[128,2048]{1,0:T(8,128)(2,1)}, u32[]{:S(2)}, u32[]{:S(2)}) collective-permute-start(bf16[128,2048]{1,0:T(8,128)(2,1)} %get-tuple-element.236), channel_id=1, source_target_pairs={{0,6},{1,7},{2,4},{3,5},{4,2},{5,3},{6,0},{7,1},{8,14},{9,15},{10,... | collective-permute-start | bytes 1572872 | tf_op jit(solution)/shard_map/ppermute | solution.py:165
  751.2 23.4 %collective-permute-start.48 = (bf16[128,2048]{1,0:T(8,128)(2,1)}, bf16[128,2048]{1,0:T(8,128)(2,1)}, u32[]{:S(2)}, u32[]{:S(2)}) collective-permute-start(bf16[128,2048]{1,0:T(8,128)(2,1)} %get-tuple-element.237), channel_id=1, source_target_pairs={{0,4},{1,5},{2,6},{3,7},{4,0},{5,1},{6,2},{7,3},{8,12},{9,13},{10,... | collective-permute-start | bytes 1572872 | tf_op jit(solution)/shard_map/ppermute | solution.py:165
  751.7 24.8 %collective-permute-start.47 = (bf16[128,2048]{1,0:T(8,128)(2,1)}, bf16[128,2048]{1,0:T(8,128)(2,1)}, u32[]{:S(2)}, u32[]{:S(2)}) collective-permute-start(bf16[128,2048]{1,0:T(8,128)(2,1)} %get-tuple-element.238), channel_id=1, source_target_pairs={{0,2},{1,3},{2,0},{3,1},{4,6},{5,7},{6,4},{7,5},{8,10},{9,11},{10,... | collective-permute-start | bytes 1572872 | tf_op jit(solution)/shard_map/ppermute | solution.py:165
  765.0 24.7 %collective-permute-start.52 = (bf16[128,2048]{1,0:T(8,128)(2,1)}, bf16[128,2048]{1,0:T(8,128)(2,1)}, u32[]{:S(2)}, u32[]{:S(2)}) collective-permute-start(bf16[128,2048]{1,0:T(8,128)(2,1)} %select_n.426), channel_id=1, source_target_pairs={{0,2},{1,3},{2,0},{3,1},{4,6},{5,7},{6,4},{7,5},{8,10},{9,11},{10,... | collective-permute-start | bytes 1572872 | tf_op jit(solution)/shard_map/ppermute | solution.py:165
  765.5 23.6 %collective-permute-start.58 = (f32[2,4224]{1,0:T(2,128)S(1)}, f32[2,4224]{1,0:T(2,128)S(1)}, u32[]{:S(2)}, u32[]{:S(2)}) collective-permute-start(f32[2,4224]{1,0:T(2,128)S(1)} %add.585), channel_id=1, source_target_pairs={{0,16},{8,24},{16,0},{24,8},{1,17},{9,25},{17,1},{25,9},{2,18},{10... | collective-permute-start | bytes 101384 | tf_op jit(solution)/shard_map/ppermute | solution.py:182
  779.9 26.3 %collective-permute-start.46 = (bf16[256,3840]{1,0:T(8,128)(2,1)}, bf16[256,3840]{1,0:T(8,128)(2,1)}, u32[]{:S(2)}, u32[]{:S(2)}) collective-permute-start(bf16[256,3840]{1,0:T(8,128)(2,1)} %constant_dynamic-update-slice_fusion.2), channel_id=1, source_target_pairs={{1,4},{3,6},{4,1},{6,3},{9,12},{11,14},{12,9},{14,11},{17,20},{19,... | collective-permute-start | bytes 5898248 | tf_op jit(solution)/shard_map/ppermute | solution.py:168
  787.1 14.0 %collective-permute-start.50 = (bf16[128,2048]{1,0:T(8,128)(2,1)}, bf16[128,2048]{1,0:T(8,128)(2,1)S(1)}, u32[]{:S(2)}, u32[]{:S(2)}) collective-permute-start(bf16[128,2048]{1,0:T(8,128)(2,1)} %select_n.423), channel_id=1, source_target_pairs={{0,2},{1,3},{2,0},{3,1},{4,6},{5,7},{6,4},{7,5},{8,10},{9,11},{10,... | collective-permute-start | bytes 1572872 | tf_op jit(solution)/shard_map/ppermute | solution.py:165
  791.4 17.9 %collective-permute-start.53 = (bf16[256,2048]{1,0:T(8,128)(2,1)S(1)}, bf16[256,2048]{1,0:T(8,128)(2,1)S(1)}, u32[]{:S(2)}, u32[]{:S(2)}) collective-permute-start(bf16[256,2048]{1,0:T(8,128)(2,1)S(1)} %maximum_select_fusion.8), channel_id=1, source_target_pairs={{0,1},{1,0},{2,3},{3,2},{4,5},{5,4},{6,7},{7,6},{8,9},{9,8},{10,11... | collective-permute-start | bytes 3145736 | tf_op jit(solution)/shard_map/ppermute | solution.py:175
  802.8 7.5 collective-permute-start.51
  811.8 20.5 %collective-permute-start.62 = (bf16[256,256]{0,1:T(8,128)(2,1)}, bf16[256,256]{0,1:T(8,128)(2,1)}, u32[]{:S(2)}, u32[]{:S(2)}) collective-permute-start(bf16[256,256]{0,1:T(8,128)(2,1)} %slice.821), channel_id=1, source_target_pairs={{0,3},{1,7},{2,1},{3,5},{4,2},{5,6},{6,0},{7,4},{8,11},{9,15},{10,... | collective-permute-start | bytes 393224 | tf_op jit(solution)/shard_map/ppermute | solution.py:172
  811.9 21.5 %collective-permute-start.61 = (bf16[256,256]{0,1:T(8,128)(2,1)}, bf16[256,256]{0,1:T(8,128)(2,1)S(1)}, u32[]{:S(2)}, u32[]{:S(2)}) collective-permute-start(bf16[256,256]{0,1:T(8,128)(2,1)} %slice.821), channel_id=1, source_target_pairs={{0,2},{1,6},{2,0},{3,4},{4,3},{5,7},{6,1},{7,5},{8,10},{9,14},{10,... | collective-permute-start | bytes 393224 | tf_op jit(solution)/shard_map/ppermute | solution.py:172
  813.3 20.1 %collective-permute-start.60 = (bf16[256,256]{0,1:T(8,128)(2,1)}, bf16[256,256]{0,1:T(8,128)(2,1)S(1)}, u32[]{:S(2)}, u32[]{:S(2)}) collective-permute-start(bf16[256,256]{0,1:T(8,128)(2,1)} %slice.821), channel_id=1, source_target_pairs={{0,1},{1,5},{2,3},{3,7},{4,0},{5,4},{6,2},{7,6},{8,9},{9,13},{10,1... | collective-permute-start | bytes 393224 | tf_op jit(solution)/shard_map/ppermute | solution.py:172
  814.0 19.4 %collective-permute-start.59 = (bf16[256,896]{0,1:T(8,128)(2,1)}, bf16[256,896]{0,1:T(8,128)(2,1)}, u32[]{:S(2)}, u32[]{:S(2)}) collective-permute-start(bf16[256,896]{0,1:T(8,128)(2,1)} %reduce-scatter.15.cloned.1.call-done), channel_id=1, source_target_pairs={{1,4},{3,6},{4,1},{6,3},{9,12},{11,14},{12,9},{14,11},{17,20},{19,... | collective-permute-start | bytes 1376264 | tf_op jit(solution)/shard_map/ppermute | solution.py:168
  (165 other events, 1949.3 us)
Sparse Core Ops, SparseCore 0:
  29.1 73.5 all-gather.3
  104.9 139.3 all-gather.5
  246.5 139.2 all-gather.7
  414.9 49.8 reduce-scatter.8
  467.0 93.6 reduce-scatter.6
  562.8 39.6 reduce-scatter.10
  610.9 50.5 reduce-scatter.12
  669.9 91.5 reduce-scatter.16
  765.6 38.9 reduce-scatter.14

commit v5 on v4

--- a/solution.py
+++ b/solution.py
@@ -233,16 +233,14 @@
         )
 
     def outward(self, array):
-        lead = array.shape[:-1]
-        d = array.shape[-1]
-        w = d // (2 * self.n)
-        own = array[..., : d // 2].reshape(lead + (self.n, w))
-        other = array[..., d // 2 :].reshape(lead + (self.n, w))
+        w = array.shape[-1] // (2 * self.n)
+        parts = [array[..., i * w : (i + 1) * w] for i in range(2 * self.n)]
+        pairs = list(zip(parts[: self.n], parts[self.n :]))
         return jnp.where(
             self.c == 0,
-            jnp.stack([own, other], axis=-2),
-            jnp.stack([other, own], axis=-2),
-        ).reshape(lead + (d,))
+            jnp.concatenate([part for pair in pairs for part in pair], axis=-1),
+            jnp.concatenate([part for pair in pairs for part in pair[::-1]], axis=-1),
+        )
 
     def both_quarters(self, rows):
         beside = self.peer(rows, 1)
@@ -531,14 +529,13 @@
         if layer + 1 < LAYERS:
             above = results[layer + 1]
             ffn_high = plan.swap(jnp.concatenate([above[1], above[2]], axis=1))
-            grad_gu, ffn_high, above[0], term_d = lax.optimization_barrier(
-                (grad_gu, ffn_high, above[0], term_d)
-            )
+            grad_gu, ffn_high, term_d = lax.optimization_barrier((grad_gu, ffn_high, term_d))
         term_gu = plan.weight_term(normed2, grad_gu)
         mid_terms = plan.out_of(grad_gu, w_gu)
         if layer + 1 == LAYERS:
             summed_mid, term_gu = plan.gather_sum(mid_terms, term_gu)
         else:
+            mid_terms, above[0] = lax.optimization_barrier((mid_terms, above[0]))
             scatter_next(layer, 2, term_d)
             summed_mid, term_gu = plan.gather_sum(mid_terms, term_gu)
             summed_mid, results[layer][2] = lax.optimization_barrier(

time: 854 us -> 849 us (level)
  other arithmetic: 88.7 us -> 98.4 us
    ppermute x28, waiting for transfers between devices: 168 us -> 141 us  [peer(): return lax.ppermute(value, ('ctx', 'tensor'), self.peers[j])]
    ppermute x3, waiting for transfers between devices: 0.99 us -> 21.3 us  [total(): value = value + lax.ppermute(value, ('ctx', 'tensor'), pairs)]
    reduce_scatter x6, waiting for transfers between devices: 10.1 us -> 1.42 us  [scatter(): return lax.psum_scatter(term, 'dp', scatter_dimension=0, tiled=True)]
    unnamed x330 -> x410, local copies, waits for them, and re-layouts: 23.5 us -> 28.7 us
  transfers between devices with their start and end apart: 72 -> 72, of which waited for: 35 -> 31; matrix products, arithmetic and copies ran while one was open for 33% -> 35% of each run, Pallas kernels for 17% -> 18%
where the time goes in v5:
time: 849 us; the launch traced here: 841 us
  waiting for transfers between devices  277 us (33%)
  matrix products  163 us (19%)
  Pallas kernels  147 us (17%)
  other arithmetic  98.4 us (12%)
  starting transfers between devices  72.8 us (9%)
  local copies, waits for them, and re-layouts  64.7 us (8%)
  between operations  18.1 us (2%)
    dot_general x52, matrix products, product(): lax.dot_general(left_side, right_side, (contract, ((), ())), preferred_el...  148 us
    pallas_call x3, Pallas kernels, join(): pl.pallas_call(join_kernel, out_shape=(jax.ShapeDtypeStruct((rows, width)...  147 us
    ppermute x28, waiting for transfers between devices, peer(): return lax.ppermute(value, ('ctx', 'tensor'), self.peers[j])  141 us
    ppermute x7, waiting for transfers between devices, swap(): moved = lax.ppermute(value, ('ctx', 'tensor'), self.swap_pairs)  72 us
    all_gather x3, waiting for transfers between devices, local(): owned.append(lax.all_gather(shard, 'dp', axis=0, tiled=True))  31.6 us
    unnamed x410, local copies, waits for them, and re-layouts  28.7 us
    ppermute x7, starting transfers between devices, swap(): moved = lax.ppermute(value, ('ctx', 'tensor'), self.swap_pairs)  27.3 us
    ppermute x28, starting transfers between devices, peer(): return lax.ppermute(value, ('ctx', 'tensor'), self.peers[j])  23.1 us
  transfers between devices with their start and end apart: 72, of which 31 were waited for; matrix products, arithmetic and copies ran while one was open for 35% of the time, Pallas kernels for 18%

profile of v5, /device:TPU:1, one launch (start us, length us, event | category | flops | bytes accessed | tf_op | source)
XLA Modules:
  0.0 841.2 jit_solution(11587058263209321981)
XLA Ops:
  12.4 4.5 collective-permute-start
  18.1 9.9 %collective-permute-done = bf16[256,1792]{0,1:T(8,128)(2,1)S(1)} collective-permute-done((bf16[256,1792]{0,1:T(8,128)(2,1)S(1)}, bf16[256,1792]{0,1:T(8,128)(2,1)S(1)}, u32[]{:S(2)}, u32[]{:S(2)}) %collective-permute-start) | collective-permute-done | bytes 917536 | tf_op jit(solution)/shard_map/ppermute | solution.py:168
  31.9 2.8 copy.61
  39.9 3.6 collective-permute-start.8
  45.0 3.9 copy.66
  53.8 23.9 %collective-permute-done.8 = bf16[256,3840]{1,0:T(8,128)(2,1)} collective-permute-done((bf16[256,3840]{1,0:T(8,128)(2,1)}, bf16[256,3840]{1,0:T(8,128)(2,1)}, u32[]{:S(2)}, u32[]{:S(2)}) %collective-permute-start.8) | collective-permute-done | bytes 1966112 | tf_op jit(solution)/shard_map/ppermute | solution.py:168
  77.7 3.3 broadcast_select_fusion.3
  81.2 3.3 collective-permute-start.3
  97.4 7.6 collective-permute-start.9
  109.7 7.8 collective-permute-done.6
  117.5 3.3 maximum_select_fusion
  122.7 18.7 %collective-permute-done.9 = bf16[256,3840]{1,0:T(8,128)(2,1)} collective-permute-done((bf16[256,3840]{1,0:T(8,128)(2,1)}, bf16[256,3840]{1,0:T(8,128)(2,1)}, u32[]{:S(2)}, u32[]{:S(2)}) %collective-permute-start.9) | collective-permute-done | bytes 1966112 | tf_op jit(solution)/shard_map/ppermute | solution.py:168
  141.4 3.0 broadcast_select_fusion.2
  161.2 50.2 %join.3 = (f32[128,2048]{1,0:T(8,128)S(1)}, bf16[512,2048]{1,0:T(8,128)(2,1)S(1)}) custom-call(bf16[512,2048]{1,0:T(8,128)(2,1)S(1)} %pad_maximum_fusion.2.terms, f32[128,2048]{1,0:T(8,128)S(1)} %slice.915.state, f32[1,2048]{1,0:T(1,128)S(1)} %get-tuple-element.363.gain), custom_call_target="tpu_custom_call" | custom-call | flops 1000 | bytes 1000 | tf_op jit(solution)/shard_map/join/pallas_call | solution.py:112
  212.7 31.5 %all-gather.6.cloned.1.call-done = bf16[1024,3840]{1,0:T(8,128)(2,1)} async-done(((bf16[256,3840]{1,0:T(8,128)(2,1)}), bf16[1024,3840]{1,0:T(8,128)(2,1)}) %all-gather.6.cloned.1.call-update) | async-done | bytes 7864336 | tf_op jit(solution)/shard_map/all_gather | solution.py:326
  245.0 3.7 fusion.21
  248.7 3.3 fusion.24
  252.0 5.1 collective-permute-done.10
  257.1 3.5 convolution_add_fusion.5
  260.6 5.8 multiply_convert_fusion.8
  266.4 3.8 fusion.61
  270.1 3.3 fusion.67
  273.6 48.9 %join.4 = (f32[128,2048]{1,0:T(8,128)S(1)}, bf16[512,2048]{1,0:T(8,128)(2,1)S(1)}) custom-call(bf16[512,2048]{1,0:T(8,128)(2,1)S(1)} %pad_maximum_fusion.3.terms, f32[128,2048]{1,0:T(8,128)S(1)} %get-tuple-element.102.state, f32[1,2048]{1,0:T(1,128)S(1)} %get-tuple-element.364.gain), custom_call_target="tpu_custom_call" | custom-call | flops 1000 | bytes 1000 | tf_op jit(solution)/shard_map/join/pallas_call | solution.py:112
  336.4 48.3 %join.5 = (f32[128,2048]{1,0:T(8,128)S(1)}, bf16[512,2048]{1,0:T(8,128)(2,1)S(1)}) custom-call(bf16[512,2048]{1,0:T(8,128)(2,1)S(1)} %pad_maximum_fusion.4.terms, f32[128,2048]{1,0:T(8,128)S(1)} %get-tuple-element.104.state, f32[1,2048]{1,0:T(1,128)S(1)} %get-tuple-element.362.gain), custom_call_target="tpu_custom_call" | custom-call | flops 1000 | bytes 1000 | tf_op jit(solution)/shard_map/join/pallas_call | solution.py:112
  387.2 3.7 fusion.17
  391.0 3.4 fusion.19
  394.4 3.3 fusion.42
  402.6 3.2 multiply_convert_fusion.3
  407.9 4.9 convolution_convert_fusion.1
  412.9 3.1 add_convert_fusion.3
  423.5 5.5 fusion.49
  429.1 2.9 fusion.55
  435.9 4.3 fusion.64
  442.7 6.6 add_convert_fusion.1
  449.3 10.2 %collective-permute-done.12 = bf16[128,2048]{1,0:T(8,128)(2,1)} collective-permute-done((bf16[128,2048]{1,0:T(8,128)(2,1)}, bf16[128,2048]{1,0:T(8,128)(2,1)}, u32[]{:S(2)}, u32[]{:S(2)}) %collective-permute-start.12) | collective-permute-done | bytes 524320 | tf_op jit(solution)/shard_map/ppermute | solution.py:165
  460.0 3.2 pad_maximum_fusion.9
  473.6 7.5 collective-permute-done.18
  481.0 10.2 %collective-permute-done.17 = bf16[128,2048]{1,0:T(8,128)(2,1)S(1)} collective-permute-done((bf16[128,2048]{1,0:T(8,128)(2,1)S(1)}, bf16[128,2048]{1,0:T(8,128)(2,1)S(1)}, u32[]{:S(2)}, u32[]{:S(2)}) %collective-permute-start.17) | collective-permute-done | bytes 524320 | tf_op jit(solution)/shard_map/ppermute | solution.py:165
  517.0 9.9 %collective-permute-done.21 = bf16[128,2048]{1,0:T(8,128)(2,1)S(1)} collective-permute-done((bf16[128,2048]{1,0:T(8,128)(2,1)S(1)}, bf16[128,2048]{1,0:T(8,128)(2,1)S(1)}, u32[]{:S(2)}, u32[]{:S(2)}) %collective-permute-start.21) | collective-permute-done | bytes 524320 | tf_op jit(solution)/shard_map/ppermute | solution.py:165
  526.9 12.0 %collective-permute-done.19 = bf16[128,2048]{1,0:T(8,128)(2,1)S(1)} collective-permute-done((bf16[128,2048]{1,0:T(8,128)(2,1)S(1)}, bf16[128,2048]{1,0:T(8,128)(2,1)S(1)}, u32[]{:S(2)}, u32[]{:S(2)}) %collective-permute-start.19) | collective-permute-done | bytes 524320 | tf_op jit(solution)/shard_map/ppermute | solution.py:165
  547.9 7.6 collective-permute-done.26
  555.5 10.3 %collective-permute-done.25 = bf16[128,2048]{1,0:T(8,128)(2,1)} collective-permute-done((bf16[128,2048]{1,0:T(8,128)(2,1)}, bf16[128,2048]{1,0:T(8,128)(2,1)}, u32[]{:S(2)}, u32[]{:S(2)}) %collective-permute-start.25) | collective-permute-done | bytes 524320 | tf_op jit(solution)/shard_map/ppermute | solution.py:165
  568.9 2.7 collective-permute-start.28
  574.9 3.5 fusion.44
  578.4 4.0 multiply_convert_fusion.5
  584.1 11.2 %collective-permute-done.28 = bf16[256,3840]{1,0:T(8,128)(2,1)S(1)} collective-permute-done((bf16[256,3840]{1,0:T(8,128)(2,1)S(1)}, bf16[256,3840]{1,0:T(8,128)(2,1)S(1)}, u32[]{:S(2)}, u32[]{:S(2)}) %collective-permute-start.28) | collective-permute-done | bytes 1966112 | tf_op jit(solution)/shard_map/ppermute | solution.py:168
  596.8 3.1 add_convert_fusion.2
  600.0 7.4 convolution_convert_fusion
  608.8 6.8 fusion.52
  615.5 5.4 fusion.58
  622.5 2.7 fusion.244
  627.8 7.3 add_convert_fusion
  635.1 4.6 collective-permute-done.32
  639.7 10.0 %collective-permute-done.31 = bf16[128,2048]{1,0:T(8,128)(2,1)S(1)} collective-permute-done((bf16[128,2048]{1,0:T(8,128)(2,1)}, bf16[128,2048]{1,0:T(8,128)(2,1)S(1)}, u32[]{:S(2)}, u32[]{:S(2)}) %collective-permute-start.31) | collective-permute-done | bytes 524320 | tf_op jit(solution)/shard_map/ppermute | solution.py:165
  672.2 6.2 collective-permute-done.36
  678.4 10.2 %collective-permute-done.35 = bf16[128,2048]{1,0:T(8,128)(2,1)S(1)} collective-permute-done((bf16[128,2048]{1,0:T(8,128)(2,1)S(1)}, bf16[128,2048]{1,0:T(8,128)(2,1)S(1)}, u32[]{:S(2)}, u32[]{:S(2)}) %collective-permute-start.35) | collective-permute-done | bytes 524320 | tf_op jit(solution)/shard_map/ppermute | solution.py:165
  715.0 8.1 collective-permute-done.43
  723.0 11.3 %collective-permute-done.41 = bf16[128,2048]{1,0:T(8,128)(2,1)S(1)} collective-permute-done((bf16[128,2048]{1,0:T(8,128)(2,1)S(1)}, bf16[128,2048]{1,0:T(8,128)(2,1)S(1)}, u32[]{:S(2)}, u32[]{:S(2)}) %collective-permute-start.41) | collective-permute-done | bytes 524320 | tf_op jit(solution)/shard_map/ppermute | solution.py:165
  742.3 21.3 %collective-permute-done.55 = f32[2,4224]{1,0:T(2,128)S(1)} collective-permute-done((f32[2,4224]{1,0:T(2,128)S(1)}, f32[2,4224]{1,0:T(2,128)S(1)}, u32[]{:S(2)}, u32[]{:S(2)}) %collective-permute-start.55) | collective-permute-done | bytes 33824 | tf_op jit(solution)/shard_map/ppermute | solution.py:179
  775.6 3.8 collective-permute-start.46
  784.5 9.0 %collective-permute-done.50 = bf16[128,2048]{1,0:T(8,128)(2,1)S(1)} collective-permute-done((bf16[128,2048]{1,0:T(8,128)(2,1)S(1)}, bf16[128,2048]{1,0:T(8,128)(2,1)S(1)}, u32[]{:S(2)}, u32[]{:S(2)}) %collective-permute-start.50) | collective-permute-done | bytes 524320 | tf_op jit(solution)/shard_map/ppermute | solution.py:165
  793.8 8.3 collective-permute-done.46
  819.8 3.3 maximum_select_fusion.1
  823.1 3.3 copy.81
  (796 shorter events, 254.6 us)
Async XLA Ops:
  7.2 97.7 %all-gather.4.cloned.1.call-start = ((), (), s32[]{:S(2)}) async-start(), calls=%async_computation.6 | async-start | bytes 4587520 | tf_op jit(solution)/shard_map/all_gather | solution.py:326
  12.4 15.6 %collective-permute-start = (bf16[256,1792]{0,1:T(8,128)(2,1)S(1)}, bf16[256,1792]{0,1:T(8,128)(2,1)S(1)}, u32[]{:S(2)}, u32[]{:S(2)}) collective-permute-start(bf16[256,1792]{0,1:T(8,128)(2,1)S(1)} %bitcast_dynamic-update-slice_fusion), channel_id=1, source_target_pairs={{1,4},{3,6},{4,1},{6,3},{9,12},{11,14},{12,9},{14,11},{17,20},{19,... | collective-permute-start | bytes 2752520 | tf_op jit(solution)/shard_map/ppermute | solution.py:168
  29.0 215.3 %all-gather.6.cloned.1.call-start = ((), (), s32[]{:S(2)}) async-start(), calls=%async_computation.7 | async-start | bytes 9830400 | tf_op jit(solution)/shard_map/all_gather | solution.py:326
  30.4 50.7 %collective-permute-start.2 = (bf16[2,528]{1,0:T(2,128)(2,1)S(1)}, bf16[2,528]{1,0:T(2,128)(2,1)S(1)}, u32[]{:S(2)}, u32[]{:S(2)}) collective-permute-start(bf16[2,528]{1,0:T(2,128)(2,1)S(1)} %copy-done.135), channel_id=1, source_target_pairs={{0,4},{4,0},{1,5},{5,1},{2,6},{6,2},{3,7},{7,3},{8,12},{12,8},{9,1... | collective-permute-start | bytes 6344 | tf_op jit(solution)/shard_map/ppermute | solution.py:336
  39.9 37.8 %collective-permute-start.8 = (bf16[256,3840]{1,0:T(8,128)(2,1)}, bf16[256,3840]{1,0:T(8,128)(2,1)}, u32[]{:S(2)}, u32[]{:S(2)}) collective-permute-start(bf16[256,3840]{1,0:T(8,128)(2,1)} %pad_maximum_fusion.11), channel_id=1, source_target_pairs={{1,4},{3,6},{4,1},{6,3},{9,12},{11,14},{12,9},{14,11},{17,20},{19,... | collective-permute-start | bytes 5898248 | tf_op jit(solution)/shard_map/ppermute | solution.py:168
  44.9 60.8 %collective-permute-start.1 = (bf16[256,2048]{1,0:T(8,128)(2,1)S(1)}, bf16[256,2048]{1,0:T(8,128)(2,1)S(1)}, u32[]{:S(2)}, u32[]{:S(2)}) collective-permute-start(bf16[256,2048]{1,0:T(8,128)(2,1)S(1)} %maximum_select_fusion.4), channel_id=1, source_target_pairs={{0,4},{1,5},{2,6},{3,7},{4,0},{5,1},{6,2},{7,3},{8,12},{9,13},{10,... | collective-permute-start | bytes 3145736 | tf_op jit(solution)/shard_map/ppermute | solution.py:165
  81.0 305.1 %all-gather.8.cloned.1.call-start = ((), (), s32[]{:S(2)}) async-start(), calls=%async_computation.8 | async-start | bytes 9830400 | tf_op jit(solution)/shard_map/all_gather | solution.py:326
  94.8 22.7 %collective-permute-start.6 = (bf16[256,2048]{1,0:T(8,128)(2,1)}, bf16[256,2048]{1,0:T(8,128)(2,1)}, u32[]{:S(2)}, u32[]{:S(2)}) collective-permute-start(bf16[256,2048]{1,0:T(8,128)(2,1)} %maximum_select_fusion.6), channel_id=1, source_target_pairs={{0,4},{1,5},{2,6},{3,7},{4,0},{5,1},{6,2},{7,3},{8,12},{9,13},{10,... | collective-permute-start | bytes 3145736 | tf_op jit(solution)/shard_map/ppermute | solution.py:165
  97.4 44.0 %collective-permute-start.9 = (bf16[256,3840]{1,0:T(8,128)(2,1)}, bf16[256,3840]{1,0:T(8,128)(2,1)}, u32[]{:S(2)}, u32[]{:S(2)}) collective-permute-start(bf16[256,3840]{1,0:T(8,128)(2,1)} %pad_maximum_fusion.10), channel_id=1, source_target_pairs={{1,4},{3,6},{4,1},{6,3},{9,12},{11,14},{12,9},{14,11},{17,20},{19,... | collective-permute-start | bytes 5898248 | tf_op jit(solution)/shard_map/ppermute | solution.py:168
  105.0 41.9 %collective-permute-start.7 = (bf16[1024,1792]{0,1:T(8,128)(2,1)}, bf16[1024,1792]{0,1:T(8,128)(2,1)}, u32[]{:S(2)}, u32[]{:S(2)}) collective-permute-start(bf16[1024,1792]{0,1:T(8,128)(2,1)} %all-gather.4.cloned.1.call-done), channel_id=1, source_target_pairs={{0,1},{1,0},{2,3},{3,2},{4,5},{5,4},{6,7},{7,6},{8,9},{9,8},{10,11... | collective-permute-start | bytes 11010056 | tf_op jit(solution)/shard_map/ppermute | solution.py:175
  244.3 12.8 %collective-permute-start.10 = (bf16[1024,3840]{1,0:T(8,128)(2,1)}, bf16[1024,3840]{1,0:T(8,128)(2,1)}, u32[]{:S(2)}, u32[]{:S(2)}) collective-permute-start(bf16[1024,3840]{1,0:T(8,128)(2,1)} %all-gather.6.cloned.1.call-done), channel_id=1, source_target_pairs={{0,1},{1,0},{2,3},{3,2},{4,5},{5,4},{6,7},{7,6},{8,9},{9,8},{10,11... | collective-permute-start | bytes 23592968 | tf_op jit(solution)/shard_map/ppermute | solution.py:175
  244.8 303.0 %reduce-scatter.9.cloned.1.call-start = ((), (), s32[]{:S(2)}) async-start(), calls=%async_computation.10 | async-start | bytes 3276800 | tf_op jit(solution)/shard_map/reduce_scatter | solution.py:192
  386.1 13.3 %collective-permute-start.11 = (bf16[1024,3840]{1,0:T(8,128)(2,1)}, bf16[1024,3840]{1,0:T(8,128)(2,1)S(1)}, u32[]{:S(2)}, u32[]{:S(2)}) collective-permute-start(bf16[1024,3840]{1,0:T(8,128)(2,1)} %all-gather.8.cloned.1.call-done), channel_id=1, source_target_pairs={{0,1},{1,0},{2,3},{3,2},{4,5},{5,4},{6,7},{7,6},{8,9},{9,8},{10,11... | collective-permute-start | bytes 23592968 | tf_op jit(solution)/shard_map/ppermute | solution.py:175
  412.7 30.0 %collective-permute-start.15 = (bf16[1024,2560]{1,0:T(8,128)(2,1)}, bf16[1024,2560]{1,0:T(8,128)(2,1)}, u32[]{:S(2)}, u32[]{:S(2)}) collective-permute-start(bf16[1024,2560]{1,0:T(8,128)(2,1)} %convolution_convert_fusion.1), channel_id=1, source_target_pairs={{0,1},{1,0},{2,3},{3,2},{4,5},{5,4},{6,7},{7,6},{8,9},{9,8},{10,11... | collective-permute-start | bytes 15728648 | tf_op jit(solution)/shard_map/ppermute | solution.py:175
  416.1 151.3 %reduce-scatter.7.cloned.1.call-start = ((), (), s32[]{:S(2)}) async-start(), calls=%async_computation.9 | async-start | bytes 6553600 | tf_op jit(solution)/shard_map/reduce_scatter | solution.py:192
  433.2 16.0 %collective-permute-start.14 = (bf16[128,2048]{1,0:T(8,128)(2,1)}, bf16[128,2048]{1,0:T(8,128)(2,1)}, u32[]{:S(2)}, u32[]{:S(2)}) collective-permute-start(bf16[128,2048]{1,0:T(8,128)(2,1)} %get-tuple-element.250), channel_id=1, source_target_pairs={{0,6},{1,7},{2,4},{3,5},{4,2},{5,3},{6,0},{7,1},{8,14},{9,15},{10,... | collective-permute-start | bytes 1572872 | tf_op jit(solution)/shard_map/ppermute | solution.py:165
  434.3 25.2 %collective-permute-start.12 = (bf16[128,2048]{1,0:T(8,128)(2,1)}, bf16[128,2048]{1,0:T(8,128)(2,1)}, u32[]{:S(2)}, u32[]{:S(2)}) collective-permute-start(bf16[128,2048]{1,0:T(8,128)(2,1)} %get-tuple-element.251), channel_id=1, source_target_pairs={{0,2},{1,3},{2,0},{3,1},{4,6},{5,7},{6,4},{7,5},{8,10},{9,11},{10,... | collective-permute-start | bytes 1572872 | tf_op jit(solution)/shard_map/ppermute | solution.py:165
  434.7 24.9 %collective-permute-start.13 = (bf16[128,2048]{1,0:T(8,128)(2,1)}, bf16[128,2048]{1,0:T(8,128)(2,1)}, u32[]{:S(2)}, u32[]{:S(2)}) collective-permute-start(bf16[128,2048]{1,0:T(8,128)(2,1)} %get-tuple-element.252), channel_id=1, source_target_pairs={{0,4},{1,5},{2,6},{3,7},{4,0},{5,1},{6,2},{7,3},{8,12},{9,13},{10,... | collective-permute-start | bytes 1572872 | tf_op jit(solution)/shard_map/ppermute | solution.py:165
  459.6 162.9 %reduce-scatter.11.cloned.1.call-start = ((), (), s32[]{:S(2)}) async-start(), calls=%async_computation.11 | async-start | bytes 2293760 | tf_op jit(solution)/shard_map/reduce_scatter | solution.py:192
  466.9 14.1 %collective-permute-start.18 = (bf16[128,2048]{1,0:T(8,128)(2,1)S(1)}, bf16[128,2048]{1,0:T(8,128)(2,1)S(1)}, u32[]{:S(2)}, u32[]{:S(2)}) collective-permute-start(bf16[128,2048]{1,0:T(8,128)(2,1)S(1)} %get-tuple-element.230), channel_id=1, source_target_pairs={{0,6},{1,7},{2,4},{3,5},{4,2},{5,3},{6,0},{7,1},{8,14},{9,15},{10,... | collective-permute-start | bytes 1572872 | tf_op jit(solution)/shard_map/ppermute | solution.py:165
  468.0 23.2 %collective-permute-start.17 = (bf16[128,2048]{1,0:T(8,128)(2,1)S(1)}, bf16[128,2048]{1,0:T(8,128)(2,1)S(1)}, u32[]{:S(2)}, u32[]{:S(2)}) collective-permute-start(bf16[128,2048]{1,0:T(8,128)(2,1)S(1)} %get-tuple-element.230), channel_id=1, source_target_pairs={{0,4},{1,5},{2,6},{3,7},{4,0},{5,1},{6,2},{7,3},{8,12},{9,13},{10,... | collective-permute-start | bytes 1572872 | tf_op jit(solution)/shard_map/ppermute | solution.py:165
  468.4 24.6 %collective-permute-start.16 = (bf16[128,2048]{1,0:T(8,128)(2,1)S(1)}, bf16[128,2048]{1,0:T(8,128)(2,1)S(1)}, u32[]{:S(2)}, u32[]{:S(2)}) collective-permute-start(bf16[128,2048]{1,0:T(8,128)(2,1)S(1)} %get-tuple-element.230), channel_id=1, source_target_pairs={{0,2},{1,3},{2,0},{3,1},{4,6},{5,7},{6,4},{7,5},{8,10},{9,11},{10,... | collective-permute-start | bytes 1572872 | tf_op jit(solution)/shard_map/ppermute | solution.py:165
  506.8 9.1 %collective-permute-start.23 = (bf16[1024,576]{0,1:T(8,128)(2,1)S(1)}, bf16[1024,576]{0,1:T(8,128)(2,1)S(1)}, u32[]{:S(2)}, u32[]{:S(2)}) collective-permute-start(bf16[1024,576]{0,1:T(8,128)(2,1)S(1)} %convolution_convert_fusion.5), channel_id=1, source_target_pairs={{0,1},{1,0},{2,3},{3,2},{4,5},{5,4},{6,7},{7,6},{8,9},{9,8},{10,11... | collective-permute-start | bytes 3538952 | tf_op jit(solution)/shard_map/ppermute | solution.py:175
  507.8 7.6 collective-permute-start.22
  512.7 14.1 %collective-permute-start.21 = (bf16[128,2048]{1,0:T(8,128)(2,1)S(1)}, bf16[128,2048]{1,0:T(8,128)(2,1)S(1)}, u32[]{:S(2)}, u32[]{:S(2)}) collective-permute-start(bf16[128,2048]{1,0:T(8,128)(2,1)S(1)} %get-tuple-element.247), channel_id=1, source_target_pairs={{0,6},{1,7},{2,4},{3,5},{4,2},{5,3},{6,0},{7,1},{8,14},{9,15},{10,... | collective-permute-start | bytes 1572872 | tf_op jit(solution)/shard_map/ppermute | solution.py:165
  513.9 25.0 %collective-permute-start.19 = (bf16[128,2048]{1,0:T(8,128)(2,1)S(1)}, bf16[128,2048]{1,0:T(8,128)(2,1)S(1)}, u32[]{:S(2)}, u32[]{:S(2)}) collective-permute-start(bf16[128,2048]{1,0:T(8,128)(2,1)S(1)} %get-tuple-element.248), channel_id=1, source_target_pairs={{0,2},{1,3},{2,0},{3,1},{4,6},{5,7},{6,4},{7,5},{8,10},{9,11},{10,... | collective-permute-start | bytes 1572872 | tf_op jit(solution)/shard_map/ppermute | solution.py:165
  514.2 24.6 %collective-permute-start.20 = (bf16[128,2048]{1,0:T(8,128)(2,1)S(1)}, bf16[128,2048]{1,0:T(8,128)(2,1)S(1)}, u32[]{:S(2)}, u32[]{:S(2)}) collective-permute-start(bf16[128,2048]{1,0:T(8,128)(2,1)S(1)} %get-tuple-element.249), channel_id=1, source_target_pairs={{0,4},{1,5},{2,6},{3,7},{4,0},{5,1},{6,2},{7,3},{8,12},{9,13},{10,... | collective-permute-start | bytes 1572872 | tf_op jit(solution)/shard_map/ppermute | solution.py:165
  541.1 14.4 %collective-permute-start.26 = (bf16[128,2048]{1,0:T(8,128)(2,1)}, bf16[128,2048]{1,0:T(8,128)(2,1)}, u32[]{:S(2)}, u32[]{:S(2)}) collective-permute-start(bf16[128,2048]{1,0:T(8,128)(2,1)} %get-tuple-element.225), channel_id=1, source_target_pairs={{0,6},{1,7},{2,4},{3,5},{4,2},{5,3},{6,0},{7,1},{8,14},{9,15},{10,... | collective-permute-start | bytes 1572872 | tf_op jit(solution)/shard_map/ppermute | solution.py:165
  542.2 23.6 %collective-permute-start.25 = (bf16[128,2048]{1,0:T(8,128)(2,1)}, bf16[128,2048]{1,0:T(8,128)(2,1)}, u32[]{:S(2)}, u32[]{:S(2)}) collective-permute-start(bf16[128,2048]{1,0:T(8,128)(2,1)} %get-tuple-element.225), channel_id=1, source_target_pairs={{0,4},{1,5},{2,6},{3,7},{4,0},{5,1},{6,2},{7,3},{8,12},{9,13},{10,... | collective-permute-start | bytes 1572872 | tf_op jit(solution)/shard_map/ppermute | solution.py:165
  542.6 24.8 %collective-permute-start.24 = (bf16[128,2048]{1,0:T(8,128)(2,1)}, bf16[128,2048]{1,0:T(8,128)(2,1)}, u32[]{:S(2)}, u32[]{:S(2)}) collective-permute-start(bf16[128,2048]{1,0:T(8,128)(2,1)} %get-tuple-element.225), channel_id=1, source_target_pairs={{0,2},{1,3},{2,0},{3,1},{4,6},{5,7},{6,4},{7,5},{8,10},{9,11},{10,... | collective-permute-start | bytes 1572872 | tf_op jit(solution)/shard_map/ppermute | solution.py:165
  547.8 112.8 %reduce-scatter.13.cloned.1.call-start = ((), (), s32[]{:S(2)}) async-start(), calls=%async_computation.12 | async-start | bytes 3276800 | tf_op jit(solution)/shard_map/reduce_scatter | solution.py:192
  568.9 26.5 %collective-permute-start.28 = (bf16[256,3840]{1,0:T(8,128)(2,1)S(1)}, bf16[256,3840]{1,0:T(8,128)(2,1)S(1)}, u32[]{:S(2)}, u32[]{:S(2)}) collective-permute-start(bf16[256,3840]{1,0:T(8,128)(2,1)S(1)} %constant_dynamic-update-slice_fusion.4), channel_id=1, source_target_pairs={{1,4},{3,6},{4,1},{6,3},{9,12},{11,14},{12,9},{14,11},{17,20},{19,... | collective-permute-start | bytes 5898248 | tf_op jit(solution)/shard_map/ppermute | solution.py:168
  574.8 22.0 %collective-permute-start.29 = (bf16[1024,1280]{1,0:T(8,128)(2,1)S(1)}, bf16[1024,1280]{1,0:T(8,128)(2,1)S(1)}, u32[]{:S(2)}, u32[]{:S(2)}) collective-permute-start(bf16[1024,1280]{1,0:T(8,128)(2,1)S(1)} %convolution_convert_fusion.2), channel_id=1, source_target_pairs={{0,1},{1,0},{2,3},{3,2},{4,5},{5,4},{6,7},{7,6},{8,9},{9,8},{10,11... | collective-permute-start | bytes 7864328 | tf_op jit(solution)/shard_map/ppermute | solution.py:175
  607.4 20.4 %collective-permute-start.33 = (bf16[1024,2560]{1,0:T(8,128)(2,1)}, bf16[1024,2560]{1,0:T(8,128)(2,1)}, u32[]{:S(2)}, u32[]{:S(2)}) collective-permute-start(bf16[1024,2560]{1,0:T(8,128)(2,1)} %convolution_convert_fusion), channel_id=1, source_target_pairs={{0,1},{1,0},{2,3},{3,2},{4,5},{5,4},{6,7},{7,6},{8,9},{9,8},{10,11... | collective-permute-start | bytes 15728648 | tf_op jit(solution)/shard_map/ppermute | solution.py:175
  607.6 165.1 %reduce-scatter.17.cloned.1.call-start = ((), (), s32[]{:S(2)}) async-start(), calls=%async_computation.14 | async-start | bytes 6553600 | tf_op jit(solution)/shard_map/reduce_scatter | solution.py:192
  625.2 14.5 %collective-permute-start.32 = (bf16[128,2048]{1,0:T(8,128)(2,1)}, bf16[128,2048]{1,0:T(8,128)(2,1)S(1)}, u32[]{:S(2)}, u32[]{:S(2)}) collective-permute-start(bf16[128,2048]{1,0:T(8,128)(2,1)} %get-tuple-element.244), channel_id=1, source_target_pairs={{0,6},{1,7},{2,4},{3,5},{4,2},{5,3},{6,0},{7,1},{8,14},{9,15},{10,... | collective-permute-start | bytes 1572872 | tf_op jit(solution)/shard_map/ppermute | solution.py:165
  625.6 24.1 %collective-permute-start.31 = (bf16[128,2048]{1,0:T(8,128)(2,1)}, bf16[128,2048]{1,0:T(8,128)(2,1)S(1)}, u32[]{:S(2)}, u32[]{:S(2)}) collective-permute-start(bf16[128,2048]{1,0:T(8,128)(2,1)} %get-tuple-element.245), channel_id=1, source_target_pairs={{0,4},{1,5},{2,6},{3,7},{4,0},{5,1},{6,2},{7,3},{8,12},{9,13},{10,... | collective-permute-start | bytes 1572872 | tf_op jit(solution)/shard_map/ppermute | solution.py:165
  626.2 25.2 %collective-permute-start.30 = (bf16[128,2048]{1,0:T(8,128)(2,1)}, bf16[128,2048]{1,0:T(8,128)(2,1)}, u32[]{:S(2)}, u32[]{:S(2)}) collective-permute-start(bf16[128,2048]{1,0:T(8,128)(2,1)} %get-tuple-element.246), channel_id=1, source_target_pairs={{0,2},{1,3},{2,0},{3,1},{4,6},{5,7},{6,4},{7,5},{8,10},{9,11},{10,... | collective-permute-start | bytes 1572872 | tf_op jit(solution)/shard_map/ppermute | solution.py:165
  653.0 11.1 %collective-permute-start.40 = (bf16[256,256]{0,1:T(8,128)(2,1)}, bf16[256,256]{0,1:T(8,128)(2,1)}, u32[]{:S(2)}, u32[]{:S(2)}) collective-permute-start(bf16[256,256]{0,1:T(8,128)(2,1)} %slice.805), channel_id=1, source_target_pairs={{0,3},{1,7},{2,1},{3,5},{4,2},{5,6},{6,0},{7,4},{8,11},{9,15},{10,... | collective-permute-start | bytes 393224 | tf_op jit(solution)/shard_map/ppermute | solution.py:172
  653.5 12.9 %collective-permute-start.39 = (bf16[256,256]{0,1:T(8,128)(2,1)}, bf16[256,256]{0,1:T(8,128)(2,1)}, u32[]{:S(2)}, u32[]{:S(2)}) collective-permute-start(bf16[256,256]{0,1:T(8,128)(2,1)} %slice.805), channel_id=1, source_target_pairs={{0,2},{1,6},{2,0},{3,4},{4,3},{5,7},{6,1},{7,5},{8,10},{9,14},{10,... | collective-permute-start | bytes 393224 | tf_op jit(solution)/shard_map/ppermute | solution.py:172
  656.1 12.7 %collective-permute-start.38 = (bf16[256,256]{0,1:T(8,128)(2,1)}, bf16[256,256]{0,1:T(8,128)(2,1)}, u32[]{:S(2)}, u32[]{:S(2)}) collective-permute-start(bf16[256,256]{0,1:T(8,128)(2,1)} %slice.805), channel_id=1, source_target_pairs={{0,1},{1,5},{2,3},{3,7},{4,0},{5,4},{6,2},{7,6},{8,9},{9,13},{10,1... | collective-permute-start | bytes 393224 | tf_op jit(solution)/shard_map/ppermute | solution.py:172
  656.1 13.6 %collective-permute-start.37 = (bf16[256,896]{0,1:T(8,128)(2,1)}, bf16[256,896]{0,1:T(8,128)(2,1)}, u32[]{:S(2)}, u32[]{:S(2)}) collective-permute-start(bf16[256,896]{0,1:T(8,128)(2,1)} %reduce-scatter.11.cloned.1.call-done), channel_id=1, source_target_pairs={{1,4},{3,6},{4,1},{6,3},{9,12},{11,14},{12,9},{14,11},{17,20},{19,... | collective-permute-start | bytes 1376264 | tf_op jit(solution)/shard_map/ppermute | solution.py:168
  660.6 145.8 %reduce-scatter.15.cloned.1.call-start = ((), (), s32[]{:S(2)}) async-start(), calls=%async_computation.13 | async-start | bytes 2293760 | tf_op jit(solution)/shard_map/reduce_scatter | solution.py:192
  663.3 15.1 %collective-permute-start.36 = (bf16[128,2048]{1,0:T(8,128)(2,1)S(1)}, bf16[128,2048]{1,0:T(8,128)(2,1)S(1)}, u32[]{:S(2)}, u32[]{:S(2)}) collective-permute-start(bf16[128,2048]{1,0:T(8,128)(2,1)S(1)} %get-tuple-element.223), channel_id=1, source_target_pairs={{0,6},{1,7},{2,4},{3,5},{4,2},{5,3},{6,0},{7,1},{8,14},{9,15},{10,... | collective-permute-start | bytes 1572872 | tf_op jit(solution)/shard_map/ppermute | solution.py:165
  664.1 24.4 %collective-permute-start.35 = (bf16[128,2048]{1,0:T(8,128)(2,1)S(1)}, bf16[128,2048]{1,0:T(8,128)(2,1)S(1)}, u32[]{:S(2)}, u32[]{:S(2)}) collective-permute-start(bf16[128,2048]{1,0:T(8,128)(2,1)S(1)} %get-tuple-element.223), channel_id=1, source_target_pairs={{0,4},{1,5},{2,6},{3,7},{4,0},{5,1},{6,2},{7,3},{8,12},{9,13},{10,... | collective-permute-start | bytes 1572872 | tf_op jit(solution)/shard_map/ppermute | solution.py:165
  666.4 23.1 %collective-permute-start.34 = (bf16[128,2048]{1,0:T(8,128)(2,1)S(1)}, bf16[128,2048]{1,0:T(8,128)(2,1)S(1)}, u32[]{:S(2)}, u32[]{:S(2)}) collective-permute-start(bf16[128,2048]{1,0:T(8,128)(2,1)S(1)} %get-tuple-element.223), channel_id=1, source_target_pairs={{0,2},{1,3},{2,0},{3,1},{4,6},{5,7},{6,4},{7,5},{8,10},{9,11},{10,... | collective-permute-start | bytes 1572872 | tf_op jit(solution)/shard_map/ppermute | solution.py:165
  703.0 10.0 %collective-permute-start.45 = (bf16[1024,576]{0,1:T(8,128)(2,1)S(1)}, bf16[1024,576]{0,1:T(8,128)(2,1)S(1)}, u32[]{:S(2)}, u32[]{:S(2)}) collective-permute-start(bf16[1024,576]{0,1:T(8,128)(2,1)S(1)} %convolution_convert_fusion.4), channel_id=1, source_target_pairs={{0,1},{1,0},{2,3},{3,2},{4,5},{5,4},{6,7},{7,6},{8,9},{9,8},{10,11... | collective-permute-start | bytes 3538952 | tf_op jit(solution)/shard_map/ppermute | solution.py:175
  708.9 14.1 %collective-permute-start.43 = (bf16[128,2048]{1,0:T(8,128)(2,1)S(1)}, bf16[128,2048]{1,0:T(8,128)(2,1)S(1)}, u32[]{:S(2)}, u32[]{:S(2)}) collective-permute-start(bf16[128,2048]{1,0:T(8,128)(2,1)S(1)} %get-tuple-element.241), channel_id=1, source_target_pairs={{0,6},{1,7},{2,4},{3,5},{4,2},{5,3},{6,0},{7,1},{8,14},{9,15},{10,... | collective-permute-start | bytes 1572872 | tf_op jit(solution)/shard_map/ppermute | solution.py:165
  709.5 24.8 %collective-permute-start.41 = (bf16[128,2048]{1,0:T(8,128)(2,1)S(1)}, bf16[128,2048]{1,0:T(8,128)(2,1)S(1)}, u32[]{:S(2)}, u32[]{:S(2)}) collective-permute-start(bf16[128,2048]{1,0:T(8,128)(2,1)S(1)} %get-tuple-element.242), channel_id=1, source_target_pairs={{0,2},{1,3},{2,0},{3,1},{4,6},{5,7},{6,4},{7,5},{8,10},{9,11},{10,... | collective-permute-start | bytes 1572872 | tf_op jit(solution)/shard_map/ppermute | solution.py:165
  709.9 24.4 %collective-permute-start.42 = (bf16[128,2048]{1,0:T(8,128)(2,1)S(1)}, bf16[128,2048]{1,0:T(8,128)(2,1)S(1)}, u32[]{:S(2)}, u32[]{:S(2)}) collective-permute-start(bf16[128,2048]{1,0:T(8,128)(2,1)S(1)} %get-tuple-element.243), channel_id=1, source_target_pairs={{0,4},{1,5},{2,6},{3,7},{4,0},{5,1},{6,2},{7,3},{8,12},{9,13},{10,... | collective-permute-start | bytes 1572872 | tf_op jit(solution)/shard_map/ppermute | solution.py:165
  738.1 32.0 %collective-permute-start.49 = (bf16[128,2048]{1,0:T(8,128)(2,1)}, bf16[128,2048]{1,0:T(8,128)(2,1)}, u32[]{:S(2)}, u32[]{:S(2)}) collective-permute-start(bf16[128,2048]{1,0:T(8,128)(2,1)} %get-tuple-element.238), channel_id=1, source_target_pairs={{0,6},{1,7},{2,4},{3,5},{4,2},{5,3},{6,0},{7,1},{8,14},{9,15},{10,... | collective-permute-start | bytes 1572872 | tf_op jit(solution)/shard_map/ppermute | solution.py:165
  739.4 30.7 %collective-permute-start.48 = (bf16[128,2048]{1,0:T(8,128)(2,1)}, bf16[128,2048]{1,0:T(8,128)(2,1)}, u32[]{:S(2)}, u32[]{:S(2)}) collective-permute-start(bf16[128,2048]{1,0:T(8,128)(2,1)} %get-tuple-element.239), channel_id=1, source_target_pairs={{0,4},{1,5},{2,6},{3,7},{4,0},{5,1},{6,2},{7,3},{8,12},{9,13},{10,... | collective-permute-start | bytes 1572872 | tf_op jit(solution)/shard_map/ppermute | solution.py:165
  740.4 29.7 %collective-permute-start.47 = (bf16[128,2048]{1,0:T(8,128)(2,1)}, bf16[128,2048]{1,0:T(8,128)(2,1)}, u32[]{:S(2)}, u32[]{:S(2)}) collective-permute-start(bf16[128,2048]{1,0:T(8,128)(2,1)} %get-tuple-element.240), channel_id=1, source_target_pairs={{0,2},{1,3},{2,0},{3,1},{4,6},{5,7},{6,4},{7,5},{8,10},{9,11},{10,... | collective-permute-start | bytes 1572872 | tf_op jit(solution)/shard_map/ppermute | solution.py:165
  741.0 22.6 %collective-permute-start.55 = (f32[2,4224]{1,0:T(2,128)S(1)}, f32[2,4224]{1,0:T(2,128)S(1)}, u32[]{:S(2)}, u32[]{:S(2)}) collective-permute-start(f32[2,4224]{1,0:T(2,128)S(1)} %fusion.238), channel_id=1, source_target_pairs={{0,4},{1,5},{2,6},{3,7},{4,0},{5,1},{6,2},{7,3},{8,12},{9,13},{10,... | collective-permute-start | bytes 101384 | tf_op jit(solution)/shard_map/ppermute | solution.py:179
  767.9 14.8 %collective-permute-start.52 = (bf16[128,2048]{1,0:T(8,128)(2,1)}, bf16[128,2048]{1,0:T(8,128)(2,1)}, u32[]{:S(2)}, u32[]{:S(2)}) collective-permute-start(bf16[128,2048]{1,0:T(8,128)(2,1)} %broadcast_select_fusion.5), channel_id=1, source_target_pairs={{0,2},{1,3},{2,0},{3,1},{4,6},{5,7},{6,4},{7,5},{8,10},{9,11},{10,... | collective-permute-start | bytes 1572872 | tf_op jit(solution)/shard_map/ppermute | solution.py:165
  769.9 12.0 %collective-permute-start.58 = (f32[2,4224]{1,0:T(2,128)}, f32[2,4224]{1,0:T(2,128)}, u32[]{:S(2)}, u32[]{:S(2)}) collective-permute-start(f32[2,4224]{1,0:T(2,128)} %add.585), channel_id=1, source_target_pairs={{0,16},{8,24},{16,0},{24,8},{1,17},{9,25},{17,1},{25,9},{2,18},{10... | collective-permute-start | bytes 101384 | tf_op jit(solution)/shard_map/ppermute | solution.py:182
  775.6 26.5 %collective-permute-start.46 = (bf16[256,3840]{1,0:T(8,128)(2,1)S(1)}, bf16[256,3840]{1,0:T(8,128)(2,1)S(1)}, u32[]{:S(2)}, u32[]{:S(2)}) collective-permute-start(bf16[256,3840]{1,0:T(8,128)(2,1)S(1)} %constant_dynamic-update-slice_fusion.6), channel_id=1, source_target_pairs={{1,4},{3,6},{4,1},{6,3},{9,12},{11,14},{12,9},{14,11},{17,20},{19,... | collective-permute-start | bytes 5898248 | tf_op jit(solution)/shard_map/ppermute | solution.py:168
  779.6 13.9 %collective-permute-start.50 = (bf16[128,2048]{1,0:T(8,128)(2,1)S(1)}, bf16[128,2048]{1,0:T(8,128)(2,1)S(1)}, u32[]{:S(2)}, u32[]{:S(2)}) collective-permute-start(bf16[128,2048]{1,0:T(8,128)(2,1)S(1)} %broadcast_select_fusion.6), channel_id=1, source_target_pairs={{0,2},{1,3},{2,0},{3,1},{4,6},{5,7},{6,4},{7,5},{8,10},{9,11},{10,... | collective-permute-start | bytes 1572872 | tf_op jit(solution)/shard_map/ppermute | solution.py:165
  784.4 19.7 %collective-permute-start.53 = (bf16[256,2048]{1,0:T(8,128)(2,1)S(1)}, bf16[256,2048]{1,0:T(8,128)(2,1)S(1)}, u32[]{:S(2)}, u32[]{:S(2)}) collective-permute-start(bf16[256,2048]{1,0:T(8,128)(2,1)S(1)} %maximum_select_fusion.8), channel_id=1, source_target_pairs={{0,1},{1,0},{2,3},{3,2},{4,5},{5,4},{6,7},{7,6},{8,9},{9,8},{10,11... | collective-permute-start | bytes 3145736 | tf_op jit(solution)/shard_map/ppermute | solution.py:175
  793.7 11.4 %collective-permute-start.51 = (bf16[256,2048]{1,0:T(8,128)(2,1)S(1)}, bf16[256,2048]{1,0:T(8,128)(2,1)}, u32[]{:S(2)}, u32[]{:S(2)}) collective-permute-start(bf16[256,2048]{1,0:T(8,128)(2,1)S(1)} %maximum_select_fusion.7), channel_id=1, source_target_pairs={{0,1},{1,0},{2,3},{3,2},{4,5},{5,4},{6,7},{7,6},{8,9},{9,8},{10,11... | collective-permute-start | bytes 3145736 | tf_op jit(solution)/shard_map/ppermute | solution.py:175
  808.1 18.9 %collective-permute-start.62 = (bf16[256,256]{0,1:T(8,128)(2,1)}, bf16[256,256]{0,1:T(8,128)(2,1)}, u32[]{:S(2)}, u32[]{:S(2)}) collective-permute-start(bf16[256,256]{0,1:T(8,128)(2,1)} %slice.877), channel_id=1, source_target_pairs={{0,3},{1,7},{2,1},{3,5},{4,2},{5,6},{6,0},{7,4},{8,11},{9,15},{10,... | collective-permute-start | bytes 393224 | tf_op jit(solution)/shard_map/ppermute | solution.py:172
  810.2 17.7 %collective-permute-start.61 = (bf16[256,256]{0,1:T(8,128)(2,1)}, bf16[256,256]{0,1:T(8,128)(2,1)}, u32[]{:S(2)}, u32[]{:S(2)}) collective-permute-start(bf16[256,256]{0,1:T(8,128)(2,1)} %slice.877), channel_id=1, source_target_pairs={{0,2},{1,6},{2,0},{3,4},{4,3},{5,7},{6,1},{7,5},{8,10},{9,14},{10,... | collective-permute-start | bytes 393224 | tf_op jit(solution)/shard_map/ppermute | solution.py:172
  811.5 17.4 %collective-permute-start.60 = (bf16[256,256]{0,1:T(8,128)(2,1)}, bf16[256,256]{0,1:T(8,128)(2,1)}, u32[]{:S(2)}, u32[]{:S(2)}) collective-permute-start(bf16[256,256]{0,1:T(8,128)(2,1)} %slice.877), channel_id=1, source_target_pairs={{0,1},{1,5},{2,3},{3,7},{4,0},{5,4},{6,2},{7,6},{8,9},{9,13},{10,1... | collective-permute-start | bytes 393224 | tf_op jit(solution)/shard_map/ppermute | solution.py:172
  811.5 18.3 %collective-permute-start.59 = (bf16[256,896]{0,1:T(8,128)(2,1)}, bf16[256,896]{0,1:T(8,128)(2,1)S(1)}, u32[]{:S(2)}, u32[]{:S(2)}) collective-permute-start(bf16[256,896]{0,1:T(8,128)(2,1)} %reduce-scatter.15.cloned.1.call-done), channel_id=1, source_target_pairs={{1,4},{3,6},{4,1},{6,3},{9,12},{11,14},{12,9},{14,11},{17,20},{19,... | collective-permute-start | bytes 1376264 | tf_op jit(solution)/shard_map/ppermute | solution.py:168
  (186 other events, 1259.3 us)
Sparse Core Ops, SparseCore 0:
  29.1 73.5 all-gather.3
  104.9 139.3 all-gather.5
  246.4 139.2 all-gather.7
  416.2 48.8 reduce-scatter.8
  467.2 93.6 reduce-scatter.6
  563.1 39.6 reduce-scatter.10
  607.7 49.2 reduce-scatter.12
  660.7 92.1 reduce-scatter.16
  768.4 37.9 reduce-scatter.14

commit v6 on v5

--- a/solution.py
+++ b/solution.py
@@ -574,10 +574,17 @@
         grad_qkv = jnp.concatenate([grad_queries, grad_keys, grad_values], axis=1)
         if layer + 1 < LAYERS:
             attn_high = finish(results[layer + 1][0])
-            grad_qkv, attn_high = lax.optimization_barrier((grad_qkv, attn_high))
+            down_low = plan.swap(results[layer][2])
+            grad_qkv, attn_high, down_low = lax.optimization_barrier(
+                (grad_qkv, attn_high, down_low)
+            )
         term_qkv = plan.weight_term(normed, grad_qkv)
-        summed_in, (term_o, term_qkv) = plan.gather_sum(
-            plan.out_of(grad_qkv, w_qkv), (term_o, term_qkv)
+        beside = [term_o, term_qkv]
+        if layer + 1 < LAYERS:
+            downs = [down_low.T, ffn_high[:, 2 * hidden_units :].T]
+            beside.append(jnp.stack(downs).astype(f32))
+        summed_in, (term_o, term_qkv, *finished) = plan.gather_sum(
+            plan.out_of(grad_qkv, w_qkv), beside
         )
         scatter_next(layer, 0, jnp.concatenate([term_qkv, term_o], axis=1))
         grad_g_attn = jnp.sum(summed_in * state * scale_in, axis=0)
@@ -594,10 +601,10 @@
     grad_input = (grad_input, plan.core(grad_input))
     all_gains = plan.total(jnp.stack(gain_grads))
 
-    ffn_low = plan.swap(jnp.concatenate([results[0][1], results[0][2]], axis=1))
-    grad_down = jnp.stack([ffn[:, 2 * hidden_units :].T for ffn in (ffn_low, ffn_high)])
+    ffn_low = plan.swap(results[0][1])
+    grad_down = finished[0]
     attn_low, ffn_low, grad_down, output, grad_input, all_gains = lax.optimization_barrier(
-        (results[0][0], ffn_low, grad_down.astype(f32), output, grad_input, all_gains)
+        (results[0][0], ffn_low, grad_down, output, grad_input, all_gains)
     )
     grad_gate = jnp.stack([ffn[:, :hidden_units] for ffn in (ffn_low, ffn_high)])
     grad_up = jnp.stack([ffn[:, hidden_units : 2 * hidden_units] for ffn in (ffn_low, ffn_high)])

time: 849 us -> 853 us (level)
  waiting for transfers between devices: 277 us -> 263 us
  other arithmetic: 98.4 us -> 111 us
    ppermute x3, waiting for transfers between devices: 21.3 us -> 2.1 us  [total(): value = value + lax.ppermute(value, ('ctx', 'tensor'), pairs)]
    ppermute x28, waiting for transfers between devices: 141 us -> 153 us  [peer(): return lax.ppermute(value, ('ctx', 'tensor'), self.peers[j])]
    ppermute x7 -> x8, waiting for transfers between devices: 72 us -> 63.6 us  [swap(): moved = lax.ppermute(value, ('ctx', 'tensor'), self.swap_pairs)]
    ppermute x7 -> x8, starting transfers between devices: 27.3 us -> 29.7 us  [swap(): moved = lax.ppermute(value, ('ctx', 'tensor'), self.swap_pairs)]
    unnamed x410 -> x387, local copies, waits for them, and re-layouts: 28.7 us -> 29 us
  transfers between devices with their start and end apart: 72 -> 73, of which waited for: 31 -> 33; matrix products, arithmetic and copies ran while one was open for 35% -> 36% of each run, Pallas kernels for 18% -> 17%
where the time goes in v6:
time: 853 us; the launch traced here: 844 us
  waiting for transfers between devices  263 us (31%)
  matrix products  159 us (19%)
  Pallas kernels  147 us (17%)
  other arithmetic  111 us (13%)
  starting transfers between devices  77.5 us (9%)
  local copies, waits for them, and re-layouts  68.2 us (8%)
  between operations  18 us (2%)
    ppermute x28, waiting for transfers between devices, peer(): return lax.ppermute(value, ('ctx', 'tensor'), self.peers[j])  153 us
    pallas_call x3, Pallas kernels, join(): pl.pallas_call(join_kernel, out_shape=(jax.ShapeDtypeStruct((rows, width)...  147 us
    dot_general x52, matrix products, product(): lax.dot_general(left_side, right_side, (contract, ((), ())), preferred_el...  144 us
    ppermute x8, waiting for transfers between devices, swap(): moved = lax.ppermute(value, ('ctx', 'tensor'), self.swap_pairs)  63.6 us
    all_gather x3, waiting for transfers between devices, local(): owned.append(lax.all_gather(shard, 'dp', axis=0, tiled=True))  31.5 us
    ppermute x8, starting transfers between devices, swap(): moved = lax.ppermute(value, ('ctx', 'tensor'), self.swap_pairs)  29.7 us
    unnamed x387, local copies, waits for them, and re-layouts  29 us
    ppermute x28, starting transfers between devices, peer(): return lax.ppermute(value, ('ctx', 'tensor'), self.peers[j])  23.6 us
  transfers between devices with their start and end apart: 73, of which 33 were waited for; matrix products, arithmetic and copies ran while one was open for 36% of the time, Pallas kernels for 17%

profile of v6, /device:TPU:1, one launch (start us, length us, event | category | flops | bytes accessed | tf_op | source)
XLA Modules:
  0.0 844.4 jit_solution(6790638186803080979)
XLA Ops:
  12.4 4.5 collective-permute-start
  18.1 9.8 %collective-permute-done = bf16[256,1792]{0,1:T(8,128)(2,1)S(1)} collective-permute-done((bf16[256,1792]{0,1:T(8,128)(2,1)S(1)}, bf16[256,1792]{0,1:T(8,128)(2,1)S(1)}, u32[]{:S(2)}, u32[]{:S(2)}) %collective-permute-start) | collective-permute-done | bytes 917536 | tf_op jit(solution)/shard_map/ppermute | solution.py:168
  31.9 2.8 copy.61
  39.9 3.6 collective-permute-start.8
  45.0 3.9 copy.66
  53.8 23.8 %collective-permute-done.8 = bf16[256,3840]{1,0:T(8,128)(2,1)} collective-permute-done((bf16[256,3840]{1,0:T(8,128)(2,1)}, bf16[256,3840]{1,0:T(8,128)(2,1)}, u32[]{:S(2)}, u32[]{:S(2)}) %collective-permute-start.8) | collective-permute-done | bytes 1966112 | tf_op jit(solution)/shard_map/ppermute | solution.py:168
  77.7 3.3 broadcast_select_fusion.2
  81.2 3.3 collective-permute-start.3
  97.4 7.6 collective-permute-start.9
  109.7 7.8 collective-permute-done.6
  117.5 3.3 maximum_select_fusion
  122.7 18.7 %collective-permute-done.9 = bf16[256,3840]{1,0:T(8,128)(2,1)} collective-permute-done((bf16[256,3840]{1,0:T(8,128)(2,1)}, bf16[256,3840]{1,0:T(8,128)(2,1)}, u32[]{:S(2)}, u32[]{:S(2)}) %collective-permute-start.9) | collective-permute-done | bytes 1966112 | tf_op jit(solution)/shard_map/ppermute | solution.py:168
  141.4 3.0 broadcast_select_fusion.1
  161.1 50.3 %join.3 = (f32[128,2048]{1,0:T(8,128)S(1)}, bf16[512,2048]{1,0:T(8,128)(2,1)S(1)}) custom-call(bf16[512,2048]{1,0:T(8,128)(2,1)S(1)} %pad_maximum_fusion.2.terms, f32[128,2048]{1,0:T(8,128)S(1)} %slice.911.state, f32[1,2048]{1,0:T(1,128)S(1)} %get-tuple-element.365.gain), custom_call_target="tpu_custom_call" | custom-call | flops 1000 | bytes 1000 | tf_op jit(solution)/shard_map/join/pallas_call | solution.py:112
  212.8 31.5 %all-gather.6.cloned.1.call-done = bf16[1024,3840]{1,0:T(8,128)(2,1)} async-done(((bf16[256,3840]{1,0:T(8,128)(2,1)}), bf16[1024,3840]{1,0:T(8,128)(2,1)}) %all-gather.6.cloned.1.call-update) | async-done | bytes 7864336 | tf_op jit(solution)/shard_map/all_gather | solution.py:326
  245.0 3.7 fusion.21
  248.7 3.3 fusion.24
  252.0 5.1 collective-permute-done.10
  257.1 3.5 convolution_add_fusion.5
  260.6 5.8 multiply_convert_fusion.8
  266.4 3.8 fusion.61
  270.1 3.3 fusion.67
  273.6 48.9 %join.4 = (f32[128,2048]{1,0:T(8,128)S(1)}, bf16[512,2048]{1,0:T(8,128)(2,1)S(1)}) custom-call(bf16[512,2048]{1,0:T(8,128)(2,1)S(1)} %pad_maximum_fusion.3.terms, f32[128,2048]{1,0:T(8,128)S(1)} %get-tuple-element.103.state, f32[1,2048]{1,0:T(1,128)S(1)} %get-tuple-element.366.gain), custom_call_target="tpu_custom_call" | custom-call | flops 1000 | bytes 1000 | tf_op jit(solution)/shard_map/join/pallas_call | solution.py:112
  336.4 48.3 %join.5 = (f32[128,2048]{1,0:T(8,128)S(1)}, bf16[512,2048]{1,0:T(8,128)(2,1)S(1)}) custom-call(bf16[512,2048]{1,0:T(8,128)(2,1)S(1)} %pad_maximum_fusion.4.terms, f32[128,2048]{1,0:T(8,128)S(1)} %get-tuple-element.105.state, f32[1,2048]{1,0:T(1,128)S(1)} %get-tuple-element.364.gain), custom_call_target="tpu_custom_call" | custom-call | flops 1000 | bytes 1000 | tf_op jit(solution)/shard_map/join/pallas_call | solution.py:112
  387.2 3.7 fusion.17
  390.9 3.4 fusion.19
  394.4 3.3 fusion.42
  402.5 3.2 multiply_convert_fusion.3
  407.8 4.9 convolution_convert_fusion.1
  412.9 3.1 add_convert_fusion.3
  423.6 5.5 fusion.49
  429.1 2.9 fusion.55
  436.0 3.3 fusion.64
  443.2 6.6 add_convert_fusion.1
  449.8 9.8 %collective-permute-done.12 = bf16[128,2048]{1,0:T(8,128)(2,1)} collective-permute-done((bf16[128,2048]{1,0:T(8,128)(2,1)}, bf16[128,2048]{1,0:T(8,128)(2,1)}, u32[]{:S(2)}, u32[]{:S(2)}) %collective-permute-start.12) | collective-permute-done | bytes 524320 | tf_op jit(solution)/shard_map/ppermute | solution.py:165
  472.9 4.7 collective-permute-done.18
  477.6 10.4 %collective-permute-done.17 = bf16[128,2048]{1,0:T(8,128)(2,1)S(1)} collective-permute-done((bf16[128,2048]{1,0:T(8,128)(2,1)S(1)}, bf16[128,2048]{1,0:T(8,128)(2,1)S(1)}, u32[]{:S(2)}, u32[]{:S(2)}) %collective-permute-start.17) | collective-permute-done | bytes 524320 | tf_op jit(solution)/shard_map/ppermute | solution.py:165
  514.1 9.7 %collective-permute-done.21 = bf16[128,2048]{1,0:T(8,128)(2,1)S(1)} collective-permute-done((bf16[128,2048]{1,0:T(8,128)(2,1)S(1)}, bf16[128,2048]{1,0:T(8,128)(2,1)S(1)}, u32[]{:S(2)}, u32[]{:S(2)}) %collective-permute-start.21) | collective-permute-done | bytes 524320 | tf_op jit(solution)/shard_map/ppermute | solution.py:165
  523.8 12.0 %collective-permute-done.19 = bf16[128,2048]{1,0:T(8,128)(2,1)S(1)} collective-permute-done((bf16[128,2048]{1,0:T(8,128)(2,1)S(1)}, bf16[128,2048]{1,0:T(8,128)(2,1)S(1)}, u32[]{:S(2)}, u32[]{:S(2)}) %collective-permute-start.19) | collective-permute-done | bytes 524320 | tf_op jit(solution)/shard_map/ppermute | solution.py:165
  544.7 7.6 collective-permute-done.26
  552.3 10.1 %collective-permute-done.25 = bf16[128,2048]{1,0:T(8,128)(2,1)} collective-permute-done((bf16[128,2048]{1,0:T(8,128)(2,1)}, bf16[128,2048]{1,0:T(8,128)(2,1)}, u32[]{:S(2)}, u32[]{:S(2)}) %collective-permute-start.25) | collective-permute-done | bytes 524320 | tf_op jit(solution)/shard_map/ppermute | solution.py:165
  571.8 3.4 fusion.44
  575.2 4.1 multiply_convert_fusion.5
  580.9 11.3 %collective-permute-done.28 = bf16[256,3840]{1,0:T(8,128)(2,1)S(1)} collective-permute-done((bf16[256,3840]{1,0:T(8,128)(2,1)S(1)}, bf16[256,3840]{1,0:T(8,128)(2,1)S(1)}, u32[]{:S(2)}, u32[]{:S(2)}) %collective-permute-start.28) | collective-permute-done | bytes 1966112 | tf_op jit(solution)/shard_map/ppermute | solution.py:168
  593.7 3.1 add_convert_fusion.2
  596.8 7.4 convolution_convert_fusion
  606.1 6.3 fusion.52
  612.5 5.4 fusion.58
  626.1 6.5 add_convert_fusion
  632.6 3.7 collective-permute-done.32
  636.3 10.6 %collective-permute-done.31 = bf16[128,2048]{1,0:T(8,128)(2,1)S(1)} collective-permute-done((bf16[128,2048]{1,0:T(8,128)(2,1)}, bf16[128,2048]{1,0:T(8,128)(2,1)S(1)}, u32[]{:S(2)}, u32[]{:S(2)}) %collective-permute-start.31) | collective-permute-done | bytes 524320 | tf_op jit(solution)/shard_map/ppermute | solution.py:165
  666.7 4.0 collective-permute-start.41
  681.8 3.7 collective-permute-done.35
  714.3 8.3 collective-permute-done.44
  722.6 11.9 %collective-permute-done.42 = bf16[128,2048]{1,0:T(8,128)(2,1)} collective-permute-done((bf16[128,2048]{1,0:T(8,128)(2,1)S(1)}, bf16[128,2048]{1,0:T(8,128)(2,1)}, u32[]{:S(2)}, u32[]{:S(2)}) %collective-permute-start.42) | collective-permute-done | bytes 524320 | tf_op jit(solution)/shard_map/ppermute | solution.py:165
  747.8 9.3 %collective-permute-done.50 = bf16[128,2048]{1,0:T(8,128)(2,1)} collective-permute-done((bf16[128,2048]{1,0:T(8,128)(2,1)}, bf16[128,2048]{1,0:T(8,128)(2,1)}, u32[]{:S(2)}, u32[]{:S(2)}) %collective-permute-start.50) | collective-permute-done | bytes 524320 | tf_op jit(solution)/shard_map/ppermute | solution.py:165
  757.1 10.9 %collective-permute-done.49 = bf16[128,2048]{1,0:T(8,128)(2,1)} collective-permute-done((bf16[128,2048]{1,0:T(8,128)(2,1)}, bf16[128,2048]{1,0:T(8,128)(2,1)}, u32[]{:S(2)}, u32[]{:S(2)}) %collective-permute-start.49) | collective-permute-done | bytes 524320 | tf_op jit(solution)/shard_map/ppermute | solution.py:165
  772.7 8.0 collective-permute-done.53
  783.3 2.8 collective-permute-start.47
  786.1 5.8 collective-permute-done.51
  806.9 4.0 collective-permute-start.62
  816.3 4.0 fusion.48
  820.2 3.2 maximum_select_fusion.1
  823.5 3.3 copy.81
  (774 shorter events, 278.0 us)
Async XLA Ops:
  7.2 97.7 %all-gather.4.cloned.1.call-start = ((), (), s32[]{:S(2)}) async-start(), calls=%async_computation.6 | async-start | bytes 4587520 | tf_op jit(solution)/shard_map/all_gather | solution.py:326
  12.4 15.6 %collective-permute-start = (bf16[256,1792]{0,1:T(8,128)(2,1)S(1)}, bf16[256,1792]{0,1:T(8,128)(2,1)S(1)}, u32[]{:S(2)}, u32[]{:S(2)}) collective-permute-start(bf16[256,1792]{0,1:T(8,128)(2,1)S(1)} %bitcast_dynamic-update-slice_fusion), channel_id=1, source_target_pairs={{1,4},{3,6},{4,1},{6,3},{9,12},{11,14},{12,9},{14,11},{17,20},{19,... | collective-permute-start | bytes 2752520 | tf_op jit(solution)/shard_map/ppermute | solution.py:168
  29.0 215.3 %all-gather.6.cloned.1.call-start = ((), (), s32[]{:S(2)}) async-start(), calls=%async_computation.7 | async-start | bytes 9830400 | tf_op jit(solution)/shard_map/all_gather | solution.py:326
  30.4 50.7 %collective-permute-start.2 = (bf16[2,528]{1,0:T(2,128)(2,1)S(1)}, bf16[2,528]{1,0:T(2,128)(2,1)S(1)}, u32[]{:S(2)}, u32[]{:S(2)}) collective-permute-start(bf16[2,528]{1,0:T(2,128)(2,1)S(1)} %copy-done.122), channel_id=1, source_target_pairs={{0,4},{4,0},{1,5},{5,1},{2,6},{6,2},{3,7},{7,3},{8,12},{12,8},{9,1... | collective-permute-start | bytes 6344 | tf_op jit(solution)/shard_map/ppermute | solution.py:336
  39.9 37.8 %collective-permute-start.8 = (bf16[256,3840]{1,0:T(8,128)(2,1)}, bf16[256,3840]{1,0:T(8,128)(2,1)}, u32[]{:S(2)}, u32[]{:S(2)}) collective-permute-start(bf16[256,3840]{1,0:T(8,128)(2,1)} %pad_maximum_fusion.11), channel_id=1, source_target_pairs={{1,4},{3,6},{4,1},{6,3},{9,12},{11,14},{12,9},{14,11},{17,20},{19,... | collective-permute-start | bytes 5898248 | tf_op jit(solution)/shard_map/ppermute | solution.py:168
  44.9 60.8 %collective-permute-start.1 = (bf16[256,2048]{1,0:T(8,128)(2,1)S(1)}, bf16[256,2048]{1,0:T(8,128)(2,1)S(1)}, u32[]{:S(2)}, u32[]{:S(2)}) collective-permute-start(bf16[256,2048]{1,0:T(8,128)(2,1)S(1)} %maximum_select_fusion.4), channel_id=1, source_target_pairs={{0,4},{1,5},{2,6},{3,7},{4,0},{5,1},{6,2},{7,3},{8,12},{9,13},{10,... | collective-permute-start | bytes 3145736 | tf_op jit(solution)/shard_map/ppermute | solution.py:165
  81.0 305.0 %all-gather.8.cloned.1.call-start = ((), (), s32[]{:S(2)}) async-start(), calls=%async_computation.8 | async-start | bytes 9830400 | tf_op jit(solution)/shard_map/all_gather | solution.py:326
  94.8 22.7 %collective-permute-start.6 = (bf16[256,2048]{1,0:T(8,128)(2,1)}, bf16[256,2048]{1,0:T(8,128)(2,1)}, u32[]{:S(2)}, u32[]{:S(2)}) collective-permute-start(bf16[256,2048]{1,0:T(8,128)(2,1)} %maximum_select_fusion.6), channel_id=1, source_target_pairs={{0,4},{1,5},{2,6},{3,7},{4,0},{5,1},{6,2},{7,3},{8,12},{9,13},{10,... | collective-permute-start | bytes 3145736 | tf_op jit(solution)/shard_map/ppermute | solution.py:165
  97.4 44.0 %collective-permute-start.9 = (bf16[256,3840]{1,0:T(8,128)(2,1)}, bf16[256,3840]{1,0:T(8,128)(2,1)}, u32[]{:S(2)}, u32[]{:S(2)}) collective-permute-start(bf16[256,3840]{1,0:T(8,128)(2,1)} %pad_maximum_fusion.10), channel_id=1, source_target_pairs={{1,4},{3,6},{4,1},{6,3},{9,12},{11,14},{12,9},{14,11},{17,20},{19,... | collective-permute-start | bytes 5898248 | tf_op jit(solution)/shard_map/ppermute | solution.py:168
  105.0 41.9 %collective-permute-start.7 = (bf16[1024,1792]{0,1:T(8,128)(2,1)}, bf16[1024,1792]{0,1:T(8,128)(2,1)}, u32[]{:S(2)}, u32[]{:S(2)}) collective-permute-start(bf16[1024,1792]{0,1:T(8,128)(2,1)} %all-gather.4.cloned.1.call-done), channel_id=1, source_target_pairs={{0,1},{1,0},{2,3},{3,2},{4,5},{5,4},{6,7},{7,6},{8,9},{9,8},{10,11... | collective-permute-start | bytes 11010056 | tf_op jit(solution)/shard_map/ppermute | solution.py:175
  244.3 12.8 %collective-permute-start.10 = (bf16[1024,3840]{1,0:T(8,128)(2,1)}, bf16[1024,3840]{1,0:T(8,128)(2,1)}, u32[]{:S(2)}, u32[]{:S(2)}) collective-permute-start(bf16[1024,3840]{1,0:T(8,128)(2,1)} %all-gather.6.cloned.1.call-done), channel_id=1, source_target_pairs={{0,1},{1,0},{2,3},{3,2},{4,5},{5,4},{6,7},{7,6},{8,9},{9,8},{10,11... | collective-permute-start | bytes 23592968 | tf_op jit(solution)/shard_map/ppermute | solution.py:175
  244.8 299.9 %reduce-scatter.9.cloned.1.call-start = ((), (), s32[]{:S(2)}) async-start(), calls=%async_computation.10 | async-start | bytes 3276800 | tf_op jit(solution)/shard_map/reduce_scatter | solution.py:192
  386.1 13.3 %collective-permute-start.11 = (bf16[1024,3840]{1,0:T(8,128)(2,1)}, bf16[1024,3840]{1,0:T(8,128)(2,1)S(1)}, u32[]{:S(2)}, u32[]{:S(2)}) collective-permute-start(bf16[1024,3840]{1,0:T(8,128)(2,1)} %all-gather.8.cloned.1.call-done), channel_id=1, source_target_pairs={{0,1},{1,0},{2,3},{3,2},{4,5},{5,4},{6,7},{7,6},{8,9},{9,8},{10,11... | collective-permute-start | bytes 23592968 | tf_op jit(solution)/shard_map/ppermute | solution.py:175
  412.7 29.6 %collective-permute-start.15 = (bf16[1024,2560]{1,0:T(8,128)(2,1)}, bf16[1024,2560]{1,0:T(8,128)(2,1)}, u32[]{:S(2)}, u32[]{:S(2)}) collective-permute-start(bf16[1024,2560]{1,0:T(8,128)(2,1)} %convolution_convert_fusion.1), channel_id=1, source_target_pairs={{0,1},{1,0},{2,3},{3,2},{4,5},{5,4},{6,7},{7,6},{8,9},{9,8},{10,11... | collective-permute-start | bytes 15728648 | tf_op jit(solution)/shard_map/ppermute | solution.py:175
  416.0 148.3 %reduce-scatter.7.cloned.1.call-start = ((), (), s32[]{:S(2)}) async-start(), calls=%async_computation.9 | async-start | bytes 6553600 | tf_op jit(solution)/shard_map/reduce_scatter | solution.py:192
  433.3 16.5 %collective-permute-start.14 = (bf16[128,2048]{1,0:T(8,128)(2,1)}, bf16[128,2048]{1,0:T(8,128)(2,1)}, u32[]{:S(2)}, u32[]{:S(2)}) collective-permute-start(bf16[128,2048]{1,0:T(8,128)(2,1)} %get-tuple-element.252), channel_id=1, source_target_pairs={{0,6},{1,7},{2,4},{3,5},{4,2},{5,3},{6,0},{7,1},{8,14},{9,15},{10,... | collective-permute-start | bytes 1572872 | tf_op jit(solution)/shard_map/ppermute | solution.py:165
  434.4 25.2 %collective-permute-start.12 = (bf16[128,2048]{1,0:T(8,128)(2,1)}, bf16[128,2048]{1,0:T(8,128)(2,1)}, u32[]{:S(2)}, u32[]{:S(2)}) collective-permute-start(bf16[128,2048]{1,0:T(8,128)(2,1)} %get-tuple-element.253), channel_id=1, source_target_pairs={{0,2},{1,3},{2,0},{3,1},{4,6},{5,7},{6,4},{7,5},{8,10},{9,11},{10,... | collective-permute-start | bytes 1572872 | tf_op jit(solution)/shard_map/ppermute | solution.py:165
  434.7 24.9 %collective-permute-start.13 = (bf16[128,2048]{1,0:T(8,128)(2,1)}, bf16[128,2048]{1,0:T(8,128)(2,1)}, u32[]{:S(2)}, u32[]{:S(2)}) collective-permute-start(bf16[128,2048]{1,0:T(8,128)(2,1)} %get-tuple-element.254), channel_id=1, source_target_pairs={{0,4},{1,5},{2,6},{3,7},{4,0},{5,1},{6,2},{7,3},{8,12},{9,13},{10,... | collective-permute-start | bytes 1572872 | tf_op jit(solution)/shard_map/ppermute | solution.py:165
  459.6 159.8 %reduce-scatter.11.cloned.1.call-start = ((), (), s32[]{:S(2)}) async-start(), calls=%async_computation.11 | async-start | bytes 2293760 | tf_op jit(solution)/shard_map/reduce_scatter | solution.py:192
  463.6 14.0 %collective-permute-start.18 = (bf16[128,2048]{1,0:T(8,128)(2,1)S(1)}, bf16[128,2048]{1,0:T(8,128)(2,1)S(1)}, u32[]{:S(2)}, u32[]{:S(2)}) collective-permute-start(bf16[128,2048]{1,0:T(8,128)(2,1)S(1)} %get-tuple-element.232), channel_id=1, source_target_pairs={{0,6},{1,7},{2,4},{3,5},{4,2},{5,3},{6,0},{7,1},{8,14},{9,15},{10,... | collective-permute-start | bytes 1572872 | tf_op jit(solution)/shard_map/ppermute | solution.py:165
  464.8 23.1 %collective-permute-start.17 = (bf16[128,2048]{1,0:T(8,128)(2,1)S(1)}, bf16[128,2048]{1,0:T(8,128)(2,1)S(1)}, u32[]{:S(2)}, u32[]{:S(2)}) collective-permute-start(bf16[128,2048]{1,0:T(8,128)(2,1)S(1)} %get-tuple-element.232), channel_id=1, source_target_pairs={{0,4},{1,5},{2,6},{3,7},{4,0},{5,1},{6,2},{7,3},{8,12},{9,13},{10,... | collective-permute-start | bytes 1572872 | tf_op jit(solution)/shard_map/ppermute | solution.py:165
  465.1 24.6 %collective-permute-start.16 = (bf16[128,2048]{1,0:T(8,128)(2,1)S(1)}, bf16[128,2048]{1,0:T(8,128)(2,1)S(1)}, u32[]{:S(2)}, u32[]{:S(2)}) collective-permute-start(bf16[128,2048]{1,0:T(8,128)(2,1)S(1)} %get-tuple-element.232), channel_id=1, source_target_pairs={{0,2},{1,3},{2,0},{3,1},{4,6},{5,7},{6,4},{7,5},{8,10},{9,11},{10,... | collective-permute-start | bytes 1572872 | tf_op jit(solution)/shard_map/ppermute | solution.py:165
  509.6 14.2 %collective-permute-start.21 = (bf16[128,2048]{1,0:T(8,128)(2,1)S(1)}, bf16[128,2048]{1,0:T(8,128)(2,1)S(1)}, u32[]{:S(2)}, u32[]{:S(2)}) collective-permute-start(bf16[128,2048]{1,0:T(8,128)(2,1)S(1)} %get-tuple-element.249), channel_id=1, source_target_pairs={{0,6},{1,7},{2,4},{3,5},{4,2},{5,3},{6,0},{7,1},{8,14},{9,15},{10,... | collective-permute-start | bytes 1572872 | tf_op jit(solution)/shard_map/ppermute | solution.py:165
  510.7 25.0 %collective-permute-start.19 = (bf16[128,2048]{1,0:T(8,128)(2,1)S(1)}, bf16[128,2048]{1,0:T(8,128)(2,1)S(1)}, u32[]{:S(2)}, u32[]{:S(2)}) collective-permute-start(bf16[128,2048]{1,0:T(8,128)(2,1)S(1)} %get-tuple-element.250), channel_id=1, source_target_pairs={{0,2},{1,3},{2,0},{3,1},{4,6},{5,7},{6,4},{7,5},{8,10},{9,11},{10,... | collective-permute-start | bytes 1572872 | tf_op jit(solution)/shard_map/ppermute | solution.py:165
  511.0 24.7 %collective-permute-start.20 = (bf16[128,2048]{1,0:T(8,128)(2,1)S(1)}, bf16[128,2048]{1,0:T(8,128)(2,1)S(1)}, u32[]{:S(2)}, u32[]{:S(2)}) collective-permute-start(bf16[128,2048]{1,0:T(8,128)(2,1)S(1)} %get-tuple-element.251), channel_id=1, source_target_pairs={{0,4},{1,5},{2,6},{3,7},{4,0},{5,1},{6,2},{7,3},{8,12},{9,13},{10,... | collective-permute-start | bytes 1572872 | tf_op jit(solution)/shard_map/ppermute | solution.py:165
  538.0 14.4 %collective-permute-start.26 = (bf16[128,2048]{1,0:T(8,128)(2,1)}, bf16[128,2048]{1,0:T(8,128)(2,1)}, u32[]{:S(2)}, u32[]{:S(2)}) collective-permute-start(bf16[128,2048]{1,0:T(8,128)(2,1)} %get-tuple-element.227), channel_id=1, source_target_pairs={{0,6},{1,7},{2,4},{3,5},{4,2},{5,3},{6,0},{7,1},{8,14},{9,15},{10,... | collective-permute-start | bytes 1572872 | tf_op jit(solution)/shard_map/ppermute | solution.py:165
  539.0 23.4 %collective-permute-start.25 = (bf16[128,2048]{1,0:T(8,128)(2,1)}, bf16[128,2048]{1,0:T(8,128)(2,1)}, u32[]{:S(2)}, u32[]{:S(2)}) collective-permute-start(bf16[128,2048]{1,0:T(8,128)(2,1)} %get-tuple-element.227), channel_id=1, source_target_pairs={{0,4},{1,5},{2,6},{3,7},{4,0},{5,1},{6,2},{7,3},{8,12},{9,13},{10,... | collective-permute-start | bytes 1572872 | tf_op jit(solution)/shard_map/ppermute | solution.py:165
  539.3 24.9 %collective-permute-start.24 = (bf16[128,2048]{1,0:T(8,128)(2,1)}, bf16[128,2048]{1,0:T(8,128)(2,1)}, u32[]{:S(2)}, u32[]{:S(2)}) collective-permute-start(bf16[128,2048]{1,0:T(8,128)(2,1)} %get-tuple-element.227), channel_id=1, source_target_pairs={{0,2},{1,3},{2,0},{3,1},{4,6},{5,7},{6,4},{7,5},{8,10},{9,11},{10,... | collective-permute-start | bytes 1572872 | tf_op jit(solution)/shard_map/ppermute | solution.py:165
  544.7 112.9 %reduce-scatter.13.cloned.1.call-start = ((), (), s32[]{:S(2)}) async-start(), calls=%async_computation.12 | async-start | bytes 3276800 | tf_op jit(solution)/shard_map/reduce_scatter | solution.py:192
  565.7 26.5 %collective-permute-start.28 = (bf16[256,3840]{1,0:T(8,128)(2,1)S(1)}, bf16[256,3840]{1,0:T(8,128)(2,1)S(1)}, u32[]{:S(2)}, u32[]{:S(2)}) collective-permute-start(bf16[256,3840]{1,0:T(8,128)(2,1)S(1)} %constant_dynamic-update-slice_fusion.4), channel_id=1, source_target_pairs={{1,4},{3,6},{4,1},{6,3},{9,12},{11,14},{12,9},{14,11},{17,20},{19,... | collective-permute-start | bytes 5898248 | tf_op jit(solution)/shard_map/ppermute | solution.py:168
  571.7 22.0 %collective-permute-start.29 = (bf16[1024,1280]{1,0:T(8,128)(2,1)S(1)}, bf16[1024,1280]{1,0:T(8,128)(2,1)S(1)}, u32[]{:S(2)}, u32[]{:S(2)}) collective-permute-start(bf16[1024,1280]{1,0:T(8,128)(2,1)S(1)} %convolution_convert_fusion.2), channel_id=1, source_target_pairs={{0,1},{1,0},{2,3},{3,2},{4,5},{5,4},{6,7},{7,6},{8,9},{9,8},{10,11... | collective-permute-start | bytes 7864328 | tf_op jit(solution)/shard_map/ppermute | solution.py:175
  604.3 21.8 %collective-permute-start.33 = (bf16[1024,2560]{1,0:T(8,128)(2,1)}, bf16[1024,2560]{1,0:T(8,128)(2,1)}, u32[]{:S(2)}, u32[]{:S(2)}) collective-permute-start(bf16[1024,2560]{1,0:T(8,128)(2,1)} %convolution_convert_fusion), channel_id=1, source_target_pairs={{0,1},{1,0},{2,3},{3,2},{4,5},{5,4},{6,7},{7,6},{8,9},{9,8},{10,11... | collective-permute-start | bytes 15728648 | tf_op jit(solution)/shard_map/ppermute | solution.py:175
  605.1 178.1 %reduce-scatter.17.cloned.1.call-start = ((), (), s32[]{:S(2)}) async-start(), calls=%async_computation.14 | async-start | bytes 6553600 | tf_op jit(solution)/shard_map/reduce_scatter | solution.py:192
  622.1 14.2 %collective-permute-start.32 = (bf16[128,2048]{1,0:T(8,128)(2,1)}, bf16[128,2048]{1,0:T(8,128)(2,1)S(1)}, u32[]{:S(2)}, u32[]{:S(2)}) collective-permute-start(bf16[128,2048]{1,0:T(8,128)(2,1)} %get-tuple-element.246), channel_id=1, source_target_pairs={{0,6},{1,7},{2,4},{3,5},{4,2},{5,3},{6,0},{7,1},{8,14},{9,15},{10,... | collective-permute-start | bytes 1572872 | tf_op jit(solution)/shard_map/ppermute | solution.py:165
  623.4 23.5 %collective-permute-start.31 = (bf16[128,2048]{1,0:T(8,128)(2,1)}, bf16[128,2048]{1,0:T(8,128)(2,1)S(1)}, u32[]{:S(2)}, u32[]{:S(2)}) collective-permute-start(bf16[128,2048]{1,0:T(8,128)(2,1)} %get-tuple-element.247), channel_id=1, source_target_pairs={{0,4},{1,5},{2,6},{3,7},{4,0},{5,1},{6,2},{7,3},{8,12},{9,13},{10,... | collective-permute-start | bytes 1572872 | tf_op jit(solution)/shard_map/ppermute | solution.py:165
  623.6 24.8 %collective-permute-start.30 = (bf16[128,2048]{1,0:T(8,128)(2,1)}, bf16[128,2048]{1,0:T(8,128)(2,1)}, u32[]{:S(2)}, u32[]{:S(2)}) collective-permute-start(bf16[128,2048]{1,0:T(8,128)(2,1)} %get-tuple-element.248), channel_id=1, source_target_pairs={{0,2},{1,3},{2,0},{3,1},{4,6},{5,7},{6,4},{7,5},{8,10},{9,11},{10,... | collective-permute-start | bytes 1572872 | tf_op jit(solution)/shard_map/ppermute | solution.py:165
  650.0 13.2 %collective-permute-start.40 = (bf16[256,256]{0,1:T(8,128)(2,1)}, bf16[256,256]{0,1:T(8,128)(2,1)}, u32[]{:S(2)}, u32[]{:S(2)}) collective-permute-start(bf16[256,256]{0,1:T(8,128)(2,1)} %slice.802), channel_id=1, source_target_pairs={{0,3},{1,7},{2,1},{3,5},{4,2},{5,6},{6,0},{7,4},{8,11},{9,15},{10,... | collective-permute-start | bytes 393224 | tf_op jit(solution)/shard_map/ppermute | solution.py:172
  651.2 13.3 %collective-permute-start.39 = (bf16[256,256]{0,1:T(8,128)(2,1)}, bf16[256,256]{0,1:T(8,128)(2,1)}, u32[]{:S(2)}, u32[]{:S(2)}) collective-permute-start(bf16[256,256]{0,1:T(8,128)(2,1)} %slice.802), channel_id=1, source_target_pairs={{0,2},{1,6},{2,0},{3,4},{4,3},{5,7},{6,1},{7,5},{8,10},{9,14},{10,... | collective-permute-start | bytes 393224 | tf_op jit(solution)/shard_map/ppermute | solution.py:172
  653.0 13.6 %collective-permute-start.38 = (bf16[256,256]{0,1:T(8,128)(2,1)}, bf16[256,256]{0,1:T(8,128)(2,1)}, u32[]{:S(2)}, u32[]{:S(2)}) collective-permute-start(bf16[256,256]{0,1:T(8,128)(2,1)} %slice.802), channel_id=1, source_target_pairs={{0,1},{1,5},{2,3},{3,7},{4,0},{5,4},{6,2},{7,6},{8,9},{9,13},{10,1... | collective-permute-start | bytes 393224 | tf_op jit(solution)/shard_map/ppermute | solution.py:172
  653.0 18.6 %collective-permute-start.37 = (bf16[256,896]{0,1:T(8,128)(2,1)}, bf16[256,896]{0,1:T(8,128)(2,1)}, u32[]{:S(2)}, u32[]{:S(2)}) collective-permute-start(bf16[256,896]{0,1:T(8,128)(2,1)} %reduce-scatter.11.cloned.1.call-done), channel_id=1, source_target_pairs={{1,4},{3,6},{4,1},{6,3},{9,12},{11,14},{12,9},{14,11},{17,20},{19,... | collective-permute-start | bytes 1376264 | tf_op jit(solution)/shard_map/ppermute | solution.py:168
  657.6 146.5 %reduce-scatter.15.cloned.1.call-start = ((), (), s32[]{:S(2)}) async-start(), calls=%async_computation.13 | async-start | bytes 2293760 | tf_op jit(solution)/shard_map/reduce_scatter | solution.py:192
  661.3 20.6 %collective-permute-start.36 = (bf16[128,2048]{1,0:T(8,128)(2,1)S(1)}, bf16[128,2048]{1,0:T(8,128)(2,1)S(1)}, u32[]{:S(2)}, u32[]{:S(2)}) collective-permute-start(bf16[128,2048]{1,0:T(8,128)(2,1)S(1)} %get-tuple-element.225), channel_id=1, source_target_pairs={{0,6},{1,7},{2,4},{3,5},{4,2},{5,3},{6,0},{7,1},{8,14},{9,15},{10,... | collective-permute-start | bytes 1572872 | tf_op jit(solution)/shard_map/ppermute | solution.py:165
  663.2 22.4 %collective-permute-start.35 = (bf16[128,2048]{1,0:T(8,128)(2,1)S(1)}, bf16[128,2048]{1,0:T(8,128)(2,1)S(1)}, u32[]{:S(2)}, u32[]{:S(2)}) collective-permute-start(bf16[128,2048]{1,0:T(8,128)(2,1)S(1)} %get-tuple-element.225), channel_id=1, source_target_pairs={{0,4},{1,5},{2,6},{3,7},{4,0},{5,1},{6,2},{7,3},{8,12},{9,13},{10,... | collective-permute-start | bytes 1572872 | tf_op jit(solution)/shard_map/ppermute | solution.py:165
  664.6 22.8 %collective-permute-start.34 = (bf16[128,2048]{1,0:T(8,128)(2,1)S(1)}, bf16[128,2048]{1,0:T(8,128)(2,1)S(1)}, u32[]{:S(2)}, u32[]{:S(2)}) collective-permute-start(bf16[128,2048]{1,0:T(8,128)(2,1)S(1)} %get-tuple-element.225), channel_id=1, source_target_pairs={{0,2},{1,3},{2,0},{3,1},{4,6},{5,7},{6,4},{7,5},{8,10},{9,11},{10,... | collective-permute-start | bytes 1572872 | tf_op jit(solution)/shard_map/ppermute | solution.py:165
  666.7 34.3 %collective-permute-start.41 = (bf16[256,1280]{1,0:T(8,128)(2,1)S(1)}, bf16[256,1280]{1,0:T(8,128)(2,1)S(1)}, u32[]{:S(2)}, u32[]{:S(2)}) collective-permute-start(bf16[256,1280]{1,0:T(8,128)(2,1)S(1)} %copy-done.54), channel_id=1, source_target_pairs={{1,4},{3,6},{4,1},{6,3},{9,12},{11,14},{12,9},{14,11},{17,20},{19,... | collective-permute-start | bytes 1966088 | tf_op jit(solution)/shard_map/ppermute | solution.py:168
  697.7 15.3 %collective-permute-start.45 = (bf16[1024,320]{0,1:T(8,128)(2,1)}, bf16[1024,320]{0,1:T(8,128)(2,1)S(1)}, u32[]{:S(2)}, u32[]{:S(2)}) collective-permute-start(bf16[1024,320]{0,1:T(8,128)(2,1)} %convolution_convert_fusion.14), channel_id=1, source_target_pairs={{0,1},{1,0},{2,3},{3,2},{4,5},{5,4},{6,7},{7,6},{8,9},{9,8},{10,11... | collective-permute-start | bytes 1966088 | tf_op jit(solution)/shard_map/ppermute | solution.py:175
  703.4 10.1 %collective-permute-start.46 = (bf16[1024,576]{0,1:T(8,128)(2,1)S(1)}, bf16[1024,576]{0,1:T(8,128)(2,1)S(1)}, u32[]{:S(2)}, u32[]{:S(2)}) collective-permute-start(bf16[1024,576]{0,1:T(8,128)(2,1)S(1)} %convolution_convert_fusion.4), channel_id=1, source_target_pairs={{0,1},{1,0},{2,3},{3,2},{4,5},{5,4},{6,7},{7,6},{8,9},{9,8},{10,11... | collective-permute-start | bytes 3538952 | tf_op jit(solution)/shard_map/ppermute | solution.py:175
  708.3 14.3 %collective-permute-start.44 = (bf16[128,2048]{1,0:T(8,128)(2,1)S(1)}, bf16[128,2048]{1,0:T(8,128)(2,1)}, u32[]{:S(2)}, u32[]{:S(2)}) collective-permute-start(bf16[128,2048]{1,0:T(8,128)(2,1)S(1)} %get-tuple-element.243), channel_id=1, source_target_pairs={{0,6},{1,7},{2,4},{3,5},{4,2},{5,3},{6,0},{7,1},{8,14},{9,15},{10,... | collective-permute-start | bytes 1572872 | tf_op jit(solution)/shard_map/ppermute | solution.py:165
  710.1 24.4 %collective-permute-start.42 = (bf16[128,2048]{1,0:T(8,128)(2,1)S(1)}, bf16[128,2048]{1,0:T(8,128)(2,1)}, u32[]{:S(2)}, u32[]{:S(2)}) collective-permute-start(bf16[128,2048]{1,0:T(8,128)(2,1)S(1)} %get-tuple-element.244), channel_id=1, source_target_pairs={{0,2},{1,3},{2,0},{3,1},{4,6},{5,7},{6,4},{7,5},{8,10},{9,11},{10,... | collective-permute-start | bytes 1572872 | tf_op jit(solution)/shard_map/ppermute | solution.py:165
  711.3 23.2 %collective-permute-start.43 = (bf16[128,2048]{1,0:T(8,128)(2,1)S(1)}, bf16[128,2048]{1,0:T(8,128)(2,1)}, u32[]{:S(2)}, u32[]{:S(2)}) collective-permute-start(bf16[128,2048]{1,0:T(8,128)(2,1)S(1)} %get-tuple-element.245), channel_id=1, source_target_pairs={{0,4},{1,5},{2,6},{3,7},{4,0},{5,1},{6,2},{7,3},{8,12},{9,13},{10,... | collective-permute-start | bytes 1572872 | tf_op jit(solution)/shard_map/ppermute | solution.py:165
  741.3 31.1 %collective-permute-start.55 = (f32[2,4224]{1,0:T(2,128)S(1)}, f32[2,4224]{1,0:T(2,128)S(1)}, u32[]{:S(2)}, u32[]{:S(2)}) collective-permute-start(f32[2,4224]{1,0:T(2,128)S(1)} %pad_maximum_fusion.37), channel_id=1, source_target_pairs={{0,2},{1,3},{2,0},{3,1},{4,6},{5,7},{6,4},{7,5},{8,10},{9,11},{10,... | collective-permute-start | bytes 101384 | tf_op jit(solution)/shard_map/ppermute | solution.py:179
  743.1 14.0 %collective-permute-start.50 = (bf16[128,2048]{1,0:T(8,128)(2,1)}, bf16[128,2048]{1,0:T(8,128)(2,1)}, u32[]{:S(2)}, u32[]{:S(2)}) collective-permute-start(bf16[128,2048]{1,0:T(8,128)(2,1)} %get-tuple-element.240), channel_id=1, source_target_pairs={{0,6},{1,7},{2,4},{3,5},{4,2},{5,3},{6,0},{7,1},{8,14},{9,15},{10,... | collective-permute-start | bytes 1572872 | tf_op jit(solution)/shard_map/ppermute | solution.py:165
  743.9 24.1 %collective-permute-start.49 = (bf16[128,2048]{1,0:T(8,128)(2,1)}, bf16[128,2048]{1,0:T(8,128)(2,1)}, u32[]{:S(2)}, u32[]{:S(2)}) collective-permute-start(bf16[128,2048]{1,0:T(8,128)(2,1)} %get-tuple-element.241), channel_id=1, source_target_pairs={{0,4},{1,5},{2,6},{3,7},{4,0},{5,1},{6,2},{7,3},{8,12},{9,13},{10,... | collective-permute-start | bytes 1572872 | tf_op jit(solution)/shard_map/ppermute | solution.py:165
  745.2 24.2 %collective-permute-start.48 = (bf16[128,2048]{1,0:T(8,128)(2,1)}, bf16[128,2048]{1,0:T(8,128)(2,1)}, u32[]{:S(2)}, u32[]{:S(2)}) collective-permute-start(bf16[128,2048]{1,0:T(8,128)(2,1)} %get-tuple-element.242), channel_id=1, source_target_pairs={{0,2},{1,3},{2,0},{3,1},{4,6},{5,7},{6,4},{7,5},{8,10},{9,11},{10,... | collective-permute-start | bytes 1572872 | tf_op jit(solution)/shard_map/ppermute | solution.py:165
  746.9 33.8 %collective-permute-start.53 = (bf16[128,2048]{1,0:T(8,128)(2,1)}, bf16[128,2048]{1,0:T(8,128)(2,1)}, u32[]{:S(2)}, u32[]{:S(2)}) collective-permute-start(bf16[128,2048]{1,0:T(8,128)(2,1)} %broadcast_select_fusion.6), channel_id=1, source_target_pairs={{0,2},{1,3},{2,0},{3,1},{4,6},{5,7},{6,4},{7,5},{8,10},{9,11},{10,... | collective-permute-start | bytes 1572872 | tf_op jit(solution)/shard_map/ppermute | solution.py:165
  771.4 20.5 %collective-permute-start.51 = (bf16[128,2048]{1,0:T(8,128)(2,1)S(1)}, bf16[128,2048]{1,0:T(8,128)(2,1)S(1)}, u32[]{:S(2)}, u32[]{:S(2)}) collective-permute-start(bf16[128,2048]{1,0:T(8,128)(2,1)S(1)} %broadcast_select_fusion.7), channel_id=1, source_target_pairs={{0,2},{1,3},{2,0},{3,1},{4,6},{5,7},{6,4},{7,5},{8,10},{9,11},{10,... | collective-permute-start | bytes 1572872 | tf_op jit(solution)/shard_map/ppermute | solution.py:165
  772.5 20.1 %collective-permute-start.56 = (f32[2,4224]{1,0:T(2,128)S(1)}, f32[2,4224]{1,0:T(2,128)S(1)}, u32[]{:S(2)}, u32[]{:S(2)}) collective-permute-start(f32[2,4224]{1,0:T(2,128)S(1)} %fusion.235), channel_id=1, source_target_pairs={{0,4},{1,5},{2,6},{3,7},{4,0},{5,1},{6,2},{7,3},{8,12},{9,13},{10,... | collective-permute-start | bytes 101384 | tf_op jit(solution)/shard_map/ppermute | solution.py:179
  782.6 21.4 %collective-permute-start.54 = (bf16[256,2048]{1,0:T(8,128)(2,1)S(1)}, bf16[256,2048]{1,0:T(8,128)(2,1)}, u32[]{:S(2)}, u32[]{:S(2)}) collective-permute-start(bf16[256,2048]{1,0:T(8,128)(2,1)S(1)} %maximum_select_fusion.8), channel_id=1, source_target_pairs={{0,1},{1,0},{2,3},{3,2},{4,5},{5,4},{6,7},{7,6},{8,9},{9,8},{10,11... | collective-permute-start | bytes 3145736 | tf_op jit(solution)/shard_map/ppermute | solution.py:175
  783.3 19.3 %collective-permute-start.47 = (bf16[256,2560]{1,0:T(8,128)(2,1)}, bf16[256,2560]{1,0:T(8,128)(2,1)}, u32[]{:S(2)}, u32[]{:S(2)}) collective-permute-start(bf16[256,2560]{1,0:T(8,128)(2,1)} %reduce-scatter.17.cloned.1.call-done), channel_id=1, source_target_pairs={{1,4},{3,6},{4,1},{6,3},{9,12},{11,14},{12,9},{14,11},{17,20},{19,... | collective-permute-start | bytes 3932168 | tf_op jit(solution)/shard_map/ppermute | solution.py:168
  792.2 11.8 %collective-permute-start.52 = (bf16[256,2048]{1,0:T(8,128)(2,1)S(1)}, bf16[256,2048]{1,0:T(8,128)(2,1)}, u32[]{:S(2)}, u32[]{:S(2)}) collective-permute-start(bf16[256,2048]{1,0:T(8,128)(2,1)S(1)} %maximum_select_fusion.7), channel_id=1, source_target_pairs={{0,1},{1,0},{2,3},{3,2},{4,5},{5,4},{6,7},{7,6},{8,9},{9,8},{10,11... | collective-permute-start | bytes 3145736 | tf_op jit(solution)/shard_map/ppermute | solution.py:175
  805.7 22.4 %collective-permute-start.63 = (bf16[256,256]{0,1:T(8,128)(2,1)}, bf16[256,256]{0,1:T(8,128)(2,1)}, u32[]{:S(2)}, u32[]{:S(2)}) collective-permute-start(bf16[256,256]{0,1:T(8,128)(2,1)} %slice.873), channel_id=1, source_target_pairs={{0,3},{1,7},{2,1},{3,5},{4,2},{5,6},{6,0},{7,4},{8,11},{9,15},{10,... | collective-permute-start | bytes 393224 | tf_op jit(solution)/shard_map/ppermute | solution.py:172
  806.9 22.1 %collective-permute-start.62 = (bf16[256,256]{0,1:T(8,128)(2,1)}, bf16[256,256]{0,1:T(8,128)(2,1)}, u32[]{:S(2)}, u32[]{:S(2)}) collective-permute-start(bf16[256,256]{0,1:T(8,128)(2,1)} %slice.873), channel_id=1, source_target_pairs={{0,2},{1,6},{2,0},{3,4},{4,3},{5,7},{6,1},{7,5},{8,10},{9,14},{10,... | collective-permute-start | bytes 393224 | tf_op jit(solution)/shard_map/ppermute | solution.py:172
  810.9 19.1 %collective-permute-start.61 = (bf16[256,256]{0,1:T(8,128)(2,1)}, bf16[256,256]{0,1:T(8,128)(2,1)S(1)}, u32[]{:S(2)}, u32[]{:S(2)}) collective-permute-start(bf16[256,256]{0,1:T(8,128)(2,1)} %slice.873), channel_id=1, source_target_pairs={{0,1},{1,5},{2,3},{3,7},{4,0},{5,4},{6,2},{7,6},{8,9},{9,13},{10,1... | collective-permute-start | bytes 393224 | tf_op jit(solution)/shard_map/ppermute | solution.py:172
  810.9 19.1 %collective-permute-start.60 = (bf16[256,896]{0,1:T(8,128)(2,1)}, bf16[256,896]{0,1:T(8,128)(2,1)}, u32[]{:S(2)}, u32[]{:S(2)}) collective-permute-start(bf16[256,896]{0,1:T(8,128)(2,1)} %reduce-scatter.15.cloned.1.call-done), channel_id=1, source_target_pairs={{1,4},{3,6},{4,1},{6,3},{9,12},{11,14},{12,9},{14,11},{17,20},{19,... | collective-permute-start | bytes 1376264 | tf_op jit(solution)/shard_map/ppermute | solution.py:168
  (176 other events, 1107.0 us)
Sparse Core Ops, SparseCore 0:
  29.1 73.5 all-gather.3
  104.9 139.3 all-gather.5
  246.4 139.2 all-gather.7
  416.1 48.9 reduce-scatter.8
  467.2 93.6 reduce-scatter.6
  563.1 39.6 reduce-scatter.10
  605.7 51.2 reduce-scatter.12
  659.3 93.6 reduce-scatter.16
  755.9 39.6 reduce-scatter.14
